TPU v7x, 32 devices: a whole 2x2x4 slice. The times are simulated.
32 devices in a mesh: section: 2 (over x), seq: 4 (over y, core), blk: 4 (over z).
Axes of the slice: x: 2, y: 2, z: 4, core: 2. Of those that a mesh axis runs over, the one named last changes fastest.
Arguments:
- inputs: bfloat16 [2, 1, 1024, 1536], P(None, None, ('seq', 'blk')), may hold values from -6 to 6
- cotangent: bfloat16 [2, 1, 1024, 1536], P(None, None, ('seq', 'blk')), may hold values from -6 to 6
- doc_lengths: int32 [2, 1, 4], replicated, may hold values from 0 to 1024, as said below
- attention_gain: bfloat16 [2, 1536], P('section', 'blk'), may hold values from 0.099609375 to 1.8984375
- w_query: bfloat16 [2, 1536, 1536], P('section', 'blk'), may hold values from -0.15625 to 0.15625
- w_key: bfloat16 [2, 1536, 768], P('section', 'blk'), may hold values from -0.15625 to 0.15625
- w_value: bfloat16 [2, 1536, 768], P('section', 'blk'), may hold values from -0.15625 to 0.15625
- w_output: bfloat16 [2, 1536, 1536], P('section', 'blk'), may hold values from -1.75 to 1.75
- mlp_gain: bfloat16 [2, 1536], P('section', 'blk'), may hold values from 0.099609375 to 1.8984375
- w_gate: bfloat16 [2, 1536, 4096], P('section', 'blk'), may hold values from -0.15625 to 0.15625
- w_up: bfloat16 [2, 1536, 4096], P('section', 'blk'), may hold values from -0.15625 to 0.15625
- w_down: bfloat16 [2, 4096, 1536], P('section', 'blk'), may hold values from -0.09375 to 0.09375
Outputs:
- activations: bfloat16 [2, 2, 1, 1024, 1536], P('section', None, None, ('seq', 'blk'))
- input_grads: bfloat16 [2, 2, 1, 1024, 1536], P('section', None, None, ('seq', 'blk'))
- grad_attention_gain: float32 [2, 1536], P('section', 'blk')
- grad_w_query: float32 [2, 1536, 1536], P('section', 'blk')
- grad_w_key: float32 [2, 1536, 768], P('section', 'blk')
- grad_w_value: float32 [2, 1536, 768], P('section', 'blk')
- grad_w_output: float32 [2, 1536, 1536], P('section', 'blk')
- grad_mlp_gain: float32 [2, 1536], P('section', 'blk')
- grad_w_gate: float32 [2, 1536, 4096], P('section', 'blk')
- grad_w_up: float32 [2, 1536, 4096], P('section', 'blk')
- grad_w_down: float32 [2, 4096, 1536], P('section', 'blk')
Inputs may be any that keep to these rules, and one draw needn't show every extreme that they name: `doc_lengths`: the 4 lengths of a sequence sum to 1024. Of all sequences, one drawn from the seed is a single document (1024 then zeros); in every other sequence each length is 1 or more.
All inputs are finite; a program needn't handle non-finite values.
Results may differ from a plain program's by a relative error of at most 0.028.
Values may be sent and summed in bfloat16 or wider, within the bound.
A program may use at most 448 MiB of HBM per device.

v0:
```python
import jax
import jax.numpy as jnp
from jax import lax
from jax.sharding import PartitionSpec as P

HEADS = 16
KV_HEADS = 8
HEAD_DIM = 96


EPS = 1e-05
THETA = 100000.0
MASKED = -1e30


def passed_along(value, axis, steps):
    count = lax.axis_size(axis)
    first, last = (max(0, -steps), min(count, count - steps))
    return lax.ppermute(value, axis, [(source, source + steps) for source in range(first, last)])


def shortened(value):
    return jax.tree.map(lambda a: a.astype(jnp.bfloat16) if a.dtype == jnp.float32 else a, value)


def product(left_side, right_side):
    return jnp.dot(left_side, right_side, preferred_element_type=jnp.float32)


def back_product(left_side, right_side):
    return lax.dot_general(
        left_side, right_side, (((1,), (1,)), ((), ())), preferred_element_type=jnp.float32
    )


def doc_info(lengths, token_index):
    doc_ends = jnp.cumsum(lengths, axis=-1)
    passed = (doc_ends[..., None, :] <= token_index[..., None]).astype(jnp.int32)
    segment = jnp.sum(passed, axis=-1)
    offset = jnp.sum(passed * lengths[..., None, :], axis=-1)
    return (segment, token_index - offset)


def rotate(field_in, position, turn_sign):
    half_dim = field_in.shape[-1] // 2
    frequency = THETA ** (-2.0 * jnp.arange(half_dim, dtype=jnp.float32) / field_in.shape[-1])
    angles = position.astype(jnp.float32)[:, None] * frequency
    cosine = jnp.cos(angles)[:, None, :]
    sine_part = turn_sign * jnp.sin(angles)[:, None, :]
    first_half = field_in[..., :half_dim]
    second_half = field_in[..., half_dim:]
    return jnp.concatenate(
        [
            first_half * cosine - second_half * sine_part,
            second_half * cosine + first_half * sine_part,
        ],
        axis=-1,
    )


def rms_forward(field_in, gain_row):
    inv_root = lax.rsqrt(jnp.mean(field_in * field_in, axis=-1, keepdims=True) + EPS)
    return (field_in * inv_root * gain_row, inv_root)


def rms_backward(field_in, gain_row, inv_root, grad_normed):
    scaled = gain_row * grad_normed
    grad_field = inv_root * scaled - field_in * inv_root**3 * jnp.mean(
        scaled * field_in, axis=-1, keepdims=True
    )
    return (grad_field, grad_normed * field_in * inv_root)


def token_place(block_id, row_ids, per_device, blk_count):
    return (row_ids // per_device * blk_count + block_id) * per_device + row_ids % per_device


def masks_for(lengths, blk_index, per_device, blk_count, seq_count):
    block_tokens = seq_count * per_device
    row_ids = jnp.arange(block_tokens, dtype=jnp.int32)
    query_index = token_place(blk_index, row_ids, per_device, blk_count)
    all_ids = jnp.arange(blk_count * block_tokens, dtype=jnp.int32)
    key_index = token_place(all_ids // block_tokens, all_ids % block_tokens, per_device, blk_count)
    query_seg, _ = doc_info(lengths, query_index)
    key_seg, _ = doc_info(lengths, key_index)
    return (query_index, key_index, query_seg, key_seg)


def head_scores(queries, key_rows, allowed, kv_local):
    grouped = queries.reshape(queries.shape[0], kv_local, -1, HEAD_DIM)
    key_heads = key_rows.reshape(key_rows.shape[0], kv_local, HEAD_DIM)
    scores = jnp.einsum(
        "rkgd,lkd->kgrl", grouped, key_heads, preferred_element_type=jnp.float32
    ) * HEAD_DIM ** (-0.5)
    return (jnp.where(allowed, scores, MASKED), grouped, key_heads)


def attend_forward(operands, query_index, key_index, kv_local):
    queries, key_rows, value_rows, query_seg, key_seg = operands
    allowed = (query_seg[:, None] == key_seg[None, :]) & (
        key_index[None, :] <= query_index[:, None]
    )
    scores, grouped, key_heads = head_scores(queries, key_rows, allowed, kv_local)
    row_top = jnp.max(scores, axis=-1, keepdims=True)
    log_total = row_top + jnp.log(jnp.sum(jnp.exp(scores - row_top), axis=-1, keepdims=True))
    weights_low = jnp.exp(scores - log_total).astype(jnp.bfloat16)
    value_heads = value_rows.reshape(value_rows.shape[0], kv_local, HEAD_DIM)
    mixed_heads = jnp.einsum(
        "kgrl,lkd->rkgd", weights_low, value_heads, preferred_element_type=jnp.float32
    )
    return (mixed_heads.reshape(queries.shape).astype(jnp.bfloat16), log_total)


def attend_backward(operands, query_index, key_index, kv_local):
    queries, key_rows, value_rows, grad_mixed, log_total, query_seg, key_seg = operands
    allowed = (query_seg[:, None] == key_seg[None, :]) & (
        key_index[None, :] <= query_index[:, None]
    )
    scores, grouped, key_heads = head_scores(queries, key_rows, allowed, kv_local)
    attn_probs = jnp.exp(scores - log_total)
    value_heads = value_rows.reshape(value_rows.shape[0], kv_local, HEAD_DIM)
    grad_heads = grad_mixed.reshape(grouped.shape)
    grad_values = jnp.einsum(
        "kgrl,rkgd->lkd",
        attn_probs.astype(jnp.bfloat16),
        grad_heads,
        preferred_element_type=jnp.float32,
    )
    grad_probs = jnp.einsum(
        "rkgd,lkd->kgrl", grad_heads, value_heads, preferred_element_type=jnp.float32
    )
    centre = jnp.sum(attn_probs * grad_probs, axis=-1, keepdims=True)
    grad_scores = (attn_probs * (grad_probs - centre)).astype(jnp.bfloat16)
    grad_queries = jnp.einsum(
        "kgrl,lkd->rkgd", grad_scores, key_heads, preferred_element_type=jnp.float32
    ) * HEAD_DIM ** (-0.5)
    grad_keys = jnp.einsum(
        "kgrl,rkgd->lkd", grad_scores, grouped, preferred_element_type=jnp.float32
    ) * HEAD_DIM ** (-0.5)
    return (
        grad_queries.reshape(queries.shape).astype(jnp.bfloat16),
        grad_keys.reshape(key_rows.shape),
        grad_values.reshape(value_rows.shape),
    )


def layer_forward(section_in, lengths, weights, placing):
    shard_id, blk_index, seq_count, blk_count = placing
    gain_attn, w_query, w_key, w_value, w_output, gain_mlp, w_gate, w_up, w_down = weights
    seqs_here, per_device, width = section_in.shape
    token_rows = seqs_here * per_device
    copies = max(1, seq_count // KV_HEADS)
    kv_local = KV_HEADS * copies // seq_count
    token_index = shard_id * per_device + jnp.arange(per_device, dtype=jnp.int32)
    _, position = doc_info(lengths, token_index)
    position = position.reshape(token_rows)
    flat_in = section_in.reshape(token_rows, width)
    normed, inv_first = rms_forward(flat_in, gain_attn.astype(jnp.float32))
    normed_low = normed.astype(jnp.bfloat16)
    query_pre = product(normed_low, w_query).reshape(token_rows, HEADS, HEAD_DIM)
    key_pre = product(normed_low, w_key).reshape(token_rows, KV_HEADS, HEAD_DIM)
    value_pre = product(normed_low, w_value).reshape(token_rows, KV_HEADS, HEAD_DIM)
    query_rot = (
        rotate(query_pre, position, 1.0).astype(jnp.bfloat16).reshape(seqs_here, per_device, width)
    )
    key_rot = rotate(key_pre, position, 1.0).astype(jnp.bfloat16)
    spread_shape = (token_rows, KV_HEADS, copies, HEAD_DIM)
    key_rep = jnp.broadcast_to(key_rot[:, :, None, :], spread_shape).reshape(
        seqs_here, per_device, -1
    )
    value_rep = jnp.broadcast_to(
        value_pre.astype(jnp.bfloat16)[:, :, None, :], spread_shape
    ).reshape(seqs_here, per_device, -1)
    heads_query, heads_key, heads_value = (
        lax.all_to_all(query_rot, "seq", split_axis=2, concat_axis=1, tiled=True),
        lax.all_to_all(key_rep, "seq", split_axis=2, concat_axis=1, tiled=True),
        lax.all_to_all(value_rep, "seq", split_axis=2, concat_axis=1, tiled=True),
    )
    keys_all, values_all = (
        lax.all_gather(heads_key, "blk", axis=1, tiled=True),
        lax.all_gather(heads_value, "blk", axis=1, tiled=True),
    )
    query_index, key_index, query_seg, key_seg = masks_for(
        lengths, blk_index, per_device, blk_count, seq_count
    )
    heads_mixed, log_total = lax.map(
        lambda operands: attend_forward(operands, query_index, key_index, kv_local),
        (heads_query, keys_all, values_all, query_seg, key_seg),
    )
    token_mixed = lax.all_to_all(
        heads_mixed, "seq", split_axis=1, concat_axis=2, tiled=True
    ).reshape(token_rows, width)
    hidden = flat_in + product(token_mixed, w_output)
    normed_mlp, inv_second = rms_forward(hidden, gain_mlp.astype(jnp.float32))
    normed_mlp_low = normed_mlp.astype(jnp.bfloat16)
    gate_pre = product(normed_mlp_low, w_gate)
    up_pre = product(normed_mlp_low, w_up)
    act_low = (jax.nn.silu(gate_pre) * up_pre).astype(jnp.bfloat16)
    result = hidden + product(act_low, w_down)
    saved_state = (
        flat_in,
        normed_low,
        inv_first,
        position,
        heads_query,
        keys_all,
        values_all,
        log_total,
        token_mixed,
        hidden,
        inv_second,
        normed_mlp_low,
        gate_pre,
        up_pre,
        act_low,
        lengths,
    )
    return (result.reshape(section_in.shape), saved_state)


def layer_backward(upstream, saved_state, weights, placing):
    shard_id, blk_index, seq_count, blk_count = placing
    gain_attn, w_query, w_key, w_value, w_output, gain_mlp, w_gate, w_up, w_down = weights
    (
        flat_in,
        normed_low,
        inv_first,
        position,
        heads_query,
        keys_all,
        values_all,
        log_total,
        token_mixed,
        hidden,
        inv_second,
        normed_mlp_low,
        gate_pre,
        up_pre,
        act_low,
        lengths,
    ) = saved_state
    seqs_here, per_device, width = upstream.shape
    token_rows = seqs_here * per_device
    copies = max(1, seq_count // KV_HEADS)
    kv_local = KV_HEADS * copies // seq_count
    grad_rows = upstream.reshape(token_rows, width)
    grad_out_low = grad_rows.astype(jnp.bfloat16)
    grad_act = back_product(grad_out_low, w_down)
    gate_sigmoid = jax.nn.sigmoid(gate_pre)
    grad_gate_low = (
        grad_act * up_pre * gate_sigmoid * (1.0 + gate_pre * (1.0 - gate_sigmoid))
    ).astype(jnp.bfloat16)
    grad_up_low = (grad_act * jax.nn.silu(gate_pre)).astype(jnp.bfloat16)
    grad_normed_mlp = back_product(grad_gate_low, w_gate) + back_product(grad_up_low, w_up)
    grad_hidden_part, gain_mlp_terms = rms_backward(
        hidden, gain_mlp.astype(jnp.float32), inv_second, grad_normed_mlp
    )
    grad_hidden = grad_rows + grad_hidden_part
    grad_branch_low = grad_hidden.astype(jnp.bfloat16)
    grad_mixed_low = (
        back_product(grad_branch_low, w_output)
        .astype(jnp.bfloat16)
        .reshape(seqs_here, per_device, width)
    )
    heads_grad = lax.all_to_all(grad_mixed_low, "seq", split_axis=2, concat_axis=1, tiled=True)
    query_index, key_index, query_seg, key_seg = masks_for(
        lengths, blk_index, per_device, blk_count, seq_count
    )
    grad_heads_query, grad_keys_all, grad_values_all = lax.map(
        lambda operands: attend_backward(operands, query_index, key_index, kv_local),
        (heads_query, keys_all, values_all, heads_grad, log_total, query_seg, key_seg),
    )
    grad_key_own, grad_value_own = (
        lax.psum_scatter(
            grad_keys_all.astype(jnp.bfloat16), "blk", scatter_dimension=1, tiled=True
        ).astype(jnp.float32),
        lax.psum_scatter(
            grad_values_all.astype(jnp.bfloat16), "blk", scatter_dimension=1, tiled=True
        ).astype(jnp.float32),
    )
    token_query, token_key, token_value = (
        lax.all_to_all(grad_heads_query, "seq", split_axis=1, concat_axis=2, tiled=True),
        lax.all_to_all(
            grad_key_own.astype(jnp.bfloat16), "seq", split_axis=1, concat_axis=2, tiled=True
        ),
        lax.all_to_all(
            grad_value_own.astype(jnp.bfloat16), "seq", split_axis=1, concat_axis=2, tiled=True
        ),
    )
    grad_key_sum = jnp.sum(
        token_key.astype(jnp.float32).reshape(token_rows, KV_HEADS, copies, HEAD_DIM), axis=2
    )
    grad_value_sum = jnp.sum(
        token_value.astype(jnp.float32).reshape(token_rows, KV_HEADS, copies, HEAD_DIM), axis=2
    )
    grad_query_low = (
        rotate(token_query.astype(jnp.float32).reshape(token_rows, HEADS, HEAD_DIM), position, -1.0)
        .astype(jnp.bfloat16)
        .reshape(token_rows, width)
    )
    grad_key_low = (
        rotate(grad_key_sum, position, -1.0)
        .astype(jnp.bfloat16)
        .reshape(token_rows, KV_HEADS * HEAD_DIM)
    )
    grad_value_low = grad_value_sum.astype(jnp.bfloat16).reshape(token_rows, KV_HEADS * HEAD_DIM)
    grad_normed = (
        back_product(grad_query_low, w_query)
        + back_product(grad_key_low, w_key)
        + back_product(grad_value_low, w_value)
    )
    grad_in_part, gain_attn_terms = rms_backward(
        flat_in, gain_attn.astype(jnp.float32), inv_first, grad_normed
    )
    grad_input = (grad_hidden + grad_in_part).reshape(upstream.shape)
    weight_rows = (
        gain_attn_terms,
        normed_low,
        grad_query_low,
        grad_key_low,
        grad_value_low,
        token_mixed,
        grad_branch_low,
        gain_mlp_terms,
        normed_mlp_low,
        grad_gate_low,
        grad_up_low,
        act_low,
        grad_out_low,
    )
    return (grad_input, weight_rows)


def weight_term(inputs_low, outputs_low):
    if outputs_low is None:
        return jnp.sum(inputs_low, axis=0)
    return lax.dot_general(
        inputs_low, outputs_low, (((0,), (0,)), ((), ())), preferred_element_type=jnp.float32
    )


def shards(
    inputs,
    cotangent,
    doc_lengths,
    attention_gain,
    w_query,
    w_key,
    w_value,
    w_output,
    mlp_gain,
    w_gate,
    w_up,
    w_down,
):
    at_first = lax.axis_index("section") == 0
    seq_count = lax.axis_size("seq")
    blk_count = lax.axis_size("blk")
    blk_index = lax.axis_index("blk")
    shard_id = lax.axis_index("seq") * blk_count + blk_index
    placing = (shard_id, blk_index, seq_count, blk_count)
    micro_count = inputs.shape[0]
    local_shards = (
        attention_gain[0],
        w_query[0],
        w_key[0],
        w_value[0],
        w_output[0],
        mlp_gain[0],
        w_gate[0],
        w_up[0],
        w_down[0],
    )
    weights = (
        lax.all_gather(local_shards[0], "blk", axis=0, tiled=True),
        lax.all_gather(local_shards[1], "blk", axis=0, tiled=True),
        lax.all_gather(local_shards[2], "blk", axis=0, tiled=True),
        lax.all_gather(local_shards[3], "blk", axis=0, tiled=True),
        lax.all_gather(local_shards[4], "blk", axis=0, tiled=True),
        lax.all_gather(local_shards[5], "blk", axis=0, tiled=True),
        lax.all_gather(local_shards[6], "blk", axis=0, tiled=True),
        lax.all_gather(local_shards[7], "blk", axis=0, tiled=True),
        lax.all_gather(local_shards[8], "blk", axis=0, tiled=True),
    )
    received = jnp.zeros(inputs.shape[1:], jnp.bfloat16)
    saved_states = []
    section_outs = []
    for tick_index in range(micro_count + 1):
        fresh_input = inputs[min(tick_index, micro_count - 1)]
        section_in = jnp.where(at_first, fresh_input, received).astype(jnp.float32)
        lengths = jnp.where(
            at_first,
            doc_lengths[min(tick_index, micro_count - 1)],
            doc_lengths[max(tick_index - 1, 0)],
        )
        result, saved_state = layer_forward(section_in, lengths, weights, placing)
        result_low = result.astype(jnp.bfloat16)
        if tick_index < micro_count:
            received = passed_along(result_low, "section", 1)
        saved_states.append(saved_state)
        section_outs.append(result_low)
    weights = (
        lax.all_gather(local_shards[0], "blk", axis=0, tiled=True),
        lax.all_gather(local_shards[1], "blk", axis=0, tiled=True),
        lax.all_gather(local_shards[2], "blk", axis=0, tiled=True),
        lax.all_gather(local_shards[3], "blk", axis=0, tiled=True),
        lax.all_gather(local_shards[4], "blk", axis=0, tiled=True),
        lax.all_gather(local_shards[5], "blk", axis=0, tiled=True),
        lax.all_gather(local_shards[6], "blk", axis=0, tiled=True),
        lax.all_gather(local_shards[7], "blk", axis=0, tiled=True),
        lax.all_gather(local_shards[8], "blk", axis=0, tiled=True),
    )
    back_in = jnp.zeros(cotangent.shape[1:], jnp.bfloat16)
    grad_outs = []
    row_sets = []
    for tick_index in range(micro_count + 1):
        saved_state = jax.tree.map(
            lambda first_pick, second_pick: jnp.where(at_first, first_pick, second_pick),
            saved_states[max(tick_index - 1, 0)],
            saved_states[min(tick_index + 1, micro_count)],
        )
        upstream = jnp.where(at_first, back_in, cotangent[min(tick_index, micro_count - 1)]).astype(
            jnp.float32
        )
        grad_input, weight_rows = layer_backward(upstream, saved_state, weights, placing)
        grad_low = grad_input.astype(jnp.bfloat16)
        if tick_index < micro_count:
            back_in = passed_along(grad_low, "section", -1)
        grad_outs.append(grad_low)
        row_sets.append(weight_rows)
    activations = jnp.stack(
        [
            jnp.where(at_first, section_outs[index_m], section_outs[index_m + 1])
            for index_m in range(micro_count)
        ]
    )[None]
    input_grads = jnp.stack(
        [
            jnp.where(at_first, grad_outs[index_m + 1], grad_outs[index_m])
            for index_m in range(micro_count)
        ]
    )[None]
    picked = [
        jax.tree.map(
            lambda first_pick, second_pick: jnp.where(at_first, first_pick, second_pick),
            row_sets[index_m + 1],
            row_sets[index_m],
        )
        for index_m in range(micro_count)
    ]
    merged = jax.tree.map(lambda *pieces: jnp.concatenate(pieces, axis=0), *picked)
    (
        gain_attn_terms,
        normed_low,
        grad_query_low,
        grad_key_low,
        grad_value_low,
        token_mixed,
        grad_branch_low,
        gain_mlp_terms,
        normed_mlp_low,
        grad_gate_low,
        grad_up_low,
        act_low,
        grad_out_low,
    ) = merged
    grad_pairs = (
        (gain_attn_terms, None),
        (normed_low, grad_query_low),
        (normed_low, grad_key_low),
        (normed_low, grad_value_low),
        (token_mixed, grad_branch_low),
        (gain_mlp_terms, None),
        (normed_mlp_low, grad_gate_low),
        (normed_mlp_low, grad_up_low),
        (act_low, grad_out_low),
    )
    shares = tuple(
        (
            lax.psum_scatter(
                weight_term(left_side, right_side).astype(jnp.bfloat16),
                "blk",
                scatter_dimension=0,
                tiled=True,
            ).astype(jnp.float32)
            for left_side, right_side in grad_pairs
        )
    )
    shares = jax.tree.map(lambda part: part.astype(jnp.float32), lax.psum(shortened(shares), "seq"))
    return (
        activations,
        input_grads,
        shares[0][None],
        shares[1][None],
        shares[2][None],
        shares[3][None],
        shares[4][None],
        shares[5][None],
        shares[6][None],
        shares[7][None],
        shares[8][None],
    )


def solution(mesh):
    placed = (
        P(None, None, ("seq", "blk"), None),
        P(None, None, ("seq", "blk"), None),
        P(),
        P("section", "blk"),
        P("section", "blk", None),
        P("section", "blk", None),
        P("section", "blk", None),
        P("section", "blk", None),
        P("section", "blk"),
        P("section", "blk", None),
        P("section", "blk", None),
        P("section", "blk", None),
    )
    return jax.shard_map(
        shards,
        mesh=mesh,
        in_specs=placed,
        out_specs=(
            P("section", None, None, ("seq", "blk"), None),
            P("section", None, None, ("seq", "blk"), None),
            P("section", "blk"),
            P("section", "blk", None),
            P("section", "blk", None),
            P("section", "blk", None),
            P("section", "blk", None),
            P("section", "blk"),
            P("section", "blk", None),
            P("section", "blk", None),
            P("section", "blk", None),
        ),
        check_vma=False,
    )
```

profile of v0, /device:TPU:18, one launch (start us, length us, event | category | flops | bytes accessed | tf_op | source)
XLA Modules:
  0.0 3036.0 jit_solution(10426564475446724185)
XLA Ops:
  27.9 32.1 %all-gather.17.cloned.1.call-done = bf16[1,1536,768]{2,1,0:T(8,128)(2,1)} async-done(((bf16[1,384,768]{2,1,0:T(8,128)(2,1)}), bf16[1,1536,768]{2,1,0:T(8,128)(2,1)}) %all-gather.17.cloned.1.call-update) | async-done | bytes 2359312 | tf_op jit(solution)/shard_map/all_gather | solution.py:378
  71.2 39.7 %all-gather.19.cloned.1.call-done = bf16[1,1536,768]{2,1,0:T(8,128)(2,1)} async-done(((bf16[1,384,768]{2,1,0:T(8,128)(2,1)}), bf16[1,1536,768]{2,1,0:T(8,128)(2,1)}) %all-gather.19.cloned.1.call-update) | async-done | bytes 2359312 | tf_op jit(solution)/shard_map/all_gather | solution.py:377
  127.0 22.2 all_gather.56
  154.4 54.4 %all-gather.21.cloned.1.call-done = bf16[1,1536,1536]{2,1,0:T(8,128)(2,1)} async-done(((bf16[1,384,1536]{2,1,0:T(8,128)(2,1)}), bf16[1,1536,1536]{2,1,0:T(8,128)(2,1)}) %all-gather.21.cloned.1.call-update) | async-done | bytes 4718608 | tf_op jit(solution)/shard_map/all_gather | solution.py:376
  239.3 23.2 all_gather.58
  286.2 11.5 all-gather.5
  309.9 214.4 %all-gather.25.cloned.1.call-done = bf16[1,1536,4096]{2,1,0:T(8,128)(2,1)} async-done(((bf16[1,384,4096]{2,1,0:T(8,128)(2,1)}), bf16[1,1536,4096]{2,1,0:T(8,128)(2,1)}) %all-gather.25.cloned.1.call-update) | async-done | bytes 12582928 | tf_op jit(solution)/shard_map/all_gather | solution.py:381
  532.2 210.0 %all-gather.27.cloned.1.call-done = bf16[1,1536,4096]{2,1,0:T(8,128)(2,1)} async-done(((bf16[1,384,4096]{2,1,0:T(8,128)(2,1)}), bf16[1,1536,4096]{2,1,0:T(8,128)(2,1)}) %all-gather.27.cloned.1.call-update) | async-done | bytes 12582928 | tf_op jit(solution)/shard_map/all_gather | solution.py:382
  750.5 209.7 %all-gather.29.cloned.1.call-done = bf16[1,4096,1536]{2,1,0:T(8,128)(2,1)} async-done(((bf16[1,1024,1536]{2,1,0:T(8,128)(2,1)}), bf16[1,4096,1536]{2,1,0:T(8,128)(2,1)}) %all-gather.29.cloned.1.call-update) | async-done | bytes 12582928 | tf_op jit(solution)/shard_map/all_gather | solution.py:383
  1032.4 16.7 all_gather.66
  1050.0 16.9 all_gather.65
  1202.0 15.9 all_gather.67
  1217.8 16.0 all_gather.68
  1333.5 82.1 %all-reduce.23.cloned.1.call-done = (bf16[1,1024,192]{2,0,1:T(2,128)(2,1)}, bf16[1,1024,192]{2,0,1:T(2,128)(2,1)}) async-done(((bf16[1,1024,192]{2,0,1:T(2,128)(2,1)}, bf16[1,1024,192]{2,0,1:T(2,128)(2,1)}), (bf16[1,1024,192]{2,0,1:T(2,128)(2,1)}, bf16[1,1024,192]{2,0,1:T(2,128)(2,1)})) %all-reduce.23.cloned.1.call-update) | async-done | bytes 786448
  1460.5 10.7 broadcast_select_fusion.13
  1541.7 78.2 %all-reduce.21.cloned.1.call-done = (bf16[1,1024,192]{2,0,1:T(2,128)(2,1)}, bf16[1,1024,192]{2,0,1:T(2,128)(2,1)}) async-done(((bf16[1,1024,192]{2,0,1:T(2,128)(2,1)}, bf16[1,1024,192]{2,0,1:T(2,128)(2,1)}), (bf16[1,1024,192]{2,0,1:T(2,128)(2,1)}, bf16[1,1024,192]{2,0,1:T(2,128)(2,1)})) %all-reduce.21.cloned.1.call-update) | async-done | bytes 786448
  1659.5 11.0 broadcast_select_fusion.12
  1746.8 85.1 %all-reduce.19.cloned.1.call-done = (bf16[1,1024,192]{2,0,1:T(2,128)(2,1)}, bf16[1,1024,192]{2,0,1:T(2,128)(2,1)}) async-done(((bf16[1,1024,192]{2,0,1:T(2,128)(2,1)}, bf16[1,1024,192]{2,0,1:T(2,128)(2,1)}), (bf16[1,1024,192]{2,0,1:T(2,128)(2,1)}, bf16[1,1024,192]{2,0,1:T(2,128)(2,1)})) %all-reduce.19.cloned.1.call-update) | async-done | bytes 786448
  1956.4 86.3 %reduce-scatter.14.cloned.1.call-done = bf16[384,1536]{1,0:T(8,128)(2,1)} async-done(((bf16[1536,1536]{1,0:T(8,128)(2,1)}), bf16[384,1536]{1,0:T(8,128)(2,1)}) %reduce-scatter.14.cloned.1.call-update) | async-done | bytes 1179664 | tf_op jit(solution)/shard_map/reduce_scatter | solution.py:480
  2042.7 88.6 %reduce-scatter.8.cloned.1.call-done = bf16[384,1536]{1,0:T(8,128)(2,1)} async-done(((bf16[1536,1536]{1,0:T(8,128)(2,1)}), bf16[384,1536]{1,0:T(8,128)(2,1)}) %reduce-scatter.8.cloned.1.call-update) | async-done | bytes 1179664 | tf_op jit(solution)/shard_map/reduce_scatter | solution.py:480
  2131.3 215.3 %reduce-scatter.16.cloned.1.call-done = bf16[384,4096]{1,0:T(8,128)(2,1)} async-done(((bf16[1536,4096]{1,0:T(8,128)(2,1)}), bf16[384,4096]{1,0:T(8,128)(2,1)}) %reduce-scatter.16.cloned.1.call-update) | async-done | bytes 3145744 | tf_op jit(solution)/shard_map/reduce_scatter | solution.py:480
  2346.6 215.3 %reduce-scatter.18.cloned.1.call-done = bf16[384,4096]{1,0:T(8,128)(2,1)} async-done(((bf16[1536,4096]{1,0:T(8,128)(2,1)}), bf16[384,4096]{1,0:T(8,128)(2,1)}) %reduce-scatter.18.cloned.1.call-update) | async-done | bytes 3145744 | tf_op jit(solution)/shard_map/reduce_scatter | solution.py:480
  2561.8 215.3 %reduce-scatter.20.cloned.1.call-done = bf16[1024,1536]{1,0:T(8,128)(2,1)} async-done(((bf16[4096,1536]{1,0:T(8,128)(2,1)}), bf16[1024,1536]{1,0:T(8,128)(2,1)}) %reduce-scatter.20.cloned.1.call-update) | async-done | bytes 3145744 | tf_op jit(solution)/shard_map/reduce_scatter | solution.py:480
  2809.5 200.4 %all-reduce.25.cloned.1.call-done = (bf16[1,384,1536]{2,1,0:T(8,128)(2,1)}, bf16[1,384,768]{2,1,0:T(8,128)(2,1)}, bf16[1,384,768]{2,1,0:T(8,128)(2,1)}, bf16[1,3...) async-done(((bf16[1,384,1536]{2,1,0:T(8,128)(2,1)}, bf16[1,384,768]{2,1,0:T(8,128)(2,1)}, ...) | async-done | bytes 12976144 | tf_op jit(solution)/shard_map/psum | solution.py:489
  (849 shorter events, 845.8 us)
Async XLA Ops:
  7.2 52.8 %all-gather.17.cloned.1.call-start = ((), (), s32[]{:S(2)}) async-start(), calls=%async_computation.38 | async-start | bytes 2949120 | tf_op jit(solution)/shard_map/all_gather | solution.py:378
  7.9 103.0 %all-gather.19.cloned.1.call-start = ((), (), s32[]{:S(2)}) async-start(), calls=%async_computation.39 | async-start | bytes 2949120 | tf_op jit(solution)/shard_map/all_gather | solution.py:377
  8.7 200.1 %all-gather.21.cloned.1.call-start = ((), (), s32[]{:S(2)}) async-start(), calls=%async_computation.40 | async-start | bytes 5898240 | tf_op jit(solution)/shard_map/all_gather | solution.py:376
  9.4 297.1 %all-gather.23.cloned.1.call-start = ((), (), s32[]{:S(2)}) async-start(), calls=%async_computation.41 | async-start | bytes 5898240 | tf_op jit(solution)/shard_map/all_gather | solution.py:379
  10.0 514.3 %all-gather.25.cloned.1.call-start = ((), (), s32[]{:S(2)}) async-start(), calls=%async_computation.42 | async-start | bytes 15728640 | tf_op jit(solution)/shard_map/all_gather | solution.py:381
  10.6 731.6 %all-gather.27.cloned.1.call-start = ((), (), s32[]{:S(2)}) async-start(), calls=%async_computation.43 | async-start | bytes 15728640 | tf_op jit(solution)/shard_map/all_gather | solution.py:382
  11.2 949.0 %all-gather.29.cloned.1.call-start = ((), (), s32[]{:S(2)}) async-start(), calls=%async_computation.44 | async-start | bytes 15728640 | tf_op jit(solution)/shard_map/all_gather | solution.py:383
  67.3 53.8 %all-to-all-start = ((bf16[4,2,6144]{2,1,0:T(2,128)(2,1)}), bf16[4,2,6144]{2,1,0:T(2,128)(2,1)}, u32[]{:S(2)}, u32[]{:S(2)}) async-start(bf16[4,2,6144]{2,1,0:T(2,128)(2,1)} %reshape.2629), calls=%async_computation | async-start | bytes 196608 | tf_op jit(solution)/shard_map/all_to_all | solution.py:177
  121.0 29.1 all-to-all-start.1
  235.3 28.1 all-to-all-start.2
  1025.5 43.4 %all-to-all-start.6 = ((bf16[4,2,12288]{2,1,0:T(2,128)(2,1)}), bf16[4,2,12288]{2,1,0:T(2,128)(2,1)}, u32[]{:S(2)}, u32[]{:S(2)}) async-start(bf16[4,2,12288]{2,1,0:T(2,128)(2,1)} %reshape.2641), calls=%async_computation.6 | async-start | bytes 393216 | tf_op jit(solution)/shard_map/all_to_all | solution.py:175
  1169.6 24.8 all-to-all-start.8
  1194.4 51.5 %all-to-all-start.10 = ((bf16[4,2,12288]{2,1,0:T(2,128)(2,1)}), bf16[4,2,12288]{2,1,0:T(2,128)(2,1)}, u32[]{:S(2)}, u32[]{:S(2)}) async-start(bf16[4,2,12288]{2,1,0:T(2,128)(2,1)} %reshape.2649), calls=%async_computation.10 | async-start | bytes 393216 | tf_op jit(solution)/shard_map/all_to_all | solution.py:175
  1321.4 94.2 %all-reduce.23.cloned.1.call-start = ((), (), s32[]{:S(2)}) async-start(), calls=%async_computation.47 | async-start | bytes 4194304
  1529.6 90.4 %all-reduce.21.cloned.1.call-start = ((), (), s32[]{:S(2)}) async-start(), calls=%async_computation.46 | async-start | bytes 4194304
  1711.4 120.5 %all-reduce.19.cloned.1.call-start = ((), (), s32[]{:S(2)}) async-start(), calls=%async_computation.45 | async-start | bytes 4194304
  1746.8 209.6 %reduce-scatter.12.cloned.1.call-start = ((), (), s32[]{:S(2)}) async-start(), calls=%async_computation.33 | async-start | bytes 2949120 | tf_op jit(solution)/shard_map/reduce_scatter | solution.py:480
  1856.4 100.0 %reduce-scatter.10.cloned.1.call-start = ((), (), s32[]{:S(2)}) async-start(), calls=%async_computation.32 | async-start | bytes 2949120 | tf_op jit(solution)/shard_map/reduce_scatter | solution.py:480
  1884.8 157.9 %reduce-scatter.14.cloned.1.call-start = ((), (), s32[]{:S(2)}) async-start(), calls=%async_computation.34 | async-start | bytes 5898240 | tf_op jit(solution)/shard_map/reduce_scatter | solution.py:480
  1890.6 240.7 %reduce-scatter.8.cloned.1.call-start = ((), (), s32[]{:S(2)}) async-start(), calls=%async_computation.31 | async-start | bytes 5898240 | tf_op jit(solution)/shard_map/reduce_scatter | solution.py:480
  1926.3 420.2 %reduce-scatter.16.cloned.1.call-start = ((), (), s32[]{:S(2)}) async-start(), calls=%async_computation.35 | async-start | bytes 15728640 | tf_op jit(solution)/shard_map/reduce_scatter | solution.py:480
  1937.8 624.0 %reduce-scatter.18.cloned.1.call-start = ((), (), s32[]{:S(2)}) async-start(), calls=%async_computation.36 | async-start | bytes 15728640 | tf_op jit(solution)/shard_map/reduce_scatter | solution.py:480
  1946.5 830.6 %reduce-scatter.20.cloned.1.call-start = ((), (), s32[]{:S(2)}) async-start(), calls=%async_computation.37 | async-start | bytes 15728640 | tf_op jit(solution)/shard_map/reduce_scatter | solution.py:480
  1956.3 1053.6 %all-reduce.25.cloned.1.call-start = ((), (), s32[]{:S(2)}) async-start(), calls=%async_computation.48 | async-start | bytes 25952256 | tf_op jit(solution)/shard_map/psum | solution.py:489
  (197 other events, 3189.7 us)
Sparse Core Ops, SparseCore 0:
  9.6 50.3 all-gather.16
  61.5 49.2 all-gather.18
  112.5 96.2 all-gather.20
  210.2 96.2 all-gather.22
  307.9 216.3 all-gather.24
  525.7 216.3 all-gather.26
  743.7 216.3 all-gather.28
  1325.8 89.7 all-reduce.22
  1533.5 86.3 all-reduce.20
  1746.9 84.9 all-reduce.18
  1856.6 46.8 reduce-scatter.11
  1906.3 47.5 reduce-scatter.9
  1956.9 85.7 reduce-scatter.13
  2045.5 85.7 reduce-scatter.7
  2133.6 212.8 reduce-scatter.15
  2348.9 212.8 reduce-scatter.17
  2564.1 212.8 reduce-scatter.19
  2780.5 229.3 all-reduce.24
where the time goes:
time: 3050 us; the launch traced here: 3040 us
  waiting for transfers between devices  2060 us (68%)
  matrix products  295 us (10%)
  local copies, waits for them, and re-layouts  222 us (7%)
  blocking collectives  173 us (6%)
  other arithmetic  171 us (6%)
  starting transfers between devices  90.6 us (3%)
    reduce_scatter x7, waiting for transfers between devices, shards(): lax.psum_scatter(weight_term(left_side, right_side).astype(jnp.bfloat16),...  821 us
    unnamed x21, waiting for transfers between devices  250 us
    all_gather x1, waiting for transfers between devices, shards(): lax.all_gather(local_shards[6], 'blk', axis=0, tiled=True)  214 us
    all_gather x1, waiting for transfers between devices, shards(): lax.all_gather(local_shards[7], 'blk', axis=0, tiled=True)  210 us
    all_gather x1, waiting for transfers between devices, shards(): lax.all_gather(local_shards[8], 'blk', axis=0, tiled=True)  210 us
    psum x1, waiting for transfers between devices, shards(): lax.psum(shortened(shares), 'seq')  200 us
    dot_general x21, matrix products, back_product(): lax.dot_general(left_side, right_side, (((1,), (1,)), ((), ())), preferre...  110 us
    unnamed x32, other arithmetic  98.9 us
  transfers between devices with their start and end apart: 43, of which 25 were waited for; matrix products, arithmetic and copies ran while one was open for 11% of the time, Pallas kernels for 0%

commit v1 on v0

--- a/solution.py
+++ b/solution.py
@@ -502,6 +502,265 @@
     )
 
 
+def group_gather(block):
+    return lax.all_gather(block, ("seq", "blk"), axis=0, tiled=True)
+
+
+def group_scatter(partial):
+    return lax.psum_scatter(
+        partial.astype(jnp.bfloat16), ("seq", "blk"), scatter_dimension=0, tiled=True
+    ).astype(jnp.float32)
+
+
+def turn(field_in, cosine, sine):
+    half_dim = HEAD_DIM // 2
+    first_half = field_in[:, :half_dim]
+    second_half = field_in[:, half_dim:]
+    return jnp.concatenate(
+        [first_half * cosine - second_half * sine, second_half * cosine + first_half * sine],
+        axis=-1,
+    )
+
+
+def swapped(own, kept_here):
+    return lax.ppermute(own, "section", [(0, 1), (1, 0)])
+
+
+def spread_weights(local_shards):
+    seq_index = lax.axis_index("seq")
+    seq_count = lax.axis_size("seq")
+    blk_count = lax.axis_size("blk")
+    gain_attn, w_query, w_key, w_value, w_output, gain_mlp, w_gate, w_up, w_down = local_shards
+    rows = w_query.shape[0]
+
+    def mine(weight, width, per_blk, place):
+        return lax.dynamic_index_in_dim(
+            weight.reshape(rows, blk_count, per_blk, width), place, 2, keepdims=False
+        )
+
+    kv_per_blk = KV_HEADS // blk_count
+    kv_place = seq_index * kv_per_blk // seq_count
+    ff_width = w_gate.shape[1] // (seq_count * blk_count)
+    attn = jnp.concatenate(
+        [
+            mine(w_query, HEAD_DIM, seq_count, seq_index),
+            mine(w_key, HEAD_DIM, kv_per_blk, kv_place),
+            mine(w_value, HEAD_DIM, kv_per_blk, kv_place),
+        ],
+        axis=-1,
+    ).transpose(1, 2, 0)
+    gains = jnp.stack([gain_attn, gain_mlp])
+    attn = jnp.concatenate(
+        [attn, jnp.broadcast_to(gains[None], (blk_count,) + gains.shape)], axis=1
+    )
+    wide = jnp.concatenate(
+        [mine(w_gate, ff_width, seq_count, seq_index), mine(w_up, ff_width, seq_count, seq_index)],
+        axis=-1,
+    ).transpose(1, 0, 2)
+    attn = lax.all_to_all(attn, "blk", split_axis=0, concat_axis=2, tiled=True)[0]
+    wide = lax.all_to_all(wide, "blk", split_axis=0, concat_axis=1, tiled=True)[0]
+    out_rows = w_output.shape[0] // seq_count
+    down_rows = w_down.shape[0] // seq_count
+    out = lax.dynamic_slice_in_dim(w_output, seq_index * out_rows, out_rows, 0)
+    down = lax.dynamic_slice_in_dim(w_down, seq_index * down_rows, down_rows, 0)
+    return attn, out, wide, down
+
+
+def own_layer(x_own, weights, info):
+    attn, out, wide, down = weights
+    allowed, cosine, sine = info
+    gain_attn = attn[3 * HEAD_DIM].astype(jnp.float32)
+    gain_mlp = attn[3 * HEAD_DIM + 1].astype(jnp.float32)
+    normed, inv_first = rms_forward(x_own, gain_attn)
+    normed_all = group_gather(normed.astype(jnp.bfloat16))
+    mixed_in = back_product(normed_all, attn[: 3 * HEAD_DIM])
+    query = turn(mixed_in[:, :HEAD_DIM], cosine, sine).astype(jnp.bfloat16)
+    key = turn(mixed_in[:, HEAD_DIM : 2 * HEAD_DIM], cosine, sine).astype(jnp.bfloat16)
+    value = mixed_in[:, 2 * HEAD_DIM :].astype(jnp.bfloat16)
+    scores = jnp.where(allowed, back_product(query, key) * HEAD_DIM ** (-0.5), MASKED)
+    row_top = jnp.max(scores, axis=-1, keepdims=True)
+    log_total = row_top + jnp.log(jnp.sum(jnp.exp(scores - row_top), axis=-1, keepdims=True))
+    mixed = product(jnp.exp(scores - log_total).astype(jnp.bfloat16), value).astype(jnp.bfloat16)
+    hidden = x_own + group_scatter(product(mixed, out))
+    normed_mlp, inv_second = rms_forward(hidden, gain_mlp)
+    normed_mlp_all = group_gather(normed_mlp.astype(jnp.bfloat16))
+    pre = product(normed_mlp_all, wide)
+    half = pre.shape[1] // 2
+    gate_pre, up_pre = pre[:, :half], pre[:, half:]
+    act_low = (jax.nn.silu(gate_pre) * up_pre).astype(jnp.bfloat16)
+    result = hidden + group_scatter(product(act_low, down))
+    saved = (
+        x_own,
+        inv_first,
+        normed_all,
+        query,
+        key,
+        value,
+        log_total,
+        mixed,
+        hidden,
+        inv_second,
+        normed_mlp_all,
+        gate_pre,
+        up_pre,
+        act_low,
+    )
+    return result, saved
+
+
+def own_layer_back(grad_own, weights, info, saved):
+    attn, out, wide, down = weights
+    allowed, cosine, sine = info
+    (
+        x_own,
+        inv_first,
+        normed_all,
+        query,
+        key,
+        value,
+        log_total,
+        mixed,
+        hidden,
+        inv_second,
+        normed_mlp_all,
+        gate_pre,
+        up_pre,
+        act_low,
+    ) = saved
+    gain_attn = attn[3 * HEAD_DIM].astype(jnp.float32)
+    gain_mlp = attn[3 * HEAD_DIM + 1].astype(jnp.float32)
+    grad_out_all = group_gather(grad_own.astype(jnp.bfloat16))
+    grad_act = back_product(grad_out_all, down)
+    gate_sigmoid = jax.nn.sigmoid(gate_pre)
+    grad_gate = (
+        grad_act * up_pre * gate_sigmoid * (1.0 + gate_pre * (1.0 - gate_sigmoid))
+    ).astype(jnp.bfloat16)
+    grad_up = (grad_act * jax.nn.silu(gate_pre)).astype(jnp.bfloat16)
+    grad_wide = jnp.concatenate([grad_gate, grad_up], axis=1)
+    grad_normed_mlp = group_scatter(back_product(grad_wide, wide))
+    grad_hidden_part, gain_mlp_terms = rms_backward(hidden, gain_mlp, inv_second, grad_normed_mlp)
+    grad_hidden = grad_own + grad_hidden_part
+    grad_branch_all = group_gather(grad_hidden.astype(jnp.bfloat16))
+    grad_mixed = back_product(grad_branch_all, out).astype(jnp.bfloat16)
+    scores = jnp.where(allowed, back_product(query, key) * HEAD_DIM ** (-0.5), MASKED)
+    probs = jnp.exp(scores - log_total)
+    grad_probs = back_product(grad_mixed, value)
+    centre = jnp.sum(probs * grad_probs, axis=-1, keepdims=True)
+    grad_scores = (probs * (grad_probs - centre)).astype(jnp.bfloat16)
+    grad_query = (product(grad_scores, key) * HEAD_DIM ** (-0.5)).astype(jnp.bfloat16)
+    grad_key = weight_term(grad_scores, query) * HEAD_DIM ** (-0.5)
+    grad_value = weight_term(probs.astype(jnp.bfloat16), grad_mixed).astype(jnp.bfloat16)
+    grad_query = turn(grad_query.astype(jnp.float32), cosine, -sine).astype(jnp.bfloat16)
+    grad_key = turn(grad_key, cosine, -sine).astype(jnp.bfloat16)
+    grad_qkv = jnp.concatenate([grad_query, grad_key, grad_value], axis=1)
+    grad_normed = group_scatter(product(grad_qkv, attn[: 3 * HEAD_DIM]))
+    grad_in_part, gain_attn_terms = rms_backward(x_own, gain_attn, inv_first, grad_normed)
+    grads = (
+        weight_term(grad_qkv, normed_all),
+        weight_term(mixed, grad_branch_all),
+        weight_term(normed_mlp_all, grad_wide),
+        weight_term(act_low, grad_out_all),
+    )
+    gains = jnp.stack([jnp.sum(gain_attn_terms, axis=0), jnp.sum(gain_mlp_terms, axis=0)])
+    return grad_hidden + grad_in_part, grads, gains
+
+
+def finish_grads(grads):
+    seq_count = lax.axis_size("seq")
+    blk_count = lax.axis_size("blk")
+    attn, out, wide, down = grads
+    attn = lax.all_to_all(attn[None], "blk", split_axis=2, concat_axis=0, tiled=True)
+    wide = lax.all_to_all(wide[None], "blk", split_axis=1, concat_axis=0, tiled=True)
+    attn, out, wide, down = [
+        lax.all_gather(part, "seq", axis=0, tiled=False).astype(jnp.float32)
+        for part in (attn, out, wide, down)
+    ]
+    rows = attn.shape[-1]
+    query = attn[:, :, :HEAD_DIM].transpose(3, 1, 0, 2).reshape(rows, -1)
+
+    def key_like(part):
+        copies = HEADS // KV_HEADS
+        part = part.reshape(seq_count // copies, copies, blk_count, HEAD_DIM, rows).sum(1)
+        return part.transpose(3, 1, 0, 2).reshape(rows, -1)
+
+    key = key_like(attn[:, :, HEAD_DIM : 2 * HEAD_DIM])
+    value = key_like(attn[:, :, 2 * HEAD_DIM :])
+    half = wide.shape[-1] // 2
+    gate = wide[..., :half].transpose(2, 1, 0, 3).reshape(rows, -1)
+    up = wide[..., half:].transpose(2, 1, 0, 3).reshape(rows, -1)
+    return query, key, value, out.reshape(-1, out.shape[-1]), gate, up, down.reshape(
+        -1, down.shape[-1]
+    )
+
+
+def head_shards(inputs, cotangent, doc_lengths, *params):
+    section = lax.axis_index("section")
+    at_first = section == 0
+    blk_index = lax.axis_index("blk")
+    tokens = inputs.shape[2] * lax.axis_size("seq") * lax.axis_size("blk")
+    own = spread_weights(tuple(weight[0] for weight in params))
+    other = tuple(swapped(part, None) for part in own)
+    first = tuple(jnp.where(at_first, a, b) for a, b in zip(own, other))
+    second = tuple(jnp.where(at_first, b, a) for a, b in zip(own, other))
+    x_own = lax.dynamic_index_in_dim(inputs, section, 0, keepdims=False)[0].astype(jnp.float32)
+    grad_own = lax.dynamic_index_in_dim(cotangent, section, 0, keepdims=False)[0].astype(
+        jnp.float32
+    )
+    lengths = lax.dynamic_index_in_dim(doc_lengths, section, 0, keepdims=False)[0]
+    token_index = jnp.arange(tokens, dtype=jnp.int32)
+    segment, position = doc_info(lengths, token_index)
+    allowed = (segment[:, None] == segment[None, :]) & (
+        token_index[None, :] <= token_index[:, None]
+    )
+    half_dim = HEAD_DIM // 2
+    frequency = THETA ** (-2.0 * jnp.arange(half_dim, dtype=jnp.float32) / HEAD_DIM)
+    angles = position.astype(jnp.float32)[:, None] * frequency
+    info = (allowed, jnp.cos(angles), jnp.sin(angles))
+    result, saved_first = own_layer(x_own, first, info)
+    between = result.astype(jnp.bfloat16)
+    result, saved_second = own_layer(between.astype(jnp.float32), second, info)
+    final = result.astype(jnp.bfloat16)
+    grad_between, grads_second, gains_second = own_layer_back(grad_own, second, info, saved_second)
+    grad_between = grad_between.astype(jnp.bfloat16)
+    grad_start, grads_first, gains_first = own_layer_back(
+        grad_between.astype(jnp.float32), first, info, saved_first
+    )
+    grad_start = grad_start.astype(jnp.bfloat16)
+
+    def by_section(for_first, for_second):
+        kept = jnp.where(at_first, for_first, for_second)
+        received = swapped(jnp.where(at_first, for_second, for_first), None)
+        return jnp.stack(
+            [jnp.where(at_first, kept, received), jnp.where(at_first, received, kept)]
+        )[None, :, None]
+
+    activations = by_section(between, final)
+    input_grads = by_section(grad_start, grad_between)
+    summed = []
+    for one, two in zip(grads_first, grads_second):
+        kept = jnp.where(at_first, one, two)
+        received = swapped(jnp.where(at_first, two, one).astype(jnp.bfloat16), None)
+        summed.append((kept + received.astype(jnp.float32)).astype(jnp.bfloat16))
+    query, key, value, out, gate, up, down = finish_grads(summed)
+    gains = lax.psum(jnp.stack([gains_first, gains_second]), ("section", "seq", "blk"))
+    gains = lax.dynamic_index_in_dim(gains, section, 0, keepdims=False)
+    rows = params[1].shape[1]
+    gains = lax.dynamic_slice_in_dim(gains, blk_index * rows, rows, 1)
+    return (
+        activations,
+        input_grads,
+        gains[0][None],
+        query[None],
+        key[None],
+        value[None],
+        out[None],
+        gains[1][None],
+        gate[None],
+        up[None],
+        down[None],
+    )
+
+
 def solution(mesh):
     placed = (
         P(None, None, ("seq", "blk"), None),
@@ -517,8 +776,9 @@
         P("section", "blk", None),
         P("section", "blk", None),
     )
+    one_head_each = mesh.shape["seq"] * mesh.shape["blk"] == HEADS
     return jax.shard_map(
-        shards,
+        head_shards if one_head_each else shards,
         mesh=mesh,
         in_specs=placed,
         out_specs=(

time: 3050 us -> 1310 us (0.43)
  waiting for transfers between devices: 2060 us -> 819 us
  matrix products: 295 us -> 93.1 us
  local copies, waits for them, and re-layouts: 222 us -> 133 us
  other arithmetic: 171 us -> 84.1 us
  starting transfers between devices: 90.6 us -> 12.7 us
    all_gather x7 -> x12, waiting for transfers between devices: 769 us -> 269 us  [the longest x8 269 us: group_gather(): return lax.all_gather(block, ('seq', 'blk'), axis=0, tiled=True)]
    reduce_scatter x7 -> x8, waiting for transfers between devices: 821 us -> 387 us  [group_scatter(): lax.psum_scatter(partial.astype(jnp.bfloat16), ('seq', 'blk'), scatter_di...]
    unnamed x21 -> x20, waiting for transfers between devices: 250 us -> 0.33 us
    psum x1 -> x0, waiting for transfers between devices: 200 us -> none  [shards(): lax.psum(shortened(shares), 'seq')]
    all_gather x8 -> x0, blocking collectives: 133 us -> none  [the longest x3 55.9 us: layer_forward(): lax.all_gather(heads_key, 'blk', axis=1, tiled=True)]
    ppermute x4 -> x10, waiting for transfers between devices: 7.06 us -> 134 us  [swapped(): return lax.ppermute(own, 'section', [(0, 1), (1, 0)])]
    all_to_all x21 -> x1, starting transfers between devices: 80.7 us -> 5.19 us  [finish_grads(): lax.all_to_all(wide[None], 'blk', split_axis=1, concat_axis=0, tiled=True)]
    all_to_all x3, blocking collectives: 26.2 us -> 101 us  [the longest x1 50.9 us: spread_weights(): lax.all_to_all(wide, 'blk', split_axis=0, concat_axis=1, tiled=True)[0]]
  transfers between devices with their start and end apart: 43 -> 31, of which waited for: 25 -> 21; matrix products, arithmetic and copies ran while one was open for 11% -> 15% of each run, Pallas kernels for 0% -> 0%
where the time goes in v1:
time: 1310 us; the launch traced here: 1300 us
  waiting for transfers between devices  819 us (63%)
  blocking collectives  143 us (11%)
  local copies, waits for them, and re-layouts  133 us (10%)
  matrix products  93.1 us (7%)
  other arithmetic  84.1 us (6%)
  between operations  16.2 us (1%)
    reduce_scatter x8, waiting for transfers between devices, group_scatter(): lax.psum_scatter(partial.astype(jnp.bfloat16), ('seq', 'blk'), scatter_di...  387 us
    all_gather x8, waiting for transfers between devices, group_gather(): return lax.all_gather(block, ('seq', 'blk'), axis=0, tiled=True)  269 us
    ppermute x10, waiting for transfers between devices, swapped(): return lax.ppermute(own, 'section', [(0, 1), (1, 0)])  134 us
    unnamed x198, local copies, waits for them, and re-layouts  57.1 us
    all_to_all x1, blocking collectives, spread_weights(): lax.all_to_all(wide, 'blk', split_axis=0, concat_axis=1, tiled=True)[0]  50.9 us
    psum x1, blocking collectives, head_shards(): lax.psum(jnp.stack([gains_first, gains_second]), ('section', 'seq', 'blk'))  42.3 us
    dot_general x12, matrix products, back_product(): lax.dot_general(left_side, right_side, (((1,), (1,)), ((), ())), preferre...  36.1 us
    dot_general x12, matrix products, product(): return jnp.dot(left_side, right_side, preferred_element_type=jnp.float32)  33.1 us
  transfers between devices with their start and end apart: 31, of which 21 were waited for; matrix products, arithmetic and copies ran while one was open for 15% of the time, Pallas kernels for 0%

profile of v1, /device:TPU:18, one launch (start us, length us, event | category | flops | bytes accessed | tf_op | source)
XLA Modules:
  0.0 1301.2 jit_solution(6878093278968986403)
XLA Ops:
  16.4 25.1 %all_to_all.51 = bf16[4,290,384]{2,1,0:T(8,128)(2,1)S(1)} all-to-all(bf16[4,290,384]{2,1,0:T(8,128)(2,1)S(1)} %pad_maximum_fusion.2), channel_id=1, replica_groups=mesh['section'=2,'seq'=4,'blk'=4] {'blk'}, dimensions={0} | all-to-all | bytes 1781760 | tf_op jit(solution)/shard_map/all_to_all | solution.py:560
  44.4 20.2 %collective-permute-done = bf16[290,1536]{1,0:T(8,128)(2,1)} collective-permute-done((bf16[290,1536]{1,0:T(8,128)(2,1)}, bf16[290,1536]{1,0:T(8,128)(2,1)}, u32[]{:S(2)}, u32[]{:S(2)}) %collective-permute-start) | collective-permute-done | bytes 890912 | tf_op jit(solution)/shard_map/ppermute | solution.py:526
  75.0 41.1 %all-gather.17.cloned.1.call-done = bf16[1024,1536]{1,0:T(8,128)(2,1)} async-done(((bf16[64,1536]{1,0:T(8,128)(2,1)}), bf16[1024,1536]{1,0:T(8,128)(2,1)}) %all-gather.17.cloned.1.call-update) | async-done | bytes 3145744 | tf_op jit(solution)/shard_map/all_gather | solution.py:506
  127.9 64.2 %reduce-scatter.9.cloned.1.call-done = bf16[64,1536]{1,0:T(8,128)(2,1)} async-done(((bf16[1024,1536]{1,0:T(8,128)(2,1)}), bf16[64,1536]{1,0:T(8,128)(2,1)}) %reduce-scatter.9.cloned.1.call-update) | async-done | bytes 196624 | tf_op jit(solution)/shard_map/reduce_scatter | solution.py:510
  215.3 50.9 %all_to_all.52 = bf16[4,384,512]{2,1,0:T(8,128)(2,1)} all-to-all(bf16[4,384,512]{2,1,0:T(8,128)(2,1)S(1)} %maximum_bitcast_fusion), channel_id=1, replica_groups=mesh['section'=2,'seq'=4,'blk'=4] {'blk'}, dimensions={0} | all-to-all | bytes 3145728 | tf_op jit(solution)/shard_map/all_to_all | solution.py:561
  269.2 34.7 %collective-permute-done.2 = bf16[1536,512]{1,0:T(8,128)(2,1)} collective-permute-done((bf16[1536,512]{1,0:T(8,128)(2,1)}, bf16[1536,512]{1,0:T(8,128)(2,1)}, u32[]{:S(2)}, u32[]{:S(2)}) %collective-permute-start.2) | collective-permute-done | bytes 1572896 | tf_op jit(solution)/shard_map/ppermute | solution.py:526
  321.6 65.8 %reduce-scatter.11.cloned.1.call-done = bf16[64,1536]{1,0:T(8,128)(2,1)} async-done(((bf16[1024,1536]{1,0:T(8,128)(2,1)}), bf16[64,1536]{1,0:T(8,128)(2,1)}) %reduce-scatter.11.cloned.1.call-update) | async-done | bytes 196624 | tf_op jit(solution)/shard_map/reduce_scatter | solution.py:510
  389.7 45.5 %all-gather.21.cloned.1.call-done = bf16[1024,1536]{1,0:T(8,128)(2,1)} async-done(((bf16[64,1536]{1,0:T(8,128)(2,1)}), bf16[1024,1536]{1,0:T(8,128)(2,1)}) %all-gather.21.cloned.1.call-update) | async-done | bytes 3145744 | tf_op jit(solution)/shard_map/all_gather | solution.py:506
  446.2 64.2 %reduce-scatter.13.cloned.1.call-done = bf16[64,1536]{1,0:T(8,128)(2,1)} async-done(((bf16[1024,1536]{1,0:T(8,128)(2,1)}), bf16[64,1536]{1,0:T(8,128)(2,1)}) %reduce-scatter.13.cloned.1.call-update) | async-done | bytes 196624 | tf_op jit(solution)/shard_map/reduce_scatter | solution.py:510
  514.1 44.3 %all-gather.23.cloned.1.call-done = bf16[1024,1536]{1,0:T(8,128)(2,1)} async-done(((bf16[64,1536]{1,0:T(8,128)(2,1)}), bf16[1024,1536]{1,0:T(8,128)(2,1)}) %all-gather.23.cloned.1.call-update) | async-done | bytes 3145744 | tf_op jit(solution)/shard_map/all_gather | solution.py:506
  563.9 41.4 %all-gather.33.cloned.1.call-done = bf16[1,1,1024,1536]{3,2,1,0:T(8,128)(2,1)} async-done(((bf16[1,1,64,1536]{3,2,1,0:T(8,128)(2,1)}), bf16[1,1,1024,1536]{3,2,1,0:T(8,128)(2,1)}) %all-gather.33.cloned.1.call-update) | async-done | bytes 3145744 | tf_op jit(solution)/shard_map/all_gather | solution.py:506
  615.9 64.2 %reduce-scatter.17.cloned.1.call-done = bf16[64,1536]{1,0:T(8,128)(2,1)} async-done(((bf16[1024,1536]{1,0:T(8,128)(2,1)}), bf16[64,1536]{1,0:T(8,128)(2,1)}) %reduce-scatter.17.cloned.1.call-update) | async-done | bytes 196624 | tf_op jit(solution)/shard_map/reduce_scatter | solution.py:510
  684.1 44.8 %all-gather.25.cloned.1.call-done = bf16[1024,1536]{1,0:T(8,128)(2,1)} async-done(((bf16[64,1536]{1,0:T(8,128)(2,1)}), bf16[1024,1536]{1,0:T(8,128)(2,1)}) %all-gather.25.cloned.1.call-update) | async-done | bytes 3145744 | tf_op jit(solution)/shard_map/all_gather | solution.py:506
  744.9 64.2 %reduce-scatter.19.cloned.1.call-done = bf16[64,1536]{1,0:T(8,128)(2,1)} async-done(((bf16[1024,1536]{1,0:T(8,128)(2,1)}), bf16[64,1536]{1,0:T(8,128)(2,1)}) %reduce-scatter.19.cloned.1.call-update) | async-done | bytes 196624 | tf_op jit(solution)/shard_map/reduce_scatter | solution.py:510
  812.8 45.0 %all-gather.27.cloned.1.call-done = bf16[1024,1536]{1,0:T(8,128)(2,1)} async-done(((bf16[64,1536]{1,0:T(8,128)(2,1)}), bf16[1024,1536]{1,0:T(8,128)(2,1)}) %all-gather.27.cloned.1.call-update) | async-done | bytes 3145744 | tf_op jit(solution)/shard_map/all_gather | solution.py:506
  867.4 64.2 %reduce-scatter.21.cloned.1.call-done = bf16[64,1536]{1,0:T(8,128)(2,1)} async-done(((bf16[1024,1536]{1,0:T(8,128)(2,1)}), bf16[64,1536]{1,0:T(8,128)(2,1)}) %reduce-scatter.21.cloned.1.call-update) | async-done | bytes 196624 | tf_op jit(solution)/shard_map/reduce_scatter | solution.py:510
  944.2 18.0 %collective-permute-done.9 = bf16[256,1536]{1,0:T(8,128)(2,1)S(1)} collective-permute-done((bf16[256,1536]{1,0:T(8,128)(2,1)S(1)}, bf16[256,1536]{1,0:T(8,128)(2,1)S(1)}, u32[]{:S(2)}, u32[]{:S(2)}) %collective-permute-start.9) | collective-permute-done | bytes 786464 | tf_op jit(solution)/shard_map/ppermute | solution.py:526
  985.4 25.8 %collective-permute-done.8 = bf16[1536,512]{1,0:T(8,128)(2,1)} collective-permute-done((bf16[1536,512]{1,0:T(8,128)(2,1)}, bf16[1536,512]{1,0:T(8,128)(2,1)}, u32[]{:S(2)}, u32[]{:S(2)}) %collective-permute-start.8) | collective-permute-done | bytes 1572896 | tf_op jit(solution)/shard_map/ppermute | solution.py:526
  1014.9 11.8 copy.130
  1027.2 11.0 reduce.9
  1049.5 28.9 %all-to-all-done.3 = bf16[4,2,98304]{2,1,0:T(2,128)(2,1)S(1)} async-done(((bf16[4,2,98304]{2,1,0:T(2,128)(2,1)}), bf16[4,2,98304]{2,1,0:T(2,128)(2,1)S(1)}, u32[]{:S(2)}, u32[]{:S(2)}) %all-to-all-start.3) | async-done | bytes 1572896 | tf_op jit(solution)/shard_map/all_to_all | solution.py:673
  1105.9 20.3 %collective-permute-done.6 = bf16[288,1536]{1,0:T(8,128)(2,1)S(1)} collective-permute-done((bf16[288,1536]{1,0:T(8,128)(2,1)S(1)}, bf16[288,1536]{1,0:T(8,128)(2,1)S(1)}, u32[]{:S(2)}, u32[]{:S(2)}) %collective-permute-start.6) | collective-permute-done | bytes 884768 | tf_op jit(solution)/shard_map/ppermute | solution.py:526
  1146.2 24.8 %all_to_all.53 = bf16[4,2,55296]{2,1,0:T(2,128)(2,1)} all-to-all(bf16[4,2,55296]{2,1,0:T(2,128)(2,1)S(1)} %reshape.207), channel_id=1, replica_groups=mesh['section'=2,'seq'=4,'blk'=4] {'blk'}, dimensions={0} | all-to-all | bytes 1769472 | tf_op jit(solution)/shard_map/all_to_all | solution.py:672
  1233.7 42.3 %psum.7 = f32[2,2,1536]{2,1,0:T(2,128)S(1)} all-reduce(f32[2,2,1536]{2,1,0:T(2,128)S(1)} %pad_maximum_fusion.19), channel_id=1, replica_groups=mesh['section'=2,'seq'=4,'blk'=4] {'section','seq','blk'}, use_global_device_ids=true, to_apply=%region_29.30 | all-reduce | flops 6144 | bytes 49152 | tf_op jit(solution)/shard_map/psum | solution.py:745
  (395 shorter events, 322.2 us)
Async XLA Ops:
  7.2 109.0 %all-gather.17.cloned.1.call-start = ((), (), s32[]{:S(2)}) async-start(), calls=%async_computation.12 | async-start | bytes 3342336 | tf_op jit(solution)/shard_map/all_gather | solution.py:506
  69.5 122.6 %reduce-scatter.9.cloned.1.call-start = ((), (), s32[]{:S(2)}) async-start(), calls=%async_computation.13 | async-start | bytes 3342336 | tf_op jit(solution)/shard_map/reduce_scatter | solution.py:510
  71.3 52.2 %collective-permute-start.1 = (bf16[96,1536]{1,0:T(8,128)(2,1)}, bf16[96,1536]{1,0:T(8,128)(2,1)}, u32[]{:S(2)}, u32[]{:S(2)}) collective-permute-start(bf16[96,1536]{1,0:T(8,128)(2,1)} %dynamic-slice_bitcast_fusion.1), channel_id=1, source_target_pairs={{0,16},{16,0},{1,17},{17,1},{2,18},{18,2},{3,19},{19,3},{4,20},{20... | collective-permute-start | bytes 884744 | tf_op jit(solution)/shard_map/ppermute | solution.py:526
  127.8 176.0 %all-gather.19.cloned.1.call-start = ((), (), s32[]{:S(2)}) async-start(), calls=%async_computation.14 | async-start | bytes 3342336 | tf_op jit(solution)/shard_map/all_gather | solution.py:506
  196.0 191.4 %reduce-scatter.11.cloned.1.call-start = ((), (), s32[]{:S(2)}) async-start(), calls=%async_computation.15 | async-start | bytes 3342336 | tf_op jit(solution)/shard_map/reduce_scatter | solution.py:510
  267.7 50.2 %collective-permute-start.3 = (bf16[256,1536]{1,0:T(8,128)(2,1)}, bf16[256,1536]{1,0:T(8,128)(2,1)S(1)}, u32[]{:S(2)}, u32[]{:S(2)}) collective-permute-start(bf16[256,1536]{1,0:T(8,128)(2,1)} %dynamic-slice_bitcast_fusion), channel_id=1, source_target_pairs={{0,16},{16,0},{1,17},{17,1},{2,18},{18,2},{3,19},{19,3},{4,20},{20... | collective-permute-start | bytes 2359304 | tf_op jit(solution)/shard_map/ppermute | solution.py:526
  320.7 114.5 %all-gather.21.cloned.1.call-start = ((), (), s32[]{:S(2)}) async-start(), calls=%async_computation.16 | async-start | bytes 3342336 | tf_op jit(solution)/shard_map/all_gather | solution.py:506
  389.4 121.1 %reduce-scatter.13.cloned.1.call-start = ((), (), s32[]{:S(2)}) async-start(), calls=%async_computation.17 | async-start | bytes 3342336 | tf_op jit(solution)/shard_map/reduce_scatter | solution.py:510
  446.2 112.2 %all-gather.23.cloned.1.call-start = ((), (), s32[]{:S(2)}) async-start(), calls=%async_computation.18 | async-start | bytes 3342336 | tf_op jit(solution)/shard_map/all_gather | solution.py:506
  513.3 92.0 %all-gather.33.cloned.1.call-start = ((), (), s32[]{:S(2)}) async-start(), calls=%async_computation.28 | async-start | bytes 3342336 | tf_op jit(solution)/shard_map/all_gather | solution.py:506
  514.1 166.1 %reduce-scatter.17.cloned.1.call-start = ((), (), s32[]{:S(2)}) async-start(), calls=%async_computation.20 | async-start | bytes 3342336 | tf_op jit(solution)/shard_map/reduce_scatter | solution.py:510
  615.9 113.0 %all-gather.25.cloned.1.call-start = ((), (), s32[]{:S(2)}) async-start(), calls=%async_computation.21 | async-start | bytes 3342336 | tf_op jit(solution)/shard_map/all_gather | solution.py:506
  683.6 125.5 %reduce-scatter.19.cloned.1.call-start = ((), (), s32[]{:S(2)}) async-start(), calls=%async_computation.22 | async-start | bytes 3342336 | tf_op jit(solution)/shard_map/reduce_scatter | solution.py:510
  744.8 113.0 %all-gather.27.cloned.1.call-start = ((), (), s32[]{:S(2)}) async-start(), calls=%async_computation.23 | async-start | bytes 3342336 | tf_op jit(solution)/shard_map/all_gather | solution.py:506
  812.7 118.9 %reduce-scatter.21.cloned.1.call-start = ((), (), s32[]{:S(2)}) async-start(), calls=%async_computation.24 | async-start | bytes 3342336 | tf_op jit(solution)/shard_map/reduce_scatter | solution.py:510
  867.3 113.2 %all-gather.29.cloned.1.call-start = ((), (), s32[]{:S(2)}) async-start(), calls=%async_computation.25 | async-start | bytes 3342336 | tf_op jit(solution)/shard_map/all_gather | solution.py:506
  935.1 247.1 %reduce-scatter.15.cloned.1.call-start = ((), (), s32[]{:S(2)}) async-start(), calls=%async_computation.19 | async-start | bytes 3342336 | tf_op jit(solution)/shard_map/reduce_scatter | solution.py:510
  939.0 251.9 %all-gather.39.cloned.1.call-start = ((), (), s32[]{:S(2)}) async-start(), calls=%async_computation.31 | async-start | bytes 3932160 | tf_op jit(solution)/shard_map/all_gather | solution.py:675
  984.8 62.9 %collective-permute-start.7 = (bf16[96,1536]{1,0:T(8,128)(2,1)}, bf16[96,1536]{1,0:T(8,128)(2,1)}, u32[]{:S(2)}, u32[]{:S(2)}) collective-permute-start(bf16[96,1536]{1,0:T(8,128)(2,1)} %get-tuple-element.140), channel_id=1, source_target_pairs={{0,16},{16,0},{1,17},{17,1},{2,18},{18,2},{3,19},{19,3},{4,20},{20... | collective-permute-start | bytes 884744 | tf_op jit(solution)/shard_map/ppermute | solution.py:526
  1047.7 148.7 %all-gather.37.cloned.1.call-start = ((), (), s32[]{:S(2)}) async-start(), calls=%async_computation.30 | async-start | bytes 1474560 | tf_op jit(solution)/shard_map/all_gather | solution.py:675
  1049.5 149.9 %all-gather.31.cloned.1.call-start = ((), (), s32[]{:S(2)}) async-start(), calls=%async_computation.27 | async-start | bytes 7864320 | tf_op jit(solution)/shard_map/all_gather | solution.py:675
  1084.9 145.6 %reduce-scatter.23.cloned.1.call-start = ((), (), s32[]{:S(2)}) async-start(), calls=%async_computation.26 | async-start | bytes 3342336 | tf_op jit(solution)/shard_map/reduce_scatter | solution.py:510
  1100.2 177.3 %all-gather.35.cloned.1.call-start = ((), (), s32[]{:S(2)}) async-start(), calls=%async_computation.29 | async-start | bytes 4423680 | tf_op jit(solution)/shard_map/all_gather | solution.py:675
  1233.2 43.5 %collective-permute-start.5 = (bf16[64,1536]{1,0:T(8,128)(2,1)S(1)}, bf16[64,1536]{1,0:T(8,128)(2,1)S(1)}, u32[]{:S(2)}, u32[]{:S(2)}) collective-permute-start(bf16[64,1536]{1,0:T(8,128)(2,1)S(1)} %get-tuple-element.93), channel_id=1, source_target_pairs={{0,16},{16,0},{1,17},{17,1},{2,18},{18,2},{3,19},{19,3},{4,20},{20... | collective-permute-start | bytes 589832 | tf_op jit(solution)/shard_map/ppermute | solution.py:526
  (98 other events, 2019.4 us)
Sparse Core Ops, SparseCore 0:
  69.7 46.4 all-gather.16
  128.0 64.0 reduce-scatter.8
  196.2 57.1 all-gather.18
  320.8 66.5 reduce-scatter.10
  390.1 44.9 all-gather.20
  446.3 64.1 reduce-scatter.12
  513.4 44.9 all-gather.22
  561.3 43.9 all-gather.32
  616.0 64.1 reduce-scatter.16
  683.8 45.0 all-gather.24
  745.0 64.1 reduce-scatter.18
  812.8 44.9 all-gather.26
  867.4 64.1 reduce-scatter.20
  935.2 45.2 all-gather.28
  984.8 66.1 reduce-scatter.14
  1052.4 31.2 all-gather.38
  1085.7 17.4 all-gather.36
  1105.2 46.3 all-gather.30
  1155.4 65.0 reduce-scatter.22
  1222.5 31.6 all-gather.34

commit v2 on v1

--- a/solution.py
+++ b/solution.py
@@ -1,6 +1,10 @@
+import functools
+
 import jax
 import jax.numpy as jnp
 from jax import lax
+from jax.experimental import pallas as pl
+from jax.experimental.pallas import tpu as pltpu
 from jax.sharding import PartitionSpec as P
 
 HEADS = 16
@@ -502,14 +506,267 @@
     )
 
 
+MESH = pl.DeviceIdType.MESH
+
+
+def remote(source, target, sent, arrived, device):
+    return pltpu.make_async_remote_copy(
+        source, target, sent, arrived, device_id=device, device_id_type=MESH
+    )
+
+
+def greet(partners):
+    barrier = pltpu.get_barrier_semaphore()
+    for device in partners:
+        pl.semaphore_signal(barrier, 1, device_id=device, device_id_type=MESH)
+    pl.semaphore_wait(barrier, len(partners))
+
+
+def greet_line(blk_index, count, partners):
+    barrier = pltpu.get_barrier_semaphore()
+    for device in partners:
+        pl.semaphore_signal(barrier, 1, device_id=device, device_id_type=MESH)
+    for step, there in ((-1, blk_index > 0), (1, blk_index < count - 1)):
+
+        @pl.when(there)
+        def _():
+            pl.semaphore_signal(
+                barrier, 1, device_id={"blk": blk_index + step}, device_id_type=MESH
+            )
+
+    inner = (blk_index > 0).astype(jnp.int32) + (blk_index < count - 1).astype(jnp.int32)
+    pl.semaphore_wait(barrier, len(partners) + inner)
+
+
+def gather_kernel(
+    count, own, out, line_sent, line_got, side_sent, side_got, core_sent, core_got, local_done
+):
+    seq = lax.axis_index("seq")
+    b = lax.axis_index("blk")
+    core, side = {"seq": seq ^ 1}, {"seq": seq ^ 2}
+    greet_line(b, count, (core, side))
+    base, side_base = seq * count, (seq ^ 2) * count
+
+    def along_line(j, way, source=None):
+        device = {"blk": b + (1 if way else -1)}
+        spot = out.at[base + j]
+        return remote(
+            spot if source is None else source, spot, line_sent.at[j, way], line_got.at[j], device
+        )
+
+    def to_side(j, source=None):
+        spot = out.at[base + j]
+        return remote(
+            spot if source is None else source, spot, side_sent.at[j], side_got.at[j], side
+        )
+
+    def to_core(turn_of, j, source=None):
+        spot = out.at[(base if turn_of == 0 else side_base) + j]
+        return remote(
+            spot if source is None else source,
+            spot,
+            core_sent.at[turn_of, j],
+            core_got.at[turn_of, j],
+            core,
+        )
+
+    local = pltpu.make_async_copy(own, out.at[base + b], local_done)
+    local.start()
+    to_side(b, own).start()
+
+    @pl.when(b > 0)
+    def _():
+        along_line(b, 0, own).start()
+
+    @pl.when(b < count - 1)
+    def _():
+        along_line(b, 1, own).start()
+
+    to_core(0, b, own).start()
+
+    def from_line(j, way):
+        spot = out.at[base + j]
+        remote(spot, spot, line_got.at[j], line_got.at[j], core).wait_recv()
+
+        @pl.when((b < count - 1) if way else (b > 0))
+        def _():
+            along_line(j, way).start()
+
+        to_side(j).start()
+        to_core(0, j).start()
+
+    def from_side(j):
+        spot = out.at[side_base + j]
+        remote(spot, spot, side_got.at[j], side_got.at[j], core).wait_recv()
+        to_core(1, j).start()
+
+    for k in range(1, count + 1):
+        if k < count:
+            pl.when(b - k >= 0)(functools.partial(from_line, b - k, 1))
+            pl.when(b + k < count)(functools.partial(from_line, b + k, 0))
+        if k == 1:
+            from_side(b)
+        else:
+            pl.when(b - k + 1 >= 0)(functools.partial(from_side, b - k + 1))
+            pl.when(b + k - 1 < count)(functools.partial(from_side, b + k - 1))
+    for half, corner in ((0, seq ^ 1), (1, seq ^ 3)):
+        for j in range(count):
+            spot = out.at[corner * count + j]
+            remote(spot, spot, core_got.at[half, j], core_got.at[half, j], core).wait_recv()
+    local.wait()
+    for j in range(count):
+        to_side(j).wait_send()
+        to_core(0, j).wait_send()
+        to_core(1, j).wait_send()
+
+    @pl.when(b > 0)
+    def _():
+        along_line(b, 0).wait_send()
+
+    @pl.when(b < count - 1)
+    def _():
+        along_line(b, 1).wait_send()
+
+    for k in range(1, count):
+
+        @pl.when((b - k >= 0) & (b < count - 1))
+        def _():
+            along_line(b - k, 1).wait_send()
+
+        @pl.when((b + k < count) & (b > 0))
+        def _():
+            along_line(b + k, 0).wait_send()
+
+
 def group_gather(block):
-    return lax.all_gather(block, ("seq", "blk"), axis=0, tiled=True)
+    seq_count, count = lax.axis_size("seq"), lax.axis_size("blk")
+    dma = pltpu.SemaphoreType.DMA
+    gathered = pl.pallas_call(
+        functools.partial(gather_kernel, count),
+        out_shape=jax.ShapeDtypeStruct((seq_count * count,) + block.shape, block.dtype),
+        in_specs=[pl.BlockSpec(memory_space=pltpu.VMEM)],
+        out_specs=pl.BlockSpec(memory_space=pltpu.VMEM),
+        scratch_shapes=[
+            dma((count, 2)),
+            dma((count,)),
+            dma((count,)),
+            dma((count,)),
+            dma((2, count)),
+            dma((2, count)),
+            dma,
+        ],
+        compiler_params=pltpu.CompilerParams(
+            collective_id=0, has_side_effects=True, vmem_limit_bytes=48 * 2**20
+        ),
+        name="gather_tokens",
+    )(block)
+    return gathered.reshape(-1, block.shape[1])
+
+
+def scatter_kernel(
+    count,
+    partial,
+    out,
+    core_slot,
+    side_slot,
+    line_slot,
+    side_out,
+    line_out,
+    core_sent,
+    core_got,
+    side_sent,
+    side_got,
+    line_sent,
+    line_got,
+):
+    seq = lax.axis_index("seq")
+    b = lax.axis_index("blk")
+    core, side = {"seq": seq ^ 1}, {"seq": seq ^ 2}
+    greet((core, side) + tuple({"blk": lax.rem(b + k, count)} for k in range(1, count)))
+    away = tuple(range(count // 2, 0, -1)) + tuple(range(count // 2 + 1, count)) + (0,)
+    place = [lax.rem(b + k, count) for k in away]
+
+    def to_core(half, k):
+        source = partial.at[(seq ^ (1 if half else 3)) * count + place[k]]
+        return remote(
+            source, core_slot.at[half, k], core_sent.at[half, k], core_got.at[half, k], core
+        )
+
+    def to_side(k):
+        return remote(side_out.at[k], side_slot.at[k], side_sent.at[k], side_got.at[k], side)
+
+    def along_line(k):
+        slot = away[k] - 1
+        return remote(
+            line_out.at[k],
+            line_slot.at[slot],
+            line_sent.at[k],
+            line_got.at[slot],
+            {"blk": place[k]},
+        )
+
+    for half in range(2):
+        for k in range(count):
+            to_core(half, k).start()
+    for k in range(count):
+        to_core(0, k).wait_recv()
+        total = partial[(seq ^ 2) * count + place[k]].astype(jnp.float32)
+        total += core_slot[0, k].astype(jnp.float32)
+        side_out[k] = total.astype(jnp.bfloat16)
+        to_side(k).start()
+    for k in range(count):
+        to_core(1, k).wait_recv()
+        to_side(k).wait_recv()
+        total = partial[seq * count + place[k]].astype(jnp.float32)
+        total += core_slot[1, k].astype(jnp.float32)
+        total += side_slot[k].astype(jnp.float32)
+        if k < count - 1:
+            line_out[k] = total.astype(jnp.bfloat16)
+            along_line(k).start()
+        else:
+            out[...] = total
+    for k in range(count - 1):
+        along_line(k).wait_recv()
+        out[...] += line_slot[away[k] - 1].astype(jnp.float32)
+    for k in range(count):
+        to_core(0, k).wait_send()
+        to_core(1, k).wait_send()
+        to_side(k).wait_send()
+        if k < count - 1:
+            along_line(k).wait_send()
 
 
 def group_scatter(partial):
-    return lax.psum_scatter(
-        partial.astype(jnp.bfloat16), ("seq", "blk"), scatter_dimension=0, tiled=True
-    ).astype(jnp.float32)
+    seq_count, count = lax.axis_size("seq"), lax.axis_size("blk")
+    rows, width = partial.shape[0] // (seq_count * count), partial.shape[1]
+    dma = pltpu.SemaphoreType.DMA
+
+    def slots(*places):
+        return pltpu.VMEM(places + (rows, width), jnp.bfloat16)
+
+    return pl.pallas_call(
+        functools.partial(scatter_kernel, count),
+        out_shape=jax.ShapeDtypeStruct((rows, width), jnp.float32),
+        in_specs=[pl.BlockSpec(memory_space=pltpu.VMEM)],
+        out_specs=pl.BlockSpec(memory_space=pltpu.VMEM),
+        scratch_shapes=[
+            slots(2, count),
+            slots(count),
+            slots(count - 1),
+            slots(count),
+            slots(count - 1),
+            dma((2, count)),
+            dma((2, count)),
+            dma((count,)),
+            dma((count,)),
+            dma((count - 1,)),
+            dma((count - 1,)),
+        ],
+        compiler_params=pltpu.CompilerParams(
+            collective_id=1, has_side_effects=True, vmem_limit_bytes=48 * 2**20
+        ),
+        name="scatter_tokens",
+    )(partial.astype(jnp.bfloat16).reshape(seq_count * count, rows, width))
 
 
 def turn(field_in, cosine, sine):
@@ -522,7 +779,7 @@
     )
 
 
-def swapped(own, kept_here):
+def swapped(own):
     return lax.ppermute(own, "section", [(0, 1), (1, 0)])
 
 
@@ -699,7 +956,7 @@
     blk_index = lax.axis_index("blk")
     tokens = inputs.shape[2] * lax.axis_size("seq") * lax.axis_size("blk")
     own = spread_weights(tuple(weight[0] for weight in params))
-    other = tuple(swapped(part, None) for part in own)
+    other = tuple(swapped(part) for part in own)
     first = tuple(jnp.where(at_first, a, b) for a, b in zip(own, other))
     second = tuple(jnp.where(at_first, b, a) for a, b in zip(own, other))
     x_own = lax.dynamic_index_in_dim(inputs, section, 0, keepdims=False)[0].astype(jnp.float32)
@@ -729,7 +986,7 @@
 
     def by_section(for_first, for_second):
         kept = jnp.where(at_first, for_first, for_second)
-        received = swapped(jnp.where(at_first, for_second, for_first), None)
+        received = swapped(jnp.where(at_first, for_second, for_first))
         return jnp.stack(
             [jnp.where(at_first, kept, received), jnp.where(at_first, received, kept)]
         )[None, :, None]
@@ -739,7 +996,7 @@
     summed = []
     for one, two in zip(grads_first, grads_second):
         kept = jnp.where(at_first, one, two)
-        received = swapped(jnp.where(at_first, two, one).astype(jnp.bfloat16), None)
+        received = swapped(jnp.where(at_first, two, one).astype(jnp.bfloat16))
         summed.append((kept + received.astype(jnp.float32)).astype(jnp.bfloat16))
     query, key, value, out, gate, up, down = finish_grads(summed)
     gains = lax.psum(jnp.stack([gains_first, gains_second]), ("section", "seq", "blk"))

time: 1310 us -> 936 us (0.71)
  waiting for transfers between devices: 819 us -> 56.6 us
  Pallas kernels: 0 us -> 460 us
  blocking collectives: 143 us -> 106 us
  matrix products: 93.1 us -> 71.6 us
  other arithmetic: 84.1 us -> 70.9 us
    pallas_call x0 -> x16, Pallas kernels: none -> 460 us  [the longest x8 251 us: group_scatter(): pl.pallas_call(functools.partial(scatter_kernel, count), out_shape=jax.Sh...]
    reduce_scatter x8 -> x0, waiting for transfers between devices: 387 us -> none  [group_scatter(): lax.psum_scatter(partial.astype(jnp.bfloat16), ('seq', 'blk'), scatter_di...]
    all_gather x8 -> x0, waiting for transfers between devices: 269 us -> none  [group_gather(): return lax.all_gather(block, ('seq', 'blk'), axis=0, tiled=True)]
    ppermute x10, waiting for transfers between devices: 134 us -> 56.5 us  [swapped(): return lax.ppermute(own, 'section', [(0, 1), (1, 0)])]
    all_to_all x2 -> x1, blocking collectives: 76 us -> 38.5 us  [finish_grads(): lax.all_to_all(wide[None], 'blk', split_axis=1, concat_axis=0, tiled=True)]
    all_to_all x1 -> x2, waiting for transfers between devices: 28.9 us -> 0.01 us  [the longest x1 0.01 us: spread_weights(): lax.all_to_all(attn, 'blk', split_axis=0, concat_axis=2, tiled=True)[0]]
  transfers between devices with their start and end apart: 31 -> 16, of which waited for: 21 -> 3; matrix products, arithmetic and copies ran while one was open for 15% -> 18% of each run, Pallas kernels for 0% -> 24%
where the time goes in v2:
time: 936 us; the launch traced here: 926 us
  Pallas kernels  460 us (49%)
  local copies, waits for them, and re-layouts  127 us (14%)
  blocking collectives  106 us (11%)
  matrix products  71.6 us (8%)
  other arithmetic  70.9 us (8%)
  waiting for transfers between devices  56.6 us (6%)
  starting transfers between devices  19.3 us (2%)
  between operations  15.9 us (2%)
    pallas_call x8, Pallas kernels, group_scatter(): pl.pallas_call(functools.partial(scatter_kernel, count), out_shape=jax.Sh...  251 us
    pallas_call x8, Pallas kernels, group_gather(): pl.pallas_call(functools.partial(gather_kernel, count), out_shape=jax.Sha...  209 us
    ppermute x10, waiting for transfers between devices, swapped(): return lax.ppermute(own, 'section', [(0, 1), (1, 0)])  56.5 us
    unnamed x198, local copies, waits for them, and re-layouts  54.1 us
    psum x1, blocking collectives, head_shards(): lax.psum(jnp.stack([gains_first, gains_second]), ('section', 'seq', 'blk'))  41.4 us
    all_to_all x1, blocking collectives, finish_grads(): lax.all_to_all(wide[None], 'blk', split_axis=1, concat_axis=0, tiled=True)  38.5 us
    unnamed x12, other arithmetic  30.6 us
    dot_general x12, matrix products, back_product(): lax.dot_general(left_side, right_side, (((1,), (1,)), ((), ())), preferre...  28.3 us
  transfers between devices with their start and end apart: 16, of which 3 were waited for; matrix products, arithmetic and copies ran while one was open for 18% of the time, Pallas kernels for 24%

profile of v2, /device:TPU:18, one launch (start us, length us, event | category | flops | bytes accessed | tf_op | source)
XLA Modules:
  0.0 926.5 jit_solution(7549854965037256996)
XLA Ops:
  52.4 50.1 %gather_tokens.12 = bf16[16,64,1536]{2,1,0:T(8,128)(2,1)S(1)} custom-call(bf16[64,1536]{1,0:T(8,128)(2,1)S(1)} %dynamic-slice_bitcast_fusion.5.own), custom_call_target="tpu_custom_call" | custom-call | tf_op jit(solution)/shard_map/gather_tokens/pallas_call | solution.py:644
  106.3 25.8 %gather_tokens.8 = bf16[16,64,1536]{2,1,0:T(8,128)(2,1)S(1)} custom-call(bf16[64,1536]{1,0:T(8,128)(2,1)S(1)} %fusion.39.own), custom_call_target="tpu_custom_call" | custom-call | tf_op jit(solution)/shard_map/gather_tokens/pallas_call | solution.py:644
  146.2 30.5 %scatter_tokens.8 = f32[64,1536]{1,0:T(8,128)S(1)} custom-call(bf16[16,64,1536]{2,1,0:T(8,128)(2,1)S(1)} %bitcast.181), custom_call_target="tpu_custom_call" | custom-call | tf_op jit(solution)/shard_map/scatter_tokens/pallas_call | solution.py:747
  177.5 22.8 %gather_tokens.9 = bf16[16,64,1536]{2,1,0:T(8,128)(2,1)S(1)} custom-call(bf16[64,1536]{1,0:T(8,128)(2,1)S(1)} %multiply_convert_fusion.9.own), custom_call_target="tpu_custom_call" | custom-call | tf_op jit(solution)/shard_map/gather_tokens/pallas_call | solution.py:644
  205.2 29.2 %scatter_tokens.9 = f32[64,1536]{1,0:T(8,128)S(1)} custom-call(bf16[16,64,1536]{2,1,0:T(8,128)(2,1)S(1)} %bitcast.174), custom_call_target="tpu_custom_call" | custom-call | tf_op jit(solution)/shard_map/scatter_tokens/pallas_call | solution.py:747
  235.2 22.4 %gather_tokens.10 = bf16[16,64,1536]{2,1,0:T(8,128)(2,1)S(1)} custom-call(bf16[64,1536]{1,0:T(8,128)(2,1)S(1)} %fusion.29.own), custom_call_target="tpu_custom_call" | custom-call | tf_op jit(solution)/shard_map/gather_tokens/pallas_call | solution.py:644
  264.5 29.3 %scatter_tokens.10 = f32[64,1536]{1,0:T(8,128)S(1)} custom-call(bf16[16,64,1536]{2,1,0:T(8,128)(2,1)S(1)} %bitcast.182), custom_call_target="tpu_custom_call" | custom-call | tf_op jit(solution)/shard_map/scatter_tokens/pallas_call | solution.py:747
  294.0 22.2 %gather_tokens.11 = bf16[16,64,1536]{2,1,0:T(8,128)(2,1)S(1)} custom-call(bf16[64,1536]{1,0:T(8,128)(2,1)S(1)} %multiply_convert_fusion.8.own), custom_call_target="tpu_custom_call" | custom-call | tf_op jit(solution)/shard_map/gather_tokens/pallas_call | solution.py:644
  326.6 29.3 %scatter_tokens.12 = f32[64,1536]{1,0:T(8,128)S(1)} custom-call(bf16[16,64,1536]{2,1,0:T(8,128)(2,1)S(1)} %bitcast.192), custom_call_target="tpu_custom_call" | custom-call | tf_op jit(solution)/shard_map/scatter_tokens/pallas_call | solution.py:747
  357.5 22.2 %gather_tokens.13 = bf16[16,64,1536]{2,1,0:T(8,128)(2,1)S(1)} custom-call(bf16[64,1536]{1,0:T(8,128)(2,1)S(1)} %get-tuple-element.97.own), custom_call_target="tpu_custom_call" | custom-call | tf_op jit(solution)/shard_map/gather_tokens/pallas_call | solution.py:644
  393.8 29.6 %scatter_tokens.13 = f32[64,1536]{1,0:T(8,128)S(1)} custom-call(bf16[16,64,1536]{2,1,0:T(8,128)(2,1)S(1)} %bitcast.191), custom_call_target="tpu_custom_call" | custom-call | tf_op jit(solution)/shard_map/scatter_tokens/pallas_call | solution.py:747
  424.3 21.8 %gather_tokens.14 = bf16[16,64,1536]{2,1,0:T(8,128)(2,1)S(1)} custom-call(bf16[64,1536]{1,0:T(8,128)(2,1)S(1)} %fusion.33.own), custom_call_target="tpu_custom_call" | custom-call | tf_op jit(solution)/shard_map/gather_tokens/pallas_call | solution.py:644
  453.6 29.7 %scatter_tokens.14 = f32[64,1536]{1,0:T(8,128)S(1)} custom-call(bf16[16,64,1536]{2,1,0:T(8,128)(2,1)S(1)} %bitcast.189), custom_call_target="tpu_custom_call" | custom-call | tf_op jit(solution)/shard_map/scatter_tokens/pallas_call | solution.py:747
  489.5 21.8 %gather_tokens.15 = bf16[16,64,1536]{2,1,0:T(8,128)(2,1)S(1)} custom-call(bf16[64,1536]{1,0:T(8,128)(2,1)S(1)} %get-tuple-element.95.own), custom_call_target="tpu_custom_call" | custom-call | tf_op jit(solution)/shard_map/gather_tokens/pallas_call | solution.py:644
  547.5 20.5 %collective-permute-done.6 = bf16[288,1536]{1,0:T(8,128)(2,1)S(1)} collective-permute-done((bf16[288,1536]{1,0:T(8,128)(2,1)S(1)}, bf16[288,1536]{1,0:T(8,128)(2,1)S(1)}, u32[]{:S(2)}, u32[]{:S(2)}) %collective-permute-start.6) | collective-permute-done | bytes 884768 | tf_op jit(solution)/shard_map/ppermute | solution.py:783
  576.3 10.4 %reduce.8 = bf16[1536,288]{1,0:T(8,128)(2,1)} reduce(bf16[1536,1,288]{2,1,0:T(2,128)(2,1)} %bitcast.197, bf16[]{:T(256)} %broadcast.176), dimensions={1}, to_apply=%bitcast.121.reduce_sub_computation | reduce | bytes 1769474
  590.8 25.6 %all_to_all.51 = bf16[4,2,55296]{2,1,0:T(2,128)(2,1)} all-to-all(bf16[4,2,55296]{2,1,0:T(2,128)(2,1)} %reshape.269), channel_id=1, replica_groups=mesh['section'=2,'seq'=4,'blk'=4] {'blk'}, dimensions={0} | all-to-all | bytes 1769472 | tf_op jit(solution)/shard_map/all_to_all | solution.py:929
  639.1 34.5 %collective-permute-done.8 = bf16[1536,512]{1,0:T(8,128)(2,1)S(1)} collective-permute-done((bf16[1536,512]{1,0:T(8,128)(2,1)S(1)}, bf16[1536,512]{1,0:T(8,128)(2,1)S(1)}, u32[]{:S(2)}, u32[]{:S(2)}) %collective-permute-start.8) | collective-permute-done | bytes 1572896 | tf_op jit(solution)/shard_map/ppermute | solution.py:783
  674.6 11.8 %copy.130 = bf16[1,1536,512]{2,0,1:T(2,128)(2,1)S(1)} copy(bf16[1,1536,512]{2,1,0:T(8,128)(2,1)S(1)} %fusion.3) | data formatting | bytes 3145728 | tf_op jit(solution)/shard_map/broadcast_in_dim | solution.py:930
  686.4 11.1 %reduce.9 = bf16[1536,512]{1,0:T(8,128)(2,1)} reduce(bf16[1536,1,512]{2,1,0:T(2,128)(2,1)S(1)} %bitcast.195, bf16[]{:T(256)} %broadcast.176), dimensions={1}, to_apply=%bitcast.167.reduce_sub_computation | reduce | bytes 3145730
  700.4 38.5 %all_to_all.52 = bf16[4,2,98304]{2,1,0:T(2,128)(2,1)} all-to-all(bf16[4,2,98304]{2,1,0:T(2,128)(2,1)S(1)} %reshape.267), channel_id=1, replica_groups=mesh['section'=2,'seq'=4,'blk'=4] {'blk'}, dimensions={0} | all-to-all | bytes 3145728 | tf_op jit(solution)/shard_map/all_to_all | solution.py:930
  746.7 35.2 %scatter_tokens.11 = f32[64,1536]{1,0:T(8,128)S(1)} custom-call(bf16[16,64,1536]{2,1,0:T(8,128)(2,1)S(1)} %bitcast.173), custom_call_target="tpu_custom_call" | custom-call | tf_op jit(solution)/shard_map/scatter_tokens/pallas_call | solution.py:747
  784.4 38.0 %scatter_tokens.15 = f32[64,1536]{1,0:T(8,128)S(1)} custom-call(bf16[16,64,1536]{2,1,0:T(8,128)(2,1)S(1)} %bitcast.190), custom_call_target="tpu_custom_call" | custom-call | tf_op jit(solution)/shard_map/scatter_tokens/pallas_call | solution.py:747
  823.5 41.4 %psum.7 = f32[2,2,1536]{2,1,0:T(2,128)S(1)} all-reduce(f32[2,2,1536]{2,1,0:T(2,128)S(1)} %pad_maximum_fusion.19), channel_id=1, replica_groups=mesh['section'=2,'seq'=4,'blk'=4] {'section','seq','blk'}, use_global_device_ids=true, to_apply=%region_21.22 | all-reduce | flops 6144 | bytes 49152 | tf_op jit(solution)/shard_map/psum | solution.py:1002
  (364 shorter events, 256.9 us)
Async XLA Ops:
  17.3 27.3 %all-to-all-start = ((bf16[4,290,384]{2,1,0:T(8,128)(2,1)}), bf16[4,290,384]{2,1,0:T(8,128)(2,1)}, u32[]{:S(2)}, u32[]{:S(2)}) async-start(bf16[4,290,384]{2,1,0:T(8,128)(2,1)} %pad_maximum_fusion.2), calls=%async_computation | async-start | bytes 1818624 | tf_op jit(solution)/shard_map/all_to_all | solution.py:817
  23.5 120.7 %copy-start.17 = (bf16[96,1536]{1,0:T(8,128)(2,1)}, bf16[96,1536]{1,0:T(8,128)(2,1)S(1)}, u32[]{:S(2)}) copy-start(bf16[96,1536]{1,0:T(8,128)(2,1)S(1)} %dynamic-slice_bitcast_fusion.1) | copy-start | bytes 884740
  23.5 120.7 %collective-permute-start.1 = (bf16[96,1536]{1,0:T(8,128)(2,1)S(1)}, bf16[96,1536]{1,0:T(8,128)(2,1)}, u32[]{:S(2)}, u32[]{:S(2)}) collective-permute-start(bf16[96,1536]{1,0:T(8,128)(2,1)S(1)} %dynamic-slice_bitcast_fusion.1), channel_id=1, source_target_pairs={{0,16},{16,0},{1,17},{17,1},{2,18},{18,2},{3,19},{19,3},{4,20},{20... | collective-permute-start | bytes 884744 | tf_op jit(solution)/shard_map/ppermute | solution.py:783
  25.0 177.6 %collective-permute-start.3 = (bf16[256,1536]{1,0:T(8,128)(2,1)}, bf16[256,1536]{1,0:T(8,128)(2,1)}, u32[]{:S(2)}, u32[]{:S(2)}) collective-permute-start(bf16[256,1536]{1,0:T(8,128)(2,1)} %dynamic-slice_bitcast_fusion), channel_id=1, source_target_pairs={{0,16},{16,0},{1,17},{17,1},{2,18},{18,2},{3,19},{19,3},{4,20},{20... | collective-permute-start | bytes 2359304 | tf_op jit(solution)/shard_map/ppermute | solution.py:783
  44.6 95.9 %all-to-all-start.1 = ((bf16[4,384,512]{2,1,0:T(8,128)(2,1)}), bf16[4,384,512]{2,1,0:T(8,128)(2,1)}, u32[]{:S(2)}, u32[]{:S(2)}) async-start(bf16[4,384,512]{2,1,0:T(8,128)(2,1)} %maximum_bitcast_fusion), calls=%async_computation.1 | async-start | bytes 3145728 | tf_op jit(solution)/shard_map/all_to_all | solution.py:818
  49.7 817.6 %all-gather.12.cloned.1.call-start = ((), (), s32[]{:S(2)}) async-start(), calls=%async_computation.6 | async-start | bytes 1474560 | tf_op jit(solution)/shard_map/all_gather | solution.py:932
  51.6 52.6 %copy-start.21 = (bf16[2,1,64,1536]{3,2,1,0:T(8,128)(2,1)S(1)}, bf16[2,1,64,1536]{3,2,1,0:T(8,128)(2,1)}, u32[]{:S(2)}) copy-start(bf16[2,1,64,1536]{3,2,1,0:T(8,128)(2,1)} %param.12) | copy-start | bytes 1179652
  51.8 53.2 %collective-permute-start = (bf16[290,1536]{1,0:T(8,128)(2,1)S(1)}, bf16[290,1536]{1,0:T(8,128)(2,1)S(1)}, u32[]{:S(2)}, u32[]{:S(2)}) collective-permute-start(bf16[290,1536]{1,0:T(8,128)(2,1)S(1)} %bitcast.206), channel_id=1, source_target_pairs={{0,16},{16,0},{1,17},{17,1},{2,18},{18,2},{3,19},{19,3},{4,20},{20... | collective-permute-start | bytes 2672648 | tf_op jit(solution)/shard_map/ppermute | solution.py:783
  104.3 154.4 %copy-start.67 = (f32[48]{0:T(128)}, f32[48]{0:T(128)S(1)}, u32[]{:S(2)}) copy-start(f32[48]{0:T(128)S(1)} %multiply_power_fusion) | copy-start | bytes 580
  140.5 59.9 %collective-permute-start.2 = (bf16[1536,512]{1,0:T(8,128)(2,1)}, bf16[1536,512]{1,0:T(8,128)(2,1)S(1)}, u32[]{:S(2)}, u32[]{:S(2)}) collective-permute-start(bf16[1536,512]{1,0:T(8,128)(2,1)} %bitcast.21), channel_id=1, source_target_pairs={{0,16},{16,0},{1,17},{17,1},{2,18},{18,2},{3,19},{19,3},{4,20},{20... | collective-permute-start | bytes 4718600 | tf_op jit(solution)/shard_map/ppermute | solution.py:783
  262.1 118.7 %copy-start.65 = (f32[1024]{0:T(1024)}, f32[1024]{0:T(1024)S(1)}, u32[]{:S(2)}) copy-start(f32[1024]{0:T(1024)S(1)} %log_add_fusion) | copy-start | bytes 12292
  293.9 62.7 %copy-start.15 = (f32[64,1536]{1,0:T(8,128)}, f32[64,1536]{1,0:T(8,128)S(1)}, u32[]{:S(2)}) copy-start(f32[64,1536]{1,0:T(8,128)S(1)} %get-tuple-element.102) | copy-start | bytes 1179652
  486.4 45.5 %collective-permute-start.9 = (bf16[256,1536]{1,0:T(8,128)(2,1)}, bf16[256,1536]{1,0:T(8,128)(2,1)}, u32[]{:S(2)}, u32[]{:S(2)}) collective-permute-start(bf16[256,1536]{1,0:T(8,128)(2,1)} %get-tuple-element.154), channel_id=1, source_target_pairs={{0,16},{16,0},{1,17},{17,1},{2,18},{18,2},{3,19},{19,3},{4,20},{20... | collective-permute-start | bytes 2359304 | tf_op jit(solution)/shard_map/ppermute | solution.py:783
  512.6 9.4 %collective-permute-start.7 = (bf16[96,1536]{1,0:T(8,128)(2,1)S(1)}, bf16[96,1536]{1,0:T(8,128)(2,1)S(1)}, u32[]{:S(2)}, u32[]{:S(2)}) collective-permute-start(bf16[96,1536]{1,0:T(8,128)(2,1)S(1)} %get-tuple-element.150), channel_id=1, source_target_pairs={{0,16},{16,0},{1,17},{17,1},{2,18},{18,2},{3,19},{19,3},{4,20},{20... | collective-permute-start | bytes 884744 | tf_op jit(solution)/shard_map/ppermute | solution.py:783
  522.8 347.4 %all-gather.14.cloned.1.call-start = ((), (), s32[]{:S(2)}) async-start(), calls=%async_computation.7 | async-start | bytes 3932160 | tf_op jit(solution)/shard_map/all_gather | solution.py:932
  534.3 341.3 %all-gather.10.cloned.1.call-start = ((), (), s32[]{:S(2)}) async-start(), calls=%async_computation.5 | async-start | bytes 4423680 | tf_op jit(solution)/shard_map/all_gather | solution.py:932
  546.9 21.2 %collective-permute-start.6 = (bf16[288,1536]{1,0:T(8,128)(2,1)S(1)}, bf16[288,1536]{1,0:T(8,128)(2,1)S(1)}, u32[]{:S(2)}, u32[]{:S(2)}) collective-permute-start(bf16[288,1536]{1,0:T(8,128)(2,1)S(1)} %get-tuple-element.148), channel_id=1, source_target_pairs={{0,16},{16,0},{1,17},{17,1},{2,18},{18,2},{3,19},{19,3},{4,20},{20... | collective-permute-start | bytes 2654216 | tf_op jit(solution)/shard_map/ppermute | solution.py:783
  632.1 256.3 %all-gather.8.cloned.1.call-start = ((), (), s32[]{:S(2)}) async-start(), calls=%async_computation.4 | async-start | bytes 7864320 | tf_op jit(solution)/shard_map/all_gather | solution.py:932
  638.3 35.4 %collective-permute-start.8 = (bf16[1536,512]{1,0:T(8,128)(2,1)S(1)}, bf16[1536,512]{1,0:T(8,128)(2,1)S(1)}, u32[]{:S(2)}, u32[]{:S(2)}) collective-permute-start(bf16[1536,512]{1,0:T(8,128)(2,1)S(1)} %get-tuple-element.152), channel_id=1, source_target_pairs={{0,16},{16,0},{1,17},{17,1},{2,18},{18,2},{3,19},{19,3},{4,20},{20... | collective-permute-start | bytes 4718600 | tf_op jit(solution)/shard_map/ppermute | solution.py:783
  782.0 83.5 %collective-permute-start.4 = (bf16[64,1536]{1,0:T(8,128)(2,1)S(1)}, bf16[64,1536]{1,0:T(8,128)(2,1)S(1)}, u32[]{:S(2)}, u32[]{:S(2)}) collective-permute-start(bf16[64,1536]{1,0:T(8,128)(2,1)S(1)} %get-tuple-element.99), channel_id=1, source_target_pairs={{0,16},{16,0},{1,17},{17,1},{2,18},{18,2},{3,19},{19,3},{4,20},{20... | collective-permute-start | bytes 589832 | tf_op jit(solution)/shard_map/ppermute | solution.py:783
  784.3 38.0 %copy-start.22 = (bf16[2,1,64,1536]{3,2,1,0:T(8,128)(2,1)S(1)}, bf16[2,1,64,1536]{3,2,1,0:T(8,128)(2,1)}, u32[]{:S(2)}) copy-start(bf16[2,1,64,1536]{3,2,1,0:T(8,128)(2,1)} %param.12) | copy-start | bytes 1179652
  784.3 38.2 %copy-start.34 = (f32[64,1536]{1,0:T(8,128)S(1)}, f32[64,1536]{1,0:T(8,128)}, u32[]{:S(2)}) copy-start(f32[64,1536]{1,0:T(8,128)} %get-tuple-element.96) | copy-start | bytes 1179652
  784.4 38.2 %copy-start.84 = (f32[64]{0:T(128)S(1)}, f32[64]{0:T(128)}, u32[]{:S(2)}) copy-start(f32[64]{0:T(128)} %get-tuple-element.132) | copy-start | bytes 772
  822.8 43.6 %collective-permute-start.5 = (bf16[64,1536]{1,0:T(8,128)(2,1)S(1)}, bf16[64,1536]{1,0:T(8,128)(2,1)S(1)}, u32[]{:S(2)}, u32[]{:S(2)}) collective-permute-start(bf16[64,1536]{1,0:T(8,128)(2,1)S(1)} %get-tuple-element.93), channel_id=1, source_target_pairs={{0,16},{16,0},{1,17},{17,1},{2,18},{18,2},{3,19},{19,3},{4,20},{20... | collective-permute-start | bytes 589832 | tf_op jit(solution)/shard_map/ppermute | solution.py:783
  (83 other events, 920.0 us)
Sparse Core Ops, SparseCore 0:
  522.9 19.4 all-gather.11
  544.5 28.5 all-gather.13
  632.2 32.0 all-gather.9
  743.7 73.5 all-gather.7

commit v3 on v2

--- a/solution.py
+++ b/solution.py
@@ -538,13 +538,19 @@
     pl.semaphore_wait(barrier, len(partners) + inner)
 
 
-def gather_kernel(
+def settled(spot, semaphore, received):
+    copy = remote(spot, spot, semaphore, semaphore, {"seq": lax.axis_index("seq") ^ 1})
+    if received:
+        copy.wait_recv()
+    else:
+        copy.wait_send()
+
+
+def gather_steps(
     count, own, out, line_sent, line_got, side_sent, side_got, core_sent, core_got, local_done
 ):
-    seq = lax.axis_index("seq")
-    b = lax.axis_index("blk")
+    seq, b = lax.axis_index("seq"), lax.axis_index("blk")
     core, side = {"seq": seq ^ 1}, {"seq": seq ^ 2}
-    greet_line(b, count, (core, side))
     base, side_base = seq * count, (seq ^ 2) * count
 
     def along_line(j, way, source=None):
@@ -560,13 +566,13 @@
             spot if source is None else source, spot, side_sent.at[j], side_got.at[j], side
         )
 
-    def to_core(turn_of, j, source=None):
-        spot = out.at[(base if turn_of == 0 else side_base) + j]
+    def to_core(half, j, source=None):
+        spot = out.at[(side_base if half else base) + j]
         return remote(
             spot if source is None else source,
             spot,
-            core_sent.at[turn_of, j],
-            core_got.at[turn_of, j],
+            core_sent.at[half, j],
+            core_got.at[half, j],
             core,
         )
 
@@ -583,10 +589,10 @@
         along_line(b, 1, own).start()
 
     to_core(0, b, own).start()
+    yield
 
     def from_line(j, way):
-        spot = out.at[base + j]
-        remote(spot, spot, line_got.at[j], line_got.at[j], core).wait_recv()
+        settled(out.at[base + j], line_got.at[j], True)
 
         @pl.when((b < count - 1) if way else (b > 0))
         def _():
@@ -596,8 +602,7 @@
         to_core(0, j).start()
 
     def from_side(j):
-        spot = out.at[side_base + j]
-        remote(spot, spot, side_got.at[j], side_got.at[j], core).wait_recv()
+        settled(out.at[side_base + j], side_got.at[j], True)
         to_core(1, j).start()
 
     for k in range(1, count + 1):
@@ -609,10 +614,10 @@
         else:
             pl.when(b - k + 1 >= 0)(functools.partial(from_side, b - k + 1))
             pl.when(b + k - 1 < count)(functools.partial(from_side, b + k - 1))
+        yield
     for half, corner in ((0, seq ^ 1), (1, seq ^ 3)):
         for j in range(count):
-            spot = out.at[corner * count + j]
-            remote(spot, spot, core_got.at[half, j], core_got.at[half, j], core).wait_recv()
+            settled(out.at[corner * count + j], core_got.at[half, j], True)
     local.wait()
     for j in range(count):
         to_side(j).wait_send()
@@ -638,23 +643,34 @@
             along_line(b + k, 0).wait_send()
 
 
+def gather_kernel(count, *refs):
+    seq, b = lax.axis_index("seq"), lax.axis_index("blk")
+    greet_line(b, count, ({"seq": seq ^ 1}, {"seq": seq ^ 2}))
+    for _ in gather_steps(count, *refs):
+        pass
+
+
+def gather_semaphores(count):
+    dma = pltpu.SemaphoreType.DMA
+    return [
+        dma((count, 2)),
+        dma((count,)),
+        dma((count,)),
+        dma((count,)),
+        dma((2, count)),
+        dma((2, count)),
+        dma,
+    ]
+
+
 def group_gather(block):
     seq_count, count = lax.axis_size("seq"), lax.axis_size("blk")
-    dma = pltpu.SemaphoreType.DMA
     gathered = pl.pallas_call(
         functools.partial(gather_kernel, count),
         out_shape=jax.ShapeDtypeStruct((seq_count * count,) + block.shape, block.dtype),
         in_specs=[pl.BlockSpec(memory_space=pltpu.VMEM)],
         out_specs=pl.BlockSpec(memory_space=pltpu.VMEM),
-        scratch_shapes=[
-            dma((count, 2)),
-            dma((count,)),
-            dma((count,)),
-            dma((count,)),
-            dma((2, count)),
-            dma((2, count)),
-            dma,
-        ],
+        scratch_shapes=gather_semaphores(count),
         compiler_params=pltpu.CompilerParams(
             collective_id=0, has_side_effects=True, vmem_limit_bytes=48 * 2**20
         ),
@@ -779,57 +795,199 @@
     )
 
 
-def swapped(own):
-    return lax.ppermute(own, "section", [(0, 1), (1, 0)])
-
-
-def spread_weights(local_shards):
-    seq_index = lax.axis_index("seq")
-    seq_count = lax.axis_size("seq")
-    blk_count = lax.axis_size("blk")
+def spread_kernel(
+    count,
+    pieces,
+    w_gate,
+    w_up,
+    w_output,
+    w_down,
+    rows_in,
+    grads_in,
+    attn,
+    gate_up,
+    out,
+    down,
+    rows_all,
+    grads_all,
+    line_sent,
+    line_got,
+    cross_sent,
+    cross_got,
+    local_done,
+    *gather_sems,
+):
+    seq, b, section = lax.axis_index("seq"), lax.axis_index("blk"), lax.axis_index("section")
+    other = {"section": 1 - section}
+    greet(
+        (other, {"seq": seq ^ 1}, {"seq": seq ^ 2})
+        + tuple({"blk": lax.rem(b + k, count)} for k in range(1, count))
+    )
+    rows, lanes = w_gate.shape[0], gate_up.shape[2] // 2
+    out_rows, down_rows = out.shape[1], down.shape[1]
+    far_first = tuple(range(count // 2, 0, -1)) + tuple(range(count // 2 + 1, count))
+
+    def source(kind, j):
+        if kind == 0:
+            return pieces.at[j]
+        weight = w_gate if kind == 1 else w_up
+        return weight.at[:, pl.ds(pl.multiple_of((j * 4 + seq) * lanes, lanes), lanes)]
+
+    def target(kind, j):
+        if kind == 0:
+            return attn.at[section, :, pl.ds(pl.multiple_of(j * rows, rows), rows)]
+        return gate_up.at[
+            section, pl.ds(pl.multiple_of(j * rows, rows), rows), pl.ds((kind - 1) * lanes, lanes)
+        ]
+
+    def along_line(kind, k):
+        j = lax.rem(b + k, count)
+        return remote(
+            source(kind, j),
+            target(kind, b),
+            line_sent.at[kind, k],
+            line_got.at[kind, k],
+            {"blk": j},
+        )
+
+    def across(kind, j, slot, begin=None):
+        spot = target(kind, j)
+        return remote(
+            spot if begin is None else begin,
+            spot,
+            cross_sent.at[kind, slot],
+            cross_got.at[kind, slot],
+            other,
+        )
+
+    def own_rows(kind):
+        weight, place, size = (w_output, out, out_rows) if kind == 3 else (w_down, down, down_rows)
+        begin = weight.at[pl.ds(pl.multiple_of(seq * size, size), size)]
+        spot = place.at[section]
+        return (
+            remote(begin, spot, cross_sent.at[kind, 0], cross_got.at[kind, 0], other),
+            pltpu.make_async_copy(begin, spot, local_done.at[kind]),
+        )
+
+    def own_piece(kind):
+        return (
+            across(kind, b, 0, source(kind, b)),
+            pltpu.make_async_copy(source(kind, b), target(kind, b), local_done.at[kind]),
+        )
+
+    def forward(kind):
+        for k in far_first:
+            j = lax.rem(b + count - k, count)
+            settled(target(kind, j), line_got.at[kind, k], True)
+            across(kind, j, k).start()
+
+    first = gather_steps(count, rows_in, rows_all, *gather_sems[:7])
+    second = gather_steps(count, grads_in, grads_all, *gather_sems[7:])
+    for k in far_first:
+        along_line(0, k).start()
+    for copy in own_piece(0) + own_rows(3):
+        copy.start()
+    next(first)
+    next(first)
+    for kind in (1, 2):
+        for k in far_first:
+            along_line(kind, k).start()
+    next(first)
+    forward(0)
+    for copy in own_piece(1) + own_piece(2) + own_rows(4):
+        copy.start()
+    for _ in first:
+        pass
+    next(second)
+    forward(1)
+    next(second)
+    next(second)
+    forward(2)
+    for _ in second:
+        pass
+    for kind in range(3):
+        for k in range(count):
+            settled(target(kind, 0), cross_got.at[kind, k], True)
+            settled(target(kind, 0), cross_sent.at[kind, k], False)
+            if k:
+                settled(target(kind, 0), line_sent.at[kind, k], False)
+        own_piece(kind)[1].wait()
+    for kind in (3, 4):
+        passed, local = own_rows(kind)
+        passed.wait()
+        local.wait()
+
+
+def spread_weights(local_shards, rows_in, grads_in):
+    seq_index, seq_count = lax.axis_index("seq"), lax.axis_size("seq")
+    count = lax.axis_size("blk")
     gain_attn, w_query, w_key, w_value, w_output, gain_mlp, w_gate, w_up, w_down = local_shards
-    rows = w_query.shape[0]
-
-    def mine(weight, width, per_blk, place):
-        return lax.dynamic_index_in_dim(
-            weight.reshape(rows, blk_count, per_blk, width), place, 2, keepdims=False
-        )
-
-    kv_per_blk = KV_HEADS // blk_count
+    rows, width = w_query.shape[0], w_query.shape[1]
+    lanes = w_gate.shape[1] // (seq_count * count)
+    pad = 16
+
+    def heads_of(weight, per_blk, place):
+        head = jnp.arange(count)[:, None] * per_blk + place
+        column = (head * HEAD_DIM + jnp.arange(HEAD_DIM)).reshape(-1)
+        chosen = jnp.arange(weight.shape[1])[:, None] == column[None, :]
+        taken = lax.dot_general(
+            chosen.astype(jnp.bfloat16),
+            weight,
+            (((0,), (1,)), ((), ())),
+            preferred_element_type=jnp.float32,
+        )
+        return taken.astype(jnp.bfloat16).reshape(count, HEAD_DIM, rows)
+
+    kv_per_blk = KV_HEADS // count
     kv_place = seq_index * kv_per_blk // seq_count
-    ff_width = w_gate.shape[1] // (seq_count * blk_count)
-    attn = jnp.concatenate(
+    gains = jnp.concatenate(
+        [jnp.stack([gain_attn, gain_mlp]), jnp.zeros((pad - 2, rows), jnp.bfloat16)]
+    )
+    pieces = jnp.concatenate(
         [
-            mine(w_query, HEAD_DIM, seq_count, seq_index),
-            mine(w_key, HEAD_DIM, kv_per_blk, kv_place),
-            mine(w_value, HEAD_DIM, kv_per_blk, kv_place),
+            heads_of(w_query, seq_count, seq_index),
+            heads_of(w_key, kv_per_blk, kv_place),
+            heads_of(w_value, kv_per_blk, kv_place),
+            jnp.broadcast_to(gains[None], (count,) + gains.shape),
         ],
-        axis=-1,
-    ).transpose(1, 2, 0)
-    gains = jnp.stack([gain_attn, gain_mlp])
-    attn = jnp.concatenate(
-        [attn, jnp.broadcast_to(gains[None], (blk_count,) + gains.shape)], axis=1
-    )
-    wide = jnp.concatenate(
-        [mine(w_gate, ff_width, seq_count, seq_index), mine(w_up, ff_width, seq_count, seq_index)],
-        axis=-1,
-    ).transpose(1, 0, 2)
-    attn = lax.all_to_all(attn, "blk", split_axis=0, concat_axis=2, tiled=True)[0]
-    wide = lax.all_to_all(wide, "blk", split_axis=0, concat_axis=1, tiled=True)[0]
-    out_rows = w_output.shape[0] // seq_count
-    down_rows = w_down.shape[0] // seq_count
-    out = lax.dynamic_slice_in_dim(w_output, seq_index * out_rows, out_rows, 0)
-    down = lax.dynamic_slice_in_dim(w_down, seq_index * down_rows, down_rows, 0)
-    return attn, out, wide, down
-
-
-def own_layer(x_own, weights, info):
+        axis=1,
+    )
+    low = jnp.bfloat16
+    out_rows, down_rows = w_output.shape[0] // seq_count, w_down.shape[0] // seq_count
+    block = rows_in.shape[0]
+    dma = pltpu.SemaphoreType.DMA
+    attn, gate_up, out, down, rows_all, grads_all = pl.pallas_call(
+        functools.partial(spread_kernel, count),
+        out_shape=[
+            jax.ShapeDtypeStruct((2, pieces.shape[1], rows * count), low),
+            jax.ShapeDtypeStruct((2, rows * count, 2 * lanes), low),
+            jax.ShapeDtypeStruct((2, out_rows, w_output.shape[1]), low),
+            jax.ShapeDtypeStruct((2, down_rows, w_down.shape[1]), low),
+            jax.ShapeDtypeStruct((seq_count * count, block, width), low),
+            jax.ShapeDtypeStruct((seq_count * count, block, width), low),
+        ],
+        in_specs=[pl.BlockSpec(memory_space=pl.ANY)] * 7,
+        out_specs=[pl.BlockSpec(memory_space=pl.ANY)] * 6,
+        scratch_shapes=[
+            dma((3, count)),
+            dma((3, count)),
+            dma((5, count)),
+            dma((5, count)),
+            dma((5,)),
+        ]
+        + gather_semaphores(count) * 2,
+        compiler_params=pltpu.CompilerParams(collective_id=2, has_side_effects=True),
+        name="spread_weights",
+    )(pieces, w_gate, w_up, w_output, w_down, rows_in, grads_in)
+    layers = tuple((attn[i], out[i], gate_up[i], down[i]) for i in range(2))
+    return layers, rows_all.reshape(-1, width), grads_all.reshape(-1, width)
+
+
+def own_layer(x_own, normed_all, weights, info):
     attn, out, wide, down = weights
     allowed, cosine, sine = info
-    gain_attn = attn[3 * HEAD_DIM].astype(jnp.float32)
     gain_mlp = attn[3 * HEAD_DIM + 1].astype(jnp.float32)
-    normed, inv_first = rms_forward(x_own, gain_attn)
-    normed_all = group_gather(normed.astype(jnp.bfloat16))
+    inv_first = lax.rsqrt(jnp.mean(x_own * x_own, axis=-1, keepdims=True) + EPS)
     mixed_in = back_product(normed_all, attn[: 3 * HEAD_DIM])
     query = turn(mixed_in[:, :HEAD_DIM], cosine, sine).astype(jnp.bfloat16)
     key = turn(mixed_in[:, HEAD_DIM : 2 * HEAD_DIM], cosine, sine).astype(jnp.bfloat16)
@@ -865,7 +1023,7 @@
     return result, saved
 
 
-def own_layer_back(grad_own, weights, info, saved):
+def own_layer_back(grad_own, grad_out_all, weights, info, saved):
     attn, out, wide, down = weights
     allowed, cosine, sine = info
     (
@@ -886,7 +1044,6 @@
     ) = saved
     gain_attn = attn[3 * HEAD_DIM].astype(jnp.float32)
     gain_mlp = attn[3 * HEAD_DIM + 1].astype(jnp.float32)
-    grad_out_all = group_gather(grad_own.astype(jnp.bfloat16))
     grad_act = back_product(grad_out_all, down)
     gate_sigmoid = jax.nn.sigmoid(gate_pre)
     grad_gate = (
@@ -912,56 +1069,353 @@
     grad_qkv = jnp.concatenate([grad_query, grad_key, grad_value], axis=1)
     grad_normed = group_scatter(product(grad_qkv, attn[: 3 * HEAD_DIM]))
     grad_in_part, gain_attn_terms = rms_backward(x_own, gain_attn, inv_first, grad_normed)
-    grads = (
-        weight_term(grad_qkv, normed_all),
-        weight_term(mixed, grad_branch_all),
-        weight_term(normed_mlp_all, grad_wide),
-        weight_term(act_low, grad_out_all),
+    grads = shortened(
+        (
+            weight_term(grad_qkv, normed_all),
+            weight_term(mixed, grad_branch_all),
+            weight_term(normed_mlp_all, grad_wide),
+            weight_term(act_low, grad_out_all),
+        )
     )
     gains = jnp.stack([jnp.sum(gain_attn_terms, axis=0), jnp.sum(gain_mlp_terms, axis=0)])
     return grad_hidden + grad_in_part, grads, gains
 
 
-def finish_grads(grads):
-    seq_count = lax.axis_size("seq")
-    blk_count = lax.axis_size("blk")
-    attn, out, wide, down = grads
-    attn = lax.all_to_all(attn[None], "blk", split_axis=2, concat_axis=0, tiled=True)
-    wide = lax.all_to_all(wide[None], "blk", split_axis=1, concat_axis=0, tiled=True)
-    attn, out, wide, down = [
-        lax.all_gather(part, "seq", axis=0, tiled=False).astype(jnp.float32)
-        for part in (attn, out, wide, down)
-    ]
-    rows = attn.shape[-1]
-    query = attn[:, :, :HEAD_DIM].transpose(3, 1, 0, 2).reshape(rows, -1)
-
-    def key_like(part):
-        copies = HEADS // KV_HEADS
-        part = part.reshape(seq_count // copies, copies, blk_count, HEAD_DIM, rows).sum(1)
-        return part.transpose(3, 1, 0, 2).reshape(rows, -1)
-
-    key = key_like(attn[:, :, HEAD_DIM : 2 * HEAD_DIM])
-    value = key_like(attn[:, :, 2 * HEAD_DIM :])
-    half = wide.shape[-1] // 2
-    gate = wide[..., :half].transpose(2, 1, 0, 3).reshape(rows, -1)
-    up = wide[..., half:].transpose(2, 1, 0, 3).reshape(rows, -1)
-    return query, key, value, out.reshape(-1, out.shape[-1]), gate, up, down.reshape(
-        -1, down.shape[-1]
+def finish_kernel(
+    count,
+    attn_one,
+    attn_two,
+    out_one,
+    out_two,
+    wide_one,
+    wide_two,
+    down_one,
+    down_two,
+    gains,
+    swap_rows,
+    attn,
+    out,
+    gate,
+    up,
+    down,
+    gains_out,
+    swapped_rows,
+    attn_in,
+    out_in,
+    wide_in,
+    down_in,
+    attn_slot,
+    wide_slot,
+    gain_in,
+    gain_sum,
+    gain_line,
+    gain_part,
+    gain_side,
+    gain_core,
+    cross_sent,
+    cross_got,
+    line_sent,
+    line_got,
+    side_sent,
+    side_got,
+    core_sent,
+    core_got,
+    local_done,
+    small_sent,
+    small_got,
+):
+    seq, b, section = lax.axis_index("seq"), lax.axis_index("blk"), lax.axis_index("section")
+    at_first = section == 0
+    core, side, other = {"seq": seq ^ 1}, {"seq": seq ^ 2}, {"section": 1 - section}
+    greet((other, core, side) + tuple({"blk": lax.rem(b + k, count)} for k in range(1, count)))
+    rows, lanes = attn.shape[2], gate.shape[1] // (4 * count)
+    far_first = tuple(range(count // 2, 0, -1)) + tuple(range(count // 2 + 1, count)) + (0,)
+    f32, low = jnp.float32, jnp.bfloat16
+
+    def piece_rows(kind, j):
+        if kind == 0:
+            return (slice(None), pl.ds(pl.multiple_of(j * rows, rows), rows))
+        return (pl.ds(pl.multiple_of(j * rows, rows), rows),)
+
+    pairs = {
+        0: (attn_one, attn_two, attn_in),
+        1: (wide_one, wide_two, wide_in),
+        2: (out_one, out_two, out_in),
+        3: (down_one, down_two, down_in),
+    }
+
+    def cross(kind, k, begin):
+        one, two, held = pairs[kind]
+        index = piece_rows(kind, lax.rem(b + k, count)) if kind < 2 else (slice(None),)
+        spots = [ref.at[index] for ref in (one, two, held)]
+        sems = (cross_sent.at[kind, k], cross_got.at[kind, k])
+        if not begin:
+            return remote(spots[0], spots[2], *sems, other)
+
+        @pl.when(at_first)
+        def _():
+            remote(spots[1], spots[2], *sems, other).start()
+
+        @pl.when(jnp.logical_not(at_first))
+        def _():
+            remote(spots[0], spots[2], *sems, other).start()
+
+    def add_up(kind, k):
+        one, two, held = pairs[kind]
+        index = piece_rows(kind, lax.rem(b + k, count)) if kind < 2 else (slice(None),)
+        cross(kind, k, False).wait_recv()
+        own = jnp.where(at_first, one[index], two[index]).astype(f32)
+        held[index] = (own + held[index].astype(f32)).astype(low)
+
+    def along_line(kind, k):
+        j = lax.rem(b + k, count)
+        slot = (attn_slot if kind == 0 else wide_slot).at[k]
+        source = pairs[kind][2].at[piece_rows(kind, j)]
+        return remote(source, slot, line_sent.at[kind, k], line_got.at[kind, k], {"blk": j})
+
+    def places(kind, k, of_seq):
+        if kind == 2:
+            size = out_in.shape[0]
+            return [out.at[pl.ds(pl.multiple_of(of_seq * size, size), size)]]
+        if kind == 3:
+            size = down_in.shape[0]
+            return [down.at[pl.ds(pl.multiple_of(of_seq * size, size), size)]]
+        head = lax.rem(b + count - k, count) * 4 + of_seq
+        if kind == 0:
+            return [attn.at[head]]
+        column = pl.ds(pl.multiple_of(head * lanes, lanes), lanes)
+        return [gate.at[:, column], up.at[:, column]]
+
+    def numbered(kind, k, of_seq):
+        base = {0: k, 1: count + 2 * k, 2: 3 * count, 3: 3 * count + 1}[kind]
+        return [(base + n, spot) for n, spot in enumerate(places(kind, k, of_seq))]
+
+    def made(kind, k):
+        if kind > 1:
+            return [pairs[kind][2].at[:]]
+        if kind == 0:
+            return [attn_in.at[piece_rows(0, b)] if k == 0 else attn_slot.at[k]]
+        whole = (lambda cut: wide_in.at[piece_rows(1, b) + (cut,)]) if k == 0 else (
+            lambda cut: wide_slot.at[k, :, cut]
+        )
+        return [whole(pl.ds(0, lanes)), whole(pl.ds(lanes, lanes))]
+
+    def sends(kind, k):
+        found = []
+        for (n, spot), begin in zip(numbered(kind, k, seq), made(kind, k)):
+            found.append(
+                (
+                    remote(begin, spot, side_sent.at[n], side_got.at[n], side),
+                    remote(begin, spot, core_sent.at[0, n], core_got.at[0, n], core),
+                    pltpu.make_async_copy(begin, spot, local_done.at[n]),
+                )
+            )
+        return found
+
+    def publish(kind, k):
+        for copies in sends(kind, k):
+            for copy in copies:
+                copy.start()
+
+    def passes(kind, k):
+        return [
+            remote(spot, spot, core_sent.at[1, n], core_got.at[1, n], core)
+            for n, spot in numbered(kind, k, seq ^ 2)
+        ]
+
+    def from_line(kind, k):
+        along_line(kind, k).wait_recv()
+        publish(kind, k)
+
+    def from_side(kind, k):
+        for n, spot in numbered(kind, k, seq ^ 2):
+            settled(spot, side_got.at[n], True)
+        for copy in passes(kind, k):
+            copy.start()
+
+    def small(n, source, slot, device):
+        return remote(source, slot, small_sent.at[n], small_got.at[n], device)
+
+    swap = small(0, swap_rows.at[:], swapped_rows.at[:], other)
+    swap.start()
+    gain_cross = small(1, gains.at[1 - section], gain_in.at[:], other)
+    gain_cross.start()
+    cross(2, 0, True)
+    for kind, k in ((1, far_first[0]), (1, 0)):
+        cross(kind, k, True)
+    cross(3, 0, True)
+    for kind in (1, 0):
+        for k in far_first:
+            if (kind, k) not in ((1, far_first[0]), (1, 0)):
+                cross(kind, k, True)
+
+    def gain_piece(j):
+        return gain_sum.at[:, pl.ds(pl.multiple_of(j * rows, rows), rows)]
+
+    def gain_send(k):
+        j = lax.rem(b + k, count)
+        return small(3 + k, gain_piece(j), gain_line.at[k], {"blk": j})
+
+    gain_cross.wait_recv()
+    gain_sum[...] = gains[section] + gain_in[...]
+    for k in range(1, count):
+        gain_send(k).start()
+
+    add_up(2, 0)
+    publish(2, 0)
+    add_up(1, far_first[0])
+    along_line(1, far_first[0]).start()
+    add_up(1, 0)
+    publish(1, 0)
+    from_side(2, 0)
+    for k in range(1, count):
+        gain_send(k).wait_recv()
+    gain_part[...] = gain_sum[:, pl.ds(pl.multiple_of(b * rows, rows), rows)]
+    for k in range(1, count):
+        gain_part[...] += gain_line[k]
+    gain_to_side = small(2, gain_part.at[:], gain_side.at[:], side)
+    gain_to_side.start()
+    add_up(3, 0)
+    publish(3, 0)
+    for k in far_first[1:-1]:
+        add_up(1, k)
+        along_line(1, k).start()
+    from_side(1, 0)
+    gain_to_side.wait_recv()
+    gain_side[...] += gain_part[...]
+    gain_to_core = small(3, gain_side.at[:], gain_core.at[:], core)
+    gain_to_core.start()
+    from_line(1, far_first[0])
+    from_side(3, 0)
+    add_up(0, far_first[0])
+    along_line(0, far_first[0]).start()
+    from_line(1, far_first[1])
+    add_up(0, far_first[1])
+    along_line(0, far_first[1]).start()
+    from_side(1, far_first[0])
+    from_line(1, far_first[2])
+    add_up(0, far_first[2])
+    along_line(0, far_first[2]).start()
+    add_up(0, 0)
+    publish(0, 0)
+    from_side(1, far_first[1])
+    gain_to_core.wait_recv()
+    gains_out[...] = gain_side[...] + gain_core[...]
+    from_line(0, far_first[0])
+    from_side(1, far_first[2])
+    from_line(0, far_first[1])
+    from_line(0, far_first[2])
+    from_side(0, 0)
+    for k in far_first[:-1]:
+        from_side(0, k)
+    every = [(0, k) for k in range(count)] + [(1, k) for k in range(count)] + [(2, 0), (3, 0)]
+    for kind, k in every:
+        cross(kind, k, False).wait_send()
+        if kind < 2 and k:
+            along_line(kind, k).wait_send()
+        for to_side, to_core, local in sends(kind, k):
+            to_side.wait_send()
+            to_core.wait_send()
+            local.wait()
+        for copy in passes(kind, k):
+            copy.wait_send()
+        for half, of_seq in ((0, seq ^ 1), (1, seq ^ 3)):
+            for n, spot in numbered(kind, k, of_seq):
+                settled(spot, core_got.at[half, n], True)
+    swap.wait()
+    gain_cross.wait_send()
+    for k in range(1, count):
+        gain_send(k).wait_send()
+    gain_to_side.wait_send()
+    gain_to_core.wait_send()
+
+
+def finish_grads(first, second, gains, swap_rows):
+    seq_count, count = lax.axis_size("seq"), lax.axis_size("blk")
+    low, f32 = jnp.bfloat16, jnp.float32
+    attn, out, wide, down = first
+    rows = wide.shape[0] // count
+    lanes = wide.shape[1] // 2
+    parts = seq_count * count
+    dma = pltpu.SemaphoreType.DMA
+    vmem = pltpu.VMEM
+    sends = 3 * count + 2
+    heads = attn.shape[0]
+    operands = [array for pair in zip(first, second) for array in pair] + [gains, swap_rows]
+    in_vmem = pl.BlockSpec(memory_space=vmem)
+    anywhere = pl.BlockSpec(memory_space=pl.ANY)
+    small = (gains.shape[1], rows)
+    attn, out, gate, up, down, gains, swapped_rows = pl.pallas_call(
+        functools.partial(finish_kernel, count),
+        out_shape=[
+            jax.ShapeDtypeStruct((parts, heads, rows), low),
+            jax.ShapeDtypeStruct((out.shape[0] * seq_count, out.shape[1]), low),
+            jax.ShapeDtypeStruct((rows, lanes * parts), low),
+            jax.ShapeDtypeStruct((rows, lanes * parts), low),
+            jax.ShapeDtypeStruct((down.shape[0] * seq_count, down.shape[1]), low),
+            jax.ShapeDtypeStruct(small, f32),
+            jax.ShapeDtypeStruct(swap_rows.shape, low),
+        ],
+        in_specs=[in_vmem] * len(operands),
+        out_specs=[anywhere] * 5 + [in_vmem, in_vmem],
+        scratch_shapes=[
+            vmem(attn.shape, low),
+            vmem(out.shape, low),
+            vmem(wide.shape, low),
+            vmem(down.shape, low),
+            vmem((count, heads, rows), low),
+            vmem((count, rows, 2 * lanes), low),
+            vmem(gains.shape[1:], f32),
+            vmem(gains.shape[1:], f32),
+            vmem((count,) + small, f32),
+            vmem(small, f32),
+            vmem(small, f32),
+            vmem(small, f32),
+            dma((4, count)),
+            dma((4, count)),
+            dma((2, count)),
+            dma((2, count)),
+            dma((sends,)),
+            dma((sends,)),
+            dma((2, sends)),
+            dma((2, sends)),
+            dma((sends,)),
+            dma((4 + count,)),
+            dma((4 + count,)),
+        ],
+        compiler_params=pltpu.CompilerParams(
+            collective_id=3, has_side_effects=True, vmem_limit_bytes=48 * 2**20
+        ),
+        name="finish_grads",
+    )(*operands)
+    attn = attn.astype(f32)
+
+    def heads_back(start, copies):
+        part = attn[:, start : start + HEAD_DIM].reshape(-1, copies, HEAD_DIM, rows).sum(1)
+        return part.reshape(-1, rows).T
+
+    copies = HEADS // KV_HEADS
+    return (
+        swapped_rows,
+        gains,
+        heads_back(0, 1),
+        heads_back(HEAD_DIM, copies),
+        heads_back(2 * HEAD_DIM, copies),
+        out.astype(f32),
+        gate.astype(f32),
+        up.astype(f32),
+        down.astype(f32),
     )
 
 
 def head_shards(inputs, cotangent, doc_lengths, *params):
     section = lax.axis_index("section")
     at_first = section == 0
-    blk_index = lax.axis_index("blk")
     tokens = inputs.shape[2] * lax.axis_size("seq") * lax.axis_size("blk")
-    own = spread_weights(tuple(weight[0] for weight in params))
-    other = tuple(swapped(part) for part in own)
-    first = tuple(jnp.where(at_first, a, b) for a, b in zip(own, other))
-    second = tuple(jnp.where(at_first, b, a) for a, b in zip(own, other))
-    x_own = lax.dynamic_index_in_dim(inputs, section, 0, keepdims=False)[0].astype(jnp.float32)
-    grad_own = lax.dynamic_index_in_dim(cotangent, section, 0, keepdims=False)[0].astype(
-        jnp.float32
+    rows_own = lax.dynamic_index_in_dim(inputs, section, 0, keepdims=False)[0]
+    grads_own = lax.dynamic_index_in_dim(cotangent, section, 0, keepdims=False)[0]
+    (first, second), rows_all, grads_all = spread_weights(
+        tuple(weight[0] for weight in params), rows_own, grads_own
     )
     lengths = lax.dynamic_index_in_dim(doc_lengths, section, 0, keepdims=False)[0]
     token_index = jnp.arange(tokens, dtype=jnp.int32)
@@ -973,39 +1427,41 @@
     frequency = THETA ** (-2.0 * jnp.arange(half_dim, dtype=jnp.float32) / HEAD_DIM)
     angles = position.astype(jnp.float32)[:, None] * frequency
     info = (allowed, jnp.cos(angles), jnp.sin(angles))
-    result, saved_first = own_layer(x_own, first, info)
+    x_own = rows_own.astype(jnp.float32)
+    gain = first[0][3 * HEAD_DIM].astype(jnp.float32)
+    normed_all = rms_forward(rows_all.astype(jnp.float32), gain)[0].astype(jnp.bfloat16)
+    result, saved_first = own_layer(x_own, normed_all, first, info)
     between = result.astype(jnp.bfloat16)
-    result, saved_second = own_layer(between.astype(jnp.float32), second, info)
+    x_own = between.astype(jnp.float32)
+    gain = second[0][3 * HEAD_DIM].astype(jnp.float32)
+    normed_all = group_gather(rms_forward(x_own, gain)[0].astype(jnp.bfloat16))
+    result, saved_second = own_layer(x_own, normed_all, second, info)
     final = result.astype(jnp.bfloat16)
-    grad_between, grads_second, gains_second = own_layer_back(grad_own, second, info, saved_second)
+    grad_between, grads_second, gains_second = own_layer_back(
+        grads_own.astype(jnp.float32), grads_all, second, info, saved_second
+    )
     grad_between = grad_between.astype(jnp.bfloat16)
     grad_start, grads_first, gains_first = own_layer_back(
-        grad_between.astype(jnp.float32), first, info, saved_first
+        grad_between.astype(jnp.float32), group_gather(grad_between), first, info, saved_first
     )
     grad_start = grad_start.astype(jnp.bfloat16)
-
-    def by_section(for_first, for_second):
-        kept = jnp.where(at_first, for_first, for_second)
-        received = swapped(jnp.where(at_first, for_second, for_first))
-        return jnp.stack(
-            [jnp.where(at_first, kept, received), jnp.where(at_first, received, kept)]
-        )[None, :, None]
-
-    activations = by_section(between, final)
-    input_grads = by_section(grad_start, grad_between)
-    summed = []
-    for one, two in zip(grads_first, grads_second):
-        kept = jnp.where(at_first, one, two)
-        received = swapped(jnp.where(at_first, two, one).astype(jnp.bfloat16))
-        summed.append((kept + received.astype(jnp.float32)).astype(jnp.bfloat16))
-    query, key, value, out, gate, up, down = finish_grads(summed)
-    gains = lax.psum(jnp.stack([gains_first, gains_second]), ("section", "seq", "blk"))
-    gains = lax.dynamic_index_in_dim(gains, section, 0, keepdims=False)
-    rows = params[1].shape[1]
-    gains = lax.dynamic_slice_in_dim(gains, blk_index * rows, rows, 1)
+    kept = jnp.where(
+        at_first, jnp.stack([between, grad_start]), jnp.stack([final, grad_between])
+    )
+    sent = jnp.where(
+        at_first, jnp.stack([final, grad_between]), jnp.stack([between, grad_start])
+    )
+    gains = jnp.stack([gains_first, gains_second])
+    gains = jnp.concatenate([gains, jnp.zeros((2, 6) + gains.shape[2:], jnp.float32)], axis=1)
+    swapped_rows, gains, query, key, value, out, gate, up, down = finish_grads(
+        grads_first, grads_second, gains, sent
+    )
+    pairs = jnp.where(
+        at_first, jnp.stack([kept, swapped_rows], axis=1), jnp.stack([swapped_rows, kept], axis=1)
+    )
     return (
-        activations,
-        input_grads,
+        pairs[0][None, :, None],
+        pairs[1][None, :, None],
         gains[0][None],
         query[None],
         key[None],
@@ -1016,7 +1472,6 @@
         up[None],
         down[None],
     )
-
 
 def solution(mesh):
     placed = (
@@ -1033,7 +1488,7 @@
         P("section", "blk", None),
         P("section", "blk", None),
     )
-    one_head_each = mesh.shape["seq"] * mesh.shape["blk"] == HEADS
+    one_head_each = mesh.shape["seq"] == 4 and mesh.shape["blk"] == HEADS // 4
     return jax.shard_map(
         head_shards if one_head_each else shards,
         mesh=mesh,

time: 936 us -> 737 us (0.79)
  Pallas kernels: 460 us -> 604 us
  local copies, waits for them, and re-layouts: 127 us -> 16.8 us
  blocking collectives: 106 us -> 0 us
  waiting for transfers between devices: 56.6 us -> 0 us
  other arithmetic: 70.9 us -> 45.8 us
  starting transfers between devices: 19.3 us -> 0 us
  matrix products: 71.6 us -> 56 us
  between operations: 15.9 us -> 2.64 us
    pallas_call x0 -> x2, Pallas kernels: none -> 234 us  [the longest x1 122 us: finish_grads(): pl.pallas_call(functools.partial(finish_kernel, count), out_shape=[jax.Sh...]
    pallas_call x8 -> x6, Pallas kernels: 209 us -> 135 us  [group_gather(): pl.pallas_call(functools.partial(gather_kernel, count), out_shape=jax.Sha...]
    all_to_all x2 -> x0, blocking collectives: 64.1 us -> none  [the longest x1 38.5 us: finish_grads(): lax.all_to_all(wide[None], 'blk', split_axis=1, concat_axis=0, tiled=True)]
    ppermute x10 -> x0, waiting for transfers between devices: 56.5 us -> none  [swapped(): return lax.ppermute(own, 'section', [(0, 1), (1, 0)])]
    unnamed x198 -> x137, local copies, waits for them, and re-layouts: 54.1 us -> 8.16 us
    psum x1 -> x0, blocking collectives: 41.4 us -> none  [head_shards(): lax.psum(jnp.stack([gains_first, gains_second]), ('section', 'seq', 'blk'))]
    unnamed x12 -> x8, other arithmetic: 30.6 us -> 6.27 us
    broadcast_in_dim x3 -> x2, local copies, waits for them, and re-layouts: 18.1 us -> 0.01 us  [the longest x1 0.01 us: spread_weights(): jnp.broadcast_to(gains[None], (count,) + gains.shape)]
  transfers between devices with their start and end apart: 16 -> 0, of which waited for: 3 -> 0; matrix products, arithmetic and copies ran while one was open for 18% -> 0% of each run, Pallas kernels for 24% -> 0%
where the time goes in v3:
time: 737 us; the launch traced here: 725 us
  Pallas kernels  604 us (82%)
  matrix products  56 us (8%)
  other arithmetic  45.8 us (6%)
  local copies, waits for them, and re-layouts  16.8 us (2%)
    pallas_call x8, Pallas kernels, group_scatter(): pl.pallas_call(functools.partial(scatter_kernel, count), out_shape=jax.Sh...  235 us
    pallas_call x6, Pallas kernels, group_gather(): pl.pallas_call(functools.partial(gather_kernel, count), out_shape=jax.Sha...  135 us
    pallas_call x1, Pallas kernels, finish_grads(): pl.pallas_call(functools.partial(finish_kernel, count), out_shape=[jax.Sh...  122 us
    pallas_call x1, Pallas kernels, spread_weights(): pl.pallas_call(functools.partial(spread_kernel, count), out_shape=[jax.Sh...  113 us
    dot_general x12, matrix products, back_product(): lax.dot_general(left_side, right_side, (((1,), (1,)), ((), ())), preferre...  20.5 us
    dot_general x12, matrix products, product(): return jnp.dot(left_side, right_side, preferred_element_type=jnp.float32)  19.1 us

profile of v3, /device:TPU:18, one launch (start us, length us, event | category | flops | bytes accessed | tf_op | source)
XLA Modules:
  0.0 725.1 jit_solution(4832911120275981863)
XLA Ops:
  9.9 112.5 %spread_weights.1 = (bf16[2,304,1536]{2,1,0:T(8,128)(2,1)}, bf16[2,1536,512]{2,1,0:T(8,128)(2,1)}, bf16[2,96,1536]{2,1,0:T(8,128)(2,1)}, bf16[2,256,1536]{2,1,0:...) custom-call(bf16[4,304,384]{2,1,0:T(8,128)(2,1)} %pad_maximum_fusion.2.pieces, ...), custom_call_target="tpu_custom_call" | custom-call | tf_op jit(solution)/shard_map/spread_weights/pallas_call | solution.py:959
  136.5 31.5 %scatter_tokens.8 = f32[64,1536]{1,0:T(8,128)S(1)} custom-call(bf16[16,64,1536]{2,1,0:T(8,128)(2,1)S(1)} %bitcast.187), custom_call_target="tpu_custom_call" | custom-call | tf_op jit(solution)/shard_map/scatter_tokens/pallas_call | solution.py:763
  168.8 22.1 %gather_tokens.6 = bf16[16,64,1536]{2,1,0:T(8,128)(2,1)S(1)} custom-call(bf16[64,1536]{1,0:T(8,128)(2,1)S(1)} %multiply_convert_fusion.10.refs_0_), custom_call_target="tpu_custom_call" | custom-call | tf_op jit(solution)/shard_map/gather_tokens/pallas_call | solution.py:668
  196.0 29.9 %scatter_tokens.9 = f32[64,1536]{1,0:T(8,128)S(1)} custom-call(bf16[16,64,1536]{2,1,0:T(8,128)(2,1)S(1)} %bitcast.186), custom_call_target="tpu_custom_call" | custom-call | tf_op jit(solution)/shard_map/scatter_tokens/pallas_call | solution.py:763
  227.1 21.8 %gather_tokens.7 = bf16[16,64,1536]{2,1,0:T(8,128)(2,1)S(1)} custom-call(bf16[64,1536]{1,0:T(8,128)(2,1)S(1)} %fusion.68.refs_0_), custom_call_target="tpu_custom_call" | custom-call | tf_op jit(solution)/shard_map/gather_tokens/pallas_call | solution.py:668
  256.3 29.2 %scatter_tokens.10 = f32[64,1536]{1,0:T(8,128)S(1)} custom-call(bf16[16,64,1536]{2,1,0:T(8,128)(2,1)S(1)} %bitcast.188), custom_call_target="tpu_custom_call" | custom-call | tf_op jit(solution)/shard_map/scatter_tokens/pallas_call | solution.py:763
  286.5 22.4 %gather_tokens.8 = bf16[16,64,1536]{2,1,0:T(8,128)(2,1)S(1)} custom-call(bf16[64,1536]{1,0:T(8,128)(2,1)S(1)} %multiply_convert_fusion.9.refs_0_), custom_call_target="tpu_custom_call" | custom-call | tf_op jit(solution)/shard_map/gather_tokens/pallas_call | solution.py:668
  308.9 3.4 fusion.7
  314.6 3.0 convolution_convert_fusion.8.wide_two
  319.4 29.0 %scatter_tokens.11 = f32[64,1536]{1,0:T(8,128)S(1)} custom-call(bf16[16,64,1536]{2,1,0:T(8,128)(2,1)S(1)} %bitcast.200), custom_call_target="tpu_custom_call" | custom-call | tf_op jit(solution)/shard_map/scatter_tokens/pallas_call | solution.py:763
  350.8 28.3 %scatter_tokens.15 = f32[64,1536]{1,0:T(8,128)S(1)} custom-call(bf16[16,64,1536]{2,1,0:T(8,128)(2,1)S(1)} %bitcast.185), custom_call_target="tpu_custom_call" | custom-call | tf_op jit(solution)/shard_map/scatter_tokens/pallas_call | solution.py:763
  383.1 23.3 %gather_tokens.9 = bf16[16,64,1536]{2,1,0:T(8,128)(2,1)S(1)} custom-call(bf16[64,1536]{1,0:T(8,128)(2,1)S(1)} %get-tuple-element.90.refs_0_), custom_call_target="tpu_custom_call" | custom-call | tf_op jit(solution)/shard_map/gather_tokens/pallas_call | solution.py:668
  421.8 29.1 %scatter_tokens.12 = f32[64,1536]{1,0:T(8,128)S(1)} custom-call(bf16[16,64,1536]{2,1,0:T(8,128)(2,1)S(1)} %bitcast.202), custom_call_target="tpu_custom_call" | custom-call | tf_op jit(solution)/shard_map/scatter_tokens/pallas_call | solution.py:763
  451.3 22.6 %gather_tokens.10 = bf16[16,64,1536]{2,1,0:T(8,128)(2,1)S(1)} custom-call(bf16[64,1536]{1,0:T(8,128)(2,1)S(1)} %fusion.72.refs_0_), custom_call_target="tpu_custom_call" | custom-call | tf_op jit(solution)/shard_map/gather_tokens/pallas_call | solution.py:668
  477.7 3.0 convolution_convert_fusion.9.wide_one
  482.6 29.0 %scatter_tokens.13 = f32[64,1536]{1,0:T(8,128)S(1)} custom-call(bf16[16,64,1536]{2,1,0:T(8,128)(2,1)S(1)} %bitcast.199), custom_call_target="tpu_custom_call" | custom-call | tf_op jit(solution)/shard_map/scatter_tokens/pallas_call | solution.py:763
  512.0 22.6 %gather_tokens.11 = bf16[16,64,1536]{2,1,0:T(8,128)(2,1)S(1)} custom-call(bf16[64,1536]{1,0:T(8,128)(2,1)S(1)} %get-tuple-element.88.refs_0_), custom_call_target="tpu_custom_call" | custom-call | tf_op jit(solution)/shard_map/gather_tokens/pallas_call | solution.py:668
  545.9 3.0 convolution_convert_fusion.2
  548.9 29.0 %scatter_tokens.14 = f32[64,1536]{1,0:T(8,128)S(1)} custom-call(bf16[16,64,1536]{2,1,0:T(8,128)(2,1)S(1)} %bitcast.201), custom_call_target="tpu_custom_call" | custom-call | tf_op jit(solution)/shard_map/scatter_tokens/pallas_call | solution.py:763
  578.6 121.6 %finish_grads.1 = (bf16[16,288,384]{2,1,0:T(8,128)(2,1)}, bf16[384,1536]{1,0:T(8,128)(2,1)S(1)}, bf16[384,4096]{1,0:T(8,128)(2,1)}, bf16[384,4096]{1,0:T(8,128)(...) custom-call(bf16[288,1536]{1,0:T(8,128)(2,1)S(1)} %convolution_convert_fusion.11.attn_one, ...), custom_call_target="tpu_custom_call" | custom-call | tf_op jit(solution)/shard_map/finish_grads/pallas_call | solution.py:1348
  705.1 3.0 copy.31
  712.0 5.5 bitcast_convert_fusion.2
  717.5 3.5 bitcast_convert_fusion.1
  721.0 3.6 bitcast_convert_fusion
  (249 shorter events, 90.6 us)
Async XLA Ops:
  0.7 7.2 copy-start.65
  0.7 131.0 %copy-start.46 = (f32[48]{0:T(128)}, f32[48]{0:T(128)S(1)}, u32[]{:S(2)}) copy-start(f32[48]{0:T(128)S(1)} %multiply_power_fusion) | copy-start | bytes 580
  2.2 130.5 %copy-start.55 = (s32[1024]{0:T(1024)}, s32[1024]{0:T(1024)S(1)}, u32[]{:S(2)}) copy-start(s32[1024]{0:T(1024)S(1)} %get-tuple-element.85) | copy-start | bytes 12292
  126.2 100.3 %copy-start.42 = (f32[1536]{0:T(1024)}, f32[1536]{0:T(1024)S(1)}, u32[]{:S(2)}) copy-start(f32[1536]{0:T(1024)S(1)} %get-tuple-element.73) | copy-start | bytes 18436
  135.5 32.5 %copy-start.8 = (bf16[64,1536]{1,0:T(8,128)(2,1)S(1)}, bf16[64,1536]{1,0:T(8,128)(2,1)}, u32[]{:S(2)}) copy-start(bf16[64,1536]{1,0:T(8,128)(2,1)} %get-tuple-element.87.rows_in) | copy-start | bytes 589828
  168.1 57.7 %copy-start.5 = (f32[64,1536]{1,0:T(8,128)}, f32[64,1536]{1,0:T(8,128)S(1)}, u32[]{:S(2)}) copy-start(f32[64,1536]{1,0:T(8,128)S(1)} %get-tuple-element.97) | copy-start | bytes 1179652
  168.1 22.8 %copy-start.61 = (bf16[2,1536,512]{2,1,0:T(8,128)(2,1)S(1)}, bf16[2,1536,512]{2,1,0:T(8,128)(2,1)}, u32[]{:S(2)}) copy-start(bf16[2,1536,512]{2,1,0:T(8,128)(2,1)} %get-tuple-element.27) | copy-start | bytes 9437188
  168.7 24.1 %copy-start.52 = (f32[64]{0:T(128)}, f32[64]{0:T(128)S(1)}, u32[]{:S(2)}) copy-start(f32[64]{0:T(128)S(1)} %get-tuple-element.121) | copy-start | bytes 772
  192.7 33.8 %copy-start.17 = (f32[1024,512]{0,1:T(8,128)}, f32[1024,512]{0,1:T(8,128)S(1)}, u32[]{:S(2)}) copy-start(f32[1024,512]{0,1:T(8,128)S(1)} %fusion.10) | copy-start | bytes 6291460
  286.3 25.9 %copy-start.54 = (f32[64]{0:T(128)}, f32[64]{0:T(128)S(1)}, u32[]{:S(2)}) copy-start(f32[64]{0:T(128)S(1)} %get-tuple-element.125) | copy-start | bytes 772
  421.8 29.1 %copy-start.43 = (f32[1536]{0:T(1024)S(1)}, f32[1536]{0:T(1024)}, u32[]{:S(2)}) copy-start(f32[1536]{0:T(1024)} %copy-done.42) | copy-start | bytes 18436
  421.8 29.1 %copy-start.51 = (f32[64]{0:T(128)S(1)}, f32[64]{0:T(128)}, u32[]{:S(2)}) copy-start(f32[64]{0:T(128)} %copy-done.50) | copy-start | bytes 772
  421.8 29.3 %copy-start.27 = (f32[64,1536]{1,0:T(8,128)S(1)}, f32[64,1536]{1,0:T(8,128)}, u32[]{:S(2)}) copy-start(f32[64,1536]{1,0:T(8,128)} %get-tuple-element.91) | copy-start | bytes 1179652
  421.8 29.3 %copy-start.60 = (f32[64]{0:T(128)S(1)}, f32[64]{0:T(128)}, u32[]{:S(2)}) copy-start(f32[64]{0:T(128)} %get-tuple-element.122) | copy-start | bytes 772
  450.9 23.0 %copy-start.26 = (bf16[2,256,1536]{2,1,0:T(8,128)(2,1)S(1)}, bf16[2,256,1536]{2,1,0:T(8,128)(2,1)}, u32[]{:S(2)}) copy-start(bf16[2,256,1536]{2,1,0:T(8,128)(2,1)} %get-tuple-element.28) | copy-start | bytes 4718596
  482.6 29.1 %copy-start.6 = (f32[64,1536]{1,0:T(8,128)S(1)}, f32[64,1536]{1,0:T(8,128)}, u32[]{:S(2)}) copy-start(f32[64,1536]{1,0:T(8,128)} %copy-done.5) | copy-start | bytes 1179652
  482.6 29.1 %copy-start.53 = (f32[64]{0:T(128)S(1)}, f32[64]{0:T(128)}, u32[]{:S(2)}) copy-start(f32[64]{0:T(128)} %copy-done.52) | copy-start | bytes 772
  482.6 29.3 %copy-start.59 = (f32[64]{0:T(128)S(1)}, f32[64]{0:T(128)}, u32[]{:S(2)}) copy-start(f32[64]{0:T(128)} %get-tuple-element.120) | copy-start | bytes 772
  511.7 23.0 %copy-start.16 = (bf16[2,96,1536]{2,1,0:T(8,128)(2,1)S(1)}, bf16[2,96,1536]{2,1,0:T(8,128)(2,1)}, u32[]{:S(2)}) copy-start(bf16[2,96,1536]{2,1,0:T(8,128)(2,1)} %get-tuple-element.26) | copy-start | bytes 1769476
  548.9 29.1 %copy-start.9 = (bf16[64,1536]{1,0:T(8,128)(2,1)S(1)}, bf16[64,1536]{1,0:T(8,128)(2,1)}, u32[]{:S(2)}) copy-start(bf16[64,1536]{1,0:T(8,128)(2,1)} %get-tuple-element.87.rows_in) | copy-start | bytes 589828
  548.9 29.1 %copy-start.57 = (f32[64]{0:T(128)S(1)}, f32[64]{0:T(128)}, u32[]{:S(2)}) copy-start(f32[64]{0:T(128)} %get-tuple-element.119) | copy-start | bytes 772
  548.9 29.3 %copy-start.58 = (f32[64]{0:T(128)S(1)}, f32[64]{0:T(128)}, u32[]{:S(2)}) copy-start(f32[64]{0:T(128)} %get-tuple-element.118) | copy-start | bytes 772
  548.9 29.4 %copy-start.49 = (f32[1,1536]{1,0:T(1,128)S(1)}, f32[1,1536]{1,0:T(1,128)}, u32[]{:S(2)}) copy-start(f32[1,1536]{1,0:T(1,128)} %stack.86) | copy-start | bytes 18436
  548.9 29.5 %copy-start.22 = (bf16[64,1536]{1,0:T(8,128)(2,1)S(1)}, bf16[64,1536]{1,0:T(8,128)(2,1)}, u32[]{:S(2)}) copy-start(bf16[64,1536]{1,0:T(8,128)(2,1)} %get-tuple-element.113) | copy-start | bytes 589828
  (43 other events, 107.1 us)

commit v4 on v3

--- a/solution.py
+++ b/solution.py
@@ -522,22 +522,6 @@
     pl.semaphore_wait(barrier, len(partners))
 
 
-def greet_line(blk_index, count, partners):
-    barrier = pltpu.get_barrier_semaphore()
-    for device in partners:
-        pl.semaphore_signal(barrier, 1, device_id=device, device_id_type=MESH)
-    for step, there in ((-1, blk_index > 0), (1, blk_index < count - 1)):
-
-        @pl.when(there)
-        def _():
-            pl.semaphore_signal(
-                barrier, 1, device_id={"blk": blk_index + step}, device_id_type=MESH
-            )
-
-    inner = (blk_index > 0).astype(jnp.int32) + (blk_index < count - 1).astype(jnp.int32)
-    pl.semaphore_wait(barrier, len(partners) + inner)
-
-
 def settled(spot, semaphore, received):
     copy = remote(spot, spot, semaphore, semaphore, {"seq": lax.axis_index("seq") ^ 1})
     if received:
@@ -589,7 +573,7 @@
         along_line(b, 1, own).start()
 
     to_core(0, b, own).start()
-    yield
+    yield "sent"
 
     def from_line(j, way):
         settled(out.at[base + j], line_got.at[j], True)
@@ -614,11 +598,13 @@
         else:
             pl.when(b - k + 1 >= 0)(functools.partial(from_side, b - k + 1))
             pl.when(b + k - 1 < count)(functools.partial(from_side, b + k - 1))
-        yield
+        if k == count - 1:
+            local.wait()
+        yield "line" if k == count - 1 else "side" if k == count else "step"
     for half, corner in ((0, seq ^ 1), (1, seq ^ 3)):
         for j in range(count):
             settled(out.at[corner * count + j], core_got.at[half, j], True)
-    local.wait()
+        yield "corner" if half else "near"
     for j in range(count):
         to_side(j).wait_send()
         to_core(0, j).wait_send()
@@ -641,13 +627,6 @@
         @pl.when((b + k < count) & (b > 0))
         def _():
             along_line(b + k, 0).wait_send()
-
-
-def gather_kernel(count, *refs):
-    seq, b = lax.axis_index("seq"), lax.axis_index("blk")
-    greet_line(b, count, ({"seq": seq ^ 1}, {"seq": seq ^ 2}))
-    for _ in gather_steps(count, *refs):
-        pass
 
 
 def gather_semaphores(count):
@@ -663,26 +642,20 @@
     ]
 
 
-def group_gather(block):
-    seq_count, count = lax.axis_size("seq"), lax.axis_size("blk")
-    gathered = pl.pallas_call(
-        functools.partial(gather_kernel, count),
-        out_shape=jax.ShapeDtypeStruct((seq_count * count,) + block.shape, block.dtype),
-        in_specs=[pl.BlockSpec(memory_space=pltpu.VMEM)],
-        out_specs=pl.BlockSpec(memory_space=pltpu.VMEM),
-        scratch_shapes=gather_semaphores(count),
-        compiler_params=pltpu.CompilerParams(
-            collective_id=0, has_side_effects=True, vmem_limit_bytes=48 * 2**20
-        ),
-        name="gather_tokens",
-    )(block)
-    return gathered.reshape(-1, block.shape[1])
-
-
-def scatter_kernel(
+def advance(steps, times):
+    for _ in range(times):
+        next(steps, None)
+
+
+def group_of(event):
+    seq = lax.axis_index("seq")
+    return {"line": seq, "side": seq ^ 2, "near": seq ^ 1, "corner": seq ^ 3}.get(event)
+
+
+def scatter_steps(
     count,
     partial,
-    out,
+    deliver,
     core_slot,
     side_slot,
     line_slot,
@@ -694,11 +667,10 @@
     side_got,
     line_sent,
     line_got,
+    compute=None,
 ):
-    seq = lax.axis_index("seq")
-    b = lax.axis_index("blk")
+    seq, b = lax.axis_index("seq"), lax.axis_index("blk")
     core, side = {"seq": seq ^ 1}, {"seq": seq ^ 2}
-    greet((core, side) + tuple({"blk": lax.rem(b + k, count)} for k in range(1, count)))
     away = tuple(range(count // 2, 0, -1)) + tuple(range(count // 2 + 1, count)) + (0,)
     place = [lax.rem(b + k, count) for k in away]
 
@@ -722,14 +694,21 @@
         )
 
     for half in range(2):
+        if compute:
+            compute(seq ^ (1 if half else 3))
         for k in range(count):
             to_core(half, k).start()
+    if compute:
+        compute(seq ^ 2)
     for k in range(count):
         to_core(0, k).wait_recv()
         total = partial[(seq ^ 2) * count + place[k]].astype(jnp.float32)
         total += core_slot[0, k].astype(jnp.float32)
         side_out[k] = total.astype(jnp.bfloat16)
         to_side(k).start()
+    if compute:
+        compute(seq)
+    yield
     for k in range(count):
         to_core(1, k).wait_recv()
         to_side(k).wait_recv()
@@ -739,11 +718,12 @@
         if k < count - 1:
             line_out[k] = total.astype(jnp.bfloat16)
             along_line(k).start()
-        else:
-            out[...] = total
+            yield
+    yield
     for k in range(count - 1):
         along_line(k).wait_recv()
-        out[...] += line_slot[away[k] - 1].astype(jnp.float32)
+        total += line_slot[away[k] - 1].astype(jnp.float32)
+    deliver(total)
     for k in range(count):
         to_core(0, k).wait_send()
         to_core(1, k).wait_send()
@@ -752,86 +732,255 @@
             along_line(k).wait_send()
 
 
-def group_scatter(partial):
-    seq_count, count = lax.axis_size("seq"), lax.axis_size("blk")
-    rows, width = partial.shape[0] // (seq_count * count), partial.shape[1]
+def scatter_scratch(count, rows, width):
     dma = pltpu.SemaphoreType.DMA
 
     def slots(*places):
         return pltpu.VMEM(places + (rows, width), jnp.bfloat16)
 
-    return pl.pallas_call(
-        functools.partial(scatter_kernel, count),
-        out_shape=jax.ShapeDtypeStruct((rows, width), jnp.float32),
-        in_specs=[pl.BlockSpec(memory_space=pltpu.VMEM)],
-        out_specs=pl.BlockSpec(memory_space=pltpu.VMEM),
-        scratch_shapes=[
-            slots(2, count),
-            slots(count),
-            slots(count - 1),
-            slots(count),
-            slots(count - 1),
-            dma((2, count)),
-            dma((2, count)),
-            dma((count,)),
-            dma((count,)),
-            dma((count - 1,)),
-            dma((count - 1,)),
-        ],
-        compiler_params=pltpu.CompilerParams(
-            collective_id=1, has_side_effects=True, vmem_limit_bytes=48 * 2**20
-        ),
-        name="scatter_tokens",
-    )(partial.astype(jnp.bfloat16).reshape(seq_count * count, rows, width))
-
-
-def turn(field_in, cosine, sine):
-    half_dim = HEAD_DIM // 2
-    first_half = field_in[:, :half_dim]
-    second_half = field_in[:, half_dim:]
-    return jnp.concatenate(
-        [first_half * cosine - second_half * sine, second_half * cosine + first_half * sine],
-        axis=-1,
-    )
-
-
-def spread_kernel(
+    return [
+        slots(2, count),
+        slots(count),
+        slots(count - 1),
+        slots(count),
+        slots(count - 1),
+        dma((2, count)),
+        dma((2, count)),
+        dma((count,)),
+        dma((count,)),
+        dma((count - 1,)),
+        dma((count - 1,)),
+    ]
+
+
+def run_with(steps, fillers):
+    fillers = list(fillers)
+    for _ in steps:
+        if fillers:
+            fillers.pop(0)()
+    for filler in fillers:
+        filler()
+
+
+def greet_group(count, more=()):
+    seq, b = lax.axis_index("seq"), lax.axis_index("blk")
+    greet(
+        tuple(more)
+        + ({"seq": seq ^ 1}, {"seq": seq ^ 2})
+        + tuple({"blk": lax.rem(b + k, count)} for k in range(1, count))
+    )
+
+
+def group_rows(ref, group, count):
+    value = ref[pl.ds(group * count, count)]
+    return value.reshape(value.shape[0] * value.shape[1], value.shape[2])
+
+
+def group_span(group, count, block):
+    size = count * block
+    return pl.ds(pl.multiple_of(group * size, size), size)
+
+
+def lane_turn(field_in, cosine, sine):
+    half_dim, lanes = HEAD_DIM // 2, field_in.shape[-1]
+    lane = lax.broadcasted_iota(jnp.int32, field_in.shape, 1)
+    partner = jnp.where(
+        lane < half_dim,
+        pltpu.roll(field_in, lanes - half_dim, 1),
+        pltpu.roll(field_in, half_dim, 1),
+    )
+    return field_in * cosine + partner * sine
+
+
+def masked_scores(query, key, first_row, start):
+    scores = back_product(query, key) * HEAD_DIM ** (-0.5)
+    key_index = lax.broadcasted_iota(jnp.int32, scores.shape, 1)
+    query_index = first_row + lax.broadcasted_iota(jnp.int32, scores.shape, 0)
+    return jnp.where((key_index >= start) & (key_index <= query_index), scores, MASKED)
+
+
+def normalise(field_in, gain_row):
+    inv_root = lax.rsqrt(jnp.mean(field_in * field_in, axis=-1, keepdims=True) + EPS)
+    return field_in * inv_root * gain_row
+
+
+PAD = 128
+
+
+def load_weights(attn, out, attn_vm, out_vm, sems):
+    copies = []
+    for part in range(3):
+        copies.append(
+            pltpu.make_async_copy(
+                attn.at[pl.ds(part * HEAD_DIM, HEAD_DIM)],
+                attn_vm.at[pl.ds(part * PAD, HEAD_DIM)],
+                sems.at[part],
+            )
+        )
+    copies.append(
+        pltpu.make_async_copy(
+            attn.at[pl.ds(3 * HEAD_DIM, 16)], attn_vm.at[pl.ds(3 * PAD, 16)], sems.at[3]
+        )
+    )
+    copies.append(pltpu.make_async_copy(out, out_vm.at[pl.ds(0, HEAD_DIM)], sems.at[4]))
+    return copies
+
+
+def clear_pads(attn_vm, out_vm):
+    empty = jnp.zeros((PAD - HEAD_DIM, attn_vm.shape[1]), jnp.bfloat16)
+    for part in range(3):
+        attn_vm[part * PAD + HEAD_DIM : (part + 1) * PAD] = empty
+    out_vm[HEAD_DIM:PAD] = empty
+
+
+def attn_kernel(count, spreading, *refs):
+    refs = iter(refs)
+
+    def take(n):
+        return [next(refs) for _ in range(n)]
+
+    if spreading:
+        pieces, w_gate, w_up, w_output, rows_in, grads_in, cosine, sine, start = take(9)
+        attn, gate_up, out, grads_all = take(4)
+    else:
+        rows_in, x_own, attn, out, cosine, sine, start = take(7)
+    hidden_out, normed_out, all_rows, heads, log_total = take(5)
+    rows_vm, attn_vm, out_vm, partial, load_done, save_done = take(6)
+    if spreading:
+        normed_vm, grads_vm = take(2)
+        spread_sems = take(5)
+        grads_sems = take(7)
+    else:
+        normed_vm = rows_vm
+    gather_sems = take(7)
+    scatter_refs = list(refs)
+    seq, section = lax.axis_index("seq"), lax.axis_index("section")
+    block = rows_vm.shape[1]
+    tokens = block * rows_vm.shape[0]
+    size = count * block
+    if spreading:
+        greet_group(count, ({"section": 1 - section},))
+        spread = spread_steps(
+            count, pieces, w_gate, w_up, w_output, attn, gate_up, out, *spread_sems
+        )
+        next(spread)
+    else:
+        greet_group(count)
+    steps = gather_steps(count, rows_in, rows_vm, *gather_sems)
+    next(steps)
+    clear_pads(attn_vm, out_vm)
+    if spreading:
+        loads = load_weights(attn.at[0], out.at[0], attn_vm, out_vm, load_done)
+    else:
+        loads = load_weights(attn.at[1], out.at[1], attn_vm, out_vm, load_done)
+        for copy in loads:
+            copy.start()
+
+    def project(group):
+        if spreading:
+            gain = attn_vm[3 * PAD : 3 * PAD + 16][0:1].astype(jnp.float32)
+            raw = rows_vm[pl.ds(group * count, count)].astype(jnp.float32)
+            normed = normalise(raw, gain[None]).astype(jnp.bfloat16)
+            normed_vm[pl.ds(group * count, count)] = normed
+            normed = normed.reshape(size, normed.shape[2])
+        else:
+            normed = group_rows(rows_vm, group, count)
+        mixed = back_product(normed, attn_vm[0 : 3 * PAD])
+        span = group_span(group, count, block)
+        cos_rows, sin_rows = cosine[span], sine[span]
+        heads[0, span] = lane_turn(mixed[:, :PAD], cos_rows, sin_rows).astype(jnp.bfloat16)
+        heads[1, span] = lane_turn(mixed[:, PAD : 2 * PAD], cos_rows, sin_rows).astype(
+            jnp.bfloat16
+        )
+        heads[2, span] = mixed[:, 2 * PAD :].astype(jnp.bfloat16)
+
+    for number, event in enumerate(steps):
+        group = group_of(event)
+        if spreading:
+            if number == 1:
+                next(spread)
+            continue
+        if event == "line":
+            for copy in loads:
+                copy.wait()
+        if group is not None:
+            project(group)
+    if spreading:
+        next(spread)
+        for copy in loads:
+            copy.start()
+        grad_steps = gather_steps(count, grads_in, grads_vm, *grads_sems)
+        next(grad_steps)
+        for copy in loads:
+            copy.wait()
+        for group in range(tokens // size):
+            project(group)
+    save = pltpu.make_async_copy(normed_vm, all_rows, save_done.at[0])
+    save.start()
+    for i in range(tokens // size):
+        here, seen = slice(i * size, (i + 1) * size), slice(0, (i + 1) * size)
+        scores = masked_scores(heads[0, here], heads[1, seen], i * size, start[here])
+        row_top = jnp.max(scores, axis=-1, keepdims=True)
+        weights = jnp.exp(scores - row_top)
+        total = jnp.sum(weights, axis=-1, keepdims=True)
+        log_total[here] = row_top + jnp.log(total)
+        weights = (weights * (1.0 / total)).astype(jnp.bfloat16)
+        heads[3, here] = product(weights, heads[2, seen]).astype(jnp.bfloat16)
+
+    def project_out(group):
+        mixed = heads[3, group_span(group, count, block)]
+        value = product(mixed, out_vm[...]).astype(jnp.bfloat16)
+        partial[pl.ds(group * count, count)] = value.reshape(count, block, -1)
+
+    def deliver(total):
+        own = rows_in[...].astype(jnp.float32) if spreading else x_own[...]
+        hidden = own + total
+        gain = attn_vm[3 * PAD : 3 * PAD + 16][1:2].astype(jnp.float32)
+        hidden_out[...] = hidden
+        normed_out[...] = normalise(hidden, gain).astype(jnp.bfloat16)
+
+    between = []
+    if spreading:
+        between = [functools.partial(advance, grad_steps, n) for n in (2, 1, 1, 2)]
+    run_with(scatter_steps(count, partial, deliver, *scatter_refs, compute=project_out), between)
+    if spreading:
+        for _ in spread:
+            pass
+        for _ in grad_steps:
+            pass
+        keep = pltpu.make_async_copy(grads_vm, grads_all, save_done.at[1])
+        keep.start()
+        keep.wait()
+    save.wait()
+
+
+def spread_steps(
     count,
     pieces,
     w_gate,
     w_up,
     w_output,
-    w_down,
-    rows_in,
-    grads_in,
     attn,
     gate_up,
     out,
-    down,
-    rows_all,
-    grads_all,
     line_sent,
     line_got,
     cross_sent,
     cross_got,
     local_done,
-    *gather_sems,
 ):
     seq, b, section = lax.axis_index("seq"), lax.axis_index("blk"), lax.axis_index("section")
+    seq_count = lax.axis_size("seq")
     other = {"section": 1 - section}
-    greet(
-        (other, {"seq": seq ^ 1}, {"seq": seq ^ 2})
-        + tuple({"blk": lax.rem(b + k, count)} for k in range(1, count))
-    )
     rows, lanes = w_gate.shape[0], gate_up.shape[2] // 2
-    out_rows, down_rows = out.shape[1], down.shape[1]
+    out_rows = out.shape[1]
     far_first = tuple(range(count // 2, 0, -1)) + tuple(range(count // 2 + 1, count))
 
     def source(kind, j):
         if kind == 0:
             return pieces.at[j]
         weight = w_gate if kind == 1 else w_up
-        return weight.at[:, pl.ds(pl.multiple_of((j * 4 + seq) * lanes, lanes), lanes)]
+        return weight.at[:, pl.ds(pl.multiple_of((j * seq_count + seq) * lanes, lanes), lanes)]
 
     def target(kind, j):
         if kind == 0:
@@ -860,13 +1009,12 @@
             other,
         )
 
-    def own_rows(kind):
-        weight, place, size = (w_output, out, out_rows) if kind == 3 else (w_down, down, down_rows)
-        begin = weight.at[pl.ds(pl.multiple_of(seq * size, size), size)]
-        spot = place.at[section]
+    def own_rows():
+        begin = w_output.at[pl.ds(pl.multiple_of(seq * out_rows, out_rows), out_rows)]
+        spot = out.at[section]
         return (
-            remote(begin, spot, cross_sent.at[kind, 0], cross_got.at[kind, 0], other),
-            pltpu.make_async_copy(begin, spot, local_done.at[kind]),
+            remote(begin, spot, cross_sent.at[3, 0], cross_got.at[3, 0], other),
+            pltpu.make_async_copy(begin, spot, local_done.at[3]),
         )
 
     def own_piece(kind):
@@ -874,6 +1022,10 @@
             across(kind, b, 0, source(kind, b)),
             pltpu.make_async_copy(source(kind, b), target(kind, b), local_done.at[kind]),
         )
+
+    def begin(copies):
+        for copy in copies:
+            copy.start()
 
     def forward(kind):
         for k in far_first:
@@ -881,204 +1033,355 @@
             settled(target(kind, j), line_got.at[kind, k], True)
             across(kind, j, k).start()
 
-    first = gather_steps(count, rows_in, rows_all, *gather_sems[:7])
-    second = gather_steps(count, grads_in, grads_all, *gather_sems[7:])
-    for k in far_first:
-        along_line(0, k).start()
-    for copy in own_piece(0) + own_rows(3):
-        copy.start()
-    next(first)
-    next(first)
-    for kind in (1, 2):
-        for k in far_first:
-            along_line(kind, k).start()
-    next(first)
-    forward(0)
-    for copy in own_piece(1) + own_piece(2) + own_rows(4):
-        copy.start()
-    for _ in first:
-        pass
-    next(second)
-    forward(1)
-    next(second)
-    next(second)
-    forward(2)
-    for _ in second:
-        pass
-    for kind in range(3):
+    def arrived(kind):
         for k in range(count):
             settled(target(kind, 0), cross_got.at[kind, k], True)
             settled(target(kind, 0), cross_sent.at[kind, k], False)
             if k:
                 settled(target(kind, 0), line_sent.at[kind, k], False)
         own_piece(kind)[1].wait()
-    for kind in (3, 4):
-        passed, local = own_rows(kind)
-        passed.wait()
-        local.wait()
-
-
-def spread_weights(local_shards, rows_in, grads_in):
-    seq_index, seq_count = lax.axis_index("seq"), lax.axis_size("seq")
-    count = lax.axis_size("blk")
-    gain_attn, w_query, w_key, w_value, w_output, gain_mlp, w_gate, w_up, w_down = local_shards
-    rows, width = w_query.shape[0], w_query.shape[1]
-    lanes = w_gate.shape[1] // (seq_count * count)
-    pad = 16
-
-    def heads_of(weight, per_blk, place):
-        head = jnp.arange(count)[:, None] * per_blk + place
-        column = (head * HEAD_DIM + jnp.arange(HEAD_DIM)).reshape(-1)
-        chosen = jnp.arange(weight.shape[1])[:, None] == column[None, :]
-        taken = lax.dot_general(
-            chosen.astype(jnp.bfloat16),
-            weight,
-            (((0,), (1,)), ((), ())),
-            preferred_element_type=jnp.float32,
-        )
-        return taken.astype(jnp.bfloat16).reshape(count, HEAD_DIM, rows)
-
-    kv_per_blk = KV_HEADS // count
-    kv_place = seq_index * kv_per_blk // seq_count
-    gains = jnp.concatenate(
-        [jnp.stack([gain_attn, gain_mlp]), jnp.zeros((pad - 2, rows), jnp.bfloat16)]
-    )
-    pieces = jnp.concatenate(
-        [
-            heads_of(w_query, seq_count, seq_index),
-            heads_of(w_key, kv_per_blk, kv_place),
-            heads_of(w_value, kv_per_blk, kv_place),
-            jnp.broadcast_to(gains[None], (count,) + gains.shape),
-        ],
-        axis=1,
-    )
-    low = jnp.bfloat16
-    out_rows, down_rows = w_output.shape[0] // seq_count, w_down.shape[0] // seq_count
-    block = rows_in.shape[0]
-    dma = pltpu.SemaphoreType.DMA
-    attn, gate_up, out, down, rows_all, grads_all = pl.pallas_call(
-        functools.partial(spread_kernel, count),
-        out_shape=[
-            jax.ShapeDtypeStruct((2, pieces.shape[1], rows * count), low),
-            jax.ShapeDtypeStruct((2, rows * count, 2 * lanes), low),
-            jax.ShapeDtypeStruct((2, out_rows, w_output.shape[1]), low),
-            jax.ShapeDtypeStruct((2, down_rows, w_down.shape[1]), low),
-            jax.ShapeDtypeStruct((seq_count * count, block, width), low),
-            jax.ShapeDtypeStruct((seq_count * count, block, width), low),
-        ],
-        in_specs=[pl.BlockSpec(memory_space=pl.ANY)] * 7,
-        out_specs=[pl.BlockSpec(memory_space=pl.ANY)] * 6,
-        scratch_shapes=[
-            dma((3, count)),
-            dma((3, count)),
-            dma((5, count)),
-            dma((5, count)),
-            dma((5,)),
-        ]
-        + gather_semaphores(count) * 2,
-        compiler_params=pltpu.CompilerParams(collective_id=2, has_side_effects=True),
-        name="spread_weights",
-    )(pieces, w_gate, w_up, w_output, w_down, rows_in, grads_in)
-    layers = tuple((attn[i], out[i], gate_up[i], down[i]) for i in range(2))
-    return layers, rows_all.reshape(-1, width), grads_all.reshape(-1, width)
-
-
-def own_layer(x_own, normed_all, weights, info):
-    attn, out, wide, down = weights
-    allowed, cosine, sine = info
-    gain_mlp = attn[3 * HEAD_DIM + 1].astype(jnp.float32)
-    inv_first = lax.rsqrt(jnp.mean(x_own * x_own, axis=-1, keepdims=True) + EPS)
-    mixed_in = back_product(normed_all, attn[: 3 * HEAD_DIM])
-    query = turn(mixed_in[:, :HEAD_DIM], cosine, sine).astype(jnp.bfloat16)
-    key = turn(mixed_in[:, HEAD_DIM : 2 * HEAD_DIM], cosine, sine).astype(jnp.bfloat16)
-    value = mixed_in[:, 2 * HEAD_DIM :].astype(jnp.bfloat16)
-    scores = jnp.where(allowed, back_product(query, key) * HEAD_DIM ** (-0.5), MASKED)
-    row_top = jnp.max(scores, axis=-1, keepdims=True)
-    log_total = row_top + jnp.log(jnp.sum(jnp.exp(scores - row_top), axis=-1, keepdims=True))
-    mixed = product(jnp.exp(scores - log_total).astype(jnp.bfloat16), value).astype(jnp.bfloat16)
-    hidden = x_own + group_scatter(product(mixed, out))
-    normed_mlp, inv_second = rms_forward(hidden, gain_mlp)
-    normed_mlp_all = group_gather(normed_mlp.astype(jnp.bfloat16))
-    pre = product(normed_mlp_all, wide)
+
+    for k in far_first:
+        along_line(0, k).start()
+    begin(own_piece(0) + own_rows())
+    yield
+    forward(0)
+    for kind in (1, 2):
+        for k in far_first:
+            along_line(kind, k).start()
+    yield
+    arrived(0)
+    passed, local = own_rows()
+    passed.wait()
+    local.wait()
+    for kind in (1, 2):
+        begin(own_piece(kind))
+        forward(kind)
+    yield
+    for kind in (1, 2):
+        arrived(kind)
+
+
+def start_all(copies):
+    for copy in copies:
+        copy.start()
+
+
+def wait_all(copies):
+    for copy in copies:
+        copy.wait()
+
+
+def gated(pre):
     half = pre.shape[1] // 2
-    gate_pre, up_pre = pre[:, :half], pre[:, half:]
-    act_low = (jax.nn.silu(gate_pre) * up_pre).astype(jnp.bfloat16)
-    result = hidden + group_scatter(product(act_low, down))
-    saved = (
-        x_own,
-        inv_first,
-        normed_all,
-        query,
-        key,
-        value,
-        log_total,
-        mixed,
-        hidden,
-        inv_second,
-        normed_mlp_all,
-        gate_pre,
-        up_pre,
-        act_low,
-    )
-    return result, saved
-
-
-def own_layer_back(grad_own, grad_out_all, weights, info, saved):
-    attn, out, wide, down = weights
-    allowed, cosine, sine = info
-    (
-        x_own,
-        inv_first,
-        normed_all,
-        query,
-        key,
-        value,
-        log_total,
-        mixed,
-        hidden,
-        inv_second,
-        normed_mlp_all,
-        gate_pre,
-        up_pre,
-        act_low,
-    ) = saved
-    gain_attn = attn[3 * HEAD_DIM].astype(jnp.float32)
-    gain_mlp = attn[3 * HEAD_DIM + 1].astype(jnp.float32)
-    grad_act = back_product(grad_out_all, down)
-    gate_sigmoid = jax.nn.sigmoid(gate_pre)
-    grad_gate = (
-        grad_act * up_pre * gate_sigmoid * (1.0 + gate_pre * (1.0 - gate_sigmoid))
-    ).astype(jnp.bfloat16)
-    grad_up = (grad_act * jax.nn.silu(gate_pre)).astype(jnp.bfloat16)
-    grad_wide = jnp.concatenate([grad_gate, grad_up], axis=1)
-    grad_normed_mlp = group_scatter(back_product(grad_wide, wide))
-    grad_hidden_part, gain_mlp_terms = rms_backward(hidden, gain_mlp, inv_second, grad_normed_mlp)
-    grad_hidden = grad_own + grad_hidden_part
-    grad_branch_all = group_gather(grad_hidden.astype(jnp.bfloat16))
-    grad_mixed = back_product(grad_branch_all, out).astype(jnp.bfloat16)
-    scores = jnp.where(allowed, back_product(query, key) * HEAD_DIM ** (-0.5), MASKED)
-    probs = jnp.exp(scores - log_total)
-    grad_probs = back_product(grad_mixed, value)
-    centre = jnp.sum(probs * grad_probs, axis=-1, keepdims=True)
-    grad_scores = (probs * (grad_probs - centre)).astype(jnp.bfloat16)
-    grad_query = (product(grad_scores, key) * HEAD_DIM ** (-0.5)).astype(jnp.bfloat16)
-    grad_key = weight_term(grad_scores, query) * HEAD_DIM ** (-0.5)
-    grad_value = weight_term(probs.astype(jnp.bfloat16), grad_mixed).astype(jnp.bfloat16)
-    grad_query = turn(grad_query.astype(jnp.float32), cosine, -sine).astype(jnp.bfloat16)
-    grad_key = turn(grad_key, cosine, -sine).astype(jnp.bfloat16)
-    grad_qkv = jnp.concatenate([grad_query, grad_key, grad_value], axis=1)
-    grad_normed = group_scatter(product(grad_qkv, attn[: 3 * HEAD_DIM]))
-    grad_in_part, gain_attn_terms = rms_backward(x_own, gain_attn, inv_first, grad_normed)
-    grads = shortened(
-        (
-            weight_term(grad_qkv, normed_all),
-            weight_term(mixed, grad_branch_all),
-            weight_term(normed_mlp_all, grad_wide),
-            weight_term(act_low, grad_out_all),
-        )
-    )
-    gains = jnp.stack([jnp.sum(gain_attn_terms, axis=0), jnp.sum(gain_mlp_terms, axis=0)])
-    return grad_hidden + grad_in_part, grads, gains
+    gate, up = pre[:, :half], pre[:, half:]
+    sigma = jax.nn.sigmoid(gate)
+    return gate, up, sigma
+
+
+def hidden_units(pre):
+    gate, up, sigma = gated(pre)
+    return (gate * sigma * up).astype(jnp.bfloat16)
+
+
+def store_gate_grads(place, span, grad_act, pre):
+    gate, up, sigma = gated(pre)
+    half = gate.shape[1]
+    place[span, 0:half] = (grad_act * up * sigma * (1.0 + gate * (1.0 - sigma))).astype(
+        jnp.bfloat16
+    )
+    place[span, half : 2 * half] = (grad_act * (gate * sigma)).astype(jnp.bfloat16)
+
+
+def mlp_kernel(count, *refs):
+    refs = iter(refs)
+
+    def take(n):
+        return [next(refs) for _ in range(n)]
+
+    rows_in, hidden, gate_up, w_down, gain_next = take(5)
+    down, result_out, normed_out, all_rows = take(4)
+    rows_vm, wide_vm, down_vm, units, partial, load_done, cross_sent, cross_got = take(8)
+    gather_sems = take(7)
+    scatter_refs = list(refs)
+    seq, section = lax.axis_index("seq"), lax.axis_index("section")
+    block = rows_vm.shape[1]
+    other = {"section": 1 - section}
+    greet_group(count, (other,))
+    load = pltpu.make_async_copy(gate_up.at[0], wide_vm, load_done.at[0])
+    load.start()
+    steps = gather_steps(count, rows_in, rows_vm, *gather_sems)
+    next(steps)
+    size = down.shape[1]
+    begin = w_down.at[pl.ds(pl.multiple_of(seq * size, size), size)]
+    across = remote(begin, down.at[section], cross_sent, cross_got, other)
+    local = pltpu.make_async_copy(begin, down.at[section], load_done.at[1])
+    across.start()
+    local.start()
+
+    def units_of(group):
+        pre = product(group_rows(rows_vm, group, count), wide_vm[...])
+        units[group_span(group, count, block)] = hidden_units(pre)
+
+    for event in steps:
+        if event == "line":
+            load.wait()
+        group = group_of(event)
+        if group is not None:
+            units_of(group)
+    save = pltpu.make_async_copy(rows_vm, all_rows, load_done.at[2])
+    save.start()
+    across.wait()
+    local.wait()
+    load = pltpu.make_async_copy(down.at[0], down_vm, load_done.at[3])
+    load.start()
+    load.wait()
+
+    def project_down(group):
+        value = product(units[group_span(group, count, block)], down_vm[...])
+        partial[pl.ds(group * count, count)] = value.astype(jnp.bfloat16).reshape(count, block, -1)
+
+    def deliver(total):
+        low = (hidden[...] + total).astype(jnp.bfloat16)
+        result_out[...] = low
+        normed_out[...] = normalise(low.astype(jnp.float32), gain_next[...]).astype(jnp.bfloat16)
+
+    run_with(scatter_steps(count, partial, deliver, *scatter_refs, compute=project_down), [])
+    save.wait()
+
+
+def wide_grads(rows_vm, pre_grads, units, grads_vm, wide_grad, down_grad):
+    tokens = pre_grads.shape[0]
+    width = rows_vm.shape[2]
+    step = width // 4
+
+    def wide_part(n):
+        cut = slice(n * step, (n + 1) * step)
+        rows = rows_vm[:, :, cut].reshape(tokens, step)
+        wide_grad[cut] = weight_term(rows, pre_grads[...]).astype(jnp.bfloat16)
+
+    def down_part(n):
+        cut = slice(n * 2 * step, (n + 1) * 2 * step)
+        rows = grads_vm[:, :, cut].reshape(tokens, 2 * step)
+        down_grad[:, cut] = weight_term(units[...], rows).astype(jnp.bfloat16)
+
+    return [functools.partial(wide_part, n) for n in range(4)] + [
+        functools.partial(down_part, n) for n in range(2)
+    ]
+
+
+def mlp_grad_sent(total, hidden, grads_own, gain, branch_out, grad_hidden_out, gain_out):
+    field_in = hidden[...]
+    inv_root = lax.rsqrt(jnp.mean(field_in * field_in, axis=-1, keepdims=True) + EPS)
+    part, terms = rms_backward(field_in, gain[...], inv_root, total)
+    grad_hidden = grads_own[...].astype(jnp.float32) + part
+    grad_hidden_out[...] = grad_hidden
+    branch_out[...] = grad_hidden.astype(jnp.bfloat16)
+    gain_out[...] = jnp.broadcast_to(jnp.sum(terms, axis=0, keepdims=True), gain_out.shape)
+
+
+def mlp_both_kernel(count, *refs):
+    refs = iter(refs)
+
+    def take(n):
+        return [next(refs) for _ in range(n)]
+
+    rows_in, hidden, gate_up, down, grads_all, grads_own, gain = take(7)
+    result_out, branch_out, grad_hidden_out, gain_out, wide_grad, down_grad = take(6)
+    rows_vm, grads_vm, wide_vm, down_vm, units, pre_grads, partial, partial_back = take(8)
+    (load_done,) = take(1)
+    gather_sems = take(7)
+    scatter_refs, scatter_back = take(11), take(11)
+    block = rows_vm.shape[1]
+    greet_group(count)
+    steps = gather_steps(count, rows_in, rows_vm, *gather_sems)
+    next(steps)
+    loads = [
+        pltpu.make_async_copy(gate_up.at[1], wide_vm, load_done.at[0]),
+        pltpu.make_async_copy(down.at[1], down_vm, load_done.at[1]),
+        pltpu.make_async_copy(grads_all, grads_vm, load_done.at[2]),
+    ]
+    start_all(loads)
+
+    def through(group):
+        span = group_span(group, count, block)
+        pre = product(group_rows(rows_vm, group, count), wide_vm[...])
+        units[span] = hidden_units(pre)
+        grad_act = back_product(group_rows(grads_vm, group, count), down_vm[...])
+        store_gate_grads(pre_grads, span, grad_act, pre)
+        value = back_product(pre_grads[span], wide_vm[...])
+        partial_back[pl.ds(group * count, count)] = value.astype(jnp.bfloat16).reshape(
+            count, block, -1
+        )
+
+    for event in steps:
+        if event == "line":
+            wait_all(loads)
+        group = group_of(event)
+        if group is not None:
+            through(group)
+
+    def project_down(group):
+        value = product(units[group_span(group, count, block)], down_vm[...])
+        partial[pl.ds(group * count, count)] = value.astype(jnp.bfloat16).reshape(count, block, -1)
+
+    def deliver(total):
+        result_out[...] = (hidden[...] + total).astype(jnp.bfloat16)
+
+    def deliver_back(total):
+        mlp_grad_sent(
+            total, hidden, grads_own, gain, branch_out, grad_hidden_out, gain_out
+        )
+
+    back = scatter_steps(count, partial_back, deliver_back, *scatter_back)
+    ahead = scatter_steps(count, partial, deliver, *scatter_refs, compute=project_down)
+    next(back)
+    next(ahead)
+    run_with(back, wide_grads(rows_vm, pre_grads, units, grads_vm, wide_grad, down_grad))
+    run_with(ahead, [])
+
+
+def mlp_back_kernel(count, *refs):
+    refs = iter(refs)
+
+    def take(n):
+        return [next(refs) for _ in range(n)]
+
+    grads_own, hidden, all_rows, gate_up, down, gain = take(6)
+    branch_out, grad_hidden_out, gain_out, wide_grad, down_grad = take(5)
+    rows_vm, grads_vm, wide_vm, down_vm, units, pre_vm, pre_grads, partial, load_done = take(9)
+    gather_sems = take(7)
+    scatter_refs = list(refs)
+    block = rows_vm.shape[1]
+    greet_group(count)
+    steps = gather_steps(count, grads_own, grads_vm, *gather_sems)
+    next(steps)
+    loads = [
+        pltpu.make_async_copy(gate_up.at[0], wide_vm, load_done.at[0]),
+        pltpu.make_async_copy(all_rows, rows_vm, load_done.at[1]),
+        pltpu.make_async_copy(down.at[0], down_vm, load_done.at[2]),
+    ]
+    start_all(loads)
+
+    def again(group):
+        span = group_span(group, count, block)
+        pre = product(group_rows(rows_vm, group, count), wide_vm[...])
+        pre_vm[span] = pre
+        units[span] = hidden_units(pre)
+
+    def through(group):
+        span = group_span(group, count, block)
+        grad_act = back_product(group_rows(grads_vm, group, count), down_vm[...])
+        store_gate_grads(pre_grads, span, grad_act, pre_vm[span])
+        value = back_product(pre_grads[span], wide_vm[...])
+        partial[pl.ds(group * count, count)] = value.astype(jnp.bfloat16).reshape(count, block, -1)
+
+    wait_all(loads)
+    for number, event in enumerate(steps):
+        if number < 2:
+            again(2 * number)
+            again(2 * number + 1)
+        group = group_of(event)
+        if group is not None:
+            through(group)
+
+    def deliver(total):
+        mlp_grad_sent(total, hidden, grads_own, gain, branch_out, grad_hidden_out, gain_out)
+
+    run_with(
+        scatter_steps(count, partial, deliver, *scatter_refs),
+        wide_grads(rows_vm, pre_grads, units, grads_vm, wide_grad, down_grad),
+    )
+
+
+def attn_back_kernel(count, layer, *refs):
+    refs = iter(refs)
+
+    def take(n):
+        return [next(refs) for _ in range(n)]
+
+    branch_in, grad_hidden, x_own, all_rows, heads_kept, log_total, attn, out = take(8)
+    cosine, sine, start, gain = take(4)
+    grad_out, gain_out, attn_grad, out_grad = take(4)
+    branch_vm, rows_vm, heads, attn_vm, out_vm, mixed_grads, probs = take(7)
+    key_grads, value_grads, joint, partial, load_done = take(5)
+    gather_sems = take(7)
+    scatter_refs = list(refs)
+    block = rows_vm.shape[1]
+    size = count * block
+    tokens = block * rows_vm.shape[0]
+    low, f32 = jnp.bfloat16, jnp.float32
+    scale = HEAD_DIM ** (-0.5)
+    greet_group(count)
+    steps = gather_steps(count, branch_in, branch_vm, *gather_sems)
+    next(steps)
+    clear_pads(attn_vm, out_vm)
+    loads = load_weights(attn.at[layer], out.at[layer], attn_vm, out_vm, load_done)
+    loads.append(pltpu.make_async_copy(heads_kept, heads, load_done.at[5]))
+    loads.append(pltpu.make_async_copy(all_rows, rows_vm, load_done.at[6]))
+    start_all(loads)
+    key_grads[...] = jnp.zeros_like(key_grads)
+    value_grads[...] = jnp.zeros_like(value_grads)
+    wait_all(loads)
+
+    def spans(i):
+        return slice(i * size, (i + 1) * size), slice(0, (i + 1) * size)
+
+    def weigh(i):
+        here, seen = spans(i)
+        scores = masked_scores(heads[0, here], heads[1, seen], i * size, start[here])
+        probs[here, seen] = jnp.exp(scores - log_total[here])
+
+    def project(group):
+        value = back_product(group_rows(branch_vm, group, count), out_vm[...])
+        mixed_grads[group_span(group, count, block)] = value.astype(low)
+
+    for number, event in enumerate(steps):
+        if number < 2:
+            weigh(2 * number)
+            weigh(2 * number + 1)
+        group = group_of(event)
+        if group is not None:
+            project(group)
+    for i in reversed(range(tokens // size)):
+        here, seen = spans(i)
+        weights = probs[here, seen]
+        grads = mixed_grads[here]
+        grad_weights = back_product(grads, heads[2, seen])
+        centre = jnp.sum(weights * grad_weights, axis=-1, keepdims=True)
+        grad_scores = (weights * (grad_weights - centre)).astype(low)
+        query_grad = (product(grad_scores, heads[1, seen]) * scale).astype(low).astype(f32)
+        joint[here, 0:PAD] = lane_turn(query_grad, cosine[here], -sine[here]).astype(low)
+        key_grads[seen] += weight_term(grad_scores, heads[0, here])
+        value_grads[seen] += weight_term(weights.astype(low), grads)
+        key_grad = (key_grads[here] * scale).astype(low).astype(f32)
+        joint[here, PAD : 2 * PAD] = lane_turn(key_grad, cosine[here], -sine[here]).astype(low)
+        joint[here, 2 * PAD : 3 * PAD] = value_grads[here].astype(low)
+
+    def project_back(group):
+        value = product(joint[group_span(group, count, block)], attn_vm[0 : 3 * PAD])
+        partial[pl.ds(group * count, count)] = value.astype(low).reshape(count, block, -1)
+
+    def attn_part(part):
+        rows = rows_vm[...].reshape(tokens, rows_vm.shape[2])
+        value = weight_term(joint[:, part * PAD : (part + 1) * PAD], rows)
+        attn_grad[part * HEAD_DIM : (part + 1) * HEAD_DIM] = value[0:HEAD_DIM].astype(low)
+
+    def out_part():
+        rows = branch_vm[...].reshape(tokens, branch_vm.shape[2])
+        out_grad[...] = weight_term(heads[3], rows)[0:HEAD_DIM].astype(low)
+
+    def deliver(total):
+        field_in = x_own[...].astype(f32)
+        inv_root = lax.rsqrt(jnp.mean(field_in * field_in, axis=-1, keepdims=True) + EPS)
+        part, terms = rms_backward(field_in, gain[...], inv_root, total)
+        grad_out[...] = (grad_hidden[...] + part).astype(low)
+        gain_out[...] = jnp.broadcast_to(jnp.sum(terms, axis=0, keepdims=True), gain_out.shape)
+
+    run_with(
+        scatter_steps(count, partial, deliver, *scatter_refs, compute=project_back),
+        [functools.partial(attn_part, part) for part in range(3)] + [out_part],
+    )
 
 
 def finish_kernel(
@@ -1408,53 +1711,243 @@
     )
 
 
+def call_kernel(kernel, name, number, operands, outputs, scratch):
+    in_vmem = pl.BlockSpec(memory_space=pltpu.VMEM)
+    anywhere = pl.BlockSpec(memory_space=pl.ANY)
+    return pl.pallas_call(
+        kernel,
+        out_shape=[jax.ShapeDtypeStruct(shape, dtype) for shape, dtype, _ in outputs],
+        in_specs=[in_vmem if near else anywhere for _, near in operands],
+        out_specs=[in_vmem if near else anywhere for _, _, near in outputs],
+        scratch_shapes=scratch,
+        compiler_params=pltpu.CompilerParams(
+            collective_id=number, has_side_effects=True, vmem_limit_bytes=56 * 2**20
+        ),
+        name=name,
+    )(*[array for array, _ in operands])
+
+
+def sliced_heads(local_shards):
+    seq_index, seq_count = lax.axis_index("seq"), lax.axis_size("seq")
+    count = lax.axis_size("blk")
+    gain_attn, w_query, w_key, w_value, _, gain_mlp, _, _, _ = local_shards
+    rows = w_query.shape[0]
+
+    def heads_of(weight, per_blk, place):
+        head = jnp.arange(count)[:, None] * per_blk + place
+        column = (head * HEAD_DIM + jnp.arange(HEAD_DIM)).reshape(-1)
+        chosen = jnp.arange(weight.shape[1])[:, None] == column[None, :]
+        taken = lax.dot_general(
+            chosen.astype(jnp.bfloat16),
+            weight,
+            (((0,), (1,)), ((), ())),
+            preferred_element_type=jnp.float32,
+        )
+        return taken.astype(jnp.bfloat16).reshape(count, HEAD_DIM, rows)
+
+    kv_per_blk = KV_HEADS // count
+    kv_place = seq_index * kv_per_blk // seq_count
+    gains = jnp.concatenate(
+        [jnp.stack([gain_attn, gain_mlp]), jnp.zeros((14, rows), jnp.bfloat16)]
+    )
+    return jnp.concatenate(
+        [
+            heads_of(w_query, seq_count, seq_index),
+            heads_of(w_key, kv_per_blk, kv_place),
+            heads_of(w_value, kv_per_blk, kv_place),
+            jnp.broadcast_to(gains[None], (count,) + gains.shape),
+        ],
+        axis=1,
+    )
+
+
 def head_shards(inputs, cotangent, doc_lengths, *params):
     section = lax.axis_index("section")
     at_first = section == 0
-    tokens = inputs.shape[2] * lax.axis_size("seq") * lax.axis_size("blk")
+    seq_count, count = lax.axis_size("seq"), lax.axis_size("blk")
+    low, f32 = jnp.bfloat16, jnp.float32
+    vmem, dma = pltpu.VMEM, pltpu.SemaphoreType.DMA
+    block, width = inputs.shape[2], inputs.shape[3]
+    blocks = seq_count * count
+    tokens = blocks * block
     rows_own = lax.dynamic_index_in_dim(inputs, section, 0, keepdims=False)[0]
     grads_own = lax.dynamic_index_in_dim(cotangent, section, 0, keepdims=False)[0]
-    (first, second), rows_all, grads_all = spread_weights(
-        tuple(weight[0] for weight in params), rows_own, grads_own
-    )
+    local = tuple(weight[0] for weight in params)
+    pieces = sliced_heads(local)
+    w_output, w_gate, w_up, w_down = local[4], local[6], local[7], local[8]
+    rows = w_gate.shape[0]
+    lanes = w_gate.shape[1] // blocks
+    out_rows, down_rows = w_output.shape[0] // seq_count, w_down.shape[0] // seq_count
     lengths = lax.dynamic_index_in_dim(doc_lengths, section, 0, keepdims=False)[0]
     token_index = jnp.arange(tokens, dtype=jnp.int32)
-    segment, position = doc_info(lengths, token_index)
-    allowed = (segment[:, None] == segment[None, :]) & (
-        token_index[None, :] <= token_index[:, None]
-    )
+    _, position = doc_info(lengths, token_index)
+    start = (token_index - position)[:, None]
     half_dim = HEAD_DIM // 2
-    frequency = THETA ** (-2.0 * jnp.arange(half_dim, dtype=jnp.float32) / HEAD_DIM)
-    angles = position.astype(jnp.float32)[:, None] * frequency
-    info = (allowed, jnp.cos(angles), jnp.sin(angles))
-    x_own = rows_own.astype(jnp.float32)
-    gain = first[0][3 * HEAD_DIM].astype(jnp.float32)
-    normed_all = rms_forward(rows_all.astype(jnp.float32), gain)[0].astype(jnp.bfloat16)
-    result, saved_first = own_layer(x_own, normed_all, first, info)
-    between = result.astype(jnp.bfloat16)
-    x_own = between.astype(jnp.float32)
-    gain = second[0][3 * HEAD_DIM].astype(jnp.float32)
-    normed_all = group_gather(rms_forward(x_own, gain)[0].astype(jnp.bfloat16))
-    result, saved_second = own_layer(x_own, normed_all, second, info)
-    final = result.astype(jnp.bfloat16)
-    grad_between, grads_second, gains_second = own_layer_back(
-        grads_own.astype(jnp.float32), grads_all, second, info, saved_second
-    )
-    grad_between = grad_between.astype(jnp.bfloat16)
-    grad_start, grads_first, gains_first = own_layer_back(
-        grad_between.astype(jnp.float32), group_gather(grad_between), first, info, saved_first
-    )
-    grad_start = grad_start.astype(jnp.bfloat16)
+    frequency = THETA ** (-2.0 * jnp.arange(half_dim, dtype=f32) / HEAD_DIM)
+    angles = position.astype(f32)[:, None] * frequency
+    cosine, sine = jnp.cos(angles), jnp.sin(angles)
+    empty = jnp.zeros((tokens, PAD - HEAD_DIM), f32)
+    cosine = jnp.concatenate([cosine, cosine, empty], axis=1)
+    sine = jnp.concatenate([-sine, sine, empty], axis=1)
+
+    def all_blocks():
+        return vmem((blocks, block, width), low)
+
+    def scatter():
+        return scatter_scratch(count, block, width)
+
+    own_low, own_wide = ((block, width), low, True), ((block, width), f32, True)
+    every = ((blocks, block, width), low, False)
+    gain_rows = ((8, width), f32, True)
+    attn_outputs = [
+        own_wide,
+        own_low,
+        every,
+        ((4, tokens, PAD), low, True),
+        ((tokens, 1), f32, True),
+    ]
+    weights_vm = [vmem((3 * PAD + 16, width), low), vmem((PAD, width), low)]
+    wide_vm, down_vm = vmem((width, 2 * lanes), low), vmem((down_rows, width), low)
+    tables = [(cosine, True), (sine, True), (start, True)]
+    attn, gate_up, out, grads_all, hidden_one, normed, rows_one, heads_one, total_one = call_kernel(
+        functools.partial(attn_kernel, count, True),
+        "first_attention",
+        2,
+        [(array, False) for array in (pieces, w_gate, w_up, w_output)]
+        + [(rows_own, True), (grads_own, True)]
+        + tables,
+        [
+            ((2, pieces.shape[1], width), low, False),
+            ((2, width, 2 * lanes), low, False),
+            ((2, out_rows, width), low, False),
+            every,
+        ]
+        + attn_outputs,
+        [all_blocks()]
+        + weights_vm
+        + [all_blocks(), dma((5,)), dma((2,)), all_blocks(), all_blocks()]
+        + [dma((3, count)), dma((3, count)), dma((4, count)), dma((4, count)), dma((4,))]
+        + gather_semaphores(count) * 2
+        + scatter(),
+    )
+    gains = attn[:, 3 * HEAD_DIM : 3 * HEAD_DIM + 2].astype(f32)
+    down, between, normed, wide_rows_one = call_kernel(
+        functools.partial(mlp_kernel, count),
+        "first_feed_forward",
+        5,
+        [
+            (normed, True),
+            (hidden_one, True),
+            (gate_up, False),
+            (w_down, False),
+            (gains[1, 0:1], True),
+        ],
+        [((2, down_rows, width), low, False), own_low, own_low, every],
+        [all_blocks(), wide_vm, down_vm, vmem((tokens, lanes), low), all_blocks(), dma((4,)), dma, dma]
+        + gather_semaphores(count)
+        + scatter(),
+    )
+    hidden_two, normed, rows_two, heads_two, total_two = call_kernel(
+        functools.partial(attn_kernel, count, False),
+        "second_attention",
+        4,
+        [(normed, True), (between.astype(f32), True), (attn, False), (out, False)] + tables,
+        attn_outputs,
+        [all_blocks()]
+        + weights_vm
+        + [all_blocks(), dma((5,)), dma((2,))]
+        + gather_semaphores(count)
+        + scatter(),
+    )
+    wide_outputs = [((width, 2 * lanes), low, True), ((down_rows, width), low, True)]
+    final, branch, grad_hidden, gain_mlp_two, wide_two, down_two = call_kernel(
+        functools.partial(mlp_both_kernel, count),
+        "second_feed_forward",
+        6,
+        [
+            (normed, True),
+            (hidden_two, True),
+            (gate_up, False),
+            (down, False),
+            (grads_all, False),
+            (grads_own, True),
+            (gains[1, 1:2], True),
+        ],
+        [own_low, own_low, own_wide, gain_rows] + wide_outputs,
+        [all_blocks(), all_blocks(), wide_vm, down_vm]
+        + [vmem((tokens, lanes), low), vmem((tokens, 2 * lanes), low)]
+        + [all_blocks(), all_blocks(), dma((3,))]
+        + gather_semaphores(count)
+        + scatter()
+        + scatter(),
+    )
+
+    def attention_back(layer, branch, grad_hidden, x_own, rows_all, heads, log_total):
+        return call_kernel(
+            functools.partial(attn_back_kernel, count, layer),
+            ("first", "second")[layer] + "_attention_back",
+            7 + layer,
+            [(branch, True), (grad_hidden, True), (x_own, True)]
+            + [(rows_all, False), (heads, False), (log_total, True), (attn, False), (out, False)]
+            + tables
+            + [(gains[layer, 0:1], True)],
+            [
+                own_low,
+                gain_rows,
+                ((3 * HEAD_DIM, width), low, True),
+                ((HEAD_DIM, width), low, True),
+            ],
+            [all_blocks(), all_blocks(), vmem((4, tokens, PAD), low)]
+            + weights_vm
+            + [vmem((tokens, PAD), low), vmem((tokens, tokens), f32)]
+            + [vmem((tokens, PAD), f32), vmem((tokens, PAD), f32), vmem((tokens, 3 * PAD), low)]
+            + [all_blocks(), dma((7,))]
+            + gather_semaphores(count)
+            + scatter(),
+        )
+
+    grad_between, gain_attn_two, attn_two, out_two = attention_back(
+        1, branch, grad_hidden, between, rows_two, heads_two, total_two
+    )
+    branch, grad_hidden, gain_mlp_one, wide_one, down_one = call_kernel(
+        functools.partial(mlp_back_kernel, count),
+        "first_feed_forward_back",
+        9,
+        [
+            (grad_between, True),
+            (hidden_one, True),
+            (wide_rows_one, False),
+            (gate_up, False),
+            (down, False),
+            (gains[0, 1:2], True),
+        ],
+        [own_low, own_wide, gain_rows] + wide_outputs,
+        [all_blocks(), all_blocks(), wide_vm, down_vm]
+        + [vmem((tokens, lanes), low), vmem((tokens, 2 * lanes), f32)]
+        + [vmem((tokens, 2 * lanes), low), all_blocks(), dma((3,))]
+        + gather_semaphores(count)
+        + scatter(),
+    )
+    grad_start, gain_attn_one, attn_one, out_one = attention_back(
+        0, branch, grad_hidden, rows_own, rows_one, heads_one, total_one
+    )
     kept = jnp.where(
         at_first, jnp.stack([between, grad_start]), jnp.stack([final, grad_between])
     )
     sent = jnp.where(
         at_first, jnp.stack([final, grad_between]), jnp.stack([between, grad_start])
     )
-    gains = jnp.stack([gains_first, gains_second])
-    gains = jnp.concatenate([gains, jnp.zeros((2, 6) + gains.shape[2:], jnp.float32)], axis=1)
-    swapped_rows, gains, query, key, value, out, gate, up, down = finish_grads(
-        grads_first, grads_second, gains, sent
+    gain_sums = jnp.stack(
+        [
+            jnp.concatenate([gain_attn_one[0:4], gain_mlp_one[0:4]]),
+            jnp.concatenate([gain_attn_two[0:4], gain_mlp_two[0:4]]),
+        ]
+    )
+    swapped_rows, gain_sums, query, key, value, out, gate, up, down = finish_grads(
+        (attn_one, out_one, wide_one, down_one),
+        (attn_two, out_two, wide_two, down_two),
+        gain_sums,
+        sent,
     )
     pairs = jnp.where(
         at_first, jnp.stack([kept, swapped_rows], axis=1), jnp.stack([swapped_rows, kept], axis=1)
@@ -1462,12 +1955,12 @@
     return (
         pairs[0][None, :, None],
         pairs[1][None, :, None],
-        gains[0][None],
+        gain_sums[0][None],
         query[None],
         key[None],
         value[None],
         out[None],
-        gains[1][None],
+        gain_sums[4][None],
         gate[None],
         up[None],
         down[None],

time: 737 us -> 658 us (0.89)
  matrix products: 56 us -> 1.84 us
  other arithmetic: 45.8 us -> 25.4 us
    dot_general x36 -> x0, matrix products: 54.2 us -> none  [the longest x12 20.5 us: back_product(): lax.dot_general(left_side, right_side, (((1,), (1,)), ((), ())), preferre...]
    reduce_sum x11 -> x0, other arithmetic: 8.22 us -> none  [the longest x4 3.18 us: rms_forward(): jnp.mean(field_in * field_in, axis=-1, keepdims=True) + EPS]
    pallas_call x15 -> x7, Pallas kernels: 482 us -> 487 us  [call_kernel(): pl.pallas_call(kernel, out_shape=[jax.ShapeDtypeStruct(shape, dtype) for...]
where the time goes in v4:
time: 658 us; the launch traced here: 650 us
  Pallas kernels  607 us (92%)
  other arithmetic  25.4 us (4%)
  local copies, waits for them, and re-layouts  14.8 us (2%)
    pallas_call x7, Pallas kernels, call_kernel(): pl.pallas_call(kernel, out_shape=[jax.ShapeDtypeStruct(shape, dtype) for...  487 us
    pallas_call x1, Pallas kernels, finish_grads(): pl.pallas_call(functools.partial(finish_kernel, count), out_shape=[jax.Sh...  120 us

profile of v4, /device:TPU:18, one launch (start us, length us, event | category | flops | bytes accessed | tf_op | source)
XLA Modules:
  0.0 650.5 jit_solution(18158792771556827659)
XLA Ops:
  5.0 1.0 pad_maximum_fusion.refs_0_
  6.8 1.0 copy.35.refs_8_.refs_6_.refs_10_
  7.8 1.9 fusion.11
  9.7 1.3 maximum_maximum_fusion.1
  11.0 125.5 %first_attention.1 = (bf16[2,304,1536]{2,1,0:T(8,128)(2,1)}, bf16[2,1536,512]{2,1,0:T(8,128)(2,1)}, bf16[2,96,1536]{2,1,0:T(8,128)(2,1)}, bf16[16,64,1536]{2,1,0...) custom-call(bf16[4,304,384]{2,1,0:T(8,128)(2,1)} %pad_maximum_fusion, ...), custom_call_target="tpu_custom_call" | custom-call | tf_op jit(solution)/shard_map/first_attention/pallas_call | solution.py:1717
  137.9 56.4 %first_feed_forward.1 = (bf16[2,256,1536]{2,1,0:T(8,128)(2,1)}, bf16[64,1536]{1,0:T(8,128)(2,1)}, bf16[64,1536]{1,0:T(8,128)(2,1)}, bf16[16,64,1536]{2,1,0:T(8,128)(2,1)}) custom-call(bf16[64,1536]{1,0:T(8,128)(2,1)} %get-tuple-element.55.refs_0_, f32[64,1536]{1,0:T(8,128)} %get-tuple-element.56.refs_1_, ...), custom_call_target="tpu_custom_call" | custom-call | tf_op jit(solution)/shard_map/first_feed_forward/pallas_call | solution.py:1717
  194.3 1.7 convert_element_type.38.refs_1_
  196.0 58.5 %second_attention.1 = (f32[64,1536]{1,0:T(8,128)}, bf16[64,1536]{1,0:T(8,128)(2,1)}, bf16[16,64,1536]{2,1,0:T(8,128)(2,1)}, bf16[4,1024,128]{2,1,0:T(8,128)(2,1)}, f32[1024,1]{1,0:T(8,128)}) custom-call(bf16[64,1536]{1,0:T(8,128)(2,1)} %get-tuple-element.60.refs_0_, f32[64,1536]{1,0:T(8,128)} %convert_element_type.38.refs_1_, ...), custom_call_target="tpu_custom_call" | custom-call | tf_op jit(solution)/shard_map/second_attention/pallas_call | solution.py:1717
  254.5 76.8 %second_feed_forward.1 = (bf16[64,1536]{1,0:T(8,128)(2,1)}, bf16[64,1536]{1,0:T(8,128)(2,1)}, f32[64,1536]{1,0:T(8,128)}, f32[8,1536]{1,0:T(8,128)}, bf16[1536,5...) custom-call(bf16[64,1536]{1,0:T(8,128)(2,1)} %get-tuple-element.62.refs_0_, f32[64,1536]{1,0:T(8,128)} %get-tuple-element.63.refs_1_, ...), custom_call_target="tpu_custom_call" | custom-call | tf_op jit(solution)/shard_map/second_feed_forward/pallas_call | solution.py:1717
  331.3 56.5 %second_attention_back.1 = (bf16[64,1536]{1,0:T(8,128)(2,1)}, f32[8,1536]{1,0:T(8,128)}, bf16[288,1536]{1,0:T(8,128)(2,1)}, bf16[96,1536]{1,0:T(8,128)(2,1)}) custom-call(bf16[64,1536]{1,0:T(8,128)(2,1)} %get-tuple-element.66.refs_0_, f32[64,1536]{1,0:T(8,128)} %get-tuple-element.67.refs_1_, bf16[64,1536]{1,0:T(8,128)(2,1)} %get-tuple-element.59.refs_2_, ...), custom_call_target="tpu_custom_call" | custom-call | tf_op jit(solution)/shard_map/second_attention_back/pallas_call | solution.py:1717
  387.8 55.3 %first_feed_forward_back.1 = (bf16[64,1536]{1,0:T(8,128)(2,1)}, f32[64,1536]{1,0:T(8,128)}, f32[8,1536]{1,0:T(8,128)}, bf16[1536,512]{1,0:T(8,128)(2,1)}, bf16[256,1536]{1,0:T(8,128)(2,1)}) custom-call(bf16[64,1536]{1,0:T(8,128)(2,1)} %get-tuple-element.71.refs_0_, f32[64,1536]{1,0:T(8,128)} %get-tuple-element.56.refs_1_, ...), custom_call_target="tpu_custom_call" | custom-call | tf_op jit(solution)/shard_map/first_feed_forward_back/pallas_call | solution.py:1717
  443.2 57.7 %first_attention_back.1 = (bf16[64,1536]{1,0:T(8,128)(2,1)}, f32[8,1536]{1,0:T(8,128)}, bf16[288,1536]{1,0:T(8,128)(2,1)}, bf16[96,1536]{1,0:T(8,128)(2,1)}) custom-call(bf16[64,1536]{1,0:T(8,128)(2,1)} %get-tuple-element.73.refs_0_, f32[64,1536]{1,0:T(8,128)} %get-tuple-element.74.refs_1_, bf16[64,1536]{1,0:T(8,128)(2,1)} %get-tuple-element.150.refs_4_.refs_2_, ...), custom_call_target="tpu_custom_call" | custom-call | tf_op jit(solution)/shard_map/first_attention_back/pallas_call | solution.py:1717
  501.0 1.0 slice.54
  502.1 1.0 maximum_select_fusion.1
  503.1 1.0 maximum_select_fusion.2.swap_rows
  505.1 120.1 %finish_grads.1 = (bf16[16,288,384]{2,1,0:T(8,128)(2,1)}, bf16[384,1536]{1,0:T(8,128)(2,1)S(1)}, bf16[384,4096]{1,0:T(8,128)(2,1)}, bf16[384,4096]{1,0:T(8,128)(...) custom-call(bf16[288,1536]{1,0:T(8,128)(2,1)S(1)} %copy-done.3, ...), custom_call_target="tpu_custom_call" | custom-call | tf_op jit(solution)/shard_map/finish_grads/pallas_call | solution.py:1651
  626.9 1.7 bitcast_convert_fusion.3
  628.6 1.6 slice.71
  630.2 3.3 copy.39
  634.6 1.4 copy.43
  636.0 1.4 copy.42
  637.4 5.5 bitcast_convert_fusion.2
  642.9 3.5 bitcast_convert_fusion.1
  646.4 3.6 bitcast_convert_fusion
  (76 shorter events, 10.2 us)
Async XLA Ops:
  0.6 2.4 copy-start
  0.7 3.2 copy-start.19
  0.7 3.8 copy-start.20
  3.9 2.1 copy-start.14
  3.9 2.1 copy-start.15
  443.1 57.8 %copy-start.17 = (f32[8,1536]{1,0:T(8,128)S(1)}, f32[8,1536]{1,0:T(8,128)}, u32[]{:S(2)}) copy-start(f32[8,1536]{1,0:T(8,128)} %get-tuple-element.90) | copy-start | bytes 147460
  443.2 58.8 %copy-start.18 = (f32[8,1536]{1,0:T(8,128)S(1)}, f32[8,1536]{1,0:T(8,128)}, u32[]{:S(2)}) copy-start(f32[8,1536]{1,0:T(8,128)} %get-tuple-element.89) | copy-start | bytes 147460
  443.2 58.8 %copy-start.16 = (f32[8,1536]{1,0:T(8,128)S(1)}, f32[8,1536]{1,0:T(8,128)}, u32[]{:S(2)}) copy-start(f32[8,1536]{1,0:T(8,128)} %get-tuple-element.91) | copy-start | bytes 147460
  443.2 58.9 %copy-start.11 = (bf16[64,1536]{1,0:T(8,128)(2,1)S(1)}, bf16[64,1536]{1,0:T(8,128)(2,1)}, u32[]{:S(2)}) copy-start(bf16[64,1536]{1,0:T(8,128)(2,1)} %get-tuple-element.59.refs_2_) | copy-start | bytes 589828
  443.2 58.9 %copy-start.12 = (bf16[64,1536]{1,0:T(8,128)(2,1)S(1)}, bf16[64,1536]{1,0:T(8,128)(2,1)}, u32[]{:S(2)}) copy-start(bf16[64,1536]{1,0:T(8,128)(2,1)} %get-tuple-element.71.refs_0_) | copy-start | bytes 589828
  443.2 58.9 %copy-start.13 = (bf16[64,1536]{1,0:T(8,128)(2,1)S(1)}, bf16[64,1536]{1,0:T(8,128)(2,1)}, u32[]{:S(2)}) copy-start(bf16[64,1536]{1,0:T(8,128)(2,1)} %get-tuple-element.79) | copy-start | bytes 589828
  443.2 60.9 %copy-start.5 = (bf16[256,1536]{1,0:T(8,128)(2,1)S(1)}, bf16[256,1536]{1,0:T(8,128)(2,1)}, u32[]{:S(2)}) copy-start(bf16[256,1536]{1,0:T(8,128)(2,1)} %get-tuple-element.86.down_one) | copy-start | bytes 2359300
  500.9 3.2 copy-start.2
  500.9 3.2 copy-start.3
  500.9 3.2 copy-start.4
  501.0 3.2 copy-start.6
  504.1 1.0 copy-start.7
  625.4 3.2 copy-start.8
  637.4 5.5 copy-start.10
  642.9 3.5 copy-start.9
  646.4 3.6 copy-start.1

commit v5 on v4

--- a/solution.py
+++ b/solution.py
@@ -661,6 +661,7 @@
     line_slot,
     side_out,
     line_out,
+    running,
     core_sent,
     core_got,
     side_sent,
@@ -671,8 +672,7 @@
 ):
     seq, b = lax.axis_index("seq"), lax.axis_index("blk")
     core, side = {"seq": seq ^ 1}, {"seq": seq ^ 2}
-    away = tuple(range(count // 2, 0, -1)) + tuple(range(count // 2 + 1, count)) + (0,)
-    place = [lax.rem(b + k, count) for k in away]
+    place = far_first(b, count)
 
     def to_core(half, k):
         source = partial.at[(seq ^ (1 if half else 3)) * count + place[k]]
@@ -683,15 +683,19 @@
     def to_side(k):
         return remote(side_out.at[k], side_slot.at[k], side_sent.at[k], side_got.at[k], side)
 
-    def along_line(k):
-        slot = away[k] - 1
+    def along_line(k, way):
+        j = place[k]
         return remote(
             line_out.at[k],
-            line_slot.at[slot],
+            line_slot.at[way, j],
             line_sent.at[k],
-            line_got.at[slot],
-            {"blk": place[k]},
-        )
+            line_got.at[way, j],
+            {"blk": b + (1 if way else -1)},
+        )
+
+    def add_from(way, j):
+        settled(line_slot.at[way, j], line_got.at[way, j], True)
+        running[...] += line_slot[way, j].astype(jnp.float32)
 
     for half in range(2):
         if compute:
@@ -710,26 +714,47 @@
         compute(seq)
     yield
     for k in range(count):
+        j = place[k]
         to_core(1, k).wait_recv()
         to_side(k).wait_recv()
-        total = partial[seq * count + place[k]].astype(jnp.float32)
+        total = partial[seq * count + j].astype(jnp.float32)
         total += core_slot[1, k].astype(jnp.float32)
-        total += side_slot[k].astype(jnp.float32)
+        running[...] = total + side_slot[k].astype(jnp.float32)
+        rightward, leftward = j >= b, j <= b
+        pl.when(rightward & (b > 0))(functools.partial(add_from, 1, j))
+        pl.when(leftward & (b < count - 1))(functools.partial(add_from, 0, j))
         if k < count - 1:
-            line_out[k] = total.astype(jnp.bfloat16)
-            along_line(k).start()
+            line_out[k] = running[...].astype(jnp.bfloat16)
+
+            @pl.when(rightward)
+            def _():
+                along_line(k, 1).start()
+
+            @pl.when(jnp.logical_not(rightward))
+            def _():
+                along_line(k, 0).start()
+
             yield
+    deliver(running[...])
     yield
-    for k in range(count - 1):
-        along_line(k).wait_recv()
-        total += line_slot[away[k] - 1].astype(jnp.float32)
-    deliver(total)
     for k in range(count):
         to_core(0, k).wait_send()
         to_core(1, k).wait_send()
         to_side(k).wait_send()
         if k < count - 1:
-            along_line(k).wait_send()
+            settled(line_out.at[k], line_sent.at[k], False)
+
+
+def far_first(b, count):
+    order = sorted(range(count), key=lambda j: -j)
+    places = []
+    for k in range(count):
+        place = 0
+        for own in range(count):
+            by_distance = sorted(order, key=lambda j: (-abs(j - own), -j if own * 2 < count else j))
+            place = jnp.where(b == own, by_distance[k], place)
+        places.append(place)
+    return places
 
 
 def scatter_scratch(count, rows, width):
@@ -741,15 +766,16 @@
     return [
         slots(2, count),
         slots(count),
-        slots(count - 1),
+        slots(2, count),
         slots(count),
         slots(count - 1),
+        pltpu.VMEM((rows, width), jnp.float32),
         dma((2, count)),
         dma((2, count)),
         dma((count,)),
         dma((count,)),
         dma((count - 1,)),
-        dma((count - 1,)),
+        dma((2, count)),
     ]
 
 
@@ -769,6 +795,24 @@
         + ({"seq": seq ^ 1}, {"seq": seq ^ 2})
         + tuple({"blk": lax.rem(b + k, count)} for k in range(1, count))
     )
+
+
+def carry(copies, from_section, what):
+    sending = lax.axis_index("section") == from_section
+    for copy in copies:
+        if what == "start":
+            pl.when(sending)(copy.start)
+        else:
+            pl.when(sending)(copy.wait_send)
+            pl.when(jnp.logical_not(sending))(copy.wait_recv)
+
+
+def carried(sources, targets, sent, got):
+    other = {"section": 1 - lax.axis_index("section")}
+    return [
+        remote(source, target, sent.at[n], got.at[n], other)
+        for n, (source, target) in enumerate(zip(sources, targets))
+    ]
 
 
 def group_rows(ref, group, count):
@@ -833,90 +877,7 @@
     out_vm[HEAD_DIM:PAD] = empty
 
 
-def attn_kernel(count, spreading, *refs):
-    refs = iter(refs)
-
-    def take(n):
-        return [next(refs) for _ in range(n)]
-
-    if spreading:
-        pieces, w_gate, w_up, w_output, rows_in, grads_in, cosine, sine, start = take(9)
-        attn, gate_up, out, grads_all = take(4)
-    else:
-        rows_in, x_own, attn, out, cosine, sine, start = take(7)
-    hidden_out, normed_out, all_rows, heads, log_total = take(5)
-    rows_vm, attn_vm, out_vm, partial, load_done, save_done = take(6)
-    if spreading:
-        normed_vm, grads_vm = take(2)
-        spread_sems = take(5)
-        grads_sems = take(7)
-    else:
-        normed_vm = rows_vm
-    gather_sems = take(7)
-    scatter_refs = list(refs)
-    seq, section = lax.axis_index("seq"), lax.axis_index("section")
-    block = rows_vm.shape[1]
-    tokens = block * rows_vm.shape[0]
-    size = count * block
-    if spreading:
-        greet_group(count, ({"section": 1 - section},))
-        spread = spread_steps(
-            count, pieces, w_gate, w_up, w_output, attn, gate_up, out, *spread_sems
-        )
-        next(spread)
-    else:
-        greet_group(count)
-    steps = gather_steps(count, rows_in, rows_vm, *gather_sems)
-    next(steps)
-    clear_pads(attn_vm, out_vm)
-    if spreading:
-        loads = load_weights(attn.at[0], out.at[0], attn_vm, out_vm, load_done)
-    else:
-        loads = load_weights(attn.at[1], out.at[1], attn_vm, out_vm, load_done)
-        for copy in loads:
-            copy.start()
-
-    def project(group):
-        if spreading:
-            gain = attn_vm[3 * PAD : 3 * PAD + 16][0:1].astype(jnp.float32)
-            raw = rows_vm[pl.ds(group * count, count)].astype(jnp.float32)
-            normed = normalise(raw, gain[None]).astype(jnp.bfloat16)
-            normed_vm[pl.ds(group * count, count)] = normed
-            normed = normed.reshape(size, normed.shape[2])
-        else:
-            normed = group_rows(rows_vm, group, count)
-        mixed = back_product(normed, attn_vm[0 : 3 * PAD])
-        span = group_span(group, count, block)
-        cos_rows, sin_rows = cosine[span], sine[span]
-        heads[0, span] = lane_turn(mixed[:, :PAD], cos_rows, sin_rows).astype(jnp.bfloat16)
-        heads[1, span] = lane_turn(mixed[:, PAD : 2 * PAD], cos_rows, sin_rows).astype(
-            jnp.bfloat16
-        )
-        heads[2, span] = mixed[:, 2 * PAD :].astype(jnp.bfloat16)
-
-    for number, event in enumerate(steps):
-        group = group_of(event)
-        if spreading:
-            if number == 1:
-                next(spread)
-            continue
-        if event == "line":
-            for copy in loads:
-                copy.wait()
-        if group is not None:
-            project(group)
-    if spreading:
-        next(spread)
-        for copy in loads:
-            copy.start()
-        grad_steps = gather_steps(count, grads_in, grads_vm, *grads_sems)
-        next(grad_steps)
-        for copy in loads:
-            copy.wait()
-        for group in range(tokens // size):
-            project(group)
-    save = pltpu.make_async_copy(normed_vm, all_rows, save_done.at[0])
-    save.start()
+def attention_rows(heads, log_total, start, size, tokens):
     for i in range(tokens // size):
         here, seen = slice(i * size, (i + 1) * size), slice(0, (i + 1) * size)
         scores = masked_scores(heads[0, here], heads[1, seen], i * size, start[here])
@@ -927,31 +888,167 @@
         weights = (weights * (1.0 / total)).astype(jnp.bfloat16)
         heads[3, here] = product(weights, heads[2, seen]).astype(jnp.bfloat16)
 
+
+def project_heads(normed, attn_vm, heads, span, cosine, sine):
+    mixed = back_product(normed, attn_vm[0 : 3 * PAD])
+    cos_rows, sin_rows = cosine[span], sine[span]
+    heads[0, span] = lane_turn(mixed[:, :PAD], cos_rows, sin_rows).astype(jnp.bfloat16)
+    heads[1, span] = lane_turn(mixed[:, PAD : 2 * PAD], cos_rows, sin_rows).astype(jnp.bfloat16)
+    heads[2, span] = mixed[:, 2 * PAD :].astype(jnp.bfloat16)
+
+
+def keep_group(partial, group, value, count):
+    block = partial.shape[1]
+    partial[pl.ds(group * count, count)] = value.astype(jnp.bfloat16).reshape(count, block, -1)
+
+
+def gain_of(ref, row):
+    return ref[3 * PAD : 3 * PAD + 16][row : row + 1].astype(jnp.float32)
+
+
+def attn_kernel(count, *refs):
+    refs = iter(refs)
+
+    def take(n):
+        return [next(refs) for _ in range(n)]
+
+    rows_in, x_own, attn, out, cosine, sine, start = take(7)
+    hidden_out, normed_out, all_rows, heads, log_total = take(5)
+    rows_vm, attn_vm, out_vm, partial, load_done, save_done = take(6)
+    gather_sems = take(7)
+    scatter_refs = list(refs)
+    block = rows_vm.shape[1]
+    tokens = block * rows_vm.shape[0]
+    size = count * block
+    greet_group(count)
+    steps = gather_steps(count, rows_in, rows_vm, *gather_sems)
+    next(steps)
+    clear_pads(attn_vm, out_vm)
+    loads = load_weights(attn.at[1], out.at[1], attn_vm, out_vm, load_done)
+    start_all(loads)
+    for event in steps:
+        if event == "line":
+            wait_all(loads)
+        group = group_of(event)
+        if group is not None:
+            span = group_span(group, count, block)
+            normed = group_rows(rows_vm, group, count)
+            project_heads(normed, attn_vm, heads, span, cosine, sine)
+    save = pltpu.make_async_copy(rows_vm, all_rows, save_done.at[0])
+    save.start()
+    attention_rows(heads, log_total, start, size, tokens)
+
     def project_out(group):
         mixed = heads[3, group_span(group, count, block)]
-        value = product(mixed, out_vm[...]).astype(jnp.bfloat16)
-        partial[pl.ds(group * count, count)] = value.reshape(count, block, -1)
+        keep_group(partial, group, product(mixed, out_vm[...]), count)
 
     def deliver(total):
-        own = rows_in[...].astype(jnp.float32) if spreading else x_own[...]
-        hidden = own + total
-        gain = attn_vm[3 * PAD : 3 * PAD + 16][1:2].astype(jnp.float32)
+        hidden = x_own[...].astype(jnp.float32) + total
         hidden_out[...] = hidden
-        normed_out[...] = normalise(hidden, gain).astype(jnp.bfloat16)
-
-    between = []
-    if spreading:
-        between = [functools.partial(advance, grad_steps, n) for n in (2, 1, 1, 2)]
-    run_with(scatter_steps(count, partial, deliver, *scatter_refs, compute=project_out), between)
-    if spreading:
-        for _ in spread:
-            pass
-        for _ in grad_steps:
-            pass
-        keep = pltpu.make_async_copy(grads_vm, grads_all, save_done.at[1])
-        keep.start()
-        keep.wait()
+        normed_out[...] = normalise(hidden, gain_of(attn_vm, 1)).astype(jnp.bfloat16)
+
+    run_with(scatter_steps(count, partial, deliver, *scatter_refs, compute=project_out), [])
     save.wait()
+
+
+def first_layer_kernel(count, *refs):
+    refs = iter(refs)
+
+    def take(n):
+        return [next(refs) for _ in range(n)]
+
+    pieces, w_gate, w_up, w_output, w_down, rows_in, grads_in, cosine, sine, start = take(10)
+    attn, gate_up, out, down, grads_all, all_rows, wide_rows = take(7)
+    hidden, result_out, normed_out, heads, log_total = take(5)
+    raw_vm, normed_vm, rows_vm, grads_vm, partial, partial_two = take(6)
+    attn_vm, out_vm, wide_vm, down_vm, units, normed_own, gain_vm = take(7)
+    load_done, save_done = take(2)
+    spread_sems = take(5)
+    first_sems, second_sems, grads_sems = take(7), take(7), take(7)
+    scatter_one, scatter_two = take(12), take(12)
+    section = lax.axis_index("section")
+    block, width = raw_vm.shape[1], raw_vm.shape[2]
+    tokens = block * raw_vm.shape[0]
+    size = count * block
+    low, f32 = jnp.bfloat16, jnp.float32
+    greet_group(count, ({"section": 1 - section},))
+    steps = gather_steps(count, rows_in, raw_vm, *first_sems)
+    next(steps)
+    spread = spread_steps(
+        count, pieces, w_gate, w_up, w_output, w_down, attn, gate_up, out, down, *spread_sems
+    )
+    next(spread)
+    clear_pads(attn_vm, out_vm)
+    for event in steps:
+        if event == "line":
+            next(spread)
+    grad_steps = gather_steps(count, grads_in, grads_vm, *grads_sems)
+    next(grad_steps)
+    next(spread)
+    next(spread)
+    loads = load_weights(attn.at[0], out.at[0], attn_vm, out_vm, load_done)
+    loads.append(
+        pltpu.make_async_copy(attn.at[1, pl.ds(3 * HEAD_DIM, 16)], gain_vm, load_done.at[5])
+    )
+    start_all(loads)
+    wait_all(loads)
+    for group in range(tokens // size):
+        raw = raw_vm[group * count : (group + 1) * count].astype(f32)
+        normed = normalise(raw, gain_of(attn_vm, 0)[None]).astype(low)
+        normed_vm[group * count : (group + 1) * count] = normed
+        span = slice(group * size, (group + 1) * size)
+        project_heads(normed.reshape(size, width), attn_vm, heads, span, cosine, sine)
+    saves = [pltpu.make_async_copy(normed_vm, all_rows, save_done.at[0])]
+    saves[0].start()
+    attention_rows(heads, log_total, start, size, tokens)
+
+    def project_out(group):
+        mixed = heads[3, group_span(group, count, block)]
+        keep_group(partial, group, product(mixed, out_vm[...]), count)
+
+    def deliver(total):
+        value = rows_in[...].astype(f32) + total
+        hidden[...] = value
+        normed_own[...] = normalise(value, gain_of(attn_vm, 1)).astype(low)
+
+    def more():
+        next(spread)
+        next(grad_steps, None)
+
+    next(grad_steps)
+    run_with(scatter_steps(count, partial, deliver, *scatter_one, compute=project_out), [more] * 5)
+    for number, event in enumerate(gather_steps(count, normed_own, rows_vm, *second_sems)):
+        if number == 0:
+            more()
+    for _ in spread:
+        pass
+    loads = [
+        pltpu.make_async_copy(gate_up.at[0], wide_vm, load_done.at[0]),
+        pltpu.make_async_copy(down.at[0], down_vm, load_done.at[1]),
+    ]
+    start_all(loads)
+    wait_all(loads)
+    saves.append(pltpu.make_async_copy(rows_vm, wide_rows, save_done.at[1]))
+    saves[1].start()
+
+    def project_down(group):
+        pre = product(group_rows(rows_vm, group, count), wide_vm[...])
+        made = hidden_units(pre)
+        units[group_span(group, count, block)] = made
+        keep_group(partial_two, group, product(made, down_vm[...]), count)
+
+    def deliver_two(total):
+        made = (hidden[...] + total).astype(low)
+        result_out[...] = made
+        gain = gain_vm[...][0:1].astype(f32)
+        normed_out[...] = normalise(made.astype(f32), gain).astype(low)
+
+    run_with(scatter_steps(count, partial_two, deliver_two, *scatter_two, compute=project_down), [])
+    for _ in grad_steps:
+        pass
+    saves.append(pltpu.make_async_copy(grads_vm, grads_all, save_done.at[2]))
+    saves[2].start()
+    wait_all(saves)
 
 
 def spread_steps(
@@ -960,9 +1057,11 @@
     w_gate,
     w_up,
     w_output,
+    w_down,
     attn,
     gate_up,
     out,
+    down,
     line_sent,
     line_got,
     cross_sent,
@@ -973,8 +1072,7 @@
     seq_count = lax.axis_size("seq")
     other = {"section": 1 - section}
     rows, lanes = w_gate.shape[0], gate_up.shape[2] // 2
-    out_rows = out.shape[1]
-    far_first = tuple(range(count // 2, 0, -1)) + tuple(range(count // 2 + 1, count))
+    turns = tuple(range(count // 2, 0, -1)) + tuple(range(count // 2 + 1, count))
 
     def source(kind, j):
         if kind == 0:
@@ -1009,12 +1107,14 @@
             other,
         )
 
-    def own_rows():
-        begin = w_output.at[pl.ds(pl.multiple_of(seq * out_rows, out_rows), out_rows)]
-        spot = out.at[section]
+    def own_rows(kind):
+        weight, place = (w_output, out) if kind == 3 else (w_down, down)
+        size = place.shape[1]
+        begin = weight.at[pl.ds(pl.multiple_of(seq * size, size), size)]
+        spot = place.at[section]
         return (
-            remote(begin, spot, cross_sent.at[3, 0], cross_got.at[3, 0], other),
-            pltpu.make_async_copy(begin, spot, local_done.at[3]),
+            remote(begin, spot, cross_sent.at[kind, 0], cross_got.at[kind, 0], other),
+            pltpu.make_async_copy(begin, spot, local_done.at[kind]),
         )
 
     def own_piece(kind):
@@ -1023,42 +1123,42 @@
             pltpu.make_async_copy(source(kind, b), target(kind, b), local_done.at[kind]),
         )
 
-    def begin(copies):
-        for copy in copies:
-            copy.start()
-
-    def forward(kind):
-        for k in far_first:
-            j = lax.rem(b + count - k, count)
-            settled(target(kind, j), line_got.at[kind, k], True)
-            across(kind, j, k).start()
+    def forward(kind, k):
+        j = lax.rem(b + count - k, count)
+        settled(target(kind, j), line_got.at[kind, k], True)
+        across(kind, j, k).start()
 
     def arrived(kind):
+        if kind > 2:
+            wait_all(own_rows(kind))
+            return
         for k in range(count):
             settled(target(kind, 0), cross_got.at[kind, k], True)
             settled(target(kind, 0), cross_sent.at[kind, k], False)
             if k:
                 settled(target(kind, 0), line_sent.at[kind, k], False)
-        own_piece(kind)[1].wait()
-
-    for k in far_first:
+        pltpu.make_async_copy(source(kind, b), target(kind, b), local_done.at[kind]).wait()
+
+    for k in turns:
         along_line(0, k).start()
-    begin(own_piece(0) + own_rows())
+    start_all(own_piece(0) + own_rows(3))
     yield
-    forward(0)
+    for k in turns:
+        forward(0, k)
+    yield
     for kind in (1, 2):
-        for k in far_first:
+        for k in turns:
             along_line(kind, k).start()
     yield
     arrived(0)
-    passed, local = own_rows()
-    passed.wait()
-    local.wait()
-    for kind in (1, 2):
-        begin(own_piece(kind))
-        forward(kind)
+    arrived(3)
+    start_all(own_piece(1) + own_piece(2) + own_rows(4))
     yield
     for kind in (1, 2):
+        for k in turns:
+            forward(kind, k)
+            yield
+    for kind in (1, 2, 4):
         arrived(kind)
 
 
@@ -1091,63 +1191,6 @@
         jnp.bfloat16
     )
     place[span, half : 2 * half] = (grad_act * (gate * sigma)).astype(jnp.bfloat16)
-
-
-def mlp_kernel(count, *refs):
-    refs = iter(refs)
-
-    def take(n):
-        return [next(refs) for _ in range(n)]
-
-    rows_in, hidden, gate_up, w_down, gain_next = take(5)
-    down, result_out, normed_out, all_rows = take(4)
-    rows_vm, wide_vm, down_vm, units, partial, load_done, cross_sent, cross_got = take(8)
-    gather_sems = take(7)
-    scatter_refs = list(refs)
-    seq, section = lax.axis_index("seq"), lax.axis_index("section")
-    block = rows_vm.shape[1]
-    other = {"section": 1 - section}
-    greet_group(count, (other,))
-    load = pltpu.make_async_copy(gate_up.at[0], wide_vm, load_done.at[0])
-    load.start()
-    steps = gather_steps(count, rows_in, rows_vm, *gather_sems)
-    next(steps)
-    size = down.shape[1]
-    begin = w_down.at[pl.ds(pl.multiple_of(seq * size, size), size)]
-    across = remote(begin, down.at[section], cross_sent, cross_got, other)
-    local = pltpu.make_async_copy(begin, down.at[section], load_done.at[1])
-    across.start()
-    local.start()
-
-    def units_of(group):
-        pre = product(group_rows(rows_vm, group, count), wide_vm[...])
-        units[group_span(group, count, block)] = hidden_units(pre)
-
-    for event in steps:
-        if event == "line":
-            load.wait()
-        group = group_of(event)
-        if group is not None:
-            units_of(group)
-    save = pltpu.make_async_copy(rows_vm, all_rows, load_done.at[2])
-    save.start()
-    across.wait()
-    local.wait()
-    load = pltpu.make_async_copy(down.at[0], down_vm, load_done.at[3])
-    load.start()
-    load.wait()
-
-    def project_down(group):
-        value = product(units[group_span(group, count, block)], down_vm[...])
-        partial[pl.ds(group * count, count)] = value.astype(jnp.bfloat16).reshape(count, block, -1)
-
-    def deliver(total):
-        low = (hidden[...] + total).astype(jnp.bfloat16)
-        result_out[...] = low
-        normed_out[...] = normalise(low.astype(jnp.float32), gain_next[...]).astype(jnp.bfloat16)
-
-    run_with(scatter_steps(count, partial, deliver, *scatter_refs, compute=project_down), [])
-    save.wait()
 
 
 def wide_grads(rows_vm, pre_grads, units, grads_vm, wide_grad, down_grad):
@@ -1191,7 +1234,7 @@
     rows_vm, grads_vm, wide_vm, down_vm, units, pre_grads, partial, partial_back = take(8)
     (load_done,) = take(1)
     gather_sems = take(7)
-    scatter_refs, scatter_back = take(11), take(11)
+    scatter_refs, scatter_back = take(12), take(12)
     block = rows_vm.shape[1]
     greet_group(count)
     steps = gather_steps(count, rows_in, rows_vm, *gather_sems)
@@ -1248,14 +1291,19 @@
         return [next(refs) for _ in range(n)]
 
     grads_own, hidden, all_rows, gate_up, down, gain = take(6)
+    carry_from = take(2)
     branch_out, grad_hidden_out, gain_out, wide_grad, down_grad = take(5)
+    carry_to = take(2)
     rows_vm, grads_vm, wide_vm, down_vm, units, pre_vm, pre_grads, partial, load_done = take(9)
+    carry_sent, carry_got = take(2)
     gather_sems = take(7)
     scatter_refs = list(refs)
     block = rows_vm.shape[1]
-    greet_group(count)
+    greet_group(count, ({"section": 1 - lax.axis_index("section")},))
     steps = gather_steps(count, grads_own, grads_vm, *gather_sems)
     next(steps)
+    copies = carried(carry_from, carry_to, carry_sent, carry_got)
+    carry(copies, 0, "start")
     loads = [
         pltpu.make_async_copy(gate_up.at[0], wide_vm, load_done.at[0]),
         pltpu.make_async_copy(all_rows, rows_vm, load_done.at[1]),
@@ -1292,6 +1340,7 @@
         scatter_steps(count, partial, deliver, *scatter_refs),
         wide_grads(rows_vm, pre_grads, units, grads_vm, wide_grad, down_grad),
     )
+    carry(copies, 0, "wait")
 
 
 def attn_back_kernel(count, layer, *refs):
@@ -1302,9 +1351,11 @@
 
     branch_in, grad_hidden, x_own, all_rows, heads_kept, log_total, attn, out = take(8)
     cosine, sine, start, gain = take(4)
+    carry_from = take(2)
     grad_out, gain_out, attn_grad, out_grad = take(4)
+    carry_to = take(2)
     branch_vm, rows_vm, heads, attn_vm, out_vm, mixed_grads, probs = take(7)
-    key_grads, value_grads, joint, partial, load_done = take(5)
+    key_grads, value_grads, joint, partial, load_done, carry_sent, carry_got = take(7)
     gather_sems = take(7)
     scatter_refs = list(refs)
     block = rows_vm.shape[1]
@@ -1312,9 +1363,11 @@
     tokens = block * rows_vm.shape[0]
     low, f32 = jnp.bfloat16, jnp.float32
     scale = HEAD_DIM ** (-0.5)
-    greet_group(count)
+    greet_group(count, ({"section": 1 - lax.axis_index("section")},))
     steps = gather_steps(count, branch_in, branch_vm, *gather_sems)
     next(steps)
+    copies = carried(carry_from, carry_to, carry_sent, carry_got)
+    carry(copies, 1 - layer, "start")
     clear_pads(attn_vm, out_vm)
     loads = load_weights(attn.at[layer], out.at[layer], attn_vm, out_vm, load_done)
     loads.append(pltpu.make_async_copy(heads_kept, heads, load_done.at[5]))
@@ -1382,57 +1435,31 @@
         scatter_steps(count, partial, deliver, *scatter_refs, compute=project_back),
         [functools.partial(attn_part, part) for part in range(3)] + [out_part],
     )
-
-
-def finish_kernel(
-    count,
-    attn_one,
-    attn_two,
-    out_one,
-    out_two,
-    wide_one,
-    wide_two,
-    down_one,
-    down_two,
-    gains,
-    swap_rows,
-    attn,
-    out,
-    gate,
-    up,
-    down,
-    gains_out,
-    swapped_rows,
-    attn_in,
-    out_in,
-    wide_in,
-    down_in,
-    attn_slot,
-    wide_slot,
-    gain_in,
-    gain_sum,
-    gain_line,
-    gain_part,
-    gain_side,
-    gain_core,
-    cross_sent,
-    cross_got,
-    line_sent,
-    line_got,
-    side_sent,
-    side_got,
-    core_sent,
-    core_got,
-    local_done,
-    small_sent,
-    small_got,
-):
+    carry(copies, 1 - layer, "wait")
+
+
+def finish_kernel(count, *refs):
+    refs = iter(refs)
+
+    def take(n):
+        return [next(refs) for _ in range(n)]
+
+    ones, twos = take(4), take(4)
+    wide_from_two, down_from_two, wide_from_one, down_from_one = take(4)
+    attn_from_one, out_from_one, gains, swap_rows = take(4)
+    attn, out, gate, up, down, gains_out, swapped_rows = take(7)
+    attn_own, out_own, wide_own, down_own, attn_in, out_in, wide_in, down_in = take(8)
+    attn_slot, wide_slot = take(2)
+    gain_in, gain_sum, gain_line, gain_part, gain_side, gain_core = take(6)
+    load_done, cross_sent, cross_got, line_sent, line_got = take(5)
+    side_sent, side_got, core_sent, core_got, local_done, small_sent, small_got = take(7)
     seq, b, section = lax.axis_index("seq"), lax.axis_index("blk"), lax.axis_index("section")
     at_first = section == 0
+    at_second = jnp.logical_not(at_first)
     core, side, other = {"seq": seq ^ 1}, {"seq": seq ^ 2}, {"section": 1 - section}
     greet((other, core, side) + tuple({"blk": lax.rem(b + k, count)} for k in range(1, count)))
     rows, lanes = attn.shape[2], gate.shape[1] // (4 * count)
-    far_first = tuple(range(count // 2, 0, -1)) + tuple(range(count // 2 + 1, count)) + (0,)
+    turns = tuple(range(count // 2, 0, -1)) + tuple(range(count // 2 + 1, count)) + (0,)
     f32, low = jnp.float32, jnp.bfloat16
 
     def piece_rows(kind, j):
@@ -1441,39 +1468,57 @@
         return (pl.ds(pl.multiple_of(j * rows, rows), rows),)
 
     pairs = {
-        0: (attn_one, attn_two, attn_in),
-        1: (wide_one, wide_two, wide_in),
-        2: (out_one, out_two, out_in),
-        3: (down_one, down_two, down_in),
+        0: (attn_own, attn_in, ones[0]),
+        1: (wide_own, wide_in, None),
+        2: (out_own, out_in, ones[1]),
+        3: (down_own, down_in, None),
     }
-
-    def cross(kind, k, begin):
-        one, two, held = pairs[kind]
+    sources = {
+        0: (ones[0], twos[0], None, attn_from_one),
+        1: (ones[2], twos[2], wide_from_two, wide_from_one),
+        2: (ones[1], twos[1], None, out_from_one),
+        3: (ones[3], twos[3], down_from_two, down_from_one),
+    }
+
+    def load(kind):
+        one, two, from_two, from_one = sources[kind]
+        own, held, _ = pairs[kind]
+
+        def copies(begins):
+            for n, (begin, end) in enumerate(zip(begins, (own, held))):
+                if begin is not None:
+                    pltpu.make_async_copy(begin, end, load_done.at[kind, n]).start()
+
+        pl.when(at_first)(functools.partial(copies, (one, from_two)))
+        pl.when(at_second)(functools.partial(copies, (two, from_one)))
+
+    def loaded(kind):
+        own, held, crossing = pairs[kind]
+        pltpu.make_async_copy(own, own, load_done.at[kind, 0]).wait()
+        copy = pltpu.make_async_copy(held, held, load_done.at[kind, 1])
+        if crossing is None:
+            copy.wait()
+        else:
+            pl.when(at_second)(copy.wait)
+
+    def cross(kind, k):
+        _, held, begin = pairs[kind]
         index = piece_rows(kind, lax.rem(b + k, count)) if kind < 2 else (slice(None),)
-        spots = [ref.at[index] for ref in (one, two, held)]
-        sems = (cross_sent.at[kind, k], cross_got.at[kind, k])
-        if not begin:
-            return remote(spots[0], spots[2], *sems, other)
-
-        @pl.when(at_first)
-        def _():
-            remote(spots[1], spots[2], *sems, other).start()
-
-        @pl.when(jnp.logical_not(at_first))
-        def _():
-            remote(spots[0], spots[2], *sems, other).start()
+        return remote(
+            begin.at[index], held.at[index], cross_sent.at[kind, k], cross_got.at[kind, k], other
+        )
 
     def add_up(kind, k):
-        one, two, held = pairs[kind]
+        own, held, crossing = pairs[kind]
+        if crossing is not None:
+            pl.when(at_first)(cross(kind, k).wait_recv)
         index = piece_rows(kind, lax.rem(b + k, count)) if kind < 2 else (slice(None),)
-        cross(kind, k, False).wait_recv()
-        own = jnp.where(at_first, one[index], two[index]).astype(f32)
-        held[index] = (own + held[index].astype(f32)).astype(low)
+        held[index] = (own[index].astype(f32) + held[index].astype(f32)).astype(low)
 
     def along_line(kind, k):
         j = lax.rem(b + k, count)
         slot = (attn_slot if kind == 0 else wide_slot).at[k]
-        source = pairs[kind][2].at[piece_rows(kind, j)]
+        source = pairs[kind][1].at[piece_rows(kind, j)]
         return remote(source, slot, line_sent.at[kind, k], line_got.at[kind, k], {"blk": j})
 
     def places(kind, k, of_seq):
@@ -1495,7 +1540,7 @@
 
     def made(kind, k):
         if kind > 1:
-            return [pairs[kind][2].at[:]]
+            return [pairs[kind][1].at[:]]
         if kind == 0:
             return [attn_in.at[piece_rows(0, b)] if k == 0 else attn_slot.at[k]]
         whole = (lambda cut: wide_in.at[piece_rows(1, b) + (cut,)]) if k == 0 else (
@@ -1543,14 +1588,11 @@
     swap.start()
     gain_cross = small(1, gains.at[1 - section], gain_in.at[:], other)
     gain_cross.start()
-    cross(2, 0, True)
-    for kind, k in ((1, far_first[0]), (1, 0)):
-        cross(kind, k, True)
-    cross(3, 0, True)
-    for kind in (1, 0):
-        for k in far_first:
-            if (kind, k) not in ((1, far_first[0]), (1, 0)):
-                cross(kind, k, True)
+    for kind in (1, 3, 2, 0):
+        load(kind)
+    crossings = [(2, 0)] + [(0, k) for k in turns]
+    for kind, k in crossings:
+        pl.when(at_second)(cross(kind, k).start)
 
     def gain_piece(j):
         return gain_sum.at[:, pl.ds(pl.multiple_of(j * rows, rows), rows)]
@@ -1564,13 +1606,15 @@
     for k in range(1, count):
         gain_send(k).start()
 
-    add_up(2, 0)
-    publish(2, 0)
-    add_up(1, far_first[0])
-    along_line(1, far_first[0]).start()
+    loaded(1)
+    for k in turns[:-1]:
+        add_up(1, k)
+        along_line(1, k).start()
+    loaded(3)
+    add_up(3, 0)
+    publish(3, 0)
     add_up(1, 0)
     publish(1, 0)
-    from_side(2, 0)
     for k in range(1, count):
         gain_send(k).wait_recv()
     gain_part[...] = gain_sum[:, pl.ds(pl.multiple_of(b * rows, rows), rows)]
@@ -1578,42 +1622,43 @@
         gain_part[...] += gain_line[k]
     gain_to_side = small(2, gain_part.at[:], gain_side.at[:], side)
     gain_to_side.start()
-    add_up(3, 0)
-    publish(3, 0)
-    for k in far_first[1:-1]:
-        add_up(1, k)
-        along_line(1, k).start()
-    from_side(1, 0)
+    loaded(2)
+    add_up(2, 0)
+    publish(2, 0)
+    from_side(3, 0)
+    from_line(1, turns[0])
     gain_to_side.wait_recv()
     gain_side[...] += gain_part[...]
     gain_to_core = small(3, gain_side.at[:], gain_core.at[:], core)
     gain_to_core.start()
-    from_line(1, far_first[0])
-    from_side(3, 0)
-    add_up(0, far_first[0])
-    along_line(0, far_first[0]).start()
-    from_line(1, far_first[1])
-    add_up(0, far_first[1])
-    along_line(0, far_first[1]).start()
-    from_side(1, far_first[0])
-    from_line(1, far_first[2])
-    add_up(0, far_first[2])
-    along_line(0, far_first[2]).start()
+    loaded(0)
+    add_up(0, turns[0])
+    along_line(0, turns[0]).start()
+    from_side(1, 0)
+    from_line(1, turns[1])
+    add_up(0, turns[1])
+    along_line(0, turns[1]).start()
+    from_side(2, 0)
+    from_line(1, turns[2])
+    add_up(0, turns[2])
+    along_line(0, turns[2]).start()
     add_up(0, 0)
     publish(0, 0)
-    from_side(1, far_first[1])
+    from_side(1, turns[0])
     gain_to_core.wait_recv()
     gains_out[...] = gain_side[...] + gain_core[...]
-    from_line(0, far_first[0])
-    from_side(1, far_first[2])
-    from_line(0, far_first[1])
-    from_line(0, far_first[2])
+    from_line(0, turns[0])
+    from_side(1, turns[1])
+    from_line(0, turns[1])
+    from_line(0, turns[2])
+    from_side(1, turns[2])
     from_side(0, 0)
-    for k in far_first[:-1]:
+    for k in turns[:-1]:
         from_side(0, k)
     every = [(0, k) for k in range(count)] + [(1, k) for k in range(count)] + [(2, 0), (3, 0)]
     for kind, k in every:
-        cross(kind, k, False).wait_send()
+        if (kind, k) in crossings:
+            pl.when(at_second)(cross(kind, k).wait_send)
         if kind < 2 and k:
             along_line(kind, k).wait_send()
         for to_side, to_core, local in sends(kind, k):
@@ -1633,7 +1678,7 @@
     gain_to_core.wait_send()
 
 
-def finish_grads(first, second, gains, swap_rows):
+def finish_grads(first, second, from_two, from_one, gains, swap_rows):
     seq_count, count = lax.axis_size("seq"), lax.axis_size("blk")
     low, f32 = jnp.bfloat16, jnp.float32
     attn, out, wide, down = first
@@ -1644,7 +1689,7 @@
     vmem = pltpu.VMEM
     sends = 3 * count + 2
     heads = attn.shape[0]
-    operands = [array for pair in zip(first, second) for array in pair] + [gains, swap_rows]
+    operands = list(first) + list(second) + list(from_two) + list(from_one) + [gains, swap_rows]
     in_vmem = pl.BlockSpec(memory_space=vmem)
     anywhere = pl.BlockSpec(memory_space=pl.ANY)
     small = (gains.shape[1], rows)
@@ -1659,9 +1704,13 @@
             jax.ShapeDtypeStruct(small, f32),
             jax.ShapeDtypeStruct(swap_rows.shape, low),
         ],
-        in_specs=[in_vmem] * len(operands),
+        in_specs=[anywhere] * (len(operands) - 2) + [in_vmem] * 2,
         out_specs=[anywhere] * 5 + [in_vmem, in_vmem],
         scratch_shapes=[
+            vmem(attn.shape, low),
+            vmem(out.shape, low),
+            vmem(wide.shape, low),
+            vmem(down.shape, low),
             vmem(attn.shape, low),
             vmem(out.shape, low),
             vmem(wide.shape, low),
@@ -1674,6 +1723,7 @@
             vmem(small, f32),
             vmem(small, f32),
             vmem(small, f32),
+            dma((4, 2)),
             dma((4, count)),
             dma((4, count)),
             dma((2, count)),
@@ -1809,49 +1859,55 @@
     weights_vm = [vmem((3 * PAD + 16, width), low), vmem((PAD, width), low)]
     wide_vm, down_vm = vmem((width, 2 * lanes), low), vmem((down_rows, width), low)
     tables = [(cosine, True), (sine, True), (start, True)]
-    attn, gate_up, out, grads_all, hidden_one, normed, rows_one, heads_one, total_one = call_kernel(
-        functools.partial(attn_kernel, count, True),
-        "first_attention",
+    (
+        attn,
+        gate_up,
+        out,
+        down,
+        grads_all,
+        rows_one,
+        wide_rows_one,
+        hidden_one,
+        between,
+        normed,
+        heads_one,
+        total_one,
+    ) = call_kernel(
+        functools.partial(first_layer_kernel, count),
+        "first_layer",
         2,
-        [(array, False) for array in (pieces, w_gate, w_up, w_output)]
+        [(array, False) for array in (pieces, w_gate, w_up, w_output, w_down)]
         + [(rows_own, True), (grads_own, True)]
         + tables,
         [
             ((2, pieces.shape[1], width), low, False),
             ((2, width, 2 * lanes), low, False),
             ((2, out_rows, width), low, False),
+            ((2, down_rows, width), low, False),
             every,
-        ]
-        + attn_outputs,
-        [all_blocks()]
+            every,
+            every,
+            own_wide,
+            own_low,
+            own_low,
+            ((4, tokens, PAD), low, True),
+            ((tokens, 1), f32, True),
+        ],
+        [all_blocks() for _ in range(6)]
         + weights_vm
-        + [all_blocks(), dma((5,)), dma((2,)), all_blocks(), all_blocks()]
-        + [dma((3, count)), dma((3, count)), dma((4, count)), dma((4, count)), dma((4,))]
-        + gather_semaphores(count) * 2
+        + [wide_vm, down_vm, vmem((tokens, lanes), low), vmem((block, width), low)]
+        + [vmem((16, width), low), dma((6,)), dma((3,))]
+        + [dma((3, count)), dma((3, count)), dma((5, count)), dma((5, count)), dma((5,))]
+        + gather_semaphores(count) * 3
+        + scatter()
         + scatter(),
     )
     gains = attn[:, 3 * HEAD_DIM : 3 * HEAD_DIM + 2].astype(f32)
-    down, between, normed, wide_rows_one = call_kernel(
-        functools.partial(mlp_kernel, count),
-        "first_feed_forward",
-        5,
-        [
-            (normed, True),
-            (hidden_one, True),
-            (gate_up, False),
-            (w_down, False),
-            (gains[1, 0:1], True),
-        ],
-        [((2, down_rows, width), low, False), own_low, own_low, every],
-        [all_blocks(), wide_vm, down_vm, vmem((tokens, lanes), low), all_blocks(), dma((4,)), dma, dma]
-        + gather_semaphores(count)
-        + scatter(),
-    )
     hidden_two, normed, rows_two, heads_two, total_two = call_kernel(
-        functools.partial(attn_kernel, count, False),
+        functools.partial(attn_kernel, count),
         "second_attention",
         4,
-        [(normed, True), (between.astype(f32), True), (attn, False), (out, False)] + tables,
+        [(normed, True), (between, True), (attn, False), (out, False)] + tables,
         attn_outputs,
         [all_blocks()]
         + weights_vm
@@ -1882,7 +1938,10 @@
         + scatter(),
     )
 
-    def attention_back(layer, branch, grad_hidden, x_own, rows_all, heads, log_total):
+    wide_carried = ((width, 2 * lanes), low, False), ((down_rows, width), low, False)
+    attn_carried = ((3 * HEAD_DIM, width), low, False), ((HEAD_DIM, width), low, False)
+
+    def attention_back(layer, branch, grad_hidden, x_own, rows_all, heads, log_total, carries):
         return call_kernel(
             functools.partial(attn_back_kernel, count, layer),
             ("first", "second")[layer] + "_attention_back",
@@ -1890,26 +1949,35 @@
             [(branch, True), (grad_hidden, True), (x_own, True)]
             + [(rows_all, False), (heads, False), (log_total, True), (attn, False), (out, False)]
             + tables
-            + [(gains[layer, 0:1], True)],
+            + [(gains[layer, 0:1], True)]
+            + [(array, False) for array in carries],
             [
                 own_low,
                 gain_rows,
                 ((3 * HEAD_DIM, width), low, True),
                 ((HEAD_DIM, width), low, True),
+                *wide_carried,
             ],
             [all_blocks(), all_blocks(), vmem((4, tokens, PAD), low)]
             + weights_vm
             + [vmem((tokens, PAD), low), vmem((tokens, tokens), f32)]
             + [vmem((tokens, PAD), f32), vmem((tokens, PAD), f32), vmem((tokens, 3 * PAD), low)]
-            + [all_blocks(), dma((7,))]
+            + [all_blocks(), dma((7,)), dma((2,)), dma((2,))]
             + gather_semaphores(count)
             + scatter(),
         )
 
-    grad_between, gain_attn_two, attn_two, out_two = attention_back(
-        1, branch, grad_hidden, between, rows_two, heads_two, total_two
-    )
-    branch, grad_hidden, gain_mlp_one, wide_one, down_one = call_kernel(
+    grad_between, gain_attn_two, attn_two, out_two, *wide_held_two = attention_back(
+        1,
+        branch,
+        grad_hidden,
+        between,
+        rows_two,
+        heads_two,
+        total_two,
+        (wide_two, down_two),
+    )
+    branch, grad_hidden, gain_mlp_one, wide_one, down_one, *attn_held_two = call_kernel(
         functools.partial(mlp_back_kernel, count),
         "first_feed_forward_back",
         9,
@@ -1920,16 +1988,25 @@
             (gate_up, False),
             (down, False),
             (gains[0, 1:2], True),
+            (attn_two, False),
+            (out_two, False),
         ],
-        [own_low, own_wide, gain_rows] + wide_outputs,
+        [own_low, own_wide, gain_rows] + wide_outputs + list(attn_carried),
         [all_blocks(), all_blocks(), wide_vm, down_vm]
         + [vmem((tokens, lanes), low), vmem((tokens, 2 * lanes), f32)]
-        + [vmem((tokens, 2 * lanes), low), all_blocks(), dma((3,))]
+        + [vmem((tokens, 2 * lanes), low), all_blocks(), dma((3,)), dma((2,)), dma((2,))]
         + gather_semaphores(count)
         + scatter(),
     )
-    grad_start, gain_attn_one, attn_one, out_one = attention_back(
-        0, branch, grad_hidden, rows_own, rows_one, heads_one, total_one
+    grad_start, gain_attn_one, attn_one, out_one, *wide_held_one = attention_back(
+        0,
+        branch,
+        grad_hidden,
+        rows_own,
+        rows_one,
+        heads_one,
+        total_one,
+        (wide_one, down_one),
     )
     kept = jnp.where(
         at_first, jnp.stack([between, grad_start]), jnp.stack([final, grad_between])
@@ -1946,6 +2023,8 @@
     swapped_rows, gain_sums, query, key, value, out, gate, up, down = finish_grads(
         (attn_one, out_one, wide_one, down_one),
         (attn_two, out_two, wide_two, down_two),
+        wide_held_one,
+        wide_held_two + attn_held_two,
         gain_sums,
         sent,
     )

time: 658 us -> 602 us (0.915)
  Pallas kernels: 607 us -> 547 us
    pallas_call x7 -> x6, Pallas kernels: 487 us -> 452 us  [call_kernel(): pl.pallas_call(kernel, out_shape=[jax.ShapeDtypeStruct(shape, dtype) for...]
    pallas_call x1, Pallas kernels: 120 us -> 95 us  [finish_grads(): pl.pallas_call(functools.partial(finish_kernel, count), out_shape=[jax.Sh...]
where the time goes in v5:
time: 602 us; the launch traced here: 590 us
  Pallas kernels  547 us (91%)
  other arithmetic  23.7 us (4%)
  local copies, waits for them, and re-layouts  15.9 us (3%)
    pallas_call x6, Pallas kernels, call_kernel(): pl.pallas_call(kernel, out_shape=[jax.ShapeDtypeStruct(shape, dtype) for...  452 us
    pallas_call x1, Pallas kernels, finish_grads(): pl.pallas_call(functools.partial(finish_kernel, count), out_shape=[jax.Sh...  95 us

profile of v5, /device:TPU:18, one launch (start us, length us, event | category | flops | bytes accessed | tf_op | source)
XLA Modules:
  0.0 590.2 jit_solution(7821874730758914902)
XLA Ops:
  5.0 1.0 pad_maximum_fusion.refs_0_
  6.8 1.0 copy.35.refs_9_.refs_6_.refs_10_
  7.8 1.9 fusion.11
  9.7 1.3 maximum_maximum_fusion.1
  11.0 154.4 %first_layer.1 = (bf16[2,304,1536]{2,1,0:T(8,128)(2,1)}, bf16[2,1536,512]{2,1,0:T(8,128)(2,1)}, bf16[2,96,1536]{2,1,0:T(8,128)(2,1)}, bf16[2,256,1536]{2,1,0:T(8...) custom-call(bf16[4,304,384]{2,1,0:T(8,128)(2,1)} %pad_maximum_fusion, ...), custom_call_target="tpu_custom_call" | custom-call | tf_op jit(solution)/shard_map/first_layer/pallas_call | solution.py:1767
  166.8 54.9 %second_attention.1 = (f32[64,1536]{1,0:T(8,128)}, bf16[64,1536]{1,0:T(8,128)(2,1)}, bf16[16,64,1536]{2,1,0:T(8,128)(2,1)}, bf16[4,1024,128]{2,1,0:T(8,128)(2,1)}, f32[1024,1]{1,0:T(8,128)}) custom-call(bf16[64,1536]{1,0:T(8,128)(2,1)} %get-tuple-element.61.refs_0_, bf16[64,1536]{1,0:T(8,128)(2,1)} %get-tuple-element.60.refs_1_.refs_2_, ...), custom_call_target="tpu_custom_call" | custom-call | tf_op jit(solution)/shard_map/second_attention/pallas_call | solution.py:1767
  221.8 73.3 %second_feed_forward.1 = (bf16[64,1536]{1,0:T(8,128)(2,1)}, bf16[64,1536]{1,0:T(8,128)(2,1)}, f32[64,1536]{1,0:T(8,128)}, f32[8,1536]{1,0:T(8,128)}, bf16[1536,5...) custom-call(bf16[64,1536]{1,0:T(8,128)(2,1)} %get-tuple-element.64.refs_0_, f32[64,1536]{1,0:T(8,128)} %get-tuple-element.65.refs_1_, ...), custom_call_target="tpu_custom_call" | custom-call | tf_op jit(solution)/shard_map/second_feed_forward/pallas_call | solution.py:1767
  295.0 56.9 %second_attention_back.1 = (bf16[64,1536]{1,0:T(8,128)(2,1)}, f32[8,1536]{1,0:T(8,128)}, bf16[288,1536]{1,0:T(8,128)(2,1)}, bf16[96,1536]{1,0:T(8,128)(2,1)}, bf...) custom-call(bf16[64,1536]{1,0:T(8,128)(2,1)} %get-tuple-element.69.refs_0_, f32[64,1536]{1,0:T(8,128)} %get-tuple-element.70.refs_1_, ...), custom_call_target="tpu_custom_call" | custom-call | tf_op jit(solution)/shard_map/second_attention_back/pallas_call | solution.py:1767
  351.9 54.8 %first_feed_forward_back.1 = (bf16[64,1536]{1,0:T(8,128)(2,1)}, f32[64,1536]{1,0:T(8,128)}, f32[8,1536]{1,0:T(8,128)}, bf16[1536,512]{1,0:T(8,128)(2,1)}, bf16[2...) custom-call(bf16[64,1536]{1,0:T(8,128)(2,1)} %get-tuple-element.76.refs_0_, ...), custom_call_target="tpu_custom_call" | custom-call | tf_op jit(solution)/shard_map/first_feed_forward_back/pallas_call | solution.py:1767
  406.8 57.9 %first_attention_back.1 = (bf16[64,1536]{1,0:T(8,128)(2,1)}, f32[8,1536]{1,0:T(8,128)}, bf16[288,1536]{1,0:T(8,128)(2,1)}, bf16[96,1536]{1,0:T(8,128)(2,1)}, bf1...) custom-call(bf16[64,1536]{1,0:T(8,128)(2,1)} %get-tuple-element.81.refs_0_, f32[64,1536]{1,0:T(8,128)} %get-tuple-element.82.refs_1_, ...), custom_call_target="tpu_custom_call" | custom-call | tf_op jit(solution)/shard_map/first_attention_back/pallas_call | solution.py:1767
  464.7 1.0 slice.53
  465.8 1.0 maximum_select_fusion.1
  466.8 1.0 maximum_select_fusion.2.refs_15_
  467.9 1.1 copy-done.7
  469.0 1.0 copy-done.9
  470.0 95.0 %finish_grads.1 = (bf16[16,288,384]{2,1,0:T(8,128)(2,1)}, bf16[384,1536]{1,0:T(8,128)(2,1)}, bf16[384,4096]{1,0:T(8,128)(2,1)}, bf16[384,4096]{1,0:T(8,128)(2,1)...) custom-call(bf16[288,1536]{1,0:T(8,128)(2,1)S(1)} %copy-done.5, ...), custom_call_target="tpu_custom_call" | custom-call | tf_op jit(solution)/shard_map/finish_grads/pallas_call | solution.py:1696
  566.6 1.7 bitcast_convert_fusion.3
  568.6 1.6 slice.70
  570.3 3.0 copy.39
  574.4 1.4 copy.43
  575.8 1.4 copy.42
  577.2 5.5 bitcast_convert_fusion.2
  582.7 3.5 bitcast_convert_fusion.1
  586.2 3.6 bitcast_convert_fusion
  (80 shorter events, 9.5 us)
Async XLA Ops:
  0.6 2.4 copy-start
  0.7 3.2 copy-start.22
  3.1 1.4 copy-start.23
  4.4 1.6 copy-start.17
  4.4 1.6 copy-start.18
  406.7 58.0 %copy-start.20 = (f32[8,1536]{1,0:T(8,128)S(1)}, f32[8,1536]{1,0:T(8,128)}, u32[]{:S(2)}) copy-start(f32[8,1536]{1,0:T(8,128)} %get-tuple-element.100) | copy-start | bytes 147460
  406.7 59.0 %copy-start.21 = (f32[8,1536]{1,0:T(8,128)S(1)}, f32[8,1536]{1,0:T(8,128)}, u32[]{:S(2)}) copy-start(f32[8,1536]{1,0:T(8,128)} %get-tuple-element.99) | copy-start | bytes 147460
  406.7 59.0 %copy-start.19 = (f32[8,1536]{1,0:T(8,128)S(1)}, f32[8,1536]{1,0:T(8,128)}, u32[]{:S(2)}) copy-start(f32[8,1536]{1,0:T(8,128)} %get-tuple-element.101) | copy-start | bytes 147460
  406.7 59.1 %copy-start.13 = (bf16[64,1536]{1,0:T(8,128)(2,1)S(1)}, bf16[64,1536]{1,0:T(8,128)(2,1)}, u32[]{:S(2)}) copy-start(bf16[64,1536]{1,0:T(8,128)(2,1)} %get-tuple-element.60.refs_1_.refs_2_) | copy-start | bytes 589828
  406.7 59.1 %copy-start.14 = (bf16[64,1536]{1,0:T(8,128)(2,1)S(1)}, bf16[64,1536]{1,0:T(8,128)(2,1)}, u32[]{:S(2)}) copy-start(bf16[64,1536]{1,0:T(8,128)(2,1)} %get-tuple-element.76.refs_0_) | copy-start | bytes 589828
  406.7 59.1 %copy-start.16 = (bf16[64,1536]{1,0:T(8,128)(2,1)S(1)}, bf16[64,1536]{1,0:T(8,128)(2,1)}, u32[]{:S(2)}) copy-start(bf16[64,1536]{1,0:T(8,128)(2,1)} %get-tuple-element.89) | copy-start | bytes 589828
  406.7 61.1 %copy-start.6 = (bf16[256,1536]{1,0:T(8,128)(2,1)S(1)}, bf16[256,1536]{1,0:T(8,128)(2,1)}, u32[]{:S(2)}) copy-start(bf16[256,1536]{1,0:T(8,128)(2,1)} %get-tuple-element.95.refs_11_) | copy-start | bytes 2359300
  406.7 61.1 %copy-start.8 = (bf16[96,1536]{1,0:T(8,128)(2,1)S(1)}, bf16[96,1536]{1,0:T(8,128)(2,1)}, u32[]{:S(2)}) copy-start(bf16[96,1536]{1,0:T(8,128)(2,1)} %get-tuple-element.97.refs_13_) | copy-start | bytes 884740
  464.7 3.2 copy-start.2
  464.7 3.2 copy-start.3
  464.7 3.2 copy-start.4
  464.7 3.2 copy-start.5
  467.9 1.1 copy-start.7
  469.0 1.0 copy-start.9
  565.0 1.7 copy-start.15
  566.1 2.5 copy-start.10
  577.2 5.5 copy-start.12
  582.7 3.5 copy-start.11
  586.2 3.6 copy-start.1

commit v6 on v5

--- a/solution.py
+++ b/solution.py
@@ -530,64 +530,74 @@
         copy.wait_send()
 
 
+CUTS = 2
+
+
 def gather_steps(
     count, own, out, line_sent, line_got, side_sent, side_got, core_sent, core_got, local_done
 ):
     seq, b = lax.axis_index("seq"), lax.axis_index("blk")
     core, side = {"seq": seq ^ 1}, {"seq": seq ^ 2}
     base, side_base = seq * count, (seq ^ 2) * count
-
-    def along_line(j, way, source=None):
+    cut = out.shape[1] // CUTS
+
+    def spot(index, h):
+        return out.at[index, pl.ds(h * cut, cut)]
+
+    def begin(index, h, first):
+        return own.at[pl.ds(h * cut, cut)] if first else spot(index, h)
+
+    def along_line(j, way, h, first=False):
         device = {"blk": b + (1 if way else -1)}
-        spot = out.at[base + j]
         return remote(
-            spot if source is None else source, spot, line_sent.at[j, way], line_got.at[j], device
-        )
-
-    def to_side(j, source=None):
-        spot = out.at[base + j]
+            begin(base + j, h, first),
+            spot(base + j, h),
+            line_sent.at[j, way, h],
+            line_got.at[j, h],
+            device,
+        )
+
+    def to_side(j, h, first=False):
         return remote(
-            spot if source is None else source, spot, side_sent.at[j], side_got.at[j], side
-        )
-
-    def to_core(half, j, source=None):
-        spot = out.at[(side_base if half else base) + j]
+            begin(base + j, h, first),
+            spot(base + j, h),
+            side_sent.at[j, h],
+            side_got.at[j, h],
+            side,
+        )
+
+    def to_core(half, j, h, first=False):
+        index = (side_base if half else base) + j
         return remote(
-            spot if source is None else source,
-            spot,
-            core_sent.at[half, j],
-            core_got.at[half, j],
+            begin(index, h, first),
+            spot(index, h),
+            core_sent.at[half, j, h],
+            core_got.at[half, j, h],
             core,
         )
 
     local = pltpu.make_async_copy(own, out.at[base + b], local_done)
     local.start()
-    to_side(b, own).start()
-
-    @pl.when(b > 0)
-    def _():
-        along_line(b, 0, own).start()
-
-    @pl.when(b < count - 1)
-    def _():
-        along_line(b, 1, own).start()
-
-    to_core(0, b, own).start()
+    for h in range(CUTS):
+        to_side(b, h, True).start()
+        pl.when(b > 0)(along_line(b, 0, h, True).start)
+        pl.when(b < count - 1)(along_line(b, 1, h, True).start)
+    for h in range(CUTS):
+        to_core(0, b, h, True).start()
     yield "sent"
 
     def from_line(j, way):
-        settled(out.at[base + j], line_got.at[j], True)
-
-        @pl.when((b < count - 1) if way else (b > 0))
-        def _():
-            along_line(j, way).start()
-
-        to_side(j).start()
-        to_core(0, j).start()
+        for h in range(CUTS):
+            settled(spot(base + j, h), line_got.at[j, h], True)
+            pl.when((b < count - 1) if way else (b > 0))(along_line(j, way, h).start)
+            to_side(j, h).start()
+        for h in range(CUTS):
+            to_core(0, j, h).start()
 
     def from_side(j):
-        settled(out.at[side_base + j], side_got.at[j], True)
-        to_core(1, j).start()
+        for h in range(CUTS):
+            settled(spot(side_base + j, h), side_got.at[j, h], True)
+            to_core(1, j, h).start()
 
     for k in range(1, count + 1):
         if k < count:
@@ -603,41 +613,91 @@
         yield "line" if k == count - 1 else "side" if k == count else "step"
     for half, corner in ((0, seq ^ 1), (1, seq ^ 3)):
         for j in range(count):
-            settled(out.at[corner * count + j], core_got.at[half, j], True)
+            for h in range(CUTS):
+                settled(spot(corner * count + j, h), core_got.at[half, j, h], True)
         yield "corner" if half else "near"
-    for j in range(count):
-        to_side(j).wait_send()
-        to_core(0, j).wait_send()
-        to_core(1, j).wait_send()
-
-    @pl.when(b > 0)
-    def _():
-        along_line(b, 0).wait_send()
-
-    @pl.when(b < count - 1)
-    def _():
-        along_line(b, 1).wait_send()
-
-    for k in range(1, count):
-
-        @pl.when((b - k >= 0) & (b < count - 1))
-        def _():
-            along_line(b - k, 1).wait_send()
-
-        @pl.when((b + k < count) & (b > 0))
-        def _():
-            along_line(b + k, 0).wait_send()
+    for h in range(CUTS):
+        for j in range(count):
+            to_side(j, h).wait_send()
+            to_core(0, j, h).wait_send()
+            to_core(1, j, h).wait_send()
+        pl.when(b > 0)(along_line(b, 0, h).wait_send)
+        pl.when(b < count - 1)(along_line(b, 1, h).wait_send)
+        for k in range(1, count):
+            pl.when((b - k >= 0) & (b < count - 1))(along_line(b - k, 1, h).wait_send)
+            pl.when((b + k < count) & (b > 0))(along_line(b + k, 0, h).wait_send)
 
 
 def gather_semaphores(count):
     dma = pltpu.SemaphoreType.DMA
     return [
-        dma((count, 2)),
-        dma((count,)),
-        dma((count,)),
-        dma((count,)),
-        dma((2, count)),
-        dma((2, count)),
+        dma((count, 2, CUTS)),
+        dma((count, CUTS)),
+        dma((count, CUTS)),
+        dma((count, CUTS)),
+        dma((2, count, CUTS)),
+        dma((2, count, CUTS)),
+        dma,
+    ]
+
+
+def line_steps(count, own, out, line_sent, line_got, core_sent, core_got, local_done):
+    seq, b = lax.axis_index("seq"), lax.axis_index("blk")
+    core, base = {"seq": seq ^ 1}, (seq % 2) * count
+    cut = out.shape[1] // CUTS
+
+    def spot(j, h):
+        return out.at[base + j, pl.ds(h * cut, cut)]
+
+    def begin(j, h, first):
+        return own.at[pl.ds(h * cut, cut)] if first else spot(j, h)
+
+    def along_line(j, way, h, first=False):
+        device = {"blk": b + (1 if way else -1)}
+        return remote(
+            begin(j, h, first), spot(j, h), line_sent.at[j, way, h], line_got.at[j, h], device
+        )
+
+    def to_core(j, h, first=False):
+        return remote(begin(j, h, first), spot(j, h), core_sent.at[j, h], core_got.at[j, h], core)
+
+    local = pltpu.make_async_copy(own, out.at[base + b], local_done)
+    local.start()
+    for h in range(CUTS):
+        pl.when(b > 0)(along_line(b, 0, h, True).start)
+        pl.when(b < count - 1)(along_line(b, 1, h, True).start)
+        to_core(b, h, True).start()
+    yield
+
+    def from_line(j, way):
+        for h in range(CUTS):
+            settled(spot(j, h), line_got.at[j, h], True)
+            pl.when((b < count - 1) if way else (b > 0))(along_line(j, way, h).start)
+            to_core(j, h).start()
+
+    for k in range(1, count):
+        pl.when(b - k >= 0)(functools.partial(from_line, b - k, 1))
+        pl.when(b + k < count)(functools.partial(from_line, b + k, 0))
+        yield
+    local.wait()
+    for h in range(CUTS):
+        for j in range(count):
+            settled(out.at[(1 - seq % 2) * count + j, pl.ds(h * cut, cut)], core_got.at[j, h], True)
+            to_core(j, h).wait_send()
+        pl.when(b > 0)(along_line(b, 0, h).wait_send)
+        pl.when(b < count - 1)(along_line(b, 1, h).wait_send)
+        for k in range(1, count):
+            pl.when((b - k >= 0) & (b < count - 1))(along_line(b - k, 1, h).wait_send)
+            pl.when((b + k < count) & (b > 0))(along_line(b + k, 0, h).wait_send)
+
+
+def line_semaphores(count):
+    dma = pltpu.SemaphoreType.DMA
+    return [
+        dma((count, 2, CUTS)),
+        dma((count, CUTS)),
+        dma((count, CUTS)),
+        dma((count, CUTS)),
         dma,
     ]
 
@@ -673,76 +733,168 @@
     seq, b = lax.axis_index("seq"), lax.axis_index("blk")
     core, side = {"seq": seq ^ 1}, {"seq": seq ^ 2}
     place = far_first(b, count)
-
-    def to_core(half, k):
-        source = partial.at[(seq ^ (1 if half else 3)) * count + place[k]]
+    size = partial.shape[1] // CUTS
+    cuts = [pl.ds(h * size, size) for h in range(CUTS)]
+
+    def to_core(half, k, h):
         return remote(
-            source, core_slot.at[half, k], core_sent.at[half, k], core_got.at[half, k], core
-        )
-
-    def to_side(k):
-        return remote(side_out.at[k], side_slot.at[k], side_sent.at[k], side_got.at[k], side)
-
-    def along_line(k, way):
+            partial.at[(seq ^ (1 if half else 3)) * count + place[k], cuts[h]],
+            core_slot.at[half, k, cuts[h]],
+            core_sent.at[half, k, h],
+            core_got.at[half, k, h],
+            core,
+        )
+
+    def to_side(k, h):
+        return remote(
+            side_out.at[k, cuts[h]],
+            side_slot.at[k, cuts[h]],
+            side_sent.at[k, h],
+            side_got.at[k, h],
+            side,
+        )
+
+    def along_line(k, way, h):
         j = place[k]
         return remote(
-            line_out.at[k],
-            line_slot.at[way, j],
-            line_sent.at[k],
-            line_got.at[way, j],
+            line_out.at[k, cuts[h]],
+            line_slot.at[way, j, cuts[h]],
+            line_sent.at[k, h],
+            line_got.at[way, j, h],
             {"blk": b + (1 if way else -1)},
         )
 
-    def add_from(way, j):
-        settled(line_slot.at[way, j], line_got.at[way, j], True)
-        running[...] += line_slot[way, j].astype(jnp.float32)
-
-    for half in range(2):
+    def add_from(way, j, h):
+        settled(line_slot.at[way, j, cuts[h]], line_got.at[way, j, h], True)
+        running[cuts[h]] += line_slot[way, j, cuts[h]].astype(jnp.float32)
+
+    def exchange(half):
         if compute:
             compute(seq ^ (1 if half else 3))
         for k in range(count):
-            to_core(half, k).start()
+            for h in range(CUTS):
+                to_core(half, k, h).start()
+
+    exchange(0)
     if compute:
         compute(seq ^ 2)
     for k in range(count):
-        to_core(0, k).wait_recv()
-        total = partial[(seq ^ 2) * count + place[k]].astype(jnp.float32)
-        total += core_slot[0, k].astype(jnp.float32)
-        side_out[k] = total.astype(jnp.bfloat16)
-        to_side(k).start()
+        for h in range(CUTS):
+            to_core(0, k, h).wait_recv()
+            total = partial[(seq ^ 2) * count + place[k], cuts[h]].astype(jnp.float32)
+            total += core_slot[0, k, cuts[h]].astype(jnp.float32)
+            side_out[k, cuts[h]] = total.astype(jnp.bfloat16)
+            to_side(k, h).start()
+    exchange(1)
     if compute:
         compute(seq)
     yield
     for k in range(count):
         j = place[k]
-        to_core(1, k).wait_recv()
-        to_side(k).wait_recv()
-        total = partial[seq * count + j].astype(jnp.float32)
-        total += core_slot[1, k].astype(jnp.float32)
-        running[...] = total + side_slot[k].astype(jnp.float32)
         rightward, leftward = j >= b, j <= b
-        pl.when(rightward & (b > 0))(functools.partial(add_from, 1, j))
-        pl.when(leftward & (b < count - 1))(functools.partial(add_from, 0, j))
+        for h in range(CUTS):
+            to_core(1, k, h).wait_recv()
+            to_side(k, h).wait_recv()
+            total = partial[seq * count + j, cuts[h]].astype(jnp.float32)
+            total += core_slot[1, k, cuts[h]].astype(jnp.float32)
+            running[cuts[h]] = total + side_slot[k, cuts[h]].astype(jnp.float32)
+            pl.when(rightward & (b > 0))(functools.partial(add_from, 1, j, h))
+            pl.when(leftward & (b < count - 1))(functools.partial(add_from, 0, j, h))
+            if k < count - 1:
+                line_out[k, cuts[h]] = running[cuts[h]].astype(jnp.bfloat16)
+                pl.when(rightward)(along_line(k, 1, h).start)
+                pl.when(jnp.logical_not(rightward))(along_line(k, 0, h).start)
         if k < count - 1:
-            line_out[k] = running[...].astype(jnp.bfloat16)
-
-            @pl.when(rightward)
-            def _():
-                along_line(k, 1).start()
-
-            @pl.when(jnp.logical_not(rightward))
-            def _():
-                along_line(k, 0).start()
-
             yield
     deliver(running[...])
     yield
     for k in range(count):
-        to_core(0, k).wait_send()
-        to_core(1, k).wait_send()
-        to_side(k).wait_send()
-        if k < count - 1:
-            settled(line_out.at[k], line_sent.at[k], False)
+        for h in range(CUTS):
+            to_core(0, k, h).wait_send()
+            to_core(1, k, h).wait_send()
+            to_side(k, h).wait_send()
+            if k < count - 1:
+                settled(line_out.at[k, cuts[h]], line_sent.at[k, h], False)
+
+
+def line_first_steps(
+    count,
+    partial,
+    deliver,
+    own,
+    core_slot,
+    line_slot,
+    line_out,
+    side_slot,
+    running,
+    own_done,
+    core_sent,
+    core_got,
+    line_sent,
+    line_got,
+    side_sent,
+    side_got,
+):
+    seq, b = lax.axis_index("seq"), lax.axis_index("blk")
+    core, side = {"seq": seq ^ 1}, {"seq": seq ^ 2}
+    place = far_first(b, count)
+
+    def to_core(half, k):
+        source = partial.at[(seq ^ (1 if half else 3)) * count + place[k]]
+        return remote(
+            source, core_slot.at[half, k], core_sent.at[half, k], core_got.at[half, k], core
+        )
+
+    def kept(half, k):
+        source = partial.at[(seq if half else seq ^ 2) * count + place[k]]
+        return pltpu.make_async_copy(source, own.at[half, k], own_done.at[half, k])
+
+    def along_line(half, k, way):
+        j = place[k]
+        return remote(
+            line_out.at[half, k],
+            line_slot.at[half, way, j],
+            line_sent.at[half, k],
+            line_got.at[half, way, j],
+            {"blk": b + (1 if way else -1)},
+        )
+
+    def add_from(half, way, j):
+        settled(line_slot.at[half, way, j], line_got.at[half, way, j], True)
+        running[...] += line_slot[half, way, j].astype(jnp.float32)
+
+    to_side = remote(line_out.at[0, count - 1], side_slot.at[0], side_sent, side_got, side)
+    for half in range(2):
+        for k in range(count):
+            kept(half, k).start()
+            to_core(half, k).start()
+    yield
+    for k in range(count):
+        j = place[k]
+        rightward, leftward = j >= b, j <= b
+        for half in range(2):
+            kept(half, k).wait()
+            to_core(half, k).wait_recv()
+            running[...] = own[half, k].astype(jnp.float32) + core_slot[half, k].astype(jnp.float32)
+            pl.when(rightward & (b > 0))(functools.partial(add_from, half, 1, j))
+            pl.when(leftward & (b < count - 1))(functools.partial(add_from, half, 0, j))
+            if half == 0 or k < count - 1:
+                line_out[half, k] = running[...].astype(jnp.bfloat16)
+            if k < count - 1:
+                pl.when(rightward)(along_line(half, k, 1).start)
+                pl.when(jnp.logical_not(rightward))(along_line(half, k, 0).start)
+            elif half == 0:
+                to_side.start()
+            else:
+                to_side.wait_recv()
+                deliver(running[...] + side_slot[0].astype(jnp.float32))
+            yield
+    to_side.wait_send()
+    for half in range(2):
+        for k in range(count):
+            to_core(half, k).wait_send()
+            if k < count - 1:
+                settled(line_out.at[half, k], line_sent.at[half, k], False)
 
 
 def far_first(b, count):
@@ -770,13 +922,18 @@
         slots(count),
         slots(count - 1),
         pltpu.VMEM((rows, width), jnp.float32),
-        dma((2, count)),
-        dma((2, count)),
-        dma((count,)),
-        dma((count,)),
-        dma((count - 1,)),
-        dma((2, count)),
+        dma((2, count, CUTS)),
+        dma((2, count, CUTS)),
+        dma((count, CUTS)),
+        dma((count, CUTS)),
+        dma((count - 1, CUTS)),
+        dma((2, count, CUTS)),
     ]
+
+
+def run_all(fillers):
+    for filler in fillers:
+        filler()
 
 
 def run_with(steps, fillers):
@@ -851,23 +1008,38 @@
 PAD = 128
 
 
-def load_weights(attn, out, attn_vm, out_vm, sems):
-    copies = []
-    for part in range(3):
+GAINS = HEAD_DIM
+OWN_PART = HEAD_DIM + 16
+
+
+def load_weights(layer, attn, twin, out, attn_vm, out_vm, sems):
+    on_key = lax.axis_index("seq") % 2 == 0
+    own, other = attn.at[layer, pl.ds(OWN_PART, HEAD_DIM)], twin.at[layer]
+
+    def part(source, n, rows):
+        return pltpu.make_async_copy(source, attn_vm.at[pl.ds(n * PAD, rows)], sems.at[n])
+
+    copies = [
+        part(attn.at[layer, pl.ds(0, HEAD_DIM)], 0, HEAD_DIM),
+        part(attn.at[layer, pl.ds(GAINS, 16)], 3, 16),
+    ]
+    if out is not None:
         copies.append(
-            pltpu.make_async_copy(
-                attn.at[pl.ds(part * HEAD_DIM, HEAD_DIM)],
-                attn_vm.at[pl.ds(part * PAD, HEAD_DIM)],
-                sems.at[part],
-            )
-        )
-    copies.append(
-        pltpu.make_async_copy(
-            attn.at[pl.ds(3 * HEAD_DIM, 16)], attn_vm.at[pl.ds(3 * PAD, 16)], sems.at[3]
-        )
-    )
-    copies.append(pltpu.make_async_copy(out, out_vm.at[pl.ds(0, HEAD_DIM)], sems.at[4]))
-    return copies
+            pltpu.make_async_copy(out.at[layer], out_vm.at[pl.ds(0, HEAD_DIM)], sems.at[4])
+        )
+    start_all(copies)
+
+    @pl.when(on_key)
+    def _():
+        part(own, 1, HEAD_DIM).start()
+        part(other, 2, HEAD_DIM).start()
+
+    @pl.when(jnp.logical_not(on_key))
+    def _():
+        part(other, 1, HEAD_DIM).start()
+        part(own, 2, HEAD_DIM).start()
+
+    return copies + [part(other, 1, HEAD_DIM), part(other, 2, HEAD_DIM)]
 
 
 def clear_pads(attn_vm, out_vm):
@@ -912,10 +1084,10 @@
     def take(n):
         return [next(refs) for _ in range(n)]
 
-    rows_in, x_own, attn, out, cosine, sine, start = take(7)
-    hidden_out, normed_out, all_rows, heads, log_total = take(5)
-    rows_vm, attn_vm, out_vm, partial, load_done, save_done = take(6)
-    gather_sems = take(7)
+    rows_in, x_own, grads_in, attn, twin, out, cosine, sine, start = take(9)
+    hidden_out, normed_out, all_rows, heads, log_total, grads_all = take(6)
+    rows_vm, attn_vm, out_vm, partial, grads_vm, load_done, save_done = take(7)
+    gather_sems, grads_sems = take(7), take(5)
     scatter_refs = list(refs)
     block = rows_vm.shape[1]
     tokens = block * rows_vm.shape[0]
@@ -924,8 +1096,7 @@
     steps = gather_steps(count, rows_in, rows_vm, *gather_sems)
     next(steps)
     clear_pads(attn_vm, out_vm)
-    loads = load_weights(attn.at[1], out.at[1], attn_vm, out_vm, load_done)
-    start_all(loads)
+    loads = load_weights(1, attn, twin, out, attn_vm, out_vm, load_done)
     for event in steps:
         if event == "line":
             wait_all(loads)
@@ -934,6 +1105,8 @@
             span = group_span(group, count, block)
             normed = group_rows(rows_vm, group, count)
             project_heads(normed, attn_vm, heads, span, cosine, sine)
+    grad_steps = line_steps(count, grads_in, grads_vm, *grads_sems)
+    next(grad_steps)
     save = pltpu.make_async_copy(rows_vm, all_rows, save_done.at[0])
     save.start()
     attention_rows(heads, log_total, start, size, tokens)
@@ -947,7 +1120,15 @@
         hidden_out[...] = hidden
         normed_out[...] = normalise(hidden, gain_of(attn_vm, 1)).astype(jnp.bfloat16)
 
-    run_with(scatter_steps(count, partial, deliver, *scatter_refs, compute=project_out), [])
+    run_with(
+        scatter_steps(count, partial, deliver, *scatter_refs, compute=project_out),
+        [functools.partial(advance, grad_steps, 1)] * 3,
+    )
+    for _ in grad_steps:
+        pass
+    keep = pltpu.make_async_copy(grads_vm, grads_all, save_done.at[1])
+    keep.start()
+    keep.wait()
     save.wait()
 
 
@@ -958,13 +1139,13 @@
         return [next(refs) for _ in range(n)]
 
     pieces, w_gate, w_up, w_output, w_down, rows_in, grads_in, cosine, sine, start = take(10)
-    attn, gate_up, out, down, grads_all, all_rows, wide_rows = take(7)
+    attn, twin, gate_up, out, down, all_rows, wide_rows, grads_near, grads_side = take(9)
     hidden, result_out, normed_out, heads, log_total = take(5)
-    raw_vm, normed_vm, rows_vm, grads_vm, partial, partial_two = take(6)
+    raw_vm, normed_vm, rows_vm, partial, partial_two, grads_vm = take(6)
     attn_vm, out_vm, wide_vm, down_vm, units, normed_own, gain_vm = take(7)
-    load_done, save_done = take(2)
+    load_done, save_done, twin_sent, twin_got = take(4)
     spread_sems = take(5)
-    first_sems, second_sems, grads_sems = take(7), take(7), take(7)
+    first_sems, second_sems, grads_sems, side_sems = take(7), take(7), take(5), take(2)
     scatter_one, scatter_two = take(12), take(12)
     section = lax.axis_index("section")
     block, width = raw_vm.shape[1], raw_vm.shape[2]
@@ -972,26 +1153,33 @@
     size = count * block
     low, f32 = jnp.bfloat16, jnp.float32
     greet_group(count, ({"section": 1 - section},))
+    spread = spread_steps(
+        count, pieces, w_gate, w_up, w_output, w_down, attn, gate_up, out, down, *spread_sems
+    )
     steps = gather_steps(count, rows_in, raw_vm, *first_sems)
     next(steps)
-    spread = spread_steps(
-        count, pieces, w_gate, w_up, w_output, w_down, attn, gate_up, out, down, *spread_sems
-    )
     next(spread)
     clear_pads(attn_vm, out_vm)
     for event in steps:
         if event == "line":
-            next(spread)
-    grad_steps = gather_steps(count, grads_in, grads_vm, *grads_sems)
-    next(grad_steps)
+            advance(spread, 3)
+    grads_across = remote(
+        grads_in, grads_side, *side_sems, {"seq": lax.axis_index("seq") ^ 2}
+    )
+    grads_across.start()
     next(spread)
-    next(spread)
-    loads = load_weights(attn.at[0], out.at[0], attn_vm, out_vm, load_done)
-    loads.append(
-        pltpu.make_async_copy(attn.at[1, pl.ds(3 * HEAD_DIM, 16)], gain_vm, load_done.at[5])
-    )
-    start_all(loads)
-    wait_all(loads)
+    pair = remote(
+        attn.at[:, pl.ds(OWN_PART, HEAD_DIM)],
+        twin,
+        twin_sent,
+        twin_got,
+        {"seq": lax.axis_index("seq") ^ 1},
+    )
+    pair.start()
+    pair.wait()
+    gain_load = pltpu.make_async_copy(attn.at[1, pl.ds(GAINS, 16)], gain_vm, load_done.at[5])
+    gain_load.start()
+    wait_all(load_weights(0, attn, twin, None, attn_vm, out_vm, load_done) + [gain_load])
     for group in range(tokens // size):
         raw = raw_vm[group * count : (group + 1) * count].astype(f32)
         normed = normalise(raw, gain_of(attn_vm, 0)[None]).astype(low)
@@ -1001,6 +1189,10 @@
     saves = [pltpu.make_async_copy(normed_vm, all_rows, save_done.at[0])]
     saves[0].start()
     attention_rows(heads, log_total, start, size, tokens)
+    next(spread)
+    load = pltpu.make_async_copy(out.at[0], out_vm.at[pl.ds(0, HEAD_DIM)], load_done.at[4])
+    load.start()
+    load.wait()
 
     def project_out(group):
         mixed = heads[3, group_span(group, count, block)]
@@ -1013,9 +1205,7 @@
 
     def more():
         next(spread)
-        next(grad_steps, None)
-
-    next(grad_steps)
+
     run_with(scatter_steps(count, partial, deliver, *scatter_one, compute=project_out), [more] * 5)
     for number, event in enumerate(gather_steps(count, normed_own, rows_vm, *second_sems)):
         if number == 0:
@@ -1037,17 +1227,24 @@
         units[group_span(group, count, block)] = made
         keep_group(partial_two, group, product(made, down_vm[...]), count)
 
+    grad_steps = line_steps(count, grads_in, grads_vm, *grads_sems)
+    next(grad_steps)
+
     def deliver_two(total):
         made = (hidden[...] + total).astype(low)
         result_out[...] = made
         gain = gain_vm[...][0:1].astype(f32)
         normed_out[...] = normalise(made.astype(f32), gain).astype(low)
 
-    run_with(scatter_steps(count, partial_two, deliver_two, *scatter_two, compute=project_down), [])
+    run_with(
+        scatter_steps(count, partial_two, deliver_two, *scatter_two, compute=project_down),
+        [functools.partial(advance, grad_steps, 1)] * 3,
+    )
     for _ in grad_steps:
         pass
-    saves.append(pltpu.make_async_copy(grads_vm, grads_all, save_done.at[2]))
+    saves.append(pltpu.make_async_copy(grads_vm, grads_near, save_done.at[2]))
     saves[2].start()
+    grads_across.wait()
     wait_all(saves)
 
 
@@ -1141,18 +1338,19 @@
 
     for k in turns:
         along_line(0, k).start()
-    start_all(own_piece(0) + own_rows(3))
+    start_all(own_piece(0))
     yield
     for k in turns:
         forward(0, k)
-    yield
+        yield
+    start_all(own_rows(3))
     for kind in (1, 2):
         for k in turns:
             along_line(kind, k).start()
+    arrived(0)
+    start_all(own_piece(1) + own_piece(2) + own_rows(4))
     yield
-    arrived(0)
     arrived(3)
-    start_all(own_piece(1) + own_piece(2) + own_rows(4))
     yield
     for kind in (1, 2):
         for k in turns:
@@ -1229,12 +1427,15 @@
     def take(n):
         return [next(refs) for _ in range(n)]
 
-    rows_in, hidden, gate_up, down, grads_all, grads_own, gain = take(7)
-    result_out, branch_out, grad_hidden_out, gain_out, wide_grad, down_grad = take(6)
+    rows_in, hidden, gate_up, down, grads_near, grads_far, grads_own, gain = take(8)
+    ahead_out, branch_out, grad_hidden_out, gain_out, wide_grad, down_grad = take(6)
     rows_vm, grads_vm, wide_vm, down_vm, units, pre_grads, partial, partial_back = take(8)
     (load_done,) = take(1)
+    size = count * rows_vm.shape[1]
+    half = rows_vm.shape[0] // 2
+    near = lax.axis_index("seq") // 2 * half
     gather_sems = take(7)
-    scatter_refs, scatter_back = take(12), take(12)
+    scatter_back = list(refs)
     block = rows_vm.shape[1]
     greet_group(count)
     steps = gather_steps(count, rows_in, rows_vm, *gather_sems)
@@ -1242,7 +1443,8 @@
     loads = [
         pltpu.make_async_copy(gate_up.at[1], wide_vm, load_done.at[0]),
         pltpu.make_async_copy(down.at[1], down_vm, load_done.at[1]),
-        pltpu.make_async_copy(grads_all, grads_vm, load_done.at[2]),
+        pltpu.make_async_copy(grads_near, grads_vm.at[pl.ds(near, half)], load_done.at[2]),
+        pltpu.make_async_copy(grads_far, grads_vm.at[pl.ds(half - near, half)], load_done.at[4]),
     ]
     start_all(loads)
 
@@ -1265,23 +1467,25 @@
             through(group)
 
     def project_down(group):
-        value = product(units[group_span(group, count, block)], down_vm[...])
-        partial[pl.ds(group * count, count)] = value.astype(jnp.bfloat16).reshape(count, block, -1)
-
-    def deliver(total):
-        result_out[...] = (hidden[...] + total).astype(jnp.bfloat16)
+        value = product(units[group * size : (group + 1) * size], down_vm[...])
+        partial[group * count : (group + 1) * count] = value.astype(jnp.bfloat16).reshape(
+            count, block, -1
+        )
 
     def deliver_back(total):
         mlp_grad_sent(
             total, hidden, grads_own, gain, branch_out, grad_hidden_out, gain_out
         )
 
-    back = scatter_steps(count, partial_back, deliver_back, *scatter_back)
-    ahead = scatter_steps(count, partial, deliver, *scatter_refs, compute=project_down)
-    next(back)
-    next(ahead)
-    run_with(back, wide_grads(rows_vm, pre_grads, units, grads_vm, wide_grad, down_grad))
-    run_with(ahead, [])
+    fillers = wide_grads(rows_vm, pre_grads, units, grads_vm, wide_grad, down_grad)
+    fillers += [functools.partial(project_down, group) for group in range(4)]
+    run_with(
+        scatter_steps(count, partial_back, deliver_back, *scatter_back),
+        [functools.partial(run_all, fillers[n::4]) for n in range(4)],
+    )
+    save = pltpu.make_async_copy(partial, ahead_out, load_done.at[3])
+    save.start()
+    save.wait()
 
 
 def mlp_back_kernel(count, *refs):
@@ -1291,9 +1495,9 @@
         return [next(refs) for _ in range(n)]
 
     grads_own, hidden, all_rows, gate_up, down, gain = take(6)
-    carry_from = take(2)
+    carry_from = take(3)
     branch_out, grad_hidden_out, gain_out, wide_grad, down_grad = take(5)
-    carry_to = take(2)
+    carry_to = take(3)
     rows_vm, grads_vm, wide_vm, down_vm, units, pre_vm, pre_grads, partial, load_done = take(9)
     carry_sent, carry_got = take(2)
     gather_sems = take(7)
@@ -1343,39 +1547,44 @@
     carry(copies, 0, "wait")
 
 
-def attn_back_kernel(count, layer, *refs):
-    refs = iter(refs)
-
-    def take(n):
-        return [next(refs) for _ in range(n)]
-
-    branch_in, grad_hidden, x_own, all_rows, heads_kept, log_total, attn, out = take(8)
-    cosine, sine, start, gain = take(4)
-    carry_from = take(2)
-    grad_out, gain_out, attn_grad, out_grad = take(4)
-    carry_to = take(2)
-    branch_vm, rows_vm, heads, attn_vm, out_vm, mixed_grads, probs = take(7)
-    key_grads, value_grads, joint, partial, load_done, carry_sent, carry_got = take(7)
-    gather_sems = take(7)
-    scatter_refs = list(refs)
+class Parts:
+    pass
+
+
+def attn_back_refs(take, attn_grad=None, out_grad=None):
+    r = Parts()
+    r.branch_vm, r.rows_vm, r.heads, r.attn_vm, r.out_vm, r.mixed_grads, r.probs = take(7)
+    r.key_grads, r.value_grads, r.joint, r.partial, r.load_done = take(5)
+    r.gather_sems = take(7)
+    r.scatter_refs = take(12)
+    return r
+
+
+def attn_back_body(count, layer, r, ins, outs, background, fillers, gathered=None):
+    branch_in, grad_hidden, x_own, all_rows, heads_kept, log_total, attn, twin, out = ins[:9]
+    cosine, sine, start, gain = ins[9:]
+    grad_out, gain_out, attn_grad, out_grad = outs
+    branch_vm, rows_vm, heads, attn_vm, out_vm = r.branch_vm, r.rows_vm, r.heads, r.attn_vm, r.out_vm
+    mixed_grads, probs, key_grads, value_grads = r.mixed_grads, r.probs, r.key_grads, r.value_grads
+    joint, partial, load_done = r.joint, r.partial, r.load_done
     block = rows_vm.shape[1]
     size = count * block
     tokens = block * rows_vm.shape[0]
     low, f32 = jnp.bfloat16, jnp.float32
     scale = HEAD_DIM ** (-0.5)
-    greet_group(count, ({"section": 1 - lax.axis_index("section")},))
-    steps = gather_steps(count, branch_in, branch_vm, *gather_sems)
+    steps = gather_steps(count, branch_in, branch_vm, *r.gather_sems)
     next(steps)
-    copies = carried(carry_from, carry_to, carry_sent, carry_got)
-    carry(copies, 1 - layer, "start")
+    background()
     clear_pads(attn_vm, out_vm)
-    loads = load_weights(attn.at[layer], out.at[layer], attn_vm, out_vm, load_done)
-    loads.append(pltpu.make_async_copy(heads_kept, heads, load_done.at[5]))
-    loads.append(pltpu.make_async_copy(all_rows, rows_vm, load_done.at[6]))
-    start_all(loads)
+    loads = load_weights(layer, attn, twin, out, attn_vm, out_vm, load_done)
+    kept = [
+        pltpu.make_async_copy(heads_kept, heads, load_done.at[5]),
+        pltpu.make_async_copy(all_rows, rows_vm, load_done.at[6]),
+    ]
+    start_all(kept)
     key_grads[...] = jnp.zeros_like(key_grads)
     value_grads[...] = jnp.zeros_like(value_grads)
-    wait_all(loads)
+    wait_all(loads + kept)
 
     def spans(i):
         return slice(i * size, (i + 1) * size), slice(0, (i + 1) * size)
@@ -1396,6 +1605,8 @@
         group = group_of(event)
         if group is not None:
             project(group)
+    if gathered:
+        gathered()
     for i in reversed(range(tokens // size)):
         here, seen = spans(i)
         weights = probs[here, seen]
@@ -1432,27 +1643,50 @@
         gain_out[...] = jnp.broadcast_to(jnp.sum(terms, axis=0, keepdims=True), gain_out.shape)
 
     run_with(
-        scatter_steps(count, partial, deliver, *scatter_refs, compute=project_back),
-        [functools.partial(attn_part, part) for part in range(3)] + [out_part],
-    )
-    carry(copies, 1 - layer, "wait")
-
-
-def finish_kernel(count, *refs):
+        scatter_steps(count, partial, deliver, *r.scatter_refs, compute=project_back),
+        [functools.partial(run_all, [functools.partial(attn_part, n) for n in range(3)] + [out_part])]
+        + fillers,
+    )
+
+
+def attn_back_kernel(count, layer, *refs):
     refs = iter(refs)
 
     def take(n):
         return [next(refs) for _ in range(n)]
 
-    ones, twos = take(4), take(4)
-    wide_from_two, down_from_two, wide_from_one, down_from_one = take(4)
-    attn_from_one, out_from_one, gains, swap_rows = take(4)
-    attn, out, gate, up, down, gains_out, swapped_rows = take(7)
+    ins, carry_from, outs, carry_to = take(13), take(1), take(4), take(1)
+    r = attn_back_refs(take)
+    carry_sent, carry_got = take(2)
+    greet_group(count, ({"section": 1 - lax.axis_index("section")},))
+    copies = carried(carry_from, carry_to, carry_sent, carry_got)
+
+    def background():
+        carry(copies, 1 - layer, "start")
+
+    attn_back_body(count, layer, r, ins, outs, background, [])
+    carry(copies, 1 - layer, "wait")
+
+
+def last_kernel(count, *refs):
+    refs = iter(refs)
+
+    def take(n):
+        return [next(refs) for _ in range(n)]
+
+    ins = take(13)
+    wide_one, down_one, attn_two, out_two, wide_two, down_two = take(6)
+    wide_from_one, down_from_one, attn_from_one, out_from_one, ahead = take(5)
+    gain_mlp_one, gain_attn_two, gain_mlp_two, between, grad_between, hidden = take(6)
+    attn, out, gate, up, down, gains_out, swapped_rows, final, grad_start = take(9)
+    attn_grad, out_grad, gain_attn_one, gains = take(4)
     attn_own, out_own, wide_own, down_own, attn_in, out_in, wide_in, down_in = take(8)
     attn_slot, wide_slot = take(2)
     gain_in, gain_sum, gain_line, gain_part, gain_side, gain_core = take(6)
     load_done, cross_sent, cross_got, line_sent, line_got = take(5)
     side_sent, side_got, core_sent, core_got, local_done, small_sent, small_got = take(7)
+    ahead_refs = take(13)
+    r = attn_back_refs(take)
     seq, b, section = lax.axis_index("seq"), lax.axis_index("blk"), lax.axis_index("section")
     at_first = section == 0
     at_second = jnp.logical_not(at_first)
@@ -1468,38 +1702,35 @@
         return (pl.ds(pl.multiple_of(j * rows, rows), rows),)
 
     pairs = {
-        0: (attn_own, attn_in, ones[0]),
-        1: (wide_own, wide_in, None),
-        2: (out_own, out_in, ones[1]),
-        3: (down_own, down_in, None),
+        0: (attn_own, attn_in, attn_grad),
+        1: (wide_own, wide_in, wide_one),
+        2: (out_own, out_in, out_grad),
+        3: (down_own, down_in, down_one),
     }
     sources = {
-        0: (ones[0], twos[0], None, attn_from_one),
-        1: (ones[2], twos[2], wide_from_two, wide_from_one),
-        2: (ones[1], twos[1], None, out_from_one),
-        3: (ones[3], twos[3], down_from_two, down_from_one),
+        0: (attn_grad, attn_two, attn_from_one),
+        1: (wide_one, wide_two, wide_from_one),
+        2: (out_grad, out_two, out_from_one),
+        3: (down_one, down_two, down_from_one),
     }
 
     def load(kind):
-        one, two, from_two, from_one = sources[kind]
+        one, two, from_one = sources[kind]
         own, held, _ = pairs[kind]
 
-        def copies(begins):
-            for n, (begin, end) in enumerate(zip(begins, (own, held))):
-                if begin is not None:
-                    pltpu.make_async_copy(begin, end, load_done.at[kind, n]).start()
-
-        pl.when(at_first)(functools.partial(copies, (one, from_two)))
-        pl.when(at_second)(functools.partial(copies, (two, from_one)))
+        @pl.when(at_first)
+        def _():
+            pltpu.make_async_copy(one, own, load_done.at[kind, 0]).start()
+
+        @pl.when(at_second)
+        def _():
+            pltpu.make_async_copy(two, own, load_done.at[kind, 0]).start()
+            pltpu.make_async_copy(from_one, held, load_done.at[kind, 1]).start()
 
     def loaded(kind):
-        own, held, crossing = pairs[kind]
+        own, held, _ = pairs[kind]
         pltpu.make_async_copy(own, own, load_done.at[kind, 0]).wait()
-        copy = pltpu.make_async_copy(held, held, load_done.at[kind, 1])
-        if crossing is None:
-            copy.wait()
-        else:
-            pl.when(at_second)(copy.wait)
+        pl.when(at_second)(pltpu.make_async_copy(held, held, load_done.at[kind, 1]).wait)
 
     def cross(kind, k):
         _, held, begin = pairs[kind]
@@ -1509,9 +1740,8 @@
         )
 
     def add_up(kind, k):
-        own, held, crossing = pairs[kind]
-        if crossing is not None:
-            pl.when(at_first)(cross(kind, k).wait_recv)
+        own, held, _ = pairs[kind]
+        pl.when(at_first)(cross(kind, k).wait_recv)
         index = piece_rows(kind, lax.rem(b + k, count)) if kind < 2 else (slice(None),)
         held[index] = (own[index].astype(f32) + held[index].astype(f32)).astype(low)
 
@@ -1584,15 +1814,61 @@
     def small(n, source, slot, device):
         return remote(source, slot, small_sent.at[n], small_got.at[n], device)
 
-    swap = small(0, swap_rows.at[:], swapped_rows.at[:], other)
-    swap.start()
+    swap_rest = small(4 + count, between, swapped_rows.at[0], other)
+    swap_final = small(4 + count, final, swapped_rows.at[0], other)
+    swap_between = small(0, grad_between, swapped_rows.at[1], other)
+    swap_start = small(0, grad_start, swapped_rows.at[1], other)
+    pl.when(at_second)(swap_rest.start)
+    pl.when(at_first)(swap_between.start)
+    wide_turns = [(1, k) for k in turns]
+    crossings = wide_turns + [(0, k) for k in turns] + [(2, 0), (3, 0)]
+
+    def begin_cross(those):
+        for kind, k in those:
+            pl.when(at_second)(cross(kind, k).start)
+
+    def background():
+        begin_cross(crossings[:count])
+        load(1)
+        load(3)
+
+    def deliver(total):
+        final[...] = (hidden[...] + total).astype(low)
+        pl.when(at_first)(swap_final.start)
+
+    def later():
+        load(0)
+        load(2)
+        begin_cross(crossings[count:])
+
+    def share(n):
+        if n == 0:
+            loaded(1)
+        add_up(1, turns[n])
+        along_line(1, turns[n]).start()
+
+    def gathered():
+        share(0)
+        share(1)
+
+    ahead_steps = line_first_steps(count, ahead, deliver, *ahead_refs)
+    attn_back_body(
+        count,
+        0,
+        r,
+        ins,
+        (grad_start, gain_attn_one, attn_grad, out_grad),
+        background,
+        [later, functools.partial(share, 2)],
+        gathered,
+    )
+    pl.when(at_second)(swap_start.start)
+    gains[0, 0:4] = gain_attn_one[0:4]
+    gains[0, 4:8] = gain_mlp_one[4:8]
+    gains[1, 0:4] = gain_attn_two[0:4]
+    gains[1, 4:8] = gain_mlp_two[4:8]
     gain_cross = small(1, gains.at[1 - section], gain_in.at[:], other)
     gain_cross.start()
-    for kind in (1, 3, 2, 0):
-        load(kind)
-    crossings = [(2, 0)] + [(0, k) for k in turns]
-    for kind, k in crossings:
-        pl.when(at_second)(cross(kind, k).start)
 
     def gain_piece(j):
         return gain_sum.at[:, pl.ds(pl.multiple_of(j * rows, rows), rows)]
@@ -1601,20 +1877,37 @@
         j = lax.rem(b + k, count)
         return small(3 + k, gain_piece(j), gain_line.at[k], {"blk": j})
 
+    add_up(1, 0)
+    publish(1, 0)
+    from_line(1, turns[0])
+    from_line(1, turns[1])
+    loaded(0)
+    for k in turns[:-1]:
+        add_up(0, k)
+        along_line(0, k).start()
+    add_up(0, 0)
+    publish(0, 0)
+    from_line(1, turns[2])
+    from_side(1, 0)
+    loaded(2)
+    add_up(2, 0)
+    publish(2, 0)
+    from_side(1, turns[0])
+    from_side(1, turns[1])
+    for k in turns[:-1]:
+        from_line(0, k)
+    loaded(3)
+    add_up(3, 0)
+    publish(3, 0)
+    next(ahead_steps)
+    from_side(0, 0)
+    from_side(1, turns[2])
     gain_cross.wait_recv()
     gain_sum[...] = gains[section] + gain_in[...]
     for k in range(1, count):
         gain_send(k).start()
-
-    loaded(1)
-    for k in turns[:-1]:
-        add_up(1, k)
-        along_line(1, k).start()
-    loaded(3)
-    add_up(3, 0)
-    publish(3, 0)
-    add_up(1, 0)
-    publish(1, 0)
+    advance(ahead_steps, 2)
+    from_side(2, 0)
     for k in range(1, count):
         gain_send(k).wait_recv()
     gain_part[...] = gain_sum[:, pl.ds(pl.multiple_of(b * rows, rows), rows)]
@@ -1622,43 +1915,22 @@
         gain_part[...] += gain_line[k]
     gain_to_side = small(2, gain_part.at[:], gain_side.at[:], side)
     gain_to_side.start()
-    loaded(2)
-    add_up(2, 0)
-    publish(2, 0)
-    from_side(3, 0)
-    from_line(1, turns[0])
+    advance(ahead_steps, 2)
+    for k in turns[:-1]:
+        from_side(0, k)
+    advance(ahead_steps, 2)
     gain_to_side.wait_recv()
     gain_side[...] += gain_part[...]
     gain_to_core = small(3, gain_side.at[:], gain_core.at[:], core)
     gain_to_core.start()
-    loaded(0)
-    add_up(0, turns[0])
-    along_line(0, turns[0]).start()
-    from_side(1, 0)
-    from_line(1, turns[1])
-    add_up(0, turns[1])
-    along_line(0, turns[1]).start()
-    from_side(2, 0)
-    from_line(1, turns[2])
-    add_up(0, turns[2])
-    along_line(0, turns[2]).start()
-    add_up(0, 0)
-    publish(0, 0)
-    from_side(1, turns[0])
+    from_side(3, 0)
+    for _ in ahead_steps:
+        pass
     gain_to_core.wait_recv()
     gains_out[...] = gain_side[...] + gain_core[...]
-    from_line(0, turns[0])
-    from_side(1, turns[1])
-    from_line(0, turns[1])
-    from_line(0, turns[2])
-    from_side(1, turns[2])
-    from_side(0, 0)
-    for k in turns[:-1]:
-        from_side(0, k)
     every = [(0, k) for k in range(count)] + [(1, k) for k in range(count)] + [(2, 0), (3, 0)]
     for kind, k in every:
-        if (kind, k) in crossings:
-            pl.when(at_second)(cross(kind, k).wait_send)
+        pl.when(at_second)(cross(kind, k).wait_send)
         if kind < 2 and k:
             along_line(kind, k).wait_send()
         for to_side, to_core, local in sends(kind, k):
@@ -1670,7 +1942,8 @@
         for half, of_seq in ((0, seq ^ 1), (1, seq ^ 3)):
             for n, spot in numbered(kind, k, of_seq):
                 settled(spot, core_got.at[half, n], True)
-    swap.wait()
+    swap_between.wait()
+    swap_rest.wait()
     gain_cross.wait_send()
     for k in range(1, count):
         gain_send(k).wait_send()
@@ -1678,69 +1951,53 @@
     gain_to_core.wait_send()
 
 
-def finish_grads(first, second, from_two, from_one, gains, swap_rows):
-    seq_count, count = lax.axis_size("seq"), lax.axis_size("blk")
+def last_layer(count, operands, like, back_scratch):
+    attn, out, wide, down, block, width, gain_rows = like
     low, f32 = jnp.bfloat16, jnp.float32
-    attn, out, wide, down = first
-    rows = wide.shape[0] // count
-    lanes = wide.shape[1] // 2
+    seq_count = lax.axis_size("seq")
+    rows = wide[0] // count
+    lanes = wide[1] // 2
     parts = seq_count * count
     dma = pltpu.SemaphoreType.DMA
     vmem = pltpu.VMEM
     sends = 3 * count + 2
-    heads = attn.shape[0]
-    operands = list(first) + list(second) + list(from_two) + list(from_one) + [gains, swap_rows]
-    in_vmem = pl.BlockSpec(memory_space=vmem)
-    anywhere = pl.BlockSpec(memory_space=pl.ANY)
-    small = (gains.shape[1], rows)
-    attn, out, gate, up, down, gains, swapped_rows = pl.pallas_call(
-        functools.partial(finish_kernel, count),
-        out_shape=[
-            jax.ShapeDtypeStruct((parts, heads, rows), low),
-            jax.ShapeDtypeStruct((out.shape[0] * seq_count, out.shape[1]), low),
-            jax.ShapeDtypeStruct((rows, lanes * parts), low),
-            jax.ShapeDtypeStruct((rows, lanes * parts), low),
-            jax.ShapeDtypeStruct((down.shape[0] * seq_count, down.shape[1]), low),
-            jax.ShapeDtypeStruct(small, f32),
-            jax.ShapeDtypeStruct(swap_rows.shape, low),
-        ],
-        in_specs=[anywhere] * (len(operands) - 2) + [in_vmem] * 2,
-        out_specs=[anywhere] * 5 + [in_vmem, in_vmem],
-        scratch_shapes=[
-            vmem(attn.shape, low),
-            vmem(out.shape, low),
-            vmem(wide.shape, low),
-            vmem(down.shape, low),
-            vmem(attn.shape, low),
-            vmem(out.shape, low),
-            vmem(wide.shape, low),
-            vmem(down.shape, low),
-            vmem((count, heads, rows), low),
-            vmem((count, rows, 2 * lanes), low),
-            vmem(gains.shape[1:], f32),
-            vmem(gains.shape[1:], f32),
-            vmem((count,) + small, f32),
-            vmem(small, f32),
-            vmem(small, f32),
-            vmem(small, f32),
-            dma((4, 2)),
-            dma((4, count)),
-            dma((4, count)),
-            dma((2, count)),
-            dma((2, count)),
-            dma((sends,)),
-            dma((sends,)),
-            dma((2, sends)),
-            dma((2, sends)),
-            dma((sends,)),
-            dma((4 + count,)),
-            dma((4 + count,)),
-        ],
-        compiler_params=pltpu.CompilerParams(
-            collective_id=3, has_side_effects=True, vmem_limit_bytes=48 * 2**20
-        ),
-        name="finish_grads",
-    )(*operands)
+    heads = attn[0]
+    small = (gain_rows, rows)
+
+    def slots(*places):
+        return vmem(places + (block, width), low)
+
+    outputs = [
+        ((parts, heads, rows), low, False),
+        ((out[0] * seq_count, out[1]), low, False),
+        ((rows, lanes * parts), low, False),
+        ((rows, lanes * parts), low, False),
+        ((down[0] * seq_count, down[1]), low, False),
+        (small, f32, True),
+        ((2, block, width), low, True),
+        ((block, width), low, True),
+        ((block, width), low, True),
+    ]
+    scratch = (
+        [vmem(attn, low), vmem(out, low), vmem((gain_rows, width), f32)]
+        + [vmem((2, gain_rows, width), f32)]
+        + [vmem(shape, low) for shape in (attn, out, wide, down)] * 2
+        + [vmem((count, heads, rows), low), vmem((count, rows, 2 * lanes), low)]
+        + [vmem((gain_rows, width), f32)] * 2
+        + [vmem((count,) + small, f32)]
+        + [vmem(small, f32)] * 3
+        + [dma((4, 2)), dma((4, count)), dma((4, count)), dma((2, count)), dma((2, count))]
+        + [dma((sends,)), dma((sends,)), dma((2, sends)), dma((2, sends)), dma((sends,))]
+        + [dma((5 + count,)), dma((5 + count,))]
+        + [slots(2, count), slots(2, count), slots(2, 2, count), slots(2, count), slots(1)]
+        + [vmem((block, width), f32)]
+        + [dma((2, count)), dma((2, count)), dma((2, count)), dma((2, count))]
+        + [dma((2, 2, count)), dma, dma]
+        + back_scratch
+    )
+    attn, out, gate, up, down, gains, swapped_rows, final, grad_start = call_kernel(
+        functools.partial(last_kernel, count), "last_layer_back", 3, operands, outputs, scratch
+    )
     attn = attn.astype(f32)
 
     def heads_back(start, copies):
@@ -1750,6 +2007,8 @@
     copies = HEADS // KV_HEADS
     return (
         swapped_rows,
+        final,
+        grad_start,
         gains,
         heads_back(0, 1),
         heads_back(HEAD_DIM, copies),
@@ -1803,9 +2062,8 @@
     return jnp.concatenate(
         [
             heads_of(w_query, seq_count, seq_index),
-            heads_of(w_key, kv_per_blk, kv_place),
-            heads_of(w_value, kv_per_blk, kv_place),
             jnp.broadcast_to(gains[None], (count,) + gains.shape),
+            heads_of(jnp.where(seq_index % 2 == 0, w_key, w_value), kv_per_blk, kv_place),
         ],
         axis=1,
     )
@@ -1833,12 +2091,12 @@
     _, position = doc_info(lengths, token_index)
     start = (token_index - position)[:, None]
     half_dim = HEAD_DIM // 2
-    frequency = THETA ** (-2.0 * jnp.arange(half_dim, dtype=f32) / HEAD_DIM)
-    angles = position.astype(f32)[:, None] * frequency
-    cosine, sine = jnp.cos(angles), jnp.sin(angles)
-    empty = jnp.zeros((tokens, PAD - HEAD_DIM), f32)
-    cosine = jnp.concatenate([cosine, cosine, empty], axis=1)
-    sine = jnp.concatenate([-sine, sine, empty], axis=1)
+    lane = jnp.arange(PAD)
+    frequency = THETA ** (-2.0 * (lane % half_dim).astype(f32) / HEAD_DIM)
+    angles = position.astype(f32)[:, None] * frequency[None, :]
+    sign = jnp.where(lane < half_dim, -1.0, 1.0).astype(f32)
+    cosine = jnp.where(lane < HEAD_DIM, jnp.cos(angles), 0.0)
+    sine = jnp.where(lane < HEAD_DIM, jnp.sin(angles) * sign, 0.0)
 
     def all_blocks():
         return vmem((blocks, block, width), low)
@@ -1846,6 +2104,8 @@
     def scatter():
         return scatter_scratch(count, block, width)
 
+    half_blocks = vmem((blocks // 2, block, width), low)
+    half = ((blocks // 2, block, width), low, False)
     own_low, own_wide = ((block, width), low, True), ((block, width), f32, True)
     every = ((blocks, block, width), low, False)
     gain_rows = ((8, width), f32, True)
@@ -1861,12 +2121,14 @@
     tables = [(cosine, True), (sine, True), (start, True)]
     (
         attn,
+        twin,
         gate_up,
         out,
         down,
-        grads_all,
         rows_one,
         wide_rows_one,
+        grads_near,
+        grads_side,
         hidden_one,
         between,
         normed,
@@ -1881,42 +2143,50 @@
         + tables,
         [
             ((2, pieces.shape[1], width), low, False),
+            ((2, HEAD_DIM, width), low, False),
             ((2, width, 2 * lanes), low, False),
             ((2, out_rows, width), low, False),
             ((2, down_rows, width), low, False),
             every,
             every,
-            every,
+            half,
+            ((block, width), low, False),
             own_wide,
             own_low,
             own_low,
             ((4, tokens, PAD), low, True),
             ((tokens, 1), f32, True),
         ],
-        [all_blocks() for _ in range(6)]
+        [all_blocks() for _ in range(5)]
+        + [half_blocks]
         + weights_vm
         + [wide_vm, down_vm, vmem((tokens, lanes), low), vmem((block, width), low)]
-        + [vmem((16, width), low), dma((6,)), dma((3,))]
+        + [vmem((16, width), low), dma((6,)), dma((3,)), dma, dma]
         + [dma((3, count)), dma((3, count)), dma((5, count)), dma((5, count)), dma((5,))]
-        + gather_semaphores(count) * 3
+        + gather_semaphores(count) * 2
+        + line_semaphores(count)
+        + [dma, dma]
         + scatter()
         + scatter(),
     )
-    gains = attn[:, 3 * HEAD_DIM : 3 * HEAD_DIM + 2].astype(f32)
-    hidden_two, normed, rows_two, heads_two, total_two = call_kernel(
+    gains = attn[:, GAINS : GAINS + 2].astype(f32)
+    hidden_two, normed, rows_two, heads_two, total_two, grads_far = call_kernel(
         functools.partial(attn_kernel, count),
         "second_attention",
         4,
-        [(normed, True), (between, True), (attn, False), (out, False)] + tables,
-        attn_outputs,
+        [(normed, True), (between, True), (grads_side, True)]
+        + [(attn, False), (twin, False), (out, False)]
+        + tables,
+        attn_outputs + [half],
         [all_blocks()]
         + weights_vm
-        + [all_blocks(), dma((5,)), dma((2,))]
+        + [all_blocks(), half_blocks, dma((5,)), dma((2,))]
         + gather_semaphores(count)
+        + line_semaphores(count)
         + scatter(),
     )
     wide_outputs = [((width, 2 * lanes), low, True), ((down_rows, width), low, True)]
-    final, branch, grad_hidden, gain_mlp_two, wide_two, down_two = call_kernel(
+    ahead, branch, grad_hidden, gain_mlp_two, wide_two, down_two = call_kernel(
         functools.partial(mlp_both_kernel, count),
         "second_feed_forward",
         6,
@@ -1925,59 +2195,56 @@
             (hidden_two, True),
             (gate_up, False),
             (down, False),
-            (grads_all, False),
+            (grads_near, False),
+            (grads_far, False),
             (grads_own, True),
             (gains[1, 1:2], True),
         ],
-        [own_low, own_low, own_wide, gain_rows] + wide_outputs,
+        [every, own_low, own_wide, gain_rows] + wide_outputs,
         [all_blocks(), all_blocks(), wide_vm, down_vm]
         + [vmem((tokens, lanes), low), vmem((tokens, 2 * lanes), low)]
-        + [all_blocks(), all_blocks(), dma((3,))]
+        + [all_blocks(), all_blocks(), dma((5,))]
+        + gather_semaphores(count)
+        + scatter(),
+    )
+
+    wide_carried = ((width, 2 * lanes), low, False)
+    rest_carried = [
+        ((down_rows, width), low, False),
+        ((3 * HEAD_DIM, width), low, False),
+        ((HEAD_DIM, width), low, False),
+    ]
+
+    back_scratch = (
+        [all_blocks(), all_blocks(), vmem((4, tokens, PAD), low)]
+        + weights_vm
+        + [vmem((tokens, PAD), low), vmem((tokens, tokens), f32)]
+        + [vmem((tokens, PAD), f32), vmem((tokens, PAD), f32), vmem((tokens, 3 * PAD), low)]
+        + [all_blocks(), dma((7,))]
         + gather_semaphores(count)
         + scatter()
-        + scatter(),
-    )
-
-    wide_carried = ((width, 2 * lanes), low, False), ((down_rows, width), low, False)
-    attn_carried = ((3 * HEAD_DIM, width), low, False), ((HEAD_DIM, width), low, False)
-
-    def attention_back(layer, branch, grad_hidden, x_own, rows_all, heads, log_total, carries):
-        return call_kernel(
-            functools.partial(attn_back_kernel, count, layer),
-            ("first", "second")[layer] + "_attention_back",
-            7 + layer,
+    )
+
+    def back_operands(layer, branch, grad_hidden, x_own, rows_all, heads, log_total):
+        return (
             [(branch, True), (grad_hidden, True), (x_own, True)]
-            + [(rows_all, False), (heads, False), (log_total, True), (attn, False), (out, False)]
+            + [(rows_all, False), (heads, False), (log_total, True)]
+            + [(attn, False), (twin, False), (out, False)]
             + tables
             + [(gains[layer, 0:1], True)]
-            + [(array, False) for array in carries],
-            [
-                own_low,
-                gain_rows,
-                ((3 * HEAD_DIM, width), low, True),
-                ((HEAD_DIM, width), low, True),
-                *wide_carried,
-            ],
-            [all_blocks(), all_blocks(), vmem((4, tokens, PAD), low)]
-            + weights_vm
-            + [vmem((tokens, PAD), low), vmem((tokens, tokens), f32)]
-            + [vmem((tokens, PAD), f32), vmem((tokens, PAD), f32), vmem((tokens, 3 * PAD), low)]
-            + [all_blocks(), dma((7,)), dma((2,)), dma((2,))]
-            + gather_semaphores(count)
-            + scatter(),
-        )
-
-    grad_between, gain_attn_two, attn_two, out_two, *wide_held_two = attention_back(
-        1,
-        branch,
-        grad_hidden,
-        between,
-        rows_two,
-        heads_two,
-        total_two,
-        (wide_two, down_two),
-    )
-    branch, grad_hidden, gain_mlp_one, wide_one, down_one, *attn_held_two = call_kernel(
+        )
+
+    attn_shape, out_shape = (3 * HEAD_DIM, width), (HEAD_DIM, width)
+    grad_between, gain_attn_two, attn_two, out_two, wide_from_one = call_kernel(
+        functools.partial(attn_back_kernel, count, 1),
+        "second_attention_back",
+        8,
+        back_operands(1, branch, grad_hidden, between, rows_two, heads_two, total_two)
+        + [(wide_two, False)],
+        [own_low, gain_rows, (attn_shape, low, True), (out_shape, low, True), wide_carried],
+        back_scratch + [dma((1,)), dma((1,))],
+    )
+    branch, grad_hidden, gain_mlp_one, wide_one, down_one, *rest_from_one = call_kernel(
         functools.partial(mlp_back_kernel, count),
         "first_feed_forward_back",
         9,
@@ -1988,45 +2255,39 @@
             (gate_up, False),
             (down, False),
             (gains[0, 1:2], True),
+            (down_two, False),
             (attn_two, False),
             (out_two, False),
         ],
-        [own_low, own_wide, gain_rows] + wide_outputs + list(attn_carried),
+        [own_low, own_wide, gain_rows] + wide_outputs + rest_carried,
         [all_blocks(), all_blocks(), wide_vm, down_vm]
         + [vmem((tokens, lanes), low), vmem((tokens, 2 * lanes), f32)]
-        + [vmem((tokens, 2 * lanes), low), all_blocks(), dma((3,)), dma((2,)), dma((2,))]
+        + [vmem((tokens, 2 * lanes), low), all_blocks(), dma((3,)), dma((3,)), dma((3,))]
         + gather_semaphores(count)
         + scatter(),
     )
-    grad_start, gain_attn_one, attn_one, out_one, *wide_held_one = attention_back(
-        0,
-        branch,
-        grad_hidden,
-        rows_own,
-        rows_one,
-        heads_one,
-        total_one,
-        (wide_one, down_one),
+    down_from_one, attn_from_one, out_from_one = rest_from_one
+    swapped_rows, final, grad_start, gain_sums, query, key, value, out, gate, up, down = last_layer(
+        count,
+        back_operands(0, branch, grad_hidden, rows_own, rows_one, heads_one, total_one)
+        + [(wide_one, False), (down_one, False), (attn_two, False), (out_two, False)]
+        + [(wide_two, False), (down_two, False), (wide_from_one, False), (down_from_one, False)]
+        + [(attn_from_one, False), (out_from_one, False), (ahead, False)]
+        + [(gain_mlp_one, True), (gain_attn_two, True), (gain_mlp_two, True)]
+        + [(between, True), (grad_between, True), (hidden_two, True)],
+        (
+            attn_shape,
+            out_shape,
+            (width, 2 * lanes),
+            (down_rows, width),
+            block,
+            width,
+            gain_rows[0][0],
+        ),
+        back_scratch,
     )
     kept = jnp.where(
         at_first, jnp.stack([between, grad_start]), jnp.stack([final, grad_between])
-    )
-    sent = jnp.where(
-        at_first, jnp.stack([final, grad_between]), jnp.stack([between, grad_start])
-    )
-    gain_sums = jnp.stack(
-        [
-            jnp.concatenate([gain_attn_one[0:4], gain_mlp_one[0:4]]),
-            jnp.concatenate([gain_attn_two[0:4], gain_mlp_two[0:4]]),
-        ]
-    )
-    swapped_rows, gain_sums, query, key, value, out, gate, up, down = finish_grads(
-        (attn_one, out_one, wide_one, down_one),
-        (attn_two, out_two, wide_two, down_two),
-        wide_held_one,
-        wide_held_two + attn_held_two,
-        gain_sums,
-        sent,
     )
     pairs = jnp.where(
         at_first, jnp.stack([kept, swapped_rows], axis=1), jnp.stack([swapped_rows, kept], axis=1)

time: 602 us -> 548 us (0.910)
  Pallas kernels: 547 us -> 500 us
    pallas_call x1 -> x0, Pallas kernels: 95 us -> none  [finish_grads(): pl.pallas_call(functools.partial(finish_kernel, count), out_shape=[jax.Sh...]
    pallas_call x6, Pallas kernels: 452 us -> 500 us  [call_kernel(): pl.pallas_call(kernel, out_shape=[jax.ShapeDtypeStruct(shape, dtype) for...]
where the time goes in v6:
time: 548 us; the launch traced here: 541 us
  Pallas kernels  500 us (91%)
  other arithmetic  23.8 us (4%)
  local copies, waits for them, and re-layouts  13.5 us (2%)
    pallas_call x6, Pallas kernels, call_kernel(): pl.pallas_call(kernel, out_shape=[jax.ShapeDtypeStruct(shape, dtype) for...  500 us

profile of v6, /device:TPU:18, one launch (start us, length us, event | category | flops | bytes accessed | tf_op | source)
XLA Modules:
  0.0 540.9 jit_solution(7696206614576410250)
XLA Ops:
  2.9 1.6 convolution_convert_fusion
  4.6 0.8 convolution_convert_fusion.1
  5.4 0.9 pad_maximum_fusion.refs_0_
  7.1 1.0 copy.35.refs_9_.refs_8_.refs_11_
  8.1 3.1 fusion.12
  11.2 129.6 %first_layer.1 = (bf16[2,208,1536]{2,1,0:T(8,128)(2,1)}, bf16[2,96,1536]{2,1,0:T(8,128)(2,1)}, bf16[2,1536,512]{2,1,0:T(8,128)(2,1)}, bf16[2,96,1536]{2,1,0:T(8,...) custom-call(bf16[4,208,384]{2,1,0:T(8,128)(2,1)} %pad_maximum_fusion, ...), custom_call_target="tpu_custom_call" | custom-call | tf_op jit(solution)/shard_map/first_layer/pallas_call | solution.py:2026
  140.8 0.8 slice_convert_fusion
  142.2 53.8 %second_attention.1 = (f32[64,1536]{1,0:T(8,128)}, bf16[64,1536]{1,0:T(8,128)(2,1)}, bf16[16,64,1536]{2,1,0:T(8,128)(2,1)}, bf16[4,1024,128]{2,1,0:T(8,128)(2,1)...) custom-call(bf16[64,1536]{1,0:T(8,128)(2,1)} %get-tuple-element.60.refs_0_, ...), custom_call_target="tpu_custom_call" | custom-call | tf_op jit(solution)/shard_map/second_attention/pallas_call | solution.py:2026
  196.0 51.5 %second_feed_forward.1 = (bf16[16,64,1536]{2,1,0:T(8,128)(2,1)}, bf16[64,1536]{1,0:T(8,128)(2,1)}, f32[64,1536]{1,0:T(8,128)}, f32[8,1536]{1,0:T(8,128)}, bf16[1...) custom-call(bf16[64,1536]{1,0:T(8,128)(2,1)} %get-tuple-element.65.refs_0_, ...), custom_call_target="tpu_custom_call" | custom-call | tf_op jit(solution)/shard_map/second_feed_forward/pallas_call | solution.py:2026
  247.5 52.7 %second_attention_back.1 = (bf16[64,1536]{1,0:T(8,128)(2,1)}, f32[8,1536]{1,0:T(8,128)}, bf16[288,1536]{1,0:T(8,128)(2,1)}, bf16[96,1536]{1,0:T(8,128)(2,1)}, bf16[1536,512]{1,0:T(8,128)(2,1)}) custom-call(bf16[64,1536]{1,0:T(8,128)(2,1)} %get-tuple-element.71.refs_0_, f32[64,1536]{1,0:T(8,128)} %get-tuple-element.72.refs_1_, ...), custom_call_target="tpu_custom_call" | custom-call | tf_op jit(solution)/shard_map/second_attention_back/pallas_call | solution.py:2026
  300.3 50.0 %first_feed_forward_back.1 = (bf16[64,1536]{1,0:T(8,128)(2,1)}, f32[64,1536]{1,0:T(8,128)}, f32[8,1536]{1,0:T(8,128)}, bf16[1536,512]{1,0:T(8,128)(2,1)}, bf16[2...) custom-call(bf16[64,1536]{1,0:T(8,128)(2,1)} %get-tuple-element.77.refs_0, ...), custom_call_target="tpu_custom_call" | custom-call | tf_op jit(solution)/shard_map/first_feed_forward_back/pallas_call | solution.py:2026
  350.3 162.2 %last_layer_back.1 = (bf16[16,288,384]{2,1,0:T(8,128)(2,1)}, bf16[384,1536]{1,0:T(8,128)(2,1)}, bf16[384,4096]{1,0:T(8,128)(2,1)}, bf16[384,4096]{1,0:T(8,128)(2...) custom-call(bf16[64,1536]{1,0:T(8,128)(2,1)} %get-tuple-element.83.r, ...), custom_call_target="tpu_custom_call" | custom-call | tf_op jit(solution)/shard_map/last_layer_back/pallas_call | solution.py:2026
  512.5 1.2 maximum_select_fusion.1
  513.7 1.3 maximum_select_fusion
  514.9 0.9 slice_bitcast_fusion
  515.9 1.7 fusion.18
  517.6 1.7 bitcast_convert_fusion.3
  519.3 1.6 slice.54
  520.9 3.0 copy.39
  525.1 1.4 copy.43
  526.4 1.4 copy.42
  527.8 5.5 %bitcast_convert_fusion.2 = f32[1,384,4096]{2,1,0:T(8,128)} fusion(bf16[384,4096]{1,0:T(8,128)(2,1)} %get-tuple-element.104), kind=kLoop, calls=%fused_computation.2 | loop fusion | flops 1572864 | bytes 9437184 | tf_op jit(solution)/shard_map/broadcast_in_dim | solution.py:2304
  533.3 3.5 bitcast_convert_fusion.1
  536.8 3.6 bitcast_convert_fusion
  (40 shorter events, 4.7 us)
Async XLA Ops:
  0.6 3.9 copy-start
  4.5 1.8 copy-start.8
  4.6 1.7 copy-start.9
  350.3 162.2 %copy-start.3 = (bf16[64,1536]{1,0:T(8,128)(2,1)S(1)}, bf16[64,1536]{1,0:T(8,128)(2,1)}, u32[]{:S(2)}) copy-start(bf16[64,1536]{1,0:T(8,128)(2,1)} %get-tuple-element.59.refs_1_.refs_2_.refs_27_) | copy-start | bytes 589828
  350.3 162.2 %copy-start.6 = (bf16[64,1536]{1,0:T(8,128)(2,1)S(1)}, bf16[64,1536]{1,0:T(8,128)(2,1)}, u32[]{:S(2)}) copy-start(bf16[64,1536]{1,0:T(8,128)(2,1)} %get-tuple-element.77.refs_0_.refs_28_) | copy-start | bytes 589828
  512.5 5.1 copy-start.7
  514.9 4.3 copy-start.2
  527.8 5.5 %copy-start.5 = (bf16[384,4096]{1,0:T(8,128)(2,1)S(1)}, bf16[384,4096]{1,0:T(8,128)(2,1)}, u32[]{:S(2)}) copy-start(bf16[384,4096]{1,0:T(8,128)(2,1)} %get-tuple-element.105) | copy-start | bytes 9437188
  533.3 3.5 copy-start.4
  536.8 3.6 copy-start.1

commit v7 on v6

--- a/solution.py
+++ b/solution.py
@@ -641,9 +641,11 @@
     ]
 
 
-def line_steps(count, own, out, line_sent, line_got, core_sent, core_got, local_done):
+def line_steps(
+    count, own, out, line_sent, line_got, core_sent, core_got, local_done, offset=0
+):
     seq, b = lax.axis_index("seq"), lax.axis_index("blk")
-    core, base = {"seq": seq ^ 1}, (seq % 2) * count
+    core, base = {"seq": seq ^ 1}, offset + (seq % 2) * count
     cut = out.shape[1] // CUTS
 
     def spot(j, h):
@@ -682,7 +684,8 @@
     local.wait()
     for h in range(CUTS):
         for j in range(count):
-            settled(out.at[(1 - seq % 2) * count + j, pl.ds(h * cut, cut)], core_got.at[j, h], True)
+            place = offset + (1 - seq % 2) * count + j
+            settled(out.at[place, pl.ds(h * cut, cut)], core_got.at[j, h], True)
             to_core(j, h).wait_send()
         pl.when(b > 0)(along_line(b, 0, h).wait_send)
         pl.when(b < count - 1)(along_line(b, 1, h).wait_send)
@@ -1078,60 +1081,6 @@
     return ref[3 * PAD : 3 * PAD + 16][row : row + 1].astype(jnp.float32)
 
 
-def attn_kernel(count, *refs):
-    refs = iter(refs)
-
-    def take(n):
-        return [next(refs) for _ in range(n)]
-
-    rows_in, x_own, grads_in, attn, twin, out, cosine, sine, start = take(9)
-    hidden_out, normed_out, all_rows, heads, log_total, grads_all = take(6)
-    rows_vm, attn_vm, out_vm, partial, grads_vm, load_done, save_done = take(7)
-    gather_sems, grads_sems = take(7), take(5)
-    scatter_refs = list(refs)
-    block = rows_vm.shape[1]
-    tokens = block * rows_vm.shape[0]
-    size = count * block
-    greet_group(count)
-    steps = gather_steps(count, rows_in, rows_vm, *gather_sems)
-    next(steps)
-    clear_pads(attn_vm, out_vm)
-    loads = load_weights(1, attn, twin, out, attn_vm, out_vm, load_done)
-    for event in steps:
-        if event == "line":
-            wait_all(loads)
-        group = group_of(event)
-        if group is not None:
-            span = group_span(group, count, block)
-            normed = group_rows(rows_vm, group, count)
-            project_heads(normed, attn_vm, heads, span, cosine, sine)
-    grad_steps = line_steps(count, grads_in, grads_vm, *grads_sems)
-    next(grad_steps)
-    save = pltpu.make_async_copy(rows_vm, all_rows, save_done.at[0])
-    save.start()
-    attention_rows(heads, log_total, start, size, tokens)
-
-    def project_out(group):
-        mixed = heads[3, group_span(group, count, block)]
-        keep_group(partial, group, product(mixed, out_vm[...]), count)
-
-    def deliver(total):
-        hidden = x_own[...].astype(jnp.float32) + total
-        hidden_out[...] = hidden
-        normed_out[...] = normalise(hidden, gain_of(attn_vm, 1)).astype(jnp.bfloat16)
-
-    run_with(
-        scatter_steps(count, partial, deliver, *scatter_refs, compute=project_out),
-        [functools.partial(advance, grad_steps, 1)] * 3,
-    )
-    for _ in grad_steps:
-        pass
-    keep = pltpu.make_async_copy(grads_vm, grads_all, save_done.at[1])
-    keep.start()
-    keep.wait()
-    save.wait()
-
-
 def first_layer_kernel(count, *refs):
     refs = iter(refs)
 
@@ -1421,132 +1370,6 @@
     gain_out[...] = jnp.broadcast_to(jnp.sum(terms, axis=0, keepdims=True), gain_out.shape)
 
 
-def mlp_both_kernel(count, *refs):
-    refs = iter(refs)
-
-    def take(n):
-        return [next(refs) for _ in range(n)]
-
-    rows_in, hidden, gate_up, down, grads_near, grads_far, grads_own, gain = take(8)
-    ahead_out, branch_out, grad_hidden_out, gain_out, wide_grad, down_grad = take(6)
-    rows_vm, grads_vm, wide_vm, down_vm, units, pre_grads, partial, partial_back = take(8)
-    (load_done,) = take(1)
-    size = count * rows_vm.shape[1]
-    half = rows_vm.shape[0] // 2
-    near = lax.axis_index("seq") // 2 * half
-    gather_sems = take(7)
-    scatter_back = list(refs)
-    block = rows_vm.shape[1]
-    greet_group(count)
-    steps = gather_steps(count, rows_in, rows_vm, *gather_sems)
-    next(steps)
-    loads = [
-        pltpu.make_async_copy(gate_up.at[1], wide_vm, load_done.at[0]),
-        pltpu.make_async_copy(down.at[1], down_vm, load_done.at[1]),
-        pltpu.make_async_copy(grads_near, grads_vm.at[pl.ds(near, half)], load_done.at[2]),
-        pltpu.make_async_copy(grads_far, grads_vm.at[pl.ds(half - near, half)], load_done.at[4]),
-    ]
-    start_all(loads)
-
-    def through(group):
-        span = group_span(group, count, block)
-        pre = product(group_rows(rows_vm, group, count), wide_vm[...])
-        units[span] = hidden_units(pre)
-        grad_act = back_product(group_rows(grads_vm, group, count), down_vm[...])
-        store_gate_grads(pre_grads, span, grad_act, pre)
-        value = back_product(pre_grads[span], wide_vm[...])
-        partial_back[pl.ds(group * count, count)] = value.astype(jnp.bfloat16).reshape(
-            count, block, -1
-        )
-
-    for event in steps:
-        if event == "line":
-            wait_all(loads)
-        group = group_of(event)
-        if group is not None:
-            through(group)
-
-    def project_down(group):
-        value = product(units[group * size : (group + 1) * size], down_vm[...])
-        partial[group * count : (group + 1) * count] = value.astype(jnp.bfloat16).reshape(
-            count, block, -1
-        )
-
-    def deliver_back(total):
-        mlp_grad_sent(
-            total, hidden, grads_own, gain, branch_out, grad_hidden_out, gain_out
-        )
-
-    fillers = wide_grads(rows_vm, pre_grads, units, grads_vm, wide_grad, down_grad)
-    fillers += [functools.partial(project_down, group) for group in range(4)]
-    run_with(
-        scatter_steps(count, partial_back, deliver_back, *scatter_back),
-        [functools.partial(run_all, fillers[n::4]) for n in range(4)],
-    )
-    save = pltpu.make_async_copy(partial, ahead_out, load_done.at[3])
-    save.start()
-    save.wait()
-
-
-def mlp_back_kernel(count, *refs):
-    refs = iter(refs)
-
-    def take(n):
-        return [next(refs) for _ in range(n)]
-
-    grads_own, hidden, all_rows, gate_up, down, gain = take(6)
-    carry_from = take(3)
-    branch_out, grad_hidden_out, gain_out, wide_grad, down_grad = take(5)
-    carry_to = take(3)
-    rows_vm, grads_vm, wide_vm, down_vm, units, pre_vm, pre_grads, partial, load_done = take(9)
-    carry_sent, carry_got = take(2)
-    gather_sems = take(7)
-    scatter_refs = list(refs)
-    block = rows_vm.shape[1]
-    greet_group(count, ({"section": 1 - lax.axis_index("section")},))
-    steps = gather_steps(count, grads_own, grads_vm, *gather_sems)
-    next(steps)
-    copies = carried(carry_from, carry_to, carry_sent, carry_got)
-    carry(copies, 0, "start")
-    loads = [
-        pltpu.make_async_copy(gate_up.at[0], wide_vm, load_done.at[0]),
-        pltpu.make_async_copy(all_rows, rows_vm, load_done.at[1]),
-        pltpu.make_async_copy(down.at[0], down_vm, load_done.at[2]),
-    ]
-    start_all(loads)
-
-    def again(group):
-        span = group_span(group, count, block)
-        pre = product(group_rows(rows_vm, group, count), wide_vm[...])
-        pre_vm[span] = pre
-        units[span] = hidden_units(pre)
-
-    def through(group):
-        span = group_span(group, count, block)
-        grad_act = back_product(group_rows(grads_vm, group, count), down_vm[...])
-        store_gate_grads(pre_grads, span, grad_act, pre_vm[span])
-        value = back_product(pre_grads[span], wide_vm[...])
-        partial[pl.ds(group * count, count)] = value.astype(jnp.bfloat16).reshape(count, block, -1)
-
-    wait_all(loads)
-    for number, event in enumerate(steps):
-        if number < 2:
-            again(2 * number)
-            again(2 * number + 1)
-        group = group_of(event)
-        if group is not None:
-            through(group)
-
-    def deliver(total):
-        mlp_grad_sent(total, hidden, grads_own, gain, branch_out, grad_hidden_out, gain_out)
-
-    run_with(
-        scatter_steps(count, partial, deliver, *scatter_refs),
-        wide_grads(rows_vm, pre_grads, units, grads_vm, wide_grad, down_grad),
-    )
-    carry(copies, 0, "wait")
-
-
 class Parts:
     pass
 
@@ -1575,16 +1398,19 @@
     steps = gather_steps(count, branch_in, branch_vm, *r.gather_sems)
     next(steps)
     background()
-    clear_pads(attn_vm, out_vm)
-    loads = load_weights(layer, attn, twin, out, attn_vm, out_vm, load_done)
-    kept = [
-        pltpu.make_async_copy(heads_kept, heads, load_done.at[5]),
-        pltpu.make_async_copy(all_rows, rows_vm, load_done.at[6]),
-    ]
-    start_all(kept)
+    loads = []
+    if layer is not None:
+        clear_pads(attn_vm, out_vm)
+        loads = load_weights(layer, attn, twin, out, attn_vm, out_vm, load_done)
+        kept = [
+            pltpu.make_async_copy(heads_kept, heads, load_done.at[5]),
+            pltpu.make_async_copy(all_rows, rows_vm, load_done.at[6]),
+        ]
+        start_all(kept)
+        loads += kept
     key_grads[...] = jnp.zeros_like(key_grads)
     value_grads[...] = jnp.zeros_like(value_grads)
-    wait_all(loads + kept)
+    wait_all(loads)
 
     def spans(i):
         return slice(i * size, (i + 1) * size), slice(0, (i + 1) * size)
@@ -1649,23 +1475,165 @@
     )
 
 
-def attn_back_kernel(count, layer, *refs):
+def middle_kernel(count, *refs):
     refs = iter(refs)
 
     def take(n):
         return [next(refs) for _ in range(n)]
 
-    ins, carry_from, outs, carry_to = take(13), take(1), take(4), take(1)
+    rows_in, between, grads_side, cosine, sine, start, attn, twin, out = take(9)
+    grads_near, gate_up, down, grads_own, hidden_one, wide_rows = take(6)
+    gain_mlp_two, gain_attn_two, gain_mlp_one = take(3)
+    hidden, ahead, grad_between, branch_out, grad_hidden_out = take(5)
+    mlp_two_sum, attn_two_sum, mlp_one_sum = take(3)
+    wide_two, down_two, attn_two, out_two, wide_one, down_one = take(6)
+    carried_to = take(4)
+    rows_two, grads_vm, partial, wide_vm, down_vm = take(5)
+    log_total, units, pre_vm, pre_grads, normed_own, branch_own, grad_hidden = take(7)
+    load_done, carry_sent, carry_got = take(3)
+    line_sems = take(5)
     r = attn_back_refs(take)
-    carry_sent, carry_got = take(2)
+    rows_one, heads, attn_vm, out_vm, partial_back = (
+        r.rows_vm,
+        r.heads,
+        r.attn_vm,
+        r.out_vm,
+        r.partial,
+    )
+    blocks, block = rows_one.shape[0], rows_one.shape[1]
+    size, tokens, half = count * block, blocks * block, blocks // 2
+    near = lax.axis_index("seq") // 2 * half
     greet_group(count, ({"section": 1 - lax.axis_index("section")},))
-    copies = carried(carry_from, carry_to, carry_sent, carry_got)
+    steps = gather_steps(count, rows_in, rows_one, *r.gather_sems)
+    next(steps)
+    clear_pads(attn_vm, out_vm)
+    loads = load_weights(1, attn, twin, out, attn_vm, out_vm, r.load_done)
+    wide_loads = [
+        pltpu.make_async_copy(gate_up.at[1], wide_vm, load_done.at[0]),
+        pltpu.make_async_copy(down.at[1], down_vm, load_done.at[1]),
+        pltpu.make_async_copy(grads_near, grads_vm.at[pl.ds(near, half)], load_done.at[2]),
+    ]
+    start_all(wide_loads)
+    for event in steps:
+        if event == "line":
+            wait_all(loads)
+        group = group_of(event)
+        if group is not None:
+            span = group_span(group, count, block)
+            normed = group_rows(rows_one, group, count)
+            project_heads(normed, attn_vm, heads, span, cosine, sine)
+    grad_steps = line_steps(count, grads_side, grads_vm, *line_sems, offset=half - near)
+    next(grad_steps)
+    attention_rows(heads, log_total, start, size, tokens)
+
+    def project_out(group):
+        mixed = heads[3, group_span(group, count, block)]
+        keep_group(partial, group, product(mixed, out_vm[...]), count)
+
+    def deliver(total):
+        value = between[...].astype(jnp.float32) + total
+        hidden[...] = value
+        normed_own[...] = normalise(value, gain_of(attn_vm, 1)).astype(jnp.bfloat16)
+
+    run_with(
+        scatter_steps(count, partial, deliver, *r.scatter_refs, compute=project_out),
+        [functools.partial(advance, grad_steps, 1)] * 3,
+    )
+    steps = gather_steps(count, normed_own, rows_two, *r.gather_sems)
+    next(steps)
+    for _ in grad_steps:
+        pass
+    wait_all(wide_loads)
+
+    def through(group):
+        span = group_span(group, count, block)
+        pre = product(group_rows(rows_two, group, count), wide_vm[...])
+        units[span] = hidden_units(pre)
+        grad_act = back_product(group_rows(grads_vm, group, count), down_vm[...])
+        store_gate_grads(pre_grads, span, grad_act, pre)
+        keep_group(partial_back, group, back_product(pre_grads[span], wide_vm[...]), count)
+
+    for event in steps:
+        group = group_of(event)
+        if group is not None:
+            through(group)
+
+    def project_down(group):
+        value = product(units[group * size : (group + 1) * size], down_vm[...])
+        partial[group * count : (group + 1) * count] = value.astype(jnp.bfloat16).reshape(
+            count, block, -1
+        )
+
+    def deliver_two(total):
+        mlp_grad_sent(
+            total, hidden, grads_own, gain_mlp_two, branch_own, grad_hidden, mlp_two_sum
+        )
+
+    fillers = wide_grads(rows_two, pre_grads, units, grads_vm, wide_two, down_two)
+    fillers += [functools.partial(project_down, group) for group in range(4)]
+    run_with(
+        scatter_steps(count, partial_back, deliver_two, *r.scatter_refs),
+        [functools.partial(run_all, fillers[n::4]) for n in range(4)],
+    )
+    save = pltpu.make_async_copy(partial, ahead, load_done.at[3])
+    save.start()
+    copies = carried(
+        (wide_two, down_two, attn_two, out_two), carried_to, carry_sent, carry_got
+    )
 
     def background():
-        carry(copies, 1 - layer, "start")
-
-    attn_back_body(count, layer, r, ins, outs, background, [])
-    carry(copies, 1 - layer, "wait")
+        carry(copies[:2], 0, "start")
+        wide_loads[0] = pltpu.make_async_copy(gate_up.at[0], wide_vm, load_done.at[0])
+        wide_loads[1] = pltpu.make_async_copy(down.at[0], down_vm, load_done.at[1])
+        wide_loads[2] = pltpu.make_async_copy(wide_rows, rows_two, load_done.at[2])
+        start_all(wide_loads)
+
+    attn_back_body(
+        count,
+        None,
+        r,
+        (branch_own, grad_hidden, between, None, None, log_total, None, None, None)
+        + (cosine, sine, start, gain_attn_two),
+        (grad_between, attn_two_sum, attn_two, out_two),
+        background,
+        [],
+    )
+    carry(copies[2:], 0, "start")
+    steps = gather_steps(count, grad_between, grads_vm, *r.gather_sems)
+    next(steps)
+    wait_all(wide_loads)
+
+    def again(group):
+        span = group_span(group, count, block)
+        pre = product(group_rows(rows_two, group, count), wide_vm[...])
+        pre_vm[span] = pre
+        units[span] = hidden_units(pre)
+
+    def through_one(group):
+        span = group_span(group, count, block)
+        grad_act = back_product(group_rows(grads_vm, group, count), down_vm[...])
+        store_gate_grads(pre_grads, span, grad_act, pre_vm[span])
+        keep_group(partial_back, group, back_product(pre_grads[span], wide_vm[...]), count)
+
+    for number, event in enumerate(steps):
+        if number < 2:
+            again(2 * number)
+            again(2 * number + 1)
+        group = group_of(event)
+        if group is not None:
+            through_one(group)
+
+    def deliver_one(total):
+        mlp_grad_sent(
+            total, hidden_one, grad_between, gain_mlp_one, branch_out, grad_hidden_out, mlp_one_sum
+        )
+
+    run_with(
+        scatter_steps(count, partial_back, deliver_one, *r.scatter_refs),
+        wide_grads(rows_two, pre_grads, units, grads_vm, wide_one, down_one),
+    )
+    carry(copies, 0, "wait")
+    save.wait()
 
 
 def last_kernel(count, *refs):
@@ -1678,7 +1646,8 @@
     wide_one, down_one, attn_two, out_two, wide_two, down_two = take(6)
     wide_from_one, down_from_one, attn_from_one, out_from_one, ahead = take(5)
     gain_mlp_one, gain_attn_two, gain_mlp_two, between, grad_between, hidden = take(6)
-    attn, out, gate, up, down, gains_out, swapped_rows, final, grad_start = take(9)
+    attn, out, gate, up, down, gains_out, rows_out, grads_out = take(8)
+    final, grad_start = take(2)
     attn_grad, out_grad, gain_attn_one, gains = take(4)
     attn_own, out_own, wide_own, down_own, attn_in, out_in, wide_in, down_in = take(8)
     attn_slot, wide_slot = take(2)
@@ -1814,10 +1783,10 @@
     def small(n, source, slot, device):
         return remote(source, slot, small_sent.at[n], small_got.at[n], device)
 
-    swap_rest = small(4 + count, between, swapped_rows.at[0], other)
-    swap_final = small(4 + count, final, swapped_rows.at[0], other)
-    swap_between = small(0, grad_between, swapped_rows.at[1], other)
-    swap_start = small(0, grad_start, swapped_rows.at[1], other)
+    swap_rest = small(4 + count, between, rows_out.at[section], other)
+    swap_final = small(4 + count, final, rows_out.at[section], other)
+    swap_between = small(0, grad_between, grads_out.at[section], other)
+    swap_start = small(0, grad_start, grads_out.at[section], other)
     pl.when(at_second)(swap_rest.start)
     pl.when(at_first)(swap_between.start)
     wide_turns = [(1, k) for k in turns]
@@ -1835,6 +1804,7 @@
     def deliver(total):
         final[...] = (hidden[...] + total).astype(low)
         pl.when(at_first)(swap_final.start)
+        rows_out[section] = jnp.where(at_first, between[...], final[...])
 
     def later():
         load(0)
@@ -1850,6 +1820,10 @@
     def gathered():
         share(0)
         share(1)
+
+    def early():
+        add_up(1, 0)
+        publish(1, 0)
 
     ahead_steps = line_first_steps(count, ahead, deliver, *ahead_refs)
     attn_back_body(
@@ -1859,10 +1833,11 @@
         ins,
         (grad_start, gain_attn_one, attn_grad, out_grad),
         background,
-        [later, functools.partial(share, 2)],
+        [later, functools.partial(share, 2), early],
         gathered,
     )
     pl.when(at_second)(swap_start.start)
+    grads_out[section] = jnp.where(at_first, grad_start[...], grad_between[...])
     gains[0, 0:4] = gain_attn_one[0:4]
     gains[0, 4:8] = gain_mlp_one[4:8]
     gains[1, 0:4] = gain_attn_two[0:4]
@@ -1877,37 +1852,35 @@
         j = lax.rem(b + k, count)
         return small(3 + k, gain_piece(j), gain_line.at[k], {"blk": j})
 
-    add_up(1, 0)
-    publish(1, 0)
-    from_line(1, turns[0])
-    from_line(1, turns[1])
     loaded(0)
     for k in turns[:-1]:
         add_up(0, k)
         along_line(0, k).start()
+    from_line(1, turns[0])
     add_up(0, 0)
     publish(0, 0)
-    from_line(1, turns[2])
+    from_line(1, turns[1])
     from_side(1, 0)
     loaded(2)
     add_up(2, 0)
     publish(2, 0)
+    from_line(1, turns[2])
+    next(ahead_steps)
     from_side(1, turns[0])
-    from_side(1, turns[1])
-    for k in turns[:-1]:
-        from_line(0, k)
+    from_side(0, 0)
     loaded(3)
     add_up(3, 0)
     publish(3, 0)
-    next(ahead_steps)
-    from_side(0, 0)
-    from_side(1, turns[2])
+    for k in turns[:-1]:
+        from_line(0, k)
+    from_side(1, turns[1])
     gain_cross.wait_recv()
     gain_sum[...] = gains[section] + gain_in[...]
     for k in range(1, count):
         gain_send(k).start()
     advance(ahead_steps, 2)
     from_side(2, 0)
+    from_side(1, turns[2])
     for k in range(1, count):
         gain_send(k).wait_recv()
     gain_part[...] = gain_sum[:, pl.ds(pl.multiple_of(b * rows, rows), rows)]
@@ -1915,17 +1888,16 @@
         gain_part[...] += gain_line[k]
     gain_to_side = small(2, gain_part.at[:], gain_side.at[:], side)
     gain_to_side.start()
-    advance(ahead_steps, 2)
-    for k in turns[:-1]:
-        from_side(0, k)
-    advance(ahead_steps, 2)
+    advance(ahead_steps, 4)
+    from_side(3, 0)
     gain_to_side.wait_recv()
     gain_side[...] += gain_part[...]
     gain_to_core = small(3, gain_side.at[:], gain_core.at[:], core)
     gain_to_core.start()
-    from_side(3, 0)
     for _ in ahead_steps:
         pass
+    for k in turns[:-1]:
+        from_side(0, k)
     gain_to_core.wait_recv()
     gains_out[...] = gain_side[...] + gain_core[...]
     every = [(0, k) for k in range(count)] + [(1, k) for k in range(count)] + [(2, 0), (3, 0)]
@@ -1951,6 +1923,57 @@
     gain_to_core.wait_send()
 
 
+def widen_kernel(pieces, attn, out, gate, up, down, query, key, value, out_f, gate_f, up_f, down_f):
+    f32 = jnp.float32
+    out_f[...] = out[...].astype(f32)
+    gate_f[...] = gate[...].astype(f32)
+    up_f[...] = up[...].astype(f32)
+    down_f[...] = down[...].astype(f32)
+
+    @pl.when(pl.program_id(0) < pieces)
+    def _():
+        parts, _, lanes = attn.shape
+        copies = HEADS // KV_HEADS
+
+        def heads(n):
+            return attn[:, n * HEAD_DIM : (n + 1) * HEAD_DIM].astype(f32)
+
+        query[...] = heads(0).reshape(parts * HEAD_DIM, lanes).T
+        for n, place in ((1, key), (2, value)):
+            total = heads(n).reshape(parts // copies, copies, HEAD_DIM, lanes).sum(1)
+            place[...] = total.reshape(parts // copies * HEAD_DIM, lanes).T
+
+
+def widen(attn, out, gate, up, down):
+    f32 = jnp.float32
+    parts, heads, rows = attn.shape
+    lanes = 128
+    pieces = rows // lanes
+    steps = 8
+    width = parts * HEAD_DIM
+    narrow = width * KV_HEADS // HEADS
+
+    def rows_of(array):
+        return pl.BlockSpec((array.shape[0] // steps, array.shape[1]), lambda i: (i, 0))
+
+    def turned(columns):
+        return pl.BlockSpec((lanes, columns), lambda i: (jnp.minimum(i, pieces - 1), 0))
+
+    flat = [out, gate, up, down]
+    taken = pl.BlockSpec((parts, heads, lanes), lambda i: (0, 0, jnp.minimum(i, pieces - 1)))
+    shapes = [(rows, width), (rows, narrow), (rows, narrow)] + [array.shape for array in flat]
+    return pl.pallas_call(
+        functools.partial(widen_kernel, pieces),
+        grid=(steps,),
+        out_shape=[jax.ShapeDtypeStruct(shape, f32) for shape in shapes],
+        in_specs=[taken] + [rows_of(array) for array in flat],
+        out_specs=[turned(width), turned(narrow), turned(narrow)]
+        + [rows_of(array) for array in flat],
+        compiler_params=pltpu.CompilerParams(vmem_limit_bytes=48 * 2**20),
+        name="widen_gradients",
+    )(attn, out, gate, up, down)
+
+
 def last_layer(count, operands, like, back_scratch):
     attn, out, wide, down, block, width, gain_rows = like
     low, f32 = jnp.bfloat16, jnp.float32
@@ -1975,11 +1998,11 @@
         ((down[0] * seq_count, down[1]), low, False),
         (small, f32, True),
         ((2, block, width), low, True),
-        ((block, width), low, True),
-        ((block, width), low, True),
+        ((2, block, width), low, True),
     ]
     scratch = (
-        [vmem(attn, low), vmem(out, low), vmem((gain_rows, width), f32)]
+        [vmem((block, width), low), vmem((block, width), low)]
+        + [vmem(attn, low), vmem(out, low), vmem((gain_rows, width), f32)]
         + [vmem((2, gain_rows, width), f32)]
         + [vmem(shape, low) for shape in (attn, out, wide, down)] * 2
         + [vmem((count, heads, rows), low), vmem((count, rows, 2 * lanes), low)]
@@ -1995,29 +2018,11 @@
         + [dma((2, 2, count)), dma, dma]
         + back_scratch
     )
-    attn, out, gate, up, down, gains, swapped_rows, final, grad_start = call_kernel(
+    attn, out, gate, up, down, gains, rows_out, grads_out = call_kernel(
         functools.partial(last_kernel, count), "last_layer_back", 3, operands, outputs, scratch
     )
-    attn = attn.astype(f32)
-
-    def heads_back(start, copies):
-        part = attn[:, start : start + HEAD_DIM].reshape(-1, copies, HEAD_DIM, rows).sum(1)
-        return part.reshape(-1, rows).T
-
-    copies = HEADS // KV_HEADS
-    return (
-        swapped_rows,
-        final,
-        grad_start,
-        gains,
-        heads_back(0, 1),
-        heads_back(HEAD_DIM, copies),
-        heads_back(2 * HEAD_DIM, copies),
-        out.astype(f32),
-        gate.astype(f32),
-        up.astype(f32),
-        down.astype(f32),
-    )
+    query, key, value, out, gate, up, down = widen(attn, out, gate, up, down)
+    return rows_out, grads_out, gains, query, key, value, out, gate, up, down
 
 
 def call_kernel(kernel, name, number, operands, outputs, scratch):
@@ -2109,13 +2114,6 @@
     own_low, own_wide = ((block, width), low, True), ((block, width), f32, True)
     every = ((blocks, block, width), low, False)
     gain_rows = ((8, width), f32, True)
-    attn_outputs = [
-        own_wide,
-        own_low,
-        every,
-        ((4, tokens, PAD), low, True),
-        ((tokens, 1), f32, True),
-    ]
     weights_vm = [vmem((3 * PAD + 16, width), low), vmem((PAD, width), low)]
     wide_vm, down_vm = vmem((width, 2 * lanes), low), vmem((down_rows, width), low)
     tables = [(cosine, True), (sine, True), (start, True)]
@@ -2170,51 +2168,6 @@
         + scatter(),
     )
     gains = attn[:, GAINS : GAINS + 2].astype(f32)
-    hidden_two, normed, rows_two, heads_two, total_two, grads_far = call_kernel(
-        functools.partial(attn_kernel, count),
-        "second_attention",
-        4,
-        [(normed, True), (between, True), (grads_side, True)]
-        + [(attn, False), (twin, False), (out, False)]
-        + tables,
-        attn_outputs + [half],
-        [all_blocks()]
-        + weights_vm
-        + [all_blocks(), half_blocks, dma((5,)), dma((2,))]
-        + gather_semaphores(count)
-        + line_semaphores(count)
-        + scatter(),
-    )
-    wide_outputs = [((width, 2 * lanes), low, True), ((down_rows, width), low, True)]
-    ahead, branch, grad_hidden, gain_mlp_two, wide_two, down_two = call_kernel(
-        functools.partial(mlp_both_kernel, count),
-        "second_feed_forward",
-        6,
-        [
-            (normed, True),
-            (hidden_two, True),
-            (gate_up, False),
-            (down, False),
-            (grads_near, False),
-            (grads_far, False),
-            (grads_own, True),
-            (gains[1, 1:2], True),
-        ],
-        [every, own_low, own_wide, gain_rows] + wide_outputs,
-        [all_blocks(), all_blocks(), wide_vm, down_vm]
-        + [vmem((tokens, lanes), low), vmem((tokens, 2 * lanes), low)]
-        + [all_blocks(), all_blocks(), dma((5,))]
-        + gather_semaphores(count)
-        + scatter(),
-    )
-
-    wide_carried = ((width, 2 * lanes), low, False)
-    rest_carried = [
-        ((down_rows, width), low, False),
-        ((3 * HEAD_DIM, width), low, False),
-        ((HEAD_DIM, width), low, False),
-    ]
-
     back_scratch = (
         [all_blocks(), all_blocks(), vmem((4, tokens, PAD), low)]
         + weights_vm
@@ -2224,52 +2177,59 @@
         + gather_semaphores(count)
         + scatter()
     )
-
-    def back_operands(layer, branch, grad_hidden, x_own, rows_all, heads, log_total):
-        return (
-            [(branch, True), (grad_hidden, True), (x_own, True)]
-            + [(rows_all, False), (heads, False), (log_total, True)]
-            + [(attn, False), (twin, False), (out, False)]
-            + tables
-            + [(gains[layer, 0:1], True)]
-        )
-
     attn_shape, out_shape = (3 * HEAD_DIM, width), (HEAD_DIM, width)
-    grad_between, gain_attn_two, attn_two, out_two, wide_from_one = call_kernel(
-        functools.partial(attn_back_kernel, count, 1),
-        "second_attention_back",
-        8,
-        back_operands(1, branch, grad_hidden, between, rows_two, heads_two, total_two)
-        + [(wide_two, False)],
-        [own_low, gain_rows, (attn_shape, low, True), (out_shape, low, True), wide_carried],
-        back_scratch + [dma((1,)), dma((1,))],
-    )
-    branch, grad_hidden, gain_mlp_one, wide_one, down_one, *rest_from_one = call_kernel(
-        functools.partial(mlp_back_kernel, count),
-        "first_feed_forward_back",
-        9,
-        [
-            (grad_between, True),
-            (hidden_one, True),
-            (wide_rows_one, False),
-            (gate_up, False),
-            (down, False),
-            (gains[0, 1:2], True),
-            (down_two, False),
-            (attn_two, False),
-            (out_two, False),
-        ],
-        [own_low, own_wide, gain_rows] + wide_outputs + rest_carried,
-        [all_blocks(), all_blocks(), wide_vm, down_vm]
-        + [vmem((tokens, lanes), low), vmem((tokens, 2 * lanes), f32)]
-        + [vmem((tokens, 2 * lanes), low), all_blocks(), dma((3,)), dma((3,)), dma((3,))]
-        + gather_semaphores(count)
-        + scatter(),
-    )
-    down_from_one, attn_from_one, out_from_one = rest_from_one
-    swapped_rows, final, grad_start, gain_sums, query, key, value, out, gate, up, down = last_layer(
+    wide_shape, down_shape = (width, 2 * lanes), (down_rows, width)
+    (
+        hidden_two,
+        ahead,
+        grad_between,
+        branch,
+        grad_hidden,
+        gain_mlp_two,
+        gain_attn_two,
+        gain_mlp_one,
+        wide_two,
+        down_two,
+        attn_two,
+        out_two,
+        wide_one,
+        down_one,
+        wide_from_one,
+        down_from_one,
+        attn_from_one,
+        out_from_one,
+    ) = call_kernel(
+        functools.partial(middle_kernel, count),
+        "second_layer",
+        4,
+        [(normed, True), (between, True), (grads_side, True)]
+        + tables
+        + [(attn, False), (twin, False), (out, False)]
+        + [(grads_near, False), (gate_up, False), (down, False)]
+        + [(grads_own, True), (hidden_one, True), (wide_rows_one, False)]
+        + [(gains[1, 1:2], True), (gains[1, 0:1], True), (gains[0, 1:2], True)],
+        [own_wide, every, own_low, own_low, own_wide, gain_rows, gain_rows, gain_rows]
+        + [(wide_shape, low, True), (down_shape, low, True)]
+        + [(attn_shape, low, True), (out_shape, low, True)]
+        + [(wide_shape, low, True), (down_shape, low, True)]
+        + [(shape, low, False) for shape in (wide_shape, down_shape, attn_shape, out_shape)],
+        [all_blocks(), all_blocks(), all_blocks(), wide_vm, down_vm]
+        + [vmem((tokens, 1), f32), vmem((tokens, lanes), low), vmem((tokens, 2 * lanes), f32)]
+        + [vmem((tokens, 2 * lanes), low), vmem((block, width), low), vmem((block, width), low)]
+        + [vmem((block, width), f32), dma((4,)), dma((4,)), dma((4,))]
+        + line_semaphores(count)
+        + back_scratch,
+    )
+    back_operands = (
+        [(branch, True), (grad_hidden, True), (rows_own, True)]
+        + [(rows_one, False), (heads_one, False), (total_one, True)]
+        + [(attn, False), (twin, False), (out, False)]
+        + tables
+        + [(gains[0, 0:1], True)]
+    )
+    rows_out, grads_out, gain_sums, query, key, value, out, gate, up, down = last_layer(
         count,
-        back_operands(0, branch, grad_hidden, rows_own, rows_one, heads_one, total_one)
+        back_operands
         + [(wide_one, False), (down_one, False), (attn_two, False), (out_two, False)]
         + [(wide_two, False), (down_two, False), (wide_from_one, False), (down_from_one, False)]
         + [(attn_from_one, False), (out_from_one, False), (ahead, False)]
@@ -2278,23 +2238,17 @@
         (
             attn_shape,
             out_shape,
-            (width, 2 * lanes),
-            (down_rows, width),
+            wide_shape,
+            down_shape,
             block,
             width,
             gain_rows[0][0],
         ),
         back_scratch,
     )
-    kept = jnp.where(
-        at_first, jnp.stack([between, grad_start]), jnp.stack([final, grad_between])
-    )
-    pairs = jnp.where(
-        at_first, jnp.stack([kept, swapped_rows], axis=1), jnp.stack([swapped_rows, kept], axis=1)
-    )
     return (
-        pairs[0][None, :, None],
-        pairs[1][None, :, None],
+        rows_out[None, :, None],
+        grads_out[None, :, None],
         gain_sums[0][None],
         query[None],
         key[None],

time: 548 us -> 518 us (0.945)
  other arithmetic: 23.8 us -> 5.99 us
  Pallas kernels: 500 us -> 491 us
    pallas_call x6 -> x3, Pallas kernels: 500 us -> 478 us  [call_kernel(): pl.pallas_call(kernel, out_shape=[jax.ShapeDtypeStruct(shape, dtype) for...]
    broadcast_in_dim x4 -> x0, other arithmetic: 14.3 us -> none  [the longest x1 5.51 us: head_shards(): gate[None]]
    pallas_call x0 -> x1, Pallas kernels: none -> 13 us  [widen(): pl.pallas_call(functools.partial(widen_kernel, pieces), grid=(steps,), ou...]
where the time goes in v7:
time: 518 us; the launch traced here: 510 us
  Pallas kernels  491 us (95%)
  local copies, waits for them, and re-layouts  9.44 us (2%)
  other arithmetic  5.99 us (1%)
    pallas_call x3, Pallas kernels, call_kernel(): pl.pallas_call(kernel, out_shape=[jax.ShapeDtypeStruct(shape, dtype) for...  478 us
    pallas_call x1, Pallas kernels, widen(): pl.pallas_call(functools.partial(widen_kernel, pieces), grid=(steps,), ou...  13 us

profile of v7, /device:TPU:18, one launch (start us, length us, event | category | flops | bytes accessed | tf_op | source)
XLA Modules:
  0.0 510.4 jit_solution(15974929390058699350)
XLA Ops:
  0.7 0.1 pad.5.clone
  0.8 0.7 fusion.17
  1.5 0.2 reduce-window.8
  1.8 0.1 add.89
  2.0 0.1 add.95
  2.0 0.1 select_reduce_fusion
  2.1 0.8 maximum_maximum_fusion
  2.9 1.6 convolution_convert_fusion
  4.6 0.8 convolution_convert_fusion.1
  5.4 0.9 pad_maximum_fusion.refs_0_
  6.3 0.8 dynamic-slice_bitcast_fusion
  7.1 1.0 copy.30.refs_9_.refs_5_.refs_11_
  8.1 3.1 fusion.12
  11.2 129.6 %first_layer.1 = (bf16[2,208,1536]{2,1,0:T(8,128)(2,1)}, bf16[2,96,1536]{2,1,0:T(8,128)(2,1)}, bf16[2,1536,512]{2,1,0:T(8,128)(2,1)}, bf16[2,96,1536]{2,1,0:T(8,...) custom-call(bf16[4,208,384]{2,1,0:T(8,128)(2,1)} %pad_maximum_fusion, ...), custom_call_target="tpu_custom_call" | custom-call | tf_op jit(solution)/shard_map/first_layer/pallas_call | solution.py:2031
  140.7 0.8 slice_convert_fusion
  141.6 0.6 slice_bitcast_fusion
  142.2 191.1 %second_layer.1 = (f32[64,1536]{1,0:T(8,128)}, bf16[16,64,1536]{2,1,0:T(8,128)(2,1)}, bf16[64,1536]{1,0:T(8,128)(2,1)}, bf16[64,1536]{1,0:T(8,128)(2,1)}, f32[64...) custom-call(bf16[64,1536]{1,0:T(8,128)(2,1)} %get-tuple-element.58.r, ...), custom_call_target="tpu_custom_call" | custom-call | tf_op jit(solution)/shard_map/second_layer/pallas_call | solution.py:2031
  333.3 157.6 %last_layer_back.1 = (bf16[16,288,384]{2,1,0:T(8,128)(2,1)}, bf16[384,1536]{1,0:T(8,128)(2,1)}, bf16[384,4096]{1,0:T(8,128)(2,1)}, bf16[384,4096]{1,0:T(8,128)(2...) custom-call(bf16[64,1536]{1,0:T(8,128)(2,1)} %get-tuple-element.69.r, ...), custom_call_target="tpu_custom_call" | custom-call | tf_op jit(solution)/shard_map/last_layer_back/pallas_call | solution.py:2031
  490.8 1.4 fusion.18
  492.2 1.9 copy-done.2
  494.1 1.3 copy-done.3
  495.4 13.0 %widen_gradients.1 = (f32[384,1536]{1,0:T(8,128)}, f32[384,768]{1,0:T(8,128)}, f32[384,768]{1,0:T(8,128)}, f32[384,1536]{1,0:T(8,128)}, f32[384,4096]{1,0:T(8,12...) custom-call(bf16[16,288,384]{2,1,0:T(8,128)(2,1)} %get-tuple-element.93.attn, bf16[384,1536]{1,0:T(8,128)(2,1)S(1)} %copy-done.3, ...), custom_call_target="tpu_custom_call" | custom-call | tf_op jit(solution)/shard_map/widen_gradients/pallas_call | solution.py:1965
  508.4 0.7 copy.37
  509.2 0.7 copy.38
  (23 shorter events, 0.2 us)
Async XLA Ops:
  0.6 3.9 copy-start
  4.5 1.7 copy-start.6
  4.6 1.7 copy-start.7
  492.2 1.9 copy-start.2
  494.1 1.3 copy-start.3
  495.4 13.0 %copy-start.5 = (bf16[2,64,1536]{2,1,0:T(8,128)(2,1)S(1)}, bf16[2,64,1536]{2,1,0:T(8,128)(2,1)}, u32[]{:S(2)}) copy-start(bf16[2,64,1536]{2,1,0:T(8,128)(2,1)} %get-tuple-element.90) | copy-start | bytes 1179652
  495.4 13.8 %copy-start.4 = (bf16[2,64,1536]{2,1,0:T(8,128)(2,1)S(1)}, bf16[2,64,1536]{2,1,0:T(8,128)(2,1)}, u32[]{:S(2)}) copy-start(bf16[2,64,1536]{2,1,0:T(8,128)(2,1)} %get-tuple-element.91) | copy-start | bytes 1179652
  495.4 14.5 %copy-start.1 = (bf16[1,384,1536]{2,1,0:T(8,128)(2,1)S(1)}, bf16[1,384,1536]{2,1,0:T(8,128)(2,1)}, u32[]{:S(2)}) copy-start(bf16[1,384,1536]{2,1,0:T(8,128)(2,1)} %param.16) | copy-start | bytes 3538948

commit v8 on v7

--- a/solution.py
+++ b/solution.py
@@ -616,6 +616,7 @@
             for h in range(CUTS):
                 settled(spot(corner * count + j, h), core_got.at[half, j, h], True)
         yield "corner" if half else "near"
+    yield "done"
     for h in range(CUTS):
         for j in range(count):
             to_side(j, h).wait_send()
@@ -708,6 +709,24 @@
 def advance(steps, times):
     for _ in range(times):
         next(steps, None)
+
+
+def until_done(steps):
+    for event in steps:
+        if event == "done":
+            return
+        yield event
+
+
+def all_but_last(compute):
+    groups = []
+
+    def some(group):
+        groups.append(group)
+        if len(groups) < 4:
+            compute(group)
+
+    return some
 
 
 def group_of(event):
@@ -1109,7 +1128,7 @@
     next(steps)
     next(spread)
     clear_pads(attn_vm, out_vm)
-    for event in steps:
+    for event in until_done(steps):
         if event == "line":
             advance(spread, 3)
     grads_across = remote(
@@ -1156,7 +1175,10 @@
         next(spread)
 
     run_with(scatter_steps(count, partial, deliver, *scatter_one, compute=project_out), [more] * 5)
-    for number, event in enumerate(gather_steps(count, normed_own, rows_vm, *second_sems)):
+    for _ in steps:
+        pass
+    steps = gather_steps(count, normed_own, rows_vm, *second_sems)
+    for number, event in enumerate(until_done(steps)):
         if number == 0:
             more()
     for _ in spread:
@@ -1190,6 +1212,8 @@
         [functools.partial(advance, grad_steps, 1)] * 3,
     )
     for _ in grad_steps:
+        pass
+    for _ in steps:
         pass
     saves.append(pltpu.make_async_copy(grads_vm, grads_near, save_done.at[2]))
     saves[2].start()
@@ -1383,7 +1407,9 @@
     return r
 
 
-def attn_back_body(count, layer, r, ins, outs, background, fillers, gathered=None):
+def attn_back_body(
+    count, layer, r, ins, outs, background, fillers, gathered=None, spare=None
+):
     branch_in, grad_hidden, x_own, all_rows, heads_kept, log_total, attn, twin, out = ins[:9]
     cosine, sine, start, gain = ins[9:]
     grad_out, gain_out, attn_grad, out_grad = outs
@@ -1424,7 +1450,7 @@
         value = back_product(group_rows(branch_vm, group, count), out_vm[...])
         mixed_grads[group_span(group, count, block)] = value.astype(low)
 
-    for number, event in enumerate(steps):
+    for number, event in enumerate(until_done(steps)):
         if number < 2:
             weigh(2 * number)
             weigh(2 * number + 1)
@@ -1468,11 +1494,15 @@
         grad_out[...] = (grad_hidden[...] + part).astype(low)
         gain_out[...] = jnp.broadcast_to(jnp.sum(terms, axis=0, keepdims=True), gain_out.shape)
 
+    parts = [functools.partial(attn_part, n) for n in range(3)] + [out_part]
+    if spare:
+        parts.append(spare)
     run_with(
         scatter_steps(count, partial, deliver, *r.scatter_refs, compute=project_back),
-        [functools.partial(run_all, [functools.partial(attn_part, n) for n in range(3)] + [out_part])]
-        + fillers,
-    )
+        [functools.partial(run_all, parts)] + fillers,
+    )
+    for _ in steps:
+        pass
 
 
 def middle_kernel(count, *refs):
@@ -1514,7 +1544,7 @@
         pltpu.make_async_copy(grads_near, grads_vm.at[pl.ds(near, half)], load_done.at[2]),
     ]
     start_all(wide_loads)
-    for event in steps:
+    for event in until_done(steps):
         if event == "line":
             wait_all(loads)
         group = group_of(event)
@@ -1539,6 +1569,8 @@
         scatter_steps(count, partial, deliver, *r.scatter_refs, compute=project_out),
         [functools.partial(advance, grad_steps, 1)] * 3,
     )
+    for _ in steps:
+        pass
     steps = gather_steps(count, normed_own, rows_two, *r.gather_sems)
     next(steps)
     for _ in grad_steps:
@@ -1553,10 +1585,9 @@
         store_gate_grads(pre_grads, span, grad_act, pre)
         keep_group(partial_back, group, back_product(pre_grads[span], wide_vm[...]), count)
 
-    for event in steps:
-        group = group_of(event)
-        if group is not None:
-            through(group)
+    for event in until_done(steps):
+        if event == "line":
+            through(group_of(event))
 
     def project_down(group):
         value = product(units[group * size : (group + 1) * size], down_vm[...])
@@ -1572,9 +1603,13 @@
     fillers = wide_grads(rows_two, pre_grads, units, grads_vm, wide_two, down_two)
     fillers += [functools.partial(project_down, group) for group in range(4)]
     run_with(
-        scatter_steps(count, partial_back, deliver_two, *r.scatter_refs),
+        scatter_steps(
+            count, partial_back, deliver_two, *r.scatter_refs, compute=all_but_last(through)
+        ),
         [functools.partial(run_all, fillers[n::4]) for n in range(4)],
     )
+    for _ in steps:
+        pass
     save = pltpu.make_async_copy(partial, ahead, load_done.at[3])
     save.start()
     copies = carried(
@@ -1615,13 +1650,12 @@
         store_gate_grads(pre_grads, span, grad_act, pre_vm[span])
         keep_group(partial_back, group, back_product(pre_grads[span], wide_vm[...]), count)
 
-    for number, event in enumerate(steps):
+    for number, event in enumerate(until_done(steps)):
         if number < 2:
             again(2 * number)
             again(2 * number + 1)
-        group = group_of(event)
-        if group is not None:
-            through_one(group)
+        if event == "line":
+            through_one(group_of(event))
 
     def deliver_one(total):
         mlp_grad_sent(
@@ -1629,9 +1663,13 @@
         )
 
     run_with(
-        scatter_steps(count, partial_back, deliver_one, *r.scatter_refs),
+        scatter_steps(
+            count, partial_back, deliver_one, *r.scatter_refs, compute=all_but_last(through_one)
+        ),
         wide_grads(rows_two, pre_grads, units, grads_vm, wide_one, down_one),
     )
+    for _ in steps:
+        pass
     carry(copies, 0, "wait")
     save.wait()
 
@@ -1790,16 +1828,16 @@
     pl.when(at_second)(swap_rest.start)
     pl.when(at_first)(swap_between.start)
     wide_turns = [(1, k) for k in turns]
-    crossings = wide_turns + [(0, k) for k in turns] + [(2, 0), (3, 0)]
+    crossings = [(3, 0)] + wide_turns + [(0, k) for k in turns] + [(2, 0)]
 
     def begin_cross(those):
         for kind, k in those:
             pl.when(at_second)(cross(kind, k).start)
 
     def background():
-        begin_cross(crossings[:count])
+        begin_cross(crossings[: count + 1])
+        load(3)
         load(1)
-        load(3)
 
     def deliver(total):
         final[...] = (hidden[...] + total).astype(low)
@@ -1809,7 +1847,7 @@
     def later():
         load(0)
         load(2)
-        begin_cross(crossings[count:])
+        begin_cross(crossings[count + 1 :])
 
     def share(n):
         if n == 0:
@@ -1818,8 +1856,13 @@
         along_line(1, turns[n]).start()
 
     def gathered():
+        loaded(3)
+        add_up(3, 0)
+        publish(3, 0)
+
+    def spare():
+        later()
         share(0)
-        share(1)
 
     def early():
         add_up(1, 0)
@@ -1833,8 +1876,9 @@
         ins,
         (grad_start, gain_attn_one, attn_grad, out_grad),
         background,
-        [later, functools.partial(share, 2), early],
+        [functools.partial(share, 1), functools.partial(share, 2), early],
         gathered,
+        spare,
     )
     pl.when(at_second)(swap_start.start)
     grads_out[section] = jnp.where(at_first, grad_start[...], grad_between[...])
@@ -1866,13 +1910,11 @@
     publish(2, 0)
     from_line(1, turns[2])
     next(ahead_steps)
+    from_side(3, 0)
     from_side(1, turns[0])
-    from_side(0, 0)
-    loaded(3)
-    add_up(3, 0)
-    publish(3, 0)
     for k in turns[:-1]:
         from_line(0, k)
+    from_side(0, 0)
     from_side(1, turns[1])
     gain_cross.wait_recv()
     gain_sum[...] = gains[section] + gain_in[...]
@@ -1889,7 +1931,6 @@
     gain_to_side = small(2, gain_part.at[:], gain_side.at[:], side)
     gain_to_side.start()
     advance(ahead_steps, 4)
-    from_side(3, 0)
     gain_to_side.wait_recv()
     gain_side[...] += gain_part[...]
     gain_to_core = small(3, gain_side.at[:], gain_core.at[:], core)
@@ -1923,13 +1964,23 @@
     gain_to_core.wait_send()
 
 
-def widen_kernel(pieces, attn, out, gate, up, down, query, key, value, out_f, gate_f, up_f, down_f):
+def widen_kernel(pieces, *refs):
+    attn, out, gate, up, down, rows_in, grads_in, gains = refs[:8]
+    query, key, value, out_f, gate_f, up_f, down_f = refs[8:15]
+    rows_out, grads_out, gain_attn, gain_mlp = refs[15:]
     f32 = jnp.float32
     out_f[...] = out[...].astype(f32)
     gate_f[...] = gate[...].astype(f32)
     up_f[...] = up[...].astype(f32)
     down_f[...] = down[...].astype(f32)
 
+    @pl.when(pl.program_id(0) == 0)
+    def _():
+        rows_out[...] = rows_in[...]
+        grads_out[...] = grads_in[...]
+        gain_attn[...] = gains[0:1]
+        gain_mlp[...] = gains[4:5]
+
     @pl.when(pl.program_id(0) < pieces)
     def _():
         parts, _, lanes = attn.shape
@@ -1944,7 +1995,7 @@
             place[...] = total.reshape(parts // copies * HEAD_DIM, lanes).T
 
 
-def widen(attn, out, gate, up, down):
+def widen(attn, out, gate, up, down, rows_out, grads_out, gains):
     f32 = jnp.float32
     parts, heads, rows = attn.shape
     lanes = 128
@@ -1959,19 +2010,28 @@
     def turned(columns):
         return pl.BlockSpec((lanes, columns), lambda i: (jnp.minimum(i, pieces - 1), 0))
 
+    def whole(shape):
+        return pl.BlockSpec(shape, lambda i: (0,) * len(shape))
+
     flat = [out, gate, up, down]
+    swaps = [whole(rows_out.shape), whole(grads_out.shape)]
+    gain = jax.ShapeDtypeStruct((1, rows), f32)
     taken = pl.BlockSpec((parts, heads, lanes), lambda i: (0, 0, jnp.minimum(i, pieces - 1)))
     shapes = [(rows, width), (rows, narrow), (rows, narrow)] + [array.shape for array in flat]
     return pl.pallas_call(
         functools.partial(widen_kernel, pieces),
         grid=(steps,),
-        out_shape=[jax.ShapeDtypeStruct(shape, f32) for shape in shapes],
-        in_specs=[taken] + [rows_of(array) for array in flat],
+        out_shape=[jax.ShapeDtypeStruct(shape, f32) for shape in shapes]
+        + [jax.ShapeDtypeStruct(array.shape, array.dtype) for array in (rows_out, grads_out)]
+        + [gain, gain],
+        in_specs=[taken] + [rows_of(array) for array in flat] + swaps + [whole(gains.shape)],
         out_specs=[turned(width), turned(narrow), turned(narrow)]
-        + [rows_of(array) for array in flat],
-        compiler_params=pltpu.CompilerParams(vmem_limit_bytes=48 * 2**20),
+        + [rows_of(array) for array in flat]
+        + swaps
+        + [whole((1, rows)), whole((1, rows))],
+        compiler_params=pltpu.CompilerParams(vmem_limit_bytes=60 * 2**20),
         name="widen_gradients",
-    )(attn, out, gate, up, down)
+    )(attn, out, gate, up, down, rows_out, grads_out, gains)
 
 
 def last_layer(count, operands, like, back_scratch):
@@ -2021,8 +2081,7 @@
     attn, out, gate, up, down, gains, rows_out, grads_out = call_kernel(
         functools.partial(last_kernel, count), "last_layer_back", 3, operands, outputs, scratch
     )
-    query, key, value, out, gate, up, down = widen(attn, out, gate, up, down)
-    return rows_out, grads_out, gains, query, key, value, out, gate, up, down
+    return widen(attn, out, gate, up, down, rows_out, grads_out, gains)
 
 
 def call_kernel(kernel, name, number, operands, outputs, scratch):
@@ -2227,7 +2286,7 @@
         + tables
         + [(gains[0, 0:1], True)]
     )
-    rows_out, grads_out, gain_sums, query, key, value, out, gate, up, down = last_layer(
+    query, key, value, out, gate, up, down, *swapped, gain_attn, gain_mlp = last_layer(
         count,
         back_operands
         + [(wide_one, False), (down_one, False), (attn_two, False), (out_two, False)]
@@ -2247,14 +2306,14 @@
         back_scratch,
     )
     return (
-        rows_out[None, :, None],
-        grads_out[None, :, None],
-        gain_sums[0][None],
+        swapped[0][None, :, None],
+        swapped[1][None, :, None],
+        gain_attn,
         query[None],
         key[None],
         value[None],
         out[None],
-        gain_sums[4][None],
+        gain_mlp,
         gate[None],
         up[None],
         down[None],

time: 518 us -> 510 us (0.985)
  local copies, waits for them, and re-layouts: 9.44 us -> 3.43 us
where the time goes in v8:
time: 510 us; the launch traced here: 503 us
  Pallas kernels  490 us (96%)
  other arithmetic  5.99 us (1%)
    pallas_call x3, Pallas kernels, call_kernel(): pl.pallas_call(kernel, out_shape=[jax.ShapeDtypeStruct(shape, dtype) for...  474 us
    pallas_call x1, Pallas kernels, widen(): pl.pallas_call(functools.partial(widen_kernel, pieces), grid=(steps,), ou...  15.8 us

profile of v8, /device:TPU:18, one launch (start us, length us, event | category | flops | bytes accessed | tf_op | source)
XLA Modules:
  0.0 502.8 jit_solution(16426996196778155728)
XLA Ops:
  0.6 0.0 copy-start
  0.7 0.1 pad.5.clone
  0.8 0.7 fusion.17
  1.5 0.2 reduce-window.8
  1.7 0.1 iota_add_fusion.1
  1.8 0.1 add.89
  1.9 0.1 iota_add_fusion
  2.0 0.1 add.95
  2.0 0.1 select_reduce_fusion
  2.1 0.8 maximum_maximum_fusion
  2.9 1.6 convolution_convert_fusion
  4.5 0.0 copy-start.2
  4.6 0.8 convolution_convert_fusion.1
  5.4 0.9 pad_maximum_fusion.refs_0_
  6.3 0.8 dynamic-slice_bitcast_fusion
  7.1 1.0 copy.30.refs_9_.refs_5_.refs_11_
  8.1 3.1 fusion.12
  11.2 131.1 %first_layer.1 = (bf16[2,208,1536]{2,1,0:T(8,128)(2,1)}, bf16[2,96,1536]{2,1,0:T(8,128)(2,1)}, bf16[2,1536,512]{2,1,0:T(8,128)(2,1)}, bf16[2,96,1536]{2,1,0:T(8,...) custom-call(bf16[4,208,384]{2,1,0:T(8,128)(2,1)} %pad_maximum_fusion, ...), custom_call_target="tpu_custom_call" | custom-call | tf_op jit(solution)/shard_map/first_layer/pallas_call | solution.py:2090
  142.3 0.8 slice_convert_fusion
  143.1 0.6 slice_bitcast_fusion
  143.7 190.3 %second_layer.1 = (f32[64,1536]{1,0:T(8,128)}, bf16[16,64,1536]{2,1,0:T(8,128)(2,1)}, bf16[64,1536]{1,0:T(8,128)(2,1)}, bf16[64,1536]{1,0:T(8,128)(2,1)}, f32[64...) custom-call(bf16[64,1536]{1,0:T(8,128)(2,1)} %get-tuple-element.62.r, ...), custom_call_target="tpu_custom_call" | custom-call | tf_op jit(solution)/shard_map/second_layer/pallas_call | solution.py:2090
  334.0 152.4 %last_layer_back.1 = (bf16[16,288,384]{2,1,0:T(8,128)(2,1)}, bf16[384,1536]{1,0:T(8,128)(2,1)}, bf16[384,4096]{1,0:T(8,128)(2,1)}, bf16[384,4096]{1,0:T(8,128)(2...) custom-call(bf16[64,1536]{1,0:T(8,128)(2,1)} %get-tuple-element.73.r, ...), custom_call_target="tpu_custom_call" | custom-call | tf_op jit(solution)/shard_map/last_layer_back/pallas_call | solution.py:2090
  486.5 0.0 copy-start.1
  486.5 15.8 %widen_gradients.1 = (f32[384,1536]{1,0:T(8,128)}, f32[384,768]{1,0:T(8,128)}, f32[384,768]{1,0:T(8,128)}, f32[384,1536]{1,0:T(8,128)}, f32[384,4096]{1,0:T(8,12...) custom-call(bf16[16,288,384]{2,1,0:T(8,128)(2,1)} %get-tuple-element, ...), custom_call_target="tpu_custom_call" | custom-call | tf_op jit(solution)/shard_map/widen_gradients/pallas_call | solution.py:2021
  (12 shorter events, 0.1 us)
Async XLA Ops:
  0.6 3.9 copy-start
  4.5 1.7 copy-start.2
  4.6 1.7 copy-start.3
  486.5 15.8 %copy-start.1 = (bf16[1,384,1536]{2,1,0:T(8,128)(2,1)S(1)}, bf16[1,384,1536]{2,1,0:T(8,128)(2,1)}, u32[]{:S(2)}) copy-start(bf16[1,384,1536]{2,1,0:T(8,128)(2,1)} %param.16) | copy-start | bytes 3538948

commit v9 on v8

--- a/solution.py
+++ b/solution.py
@@ -1100,17 +1100,36 @@
     return ref[3 * PAD : 3 * PAD + 16][row : row + 1].astype(jnp.float32)
 
 
+def fill_tables(lengths, frequency, cosine, sine, start):
+    section = lax.axis_index("section")
+    token = lax.broadcasted_iota(jnp.int32, start.shape, 0)
+    end, begin = 0, jnp.zeros(start.shape, jnp.int32)
+    for n in range(lengths.shape[2]):
+        length = lengths[section, 0, n]
+        end = end + length
+        begin = begin + jnp.where(end <= token, length, 0)
+    start[...] = begin
+    lane = lax.broadcasted_iota(jnp.int32, cosine.shape, 1)
+    angles = (token - begin).astype(jnp.float32) * frequency[...]
+    cosine[...] = jnp.where(lane < HEAD_DIM, jnp.cos(angles), 0.0)
+    turned = jnp.where(lane < HEAD_DIM, jnp.sin(angles), 0.0)
+    sine[...] = jnp.where(lane < HEAD_DIM // 2, -turned, turned)
+
+
 def first_layer_kernel(count, *refs):
     refs = iter(refs)
 
     def take(n):
         return [next(refs) for _ in range(n)]
 
-    pieces, w_gate, w_up, w_output, w_down, rows_in, grads_in, cosine, sine, start = take(10)
+    w_query, w_key, w_value, w_gate, w_up, w_output, w_down = take(7)
+    gain_attn, gain_mlp, inputs, cotangent, lengths, frequency = take(6)
     attn, twin, gate_up, out, down, all_rows, wide_rows, grads_near, grads_side = take(9)
+    cosine, sine, start = take(3)
     hidden, result_out, normed_out, heads, log_total = take(5)
     raw_vm, normed_vm, rows_vm, partial, partial_two, grads_vm = take(6)
     attn_vm, out_vm, wide_vm, down_vm, units, normed_own, gain_vm = take(7)
+    pieces, query_vm, other_vm, query_turned, other_turned, weights_done = take(6)
     load_done, save_done, twin_sent, twin_got = take(4)
     spread_sems = take(5)
     first_sems, second_sems, grads_sems, side_sems = take(7), take(7), take(5), take(2)
@@ -1120,13 +1139,39 @@
     tokens = block * raw_vm.shape[0]
     size = count * block
     low, f32 = jnp.bfloat16, jnp.float32
+    seq = lax.axis_index("seq")
+    rows_in, grads_in = inputs.at[section, 0], cotangent.at[section, 0]
+    query_load = pltpu.make_async_copy(w_query, query_vm, weights_done.at[0])
+    query_load.start()
+    key_load = pltpu.make_async_copy(w_key, other_vm, weights_done.at[1])
+    value_load = pltpu.make_async_copy(w_value, other_vm, weights_done.at[1])
+    pl.when(seq % 2 == 0)(key_load.start)
+    pl.when(seq % 2 == 1)(value_load.start)
     greet_group(count, ({"section": 1 - section},))
+    steps = gather_steps(count, rows_in, raw_vm, *first_sems)
+    next(steps)
+    query_load.wait()
+    key_load.wait()
+    query_turned[...] = query_vm[...].astype(f32).T.astype(low)
+    other_turned[...] = other_vm[...].astype(f32).T.astype(low)
+    row = lax.broadcasted_iota(jnp.int32, (16, gain_attn.shape[1]), 0)
+    own_gains = jnp.where(row == 0, gain_attn[...], jnp.where(row == 1, gain_mlp[...], 0))
+    per_blk = other_turned.shape[0] // HEAD_DIM // count
+    for j in range(count):
+        head = j * 4 + seq
+        other_head = j * per_blk + seq * per_blk // 4
+        for place, turned, index in (
+            (0, query_turned, head),
+            (OWN_PART, other_turned, other_head),
+        ):
+            rows = pl.ds(pl.multiple_of(index * HEAD_DIM, 16), HEAD_DIM)
+            pieces[j, place : place + HEAD_DIM] = turned[rows]
+        pieces[j, GAINS : GAINS + 16] = own_gains.astype(low)
     spread = spread_steps(
         count, pieces, w_gate, w_up, w_output, w_down, attn, gate_up, out, down, *spread_sems
     )
-    steps = gather_steps(count, rows_in, raw_vm, *first_sems)
-    next(steps)
     next(spread)
+    fill_tables(lengths, frequency, cosine, sine, start)
     clear_pads(attn_vm, out_vm)
     for event in until_done(steps):
         if event == "line":
@@ -1512,7 +1557,8 @@
         return [next(refs) for _ in range(n)]
 
     rows_in, between, grads_side, cosine, sine, start, attn, twin, out = take(9)
-    grads_near, gate_up, down, grads_own, hidden_one, wide_rows = take(6)
+    grads_near, gate_up, down, cotangent, hidden_one, wide_rows = take(6)
+    grads_own = cotangent.at[lax.axis_index("section"), 0]
     gain_mlp_two, gain_attn_two, gain_mlp_one = take(3)
     hidden, ahead, grad_between, branch_out, grad_hidden_out = take(5)
     mlp_two_sum, attn_two_sum, mlp_one_sum = take(3)
@@ -1681,6 +1727,7 @@
         return [next(refs) for _ in range(n)]
 
     ins = take(13)
+    ins[2] = ins[2].at[lax.axis_index("section"), 0]
     wide_one, down_one, attn_two, out_two, wide_two, down_two = take(6)
     wide_from_one, down_from_one, attn_from_one, out_from_one, ahead = take(5)
     gain_mlp_one, gain_attn_two, gain_mlp_two, between, grad_between, hidden = take(6)
@@ -2087,10 +2134,11 @@
 def call_kernel(kernel, name, number, operands, outputs, scratch):
     in_vmem = pl.BlockSpec(memory_space=pltpu.VMEM)
     anywhere = pl.BlockSpec(memory_space=pl.ANY)
+    places = {True: in_vmem, False: anywhere, None: pl.BlockSpec(memory_space=pltpu.SMEM)}
     return pl.pallas_call(
         kernel,
         out_shape=[jax.ShapeDtypeStruct(shape, dtype) for shape, dtype, _ in outputs],
-        in_specs=[in_vmem if near else anywhere for _, near in operands],
+        in_specs=[places[near] for _, near in operands],
         out_specs=[in_vmem if near else anywhere for _, _, near in outputs],
         scratch_shapes=scratch,
         compiler_params=pltpu.CompilerParams(
@@ -2100,67 +2148,21 @@
     )(*[array for array, _ in operands])
 
 
-def sliced_heads(local_shards):
-    seq_index, seq_count = lax.axis_index("seq"), lax.axis_size("seq")
-    count = lax.axis_size("blk")
-    gain_attn, w_query, w_key, w_value, _, gain_mlp, _, _, _ = local_shards
-    rows = w_query.shape[0]
-
-    def heads_of(weight, per_blk, place):
-        head = jnp.arange(count)[:, None] * per_blk + place
-        column = (head * HEAD_DIM + jnp.arange(HEAD_DIM)).reshape(-1)
-        chosen = jnp.arange(weight.shape[1])[:, None] == column[None, :]
-        taken = lax.dot_general(
-            chosen.astype(jnp.bfloat16),
-            weight,
-            (((0,), (1,)), ((), ())),
-            preferred_element_type=jnp.float32,
-        )
-        return taken.astype(jnp.bfloat16).reshape(count, HEAD_DIM, rows)
-
-    kv_per_blk = KV_HEADS // count
-    kv_place = seq_index * kv_per_blk // seq_count
-    gains = jnp.concatenate(
-        [jnp.stack([gain_attn, gain_mlp]), jnp.zeros((14, rows), jnp.bfloat16)]
-    )
-    return jnp.concatenate(
-        [
-            heads_of(w_query, seq_count, seq_index),
-            jnp.broadcast_to(gains[None], (count,) + gains.shape),
-            heads_of(jnp.where(seq_index % 2 == 0, w_key, w_value), kv_per_blk, kv_place),
-        ],
-        axis=1,
-    )
-
-
 def head_shards(inputs, cotangent, doc_lengths, *params):
-    section = lax.axis_index("section")
-    at_first = section == 0
     seq_count, count = lax.axis_size("seq"), lax.axis_size("blk")
     low, f32 = jnp.bfloat16, jnp.float32
     vmem, dma = pltpu.VMEM, pltpu.SemaphoreType.DMA
     block, width = inputs.shape[2], inputs.shape[3]
     blocks = seq_count * count
     tokens = blocks * block
-    rows_own = lax.dynamic_index_in_dim(inputs, section, 0, keepdims=False)[0]
-    grads_own = lax.dynamic_index_in_dim(cotangent, section, 0, keepdims=False)[0]
     local = tuple(weight[0] for weight in params)
-    pieces = sliced_heads(local)
+    piece_shape = (count, 2 * HEAD_DIM + 16, local[1].shape[0])
     w_output, w_gate, w_up, w_down = local[4], local[6], local[7], local[8]
     rows = w_gate.shape[0]
     lanes = w_gate.shape[1] // blocks
     out_rows, down_rows = w_output.shape[0] // seq_count, w_down.shape[0] // seq_count
-    lengths = lax.dynamic_index_in_dim(doc_lengths, section, 0, keepdims=False)[0]
-    token_index = jnp.arange(tokens, dtype=jnp.int32)
-    _, position = doc_info(lengths, token_index)
-    start = (token_index - position)[:, None]
-    half_dim = HEAD_DIM // 2
-    lane = jnp.arange(PAD)
-    frequency = THETA ** (-2.0 * (lane % half_dim).astype(f32) / HEAD_DIM)
-    angles = position.astype(f32)[:, None] * frequency[None, :]
-    sign = jnp.where(lane < half_dim, -1.0, 1.0).astype(f32)
-    cosine = jnp.where(lane < HEAD_DIM, jnp.cos(angles), 0.0)
-    sine = jnp.where(lane < HEAD_DIM, jnp.sin(angles) * sign, 0.0)
+    lane = jnp.arange(PAD) % (HEAD_DIM // 2)
+    frequency = (THETA ** (-2.0 * lane.astype(f32) / HEAD_DIM))[None]
 
     def all_blocks():
         return vmem((blocks, block, width), low)
@@ -2175,7 +2177,6 @@
     gain_rows = ((8, width), f32, True)
     weights_vm = [vmem((3 * PAD + 16, width), low), vmem((PAD, width), low)]
     wide_vm, down_vm = vmem((width, 2 * lanes), low), vmem((down_rows, width), low)
-    tables = [(cosine, True), (sine, True), (start, True)]
     (
         attn,
         twin,
@@ -2186,6 +2187,9 @@
         wide_rows_one,
         grads_near,
         grads_side,
+        cosine,
+        sine,
+        start,
         hidden_one,
         between,
         normed,
@@ -2195,11 +2199,11 @@
         functools.partial(first_layer_kernel, count),
         "first_layer",
         2,
-        [(array, False) for array in (pieces, w_gate, w_up, w_output, w_down)]
-        + [(rows_own, True), (grads_own, True)]
-        + tables,
+        [(array, False) for array in local[1:4] + (w_gate, w_up, w_output, w_down)]
+        + [(local[0][None], True), (local[5][None], True)]
+        + [(inputs, True), (cotangent, True), (doc_lengths, None), (frequency, True)],
         [
-            ((2, pieces.shape[1], width), low, False),
+            ((2, piece_shape[1], width), low, False),
             ((2, HEAD_DIM, width), low, False),
             ((2, width, 2 * lanes), low, False),
             ((2, out_rows, width), low, False),
@@ -2208,6 +2212,9 @@
             every,
             half,
             ((block, width), low, False),
+            ((tokens, PAD), f32, True),
+            ((tokens, PAD), f32, True),
+            ((tokens, 1), jnp.int32, True),
             own_wide,
             own_low,
             own_low,
@@ -2218,7 +2225,10 @@
         + [half_blocks]
         + weights_vm
         + [wide_vm, down_vm, vmem((tokens, lanes), low), vmem((block, width), low)]
-        + [vmem((16, width), low), dma((6,)), dma((3,)), dma, dma]
+        + [vmem((16, width), low), vmem(piece_shape, low)]
+        + [vmem(local[1].shape, low), vmem(local[2].shape, low)]
+        + [vmem(local[1].shape[::-1], low), vmem(local[2].shape[::-1], low), dma((2,))]
+        + [dma((6,)), dma((3,)), dma, dma]
         + [dma((3, count)), dma((3, count)), dma((5, count)), dma((5, count)), dma((5,))]
         + gather_semaphores(count) * 2
         + line_semaphores(count)
@@ -2226,6 +2236,7 @@
         + scatter()
         + scatter(),
     )
+    tables = [(cosine, True), (sine, True), (start, True)]
     gains = attn[:, GAINS : GAINS + 2].astype(f32)
     back_scratch = (
         [all_blocks(), all_blocks(), vmem((4, tokens, PAD), low)]
@@ -2265,7 +2276,7 @@
         + tables
         + [(attn, False), (twin, False), (out, False)]
         + [(grads_near, False), (gate_up, False), (down, False)]
-        + [(grads_own, True), (hidden_one, True), (wide_rows_one, False)]
+        + [(cotangent, True), (hidden_one, True), (wide_rows_one, False)]
         + [(gains[1, 1:2], True), (gains[1, 0:1], True), (gains[0, 1:2], True)],
         [own_wide, every, own_low, own_low, own_wide, gain_rows, gain_rows, gain_rows]
         + [(wide_shape, low, True), (down_shape, low, True)]
@@ -2280,7 +2291,7 @@
         + back_scratch,
     )
     back_operands = (
-        [(branch, True), (grad_hidden, True), (rows_own, True)]
+        [(branch, True), (grad_hidden, True), (inputs, True)]
         + [(rows_one, False), (heads_one, False), (total_one, True)]
         + [(attn, False), (twin, False), (out, False)]
         + tables

time: 510 us -> 501 us (0.982)
  no operation moved by 1% of the time
where the time goes in v9:
time: 501 us; the launch traced here: 493 us
  Pallas kernels  490 us (98%)
    pallas_call x3, Pallas kernels, call_kernel(): pl.pallas_call(kernel, out_shape=[jax.ShapeDtypeStruct(shape, dtype) for...  474 us
    pallas_call x1, Pallas kernels, widen(): pl.pallas_call(functools.partial(widen_kernel, pieces), grid=(steps,), ou...  15.7 us

profile of v9, /device:TPU:18, one launch (start us, length us, event | category | flops | bytes accessed | tf_op | source)
XLA Modules:
  0.0 492.9 jit_solution(164956076129631892)
XLA Ops:
  0.6 0.5 fusion.2.refs_12_
  1.2 131.4 %first_layer.1 = (bf16[2,208,1536]{2,1,0:T(8,128)(2,1)}, bf16[2,96,1536]{2,1,0:T(8,128)(2,1)}, bf16[2,1536,512]{2,1,0:T(8,128)(2,1)}, bf16[2,96,1536]{2,1,0:T(8,...) custom-call(bf16[384,1536]{1,0:T(8,128)(2,1)} %bitcast.31, ...), custom_call_target="tpu_custom_call" | custom-call | tf_op jit(solution)/shard_map/first_layer/pallas_call | solution.py:2138
  132.6 0.8 slice_convert_fusion
  133.4 0.6 slice_bitcast_fusion
  134.0 190.2 %second_layer.1 = (f32[64,1536]{1,0:T(8,128)}, bf16[16,64,1536]{2,1,0:T(8,128)(2,1)}, bf16[64,1536]{1,0:T(8,128)(2,1)}, bf16[64,1536]{1,0:T(8,128)(2,1)}, f32[64...) custom-call(bf16[64,1536]{1,0:T(8,128)(2,1)} %get-tuple-element.65.r, ...), custom_call_target="tpu_custom_call" | custom-call | tf_op jit(solution)/shard_map/second_layer/pallas_call | solution.py:2138
  324.3 152.4 %last_layer_back.1 = (bf16[16,288,384]{2,1,0:T(8,128)(2,1)}, bf16[384,1536]{1,0:T(8,128)(2,1)}, bf16[384,4096]{1,0:T(8,128)(2,1)}, bf16[384,4096]{1,0:T(8,128)(2...) custom-call(bf16[64,1536]{1,0:T(8,128)(2,1)} %get-tuple-element.79.r, ...), custom_call_target="tpu_custom_call" | custom-call | tf_op jit(solution)/shard_map/last_layer_back/pallas_call | solution.py:2138
  476.7 15.7 %widen_gradients.1 = (f32[384,1536]{1,0:T(8,128)}, f32[384,768]{1,0:T(8,128)}, f32[384,768]{1,0:T(8,128)}, f32[384,1536]{1,0:T(8,128)}, f32[384,4096]{1,0:T(8,12...) custom-call(bf16[16,288,384]{2,1,0:T(8,128)(2,1)} %get-tuple-element, ...), custom_call_target="tpu_custom_call" | custom-call | tf_op jit(solution)/shard_map/widen_gradients/pallas_call | solution.py:2068

commit v10 on v9

--- a/solution.py
+++ b/solution.py
@@ -1126,6 +1126,7 @@
     gain_attn, gain_mlp, inputs, cotangent, lengths, frequency = take(6)
     attn, twin, gate_up, out, down, all_rows, wide_rows, grads_near, grads_side = take(9)
     cosine, sine, start = take(3)
+    gain_rows = take(4)
     hidden, result_out, normed_out, heads, log_total = take(5)
     raw_vm, normed_vm, rows_vm, partial, partial_two, grads_vm = take(6)
     attn_vm, out_vm, wide_vm, down_vm, units, normed_own, gain_vm = take(7)
@@ -1174,7 +1175,7 @@
     fill_tables(lengths, frequency, cosine, sine, start)
     clear_pads(attn_vm, out_vm)
     for event in until_done(steps):
-        if event == "line":
+        if event == "side":
             advance(spread, 3)
     grads_across = remote(
         grads_in, grads_side, *side_sems, {"seq": lax.axis_index("seq") ^ 2}
@@ -1246,10 +1247,15 @@
     grad_steps = line_steps(count, grads_in, grads_vm, *grads_sems)
     next(grad_steps)
 
+    for n in range(2):
+        gain_rows[n][...] = gain_of(attn_vm, n)
+
     def deliver_two(total):
         made = (hidden[...] + total).astype(low)
         result_out[...] = made
         gain = gain_vm[...][0:1].astype(f32)
+        gain_rows[2][...] = gain
+        gain_rows[3][...] = gain_vm[...][1:2].astype(f32)
         normed_out[...] = normalise(made.astype(f32), gain).astype(low)
 
     run_with(
@@ -1562,11 +1568,12 @@
     gain_mlp_two, gain_attn_two, gain_mlp_one = take(3)
     hidden, ahead, grad_between, branch_out, grad_hidden_out = take(5)
     mlp_two_sum, attn_two_sum, mlp_one_sum = take(3)
-    wide_two, down_two, attn_two, out_two, wide_one, down_one = take(6)
+    grads_kept = take(6)
     carried_to = take(4)
     rows_two, grads_vm, partial, wide_vm, down_vm = take(5)
     log_total, units, pre_vm, pre_grads, normed_own, branch_own, grad_hidden = take(7)
-    load_done, carry_sent, carry_got = take(3)
+    load_done, carry_sent, carry_got, keep_done = take(4)
+    wide_two, down_two, attn_two, out_two, wide_one, down_one = take(6)
     line_sems = take(5)
     r = attn_back_refs(take)
     rows_one, heads, attn_vm, out_vm, partial_back = (
@@ -1662,8 +1669,15 @@
         (wide_two, down_two, attn_two, out_two), carried_to, carry_sent, carry_got
     )
 
+    made = (wide_two, down_two, attn_two, out_two, wide_one, down_one)
+    keeps = [
+        pltpu.make_async_copy(begin, end, keep_done.at[n])
+        for n, (begin, end) in enumerate(zip(made, grads_kept))
+    ]
+
     def background():
         carry(copies[:2], 0, "start")
+        start_all(keeps[:2])
         wide_loads[0] = pltpu.make_async_copy(gate_up.at[0], wide_vm, load_done.at[0])
         wide_loads[1] = pltpu.make_async_copy(down.at[0], down_vm, load_done.at[1])
         wide_loads[2] = pltpu.make_async_copy(wide_rows, rows_two, load_done.at[2])
@@ -1680,6 +1694,7 @@
         [],
     )
     carry(copies[2:], 0, "start")
+    start_all(keeps[2:4])
     steps = gather_steps(count, grad_between, grads_vm, *r.gather_sems)
     next(steps)
     wait_all(wide_loads)
@@ -1716,8 +1731,10 @@
     )
     for _ in steps:
         pass
+    start_all(keeps[4:])
     carry(copies, 0, "wait")
     save.wait()
+    wait_all(keeps)
 
 
 def last_kernel(count, *refs):
@@ -2174,7 +2191,7 @@
     half = ((blocks // 2, block, width), low, False)
     own_low, own_wide = ((block, width), low, True), ((block, width), f32, True)
     every = ((blocks, block, width), low, False)
-    gain_rows = ((8, width), f32, True)
+    gain_rows, one_row = ((8, width), f32, True), ((1, width), f32, True)
     weights_vm = [vmem((3 * PAD + 16, width), low), vmem((PAD, width), low)]
     wide_vm, down_vm = vmem((width, 2 * lanes), low), vmem((down_rows, width), low)
     (
@@ -2190,6 +2207,10 @@
         cosine,
         sine,
         start,
+        gain_attn_first,
+        gain_mlp_first,
+        gain_attn_second,
+        gain_mlp_second,
         hidden_one,
         between,
         normed,
@@ -2215,6 +2236,10 @@
             ((tokens, PAD), f32, True),
             ((tokens, PAD), f32, True),
             ((tokens, 1), jnp.int32, True),
+            one_row,
+            one_row,
+            one_row,
+            one_row,
             own_wide,
             own_low,
             own_low,
@@ -2237,7 +2262,6 @@
         + scatter(),
     )
     tables = [(cosine, True), (sine, True), (start, True)]
-    gains = attn[:, GAINS : GAINS + 2].astype(f32)
     back_scratch = (
         [all_blocks(), all_blocks(), vmem((4, tokens, PAD), low)]
         + weights_vm
@@ -2249,6 +2273,7 @@
     )
     attn_shape, out_shape = (3 * HEAD_DIM, width), (HEAD_DIM, width)
     wide_shape, down_shape = (width, 2 * lanes), (down_rows, width)
+    kept_shapes = [wide_shape, down_shape, attn_shape, out_shape, wide_shape, down_shape]
     (
         hidden_two,
         ahead,
@@ -2277,16 +2302,15 @@
         + [(attn, False), (twin, False), (out, False)]
         + [(grads_near, False), (gate_up, False), (down, False)]
         + [(cotangent, True), (hidden_one, True), (wide_rows_one, False)]
-        + [(gains[1, 1:2], True), (gains[1, 0:1], True), (gains[0, 1:2], True)],
+        + [(gain_mlp_second, True), (gain_attn_second, True), (gain_mlp_first, True)],
         [own_wide, every, own_low, own_low, own_wide, gain_rows, gain_rows, gain_rows]
-        + [(wide_shape, low, True), (down_shape, low, True)]
-        + [(attn_shape, low, True), (out_shape, low, True)]
-        + [(wide_shape, low, True), (down_shape, low, True)]
+        + [(shape, low, False) for shape in kept_shapes]
         + [(shape, low, False) for shape in (wide_shape, down_shape, attn_shape, out_shape)],
         [all_blocks(), all_blocks(), all_blocks(), wide_vm, down_vm]
         + [vmem((tokens, 1), f32), vmem((tokens, lanes), low), vmem((tokens, 2 * lanes), f32)]
         + [vmem((tokens, 2 * lanes), low), vmem((block, width), low), vmem((block, width), low)]
-        + [vmem((block, width), f32), dma((4,)), dma((4,)), dma((4,))]
+        + [vmem((block, width), f32), dma((4,)), dma((4,)), dma((4,)), dma((6,))]
+        + [vmem(shape, low) for shape in kept_shapes]
         + line_semaphores(count)
         + back_scratch,
     )
@@ -2295,7 +2319,7 @@
         + [(rows_one, False), (heads_one, False), (total_one, True)]
         + [(attn, False), (twin, False), (out, False)]
         + tables
-        + [(gains[0, 0:1], True)]
+        + [(gain_attn_first, True)]
     )
     query, key, value, out, gate, up, down, *swapped, gain_attn, gain_mlp = last_layer(
         count,

time: 501 us -> 497 us (level)
  no operation moved by 1% of the time
where the time goes in v10:
time: 497 us; the launch traced here: 489 us
  Pallas kernels  487 us (98%)
    pallas_call x3, Pallas kernels, call_kernel(): pl.pallas_call(kernel, out_shape=[jax.ShapeDtypeStruct(shape, dtype) for...  471 us
    pallas_call x1, Pallas kernels, widen(): pl.pallas_call(functools.partial(widen_kernel, pieces), grid=(steps,), ou...  15.7 us

profile of v10, /device:TPU:18, one launch (start us, length us, event | category | flops | bytes accessed | tf_op | source)
XLA Modules:
  0.0 488.6 jit_solution(16492794303282917961)
XLA Ops:
  0.6 0.5 fusion.2.refs_12_
  1.2 132.1 %first_layer.1 = (bf16[2,208,1536]{2,1,0:T(8,128)(2,1)}, bf16[2,96,1536]{2,1,0:T(8,128)(2,1)}, bf16[2,1536,512]{2,1,0:T(8,128)(2,1)}, bf16[2,96,1536]{2,1,0:T(8,...) custom-call(bf16[384,1536]{1,0:T(8,128)(2,1)} %bitcast.23, ...), custom_call_target="tpu_custom_call" | custom-call | tf_op jit(solution)/shard_map/first_layer/pallas_call | solution.py:2155
  133.3 187.0 %second_layer.1 = (f32[64,1536]{1,0:T(8,128)}, bf16[16,64,1536]{2,1,0:T(8,128)(2,1)}, bf16[64,1536]{1,0:T(8,128)(2,1)}, bf16[64,1536]{1,0:T(8,128)(2,1)}, f32[64...) custom-call(bf16[64,1536]{1,0:T(8,128)(2,1)} %get-tuple-element.69.r, ...), custom_call_target="tpu_custom_call" | custom-call | tf_op jit(solution)/shard_map/second_layer/pallas_call | solution.py:2155
  320.4 152.0 %last_layer_back.1 = (bf16[16,288,384]{2,1,0:T(8,128)(2,1)}, bf16[384,1536]{1,0:T(8,128)(2,1)}, bf16[384,4096]{1,0:T(8,128)(2,1)}, bf16[384,4096]{1,0:T(8,128)(2...) custom-call(bf16[64,1536]{1,0:T(8,128)(2,1)} %get-tuple-element.86.r, ...), custom_call_target="tpu_custom_call" | custom-call | tf_op jit(solution)/shard_map/last_layer_back/pallas_call | solution.py:2155
  472.4 15.7 %widen_gradients.1 = (f32[384,1536]{1,0:T(8,128)}, f32[384,768]{1,0:T(8,128)}, f32[384,768]{1,0:T(8,128)}, f32[384,1536]{1,0:T(8,128)}, f32[384,4096]{1,0:T(8,12...) custom-call(bf16[16,288,384]{2,1,0:T(8,128)(2,1)} %get-tuple-element, ...), custom_call_target="tpu_custom_call" | custom-call | tf_op jit(solution)/shard_map/widen_gradients/pallas_call | solution.py:2085

commit v11 on v10

--- a/solution.py
+++ b/solution.py
@@ -1131,7 +1131,7 @@
     raw_vm, normed_vm, rows_vm, partial, partial_two, grads_vm = take(6)
     attn_vm, out_vm, wide_vm, down_vm, units, normed_own, gain_vm = take(7)
     pieces, query_vm, other_vm, query_turned, other_turned, weights_done = take(6)
-    load_done, save_done, twin_sent, twin_got = take(4)
+    roots, load_done, save_done, twin_sent, twin_got = take(5)
     spread_sems = take(5)
     first_sems, second_sems, grads_sems, side_sems = take(7), take(7), take(5), take(2)
     scatter_one, scatter_two = take(12), take(12)
@@ -1177,6 +1177,11 @@
     for event in until_done(steps):
         if event == "side":
             advance(spread, 3)
+        group = group_of(event)
+        if group is not None:
+            span = pl.ds(group * count, count)
+            raw = raw_vm[span].astype(f32)
+            roots[span] = lax.rsqrt(jnp.mean(raw * raw, axis=-1, keepdims=True) + EPS)
     grads_across = remote(
         grads_in, grads_side, *side_sems, {"seq": lax.axis_index("seq") ^ 2}
     )
@@ -1196,7 +1201,8 @@
     wait_all(load_weights(0, attn, twin, None, attn_vm, out_vm, load_done) + [gain_load])
     for group in range(tokens // size):
         raw = raw_vm[group * count : (group + 1) * count].astype(f32)
-        normed = normalise(raw, gain_of(attn_vm, 0)[None]).astype(low)
+        root = roots[group * count : (group + 1) * count]
+        normed = (raw * root * gain_of(attn_vm, 0)[None]).astype(low)
         normed_vm[group * count : (group + 1) * count] = normed
         span = slice(group * size, (group + 1) * size)
         project_heads(normed.reshape(size, width), attn_vm, heads, span, cosine, sine)
@@ -2253,7 +2259,7 @@
         + [vmem((16, width), low), vmem(piece_shape, low)]
         + [vmem(local[1].shape, low), vmem(local[2].shape, low)]
         + [vmem(local[1].shape[::-1], low), vmem(local[2].shape[::-1], low), dma((2,))]
-        + [dma((6,)), dma((3,)), dma, dma]
+        + [vmem((blocks, block, 1), f32), dma((6,)), dma((3,)), dma, dma]
         + [dma((3, count)), dma((3, count)), dma((5, count)), dma((5, count)), dma((5,))]
         + gather_semaphores(count) * 2
         + line_semaphores(count)

time: 497 us -> 497 us (level)
  no operation moved by 1% of the time
where the time goes in v11:
time: 497 us; the launch traced here: 489 us
  Pallas kernels  487 us (98%)
    pallas_call x3, Pallas kernels, call_kernel(): pl.pallas_call(kernel, out_shape=[jax.ShapeDtypeStruct(shape, dtype) for...  471 us
    pallas_call x1, Pallas kernels, widen(): pl.pallas_call(functools.partial(widen_kernel, pieces), grid=(steps,), ou...  15.7 us

profile of v11, /device:TPU:18, one launch (start us, length us, event | category | flops | bytes accessed | tf_op | source)
XLA Modules:
  0.0 488.6 jit_solution(13203325941101901968)
XLA Ops:
  0.6 0.5 fusion.2.refs_12_
  1.2 132.1 %first_layer.1 = (bf16[2,208,1536]{2,1,0:T(8,128)(2,1)}, bf16[2,96,1536]{2,1,0:T(8,128)(2,1)}, bf16[2,1536,512]{2,1,0:T(8,128)(2,1)}, bf16[2,96,1536]{2,1,0:T(8,...) custom-call(bf16[384,1536]{1,0:T(8,128)(2,1)} %bitcast.23, ...), custom_call_target="tpu_custom_call" | custom-call | tf_op jit(solution)/shard_map/first_layer/pallas_call | solution.py:2161
  133.3 187.0 %second_layer.1 = (f32[64,1536]{1,0:T(8,128)}, bf16[16,64,1536]{2,1,0:T(8,128)(2,1)}, bf16[64,1536]{1,0:T(8,128)(2,1)}, bf16[64,1536]{1,0:T(8,128)(2,1)}, f32[64...) custom-call(bf16[64,1536]{1,0:T(8,128)(2,1)} %get-tuple-element.69.r, ...), custom_call_target="tpu_custom_call" | custom-call | tf_op jit(solution)/shard_map/second_layer/pallas_call | solution.py:2161
  320.4 152.0 %last_layer_back.1 = (bf16[16,288,384]{2,1,0:T(8,128)(2,1)}, bf16[384,1536]{1,0:T(8,128)(2,1)}, bf16[384,4096]{1,0:T(8,128)(2,1)}, bf16[384,4096]{1,0:T(8,128)(2...) custom-call(bf16[64,1536]{1,0:T(8,128)(2,1)} %get-tuple-element.86.r, ...), custom_call_target="tpu_custom_call" | custom-call | tf_op jit(solution)/shard_map/last_layer_back/pallas_call | solution.py:2161
  472.4 15.7 %widen_gradients.1 = (f32[384,1536]{1,0:T(8,128)}, f32[384,768]{1,0:T(8,128)}, f32[384,768]{1,0:T(8,128)}, f32[384,1536]{1,0:T(8,128)}, f32[384,4096]{1,0:T(8,12...) custom-call(bf16[16,288,384]{2,1,0:T(8,128)(2,1)} %get-tuple-element, ...), custom_call_target="tpu_custom_call" | custom-call | tf_op jit(solution)/shard_map/widen_gradients/pallas_call | solution.py:2091
